TPU v7x, 32 devices: a whole 2x2x4 slice. The times are simulated.
32 devices in a mesh: region: 2 (over core), patch: 16 (over z, y, x).
Axes of the slice: x: 2, y: 2, z: 4, core: 2. Of those that a mesh axis runs over, the one named last changes fastest.
Arguments:
- fine_input: bfloat16 [32, 64, 4096], P(('region', 'patch')), may hold values from -6 to 6
- fine_weight: bfloat16 [576, 64], replicated, may hold values from -0.25 to 0.25
- fine_bias: float32 [64], replicated, may hold values from -3 to 3
- cotangent: bfloat16 [32, 64, 4096], P(('region', 'patch')), may hold values from -6 to 6
- halo_index: int32 [32, 260], P('region'), may hold values from 0 to 8191, as said below
Outputs:
- input_grad: bfloat16 [32, 64, 4096], P(('region', 'patch'))
- weight_grad: float32 [576, 64], replicated
- bias_grad: float32 [64], replicated
Inputs may be any that keep to these rules, and one draw needn't show every extreme that they name: `halo_index`: entries in the top and bottom halo rows outside their first and last cell name top- or bottom-row rim entries of patches in the same region. All other entries (the four corner cells and the left and right halo columns) name left- or right-column rim entries of the patch at the same owner index in the region just before or just after (regions form a closed loop).
All inputs are finite; a program needn't handle non-finite values.
Results may differ from a plain program's by a relative error of at most 0.0075.
Values may be sent and summed in bfloat16 or wider, within the bound.
No kernel may reach another device: no remote copies, remote signals or barrier semaphores. Data moves between devices by JAX's collectives and lax.ppermute only.
A program may use at most 64 MiB of HBM per device.

v0:
```python
import functools
import math

import jax
import jax.numpy as jnp
from jax import lax
from jax.experimental import pallas as pl
from jax.experimental.pallas import tpu as pltpu
from jax.sharding import PartitionSpec as P

CHANNELS = 64
SIDE = 64
PAIRS = SIDE // 2
LANES = 2 * CHANNELS
ROWS = PAIRS * SIDE
WROWS = 5 * CHANNELS
F32 = jnp.float32
BF16 = jnp.bfloat16


def call(kernel, outs, *args, scratch=(), flops=0, moved=0):
    whole = pl.BlockSpec(memory_space=pltpu.VMEM)
    shapes = [jax.ShapeDtypeStruct(s, d) for s, d in outs]
    return pl.pallas_call(
        kernel,
        out_shape=shapes,
        in_specs=[whole] * len(args),
        out_specs=[whole] * len(outs),
        scratch_shapes=list(scratch),
        compiler_params=pltpu.CompilerParams(vmem_limit_bytes=48 * 2**20),
        cost_estimate=pl.CostEstimate(flops=flops, bytes_accessed=moved, transcendentals=0),
    )(*args)


def iota(shape, dim):
    return lax.broadcasted_iota(jnp.int32, shape, dim)


def low(shape):
    return iota(shape, len(shape) - 1) < CHANNELS


def turn(x):
    return pltpu.roll(x, CHANNELS, 1)


def tile(q):
    return pl.ds(pl.multiple_of(q * LANES, LANES), LANES)


def block(q):
    return pl.ds(pl.multiple_of(q * SIDE, SIDE), SIDE)


def dot(a, b, dims=((1,), (0,))):
    return lax.dot_general(a, b, (dims, ((), ())), preferred_element_type=F32)


NT = ((1,), (1,))
TN = ((0,), (0,))


def shifted_copies(load, p0, p1, p2):
    is_low = low((SIDE, LANES))
    row = iota((SIDE, LANES), 0)

    def put(q, before, now):
        v = jnp.where(is_low, before, now)
        p1[block(q), :] = v.astype(BF16)
        p0[block(q), :] = jnp.where(row == 0, 0.0, pltpu.roll(v, 1, 0)).astype(BF16)
        p2[block(q), :] = jnp.where(row == SIDE - 1, 0.0, pltpu.roll(v, SIDE - 1, 0)).astype(BF16)

    def step(q, before):
        now = turn(load(q))
        put(q, before, now)
        return now

    zero = jnp.zeros((SIDE, LANES), F32)
    last = lax.fori_loop(0, PAIRS, step, zero, unroll=2)
    put(PAIRS, last, zero)


def product(p0, p1, p2, w_ref, start, n, dims):
    total = None
    for a, p in enumerate((p0, p1, p2)):
        window = jnp.concatenate([p[pl.ds(start, n), :], p[pl.ds(start + SIDE, n), :]], axis=1)
        term = dot(window, w_ref[a], dims)
        total = term if total is None else total + term
    return total


def rim_kernel(x_ref, rows_ref, cols_ref, scr):
    for q in range(PAIRS):
        lanes = slice(q * LANES, (q + 1) * LANES)
        scr[q : q + 1, :] = x_ref[0:16, lanes].astype(F32)[0:1]
        scr[PAIRS + q : PAIRS + q + 1, :] = x_ref[SIDE - 16 : SIDE, lanes].astype(F32)[15:16]
    rows_ref[...] = scr[...].astype(BF16)
    first = x_ref[:, 0:LANES].astype(F32)
    last = x_ref[:, (PAIRS - 1) * LANES :].astype(F32)
    cols_ref[...] = jnp.where(low((SIDE, LANES)), first, last).astype(BF16)


def before_kernel(x_ref, w_ref, bias_ref, p0, p1, p2, s_ref):
    shifted_copies(lambda q: x_ref[:, tile(q)].astype(F32), p0, p1, p2)
    n = 4 * SIDE

    def step(c, carry):
        start = pl.multiple_of(c * n, n)
        s_ref[pl.ds(start, n), :] = product(p0, p1, p2, w_ref, start, n, NT) + bias_ref[0:1, :]
        return carry

    lax.fori_loop(0, ROWS // n, step, 0)


def slope_times(signal, upstream):
    sigma = 1.0 / (1.0 + jnp.exp(-signal))
    return upstream * (sigma * (1.0 + signal * (1.0 - sigma)))


def halves(even, odd):
    return jnp.where(low(even.shape), even, odd)


def middle_kernel(
    s_in, cot_ref, p0, p1, p2, rows_ref, cols_ref, hot_ref, half_ref, w_ref, wb_ref, wc_ref, scat_ref,
    g_ref, msg_ref, own_ref, sums_ref, s_ref, ht, hb, gt, gb, gc,
):
    many = rows_ref.shape[0]
    cells = dot(hot_ref[:, :many], rows_ref[...]) + dot(hot_ref[:, many:], cols_ref[...])
    other = turn(cells)
    upper = half_ref[...] > 0.5
    as_low = jnp.where(upper, other, cells)
    as_high = jnp.where(upper, cells, other)
    ht[...] = halves(as_low[0:40], as_high[40:80])
    hb[...] = halves(as_low[80:120], as_high[120:160])
    sides = halves(as_low[160:224], as_high[224:288])
    is_low = low((SIDE, LANES))
    row = iota((SIDE, LANES), 0)
    top = jnp.concatenate([ht[0:PAIRS, :], ht[1 : PAIRS + 1, :]], axis=1).astype(BF16)
    bottom = jnp.concatenate([hb[0:PAIRS, :], hb[1 : PAIRS + 1, :]], axis=1).astype(BF16)
    s_ref[...] = s_in[...]
    first = pl.ds(0, PAIRS, stride=SIDE)
    final = pl.ds(SIDE - 1, PAIRS, stride=SIDE)
    s_ref[first, :] += dot(top, w_ref[0], NT)
    s_ref[final, :] += dot(bottom, w_ref[2], NT)
    moved = (
        jnp.where(row == 0, 0.0, pltpu.roll(sides, 1, 0)),
        sides,
        jnp.where(row == SIDE - 1, 0.0, pltpu.roll(sides, SIDE - 1, 0)),
    )
    lefts = [jnp.where(is_low, m, 0.0).astype(BF16) for m in moved]
    rights = [jnp.where(is_low, 0.0, m).astype(BF16) for m in moved]
    for a in range(3):
        s_ref[0:SIDE, :] += dot(lefts[a], w_ref[a, :, 0:LANES], NT)
        s_ref[ROWS - SIDE : ROWS, :] += dot(rights[a], w_ref[a, :, LANES:], NT)

    def step(q, carry):
        bias, before = carry
        g = slope_times(s_ref[block(q), :], cot_ref[:, tile(q)].astype(F32)).astype(BF16)
        g_ref[block(q), :] = g
        wide = g.astype(F32)
        now = turn(wide)
        pair = jnp.where(is_low, before, now)
        gt[pl.ds(q, 1), :] = pair[0:1]
        gb[pl.ds(q, 1), :] = pair[SIDE - 1 :]
        s_ref[block(q), :] = wide
        return bias + jnp.sum(wide.reshape(8, 8, LANES), axis=0), now

    zero = jnp.zeros((SIDE, LANES), F32)
    bias, last = lax.fori_loop(0, PAIRS, step, (jnp.zeros((8, LANES), F32), zero), unroll=2)
    pair = jnp.where(is_low, last, 0.0)
    gt[PAIRS : PAIRS + 1, :] = pair[0:1]
    gb[PAIRS : PAIRS + 1, :] = pair[SIDE - 1 :]

    g = g_ref[...]
    g_first = s_ref[first, :].astype(BF16)
    g_final = s_ref[final, :].astype(BF16)
    terms = []
    for a, p in enumerate((p0, p1, p2)):
        for shift in (0, 1):
            t = dot(g, p[shift * SIDE : shift * SIDE + ROWS, :], TN)
            lanes = slice(shift * LANES, (shift + 1) * LANES)
            if a == 0:
                t += dot(g_first, top[:, lanes], TN)
            if a == 2:
                t += dot(g_final, bottom[:, lanes], TN)
            if shift == 0:
                t += dot(g[0:SIDE], lefts[a], TN)
            else:
                t += dot(g[ROWS - SIDE :], rights[a], TN)
            terms.append(t)

    def tap(m, high):
        a, b = m // 3, m % 3
        result = 0.0
        for e in (0, 1):
            w = e + b
            part = terms[2 * a + w // 2][e * CHANNELS : (e + 1) * CHANNELS]
            result = result + (part if (w % 2 == 1) == high else turn(part))
        return result

    total = jnp.sum(bias, axis=0, keepdims=True)
    total = total + turn(total)
    coarse = total.astype(BF16).astype(F32)
    fine = total - coarse
    for t in range(5):
        if t < 4:
            high = tap(2 * t + 1, True)
        else:
            high = jnp.where(row == 0, coarse, jnp.where(row == 1, fine, 0.0))
        msg_ref[t * SIDE : (t + 1) * SIDE, :] = halves(tap(2 * t, False), high).astype(BF16)

    for dest, src, tap_row in ((0, gt, 2), (1, gb, 0)):
        window = jnp.concatenate([src[0:PAIRS, :], src[1 : PAIRS + 1, :]], axis=1).astype(BF16)
        own_ref[dest * PAIRS : (dest + 1) * PAIRS, :] = dot(window, wb_ref[tap_row]).astype(BF16)

    gc[...] = jnp.zeros(gc.shape, F32)
    gc[8 : 8 + SIDE, :] = jnp.where(is_low, s_ref[0:SIDE, :], s_ref[ROWS - SIDE : ROWS, :])
    grads = dot(gc[8:88, :].astype(BF16), wc_ref[0])
    grads = grads + dot(gc[7:87, :].astype(BF16), wc_ref[1])
    grads = grads + dot(gc[6:86, :].astype(BF16), wc_ref[2])
    spread = dot(scat_ref[...], grads.astype(BF16))
    n = spread.shape[0] // 4
    l0, l1, r0, r1 = (spread[i * n : (i + 1) * n] for i in range(4))
    sums_ref[...] = halves(l0 + turn(r0), turn(l1) + r1).astype(BF16)


def inner_kernel(g_ref, wb_ref, out_ref, p0, p1, p2):
    shifted_copies(lambda q: g_ref[block(q), :].astype(F32), p0, p1, p2)
    n = 4 * SIDE

    def step(c, carry):
        start = pl.multiple_of(c * n, n)
        out_ref[pl.ds(start, n), :] = product(p0, p1, p2, wb_ref, start, n, ((1,), (0,)))
        return carry

    lax.fori_loop(0, ROWS // n, step, 0)


def added_weights(mine, other):
    total = mine[0:WROWS, :].astype(F32) + other[0:WROWS, :].astype(F32)
    tail = total[WROWS - SIDE :]
    whole = tail + pltpu.roll(tail, SIDE - 1, 0)
    return total[: WROWS - SIDE], tail, whole


def join_kernel(mine, other, *rest):
    extra, out = rest[:-1], rest[-1]
    total, tail, whole = added_weights(mine, other)
    out[0 : WROWS - SIDE, :] = total.astype(BF16)
    row = iota(tail.shape, 0)
    coarse = whole.astype(BF16).astype(F32)
    fine = pltpu.roll(whole - coarse, 1, 0)
    is_low = low(tail.shape)
    out[WROWS - SIDE : WROWS, :] = jnp.where(
        is_low, tail, jnp.where(row == 0, coarse, jnp.where(row == 1, fine, 0.0))
    ).astype(BF16)
    n = mine.shape[0] - WROWS
    if n:
        out[WROWS : WROWS + n, :] = mine[WROWS:, :]
        out[WROWS + n :, :] = other[WROWS:, :]
    if extra:
        out[WROWS:, :] = extra[0][...]


def last_kernel(scale, mine, other, inner, pick, side_a, side_b, grad_ref, wt_ref, bias_ref):
    total, tail, whole = added_weights(mine, other)
    for t in range(4):
        wt_ref[:, t * LANES : (t + 1) * LANES] = total[t * SIDE : (t + 1) * SIDE] * scale
    wt_ref[:, 4 * LANES :] = tail[:, :CHANNELS] * scale
    bias_ref[...] = turn(whole)[0:8] * scale
    n = mine.shape[0] - WROWS
    got = dot(pick[:, :n], mine[WROWS:, :]) + dot(pick[:, n:], other[WROWS:, :])
    a, b, c, d = (got[i * SIDE : (i + 1) * SIDE] for i in range(4))
    rims = halves(a + turn(b), turn(c) + d)
    sides = side_a[...].astype(F32)
    if side_b is not None:
        sides = sides + side_b[...].astype(F32)
    row = iota((SIDE, LANES), 0)
    is_low = low((SIDE, LANES))
    for q in range(PAIRS):
        v = inner[q * SIDE : (q + 1) * SIDE, :]
        v = v + jnp.where(row == 0, rims[q : q + 1], jnp.where(row == SIDE - 1, rims[PAIRS + q : PAIRS + q + 1], 0.0))
        if q == 0:
            v = v + jnp.where(is_low, sides, 0.0)
        if q == PAIRS - 1:
            v = v + jnp.where(is_low, 0.0, sides)
        grad_ref[:, q * LANES : (q + 1) * LANES] = v.astype(BF16)


def swap(x, axis, k):
    n = lax.axis_size(axis)
    return lax.ppermute(x, axis, [(i, i ^ k) for i in range(n)])


def shift(x, axis, by):
    n = lax.axis_size(axis)
    return lax.ppermute(x, axis, [(i, (i + by) % n) for i in range(n)])


def steps_of(n):
    ks = []
    k = n // 2
    while k:
        ks.append(k)
        k //= 2
    return ks


def slot_of(relative, ks):
    slot = jnp.zeros_like(relative)
    for bit, k in enumerate(ks):
        slot = slot + jnp.where((relative & k) != 0, 1 << bit, 0)
    return slot


def owner_of(slot, ks):
    result = jnp.zeros_like(slot)
    for bit, k in enumerate(ks):
        result = result + jnp.where((slot >> bit) & 1 != 0, k, 0)
    return result


def weights_of(fine_weight):
    wt = fine_weight.T.reshape(CHANNELS, 3, 3 * CHANNELS)
    zero = jnp.zeros((CHANNELS, CHANNELS), BF16)
    forward, backward, columns = [], [], []
    for a in range(3):
        rows = wt[:, a]
        forward.append(
            jnp.concatenate(
                [jnp.concatenate([rows, zero], axis=1), jnp.concatenate([zero, rows], axis=1)], axis=0
            )
        )
        taps = [wt[:, 2 - a, b * CHANNELS : (b + 1) * CHANNELS] for b in (2, 1, 0)]
        backward.append(
            jnp.concatenate(
                [jnp.concatenate(taps + [zero], axis=0), jnp.concatenate([zero] + taps, axis=0)], axis=1
            )
        )
        columns.append(
            jnp.concatenate(
                [
                    jnp.concatenate([rows[:, :CHANNELS], zero], axis=1),
                    jnp.concatenate([zero, rows[:, 2 * CHANNELS :]], axis=1),
                ],
                axis=0,
            )
        )
    return jnp.stack(forward), jnp.stack(backward), jnp.stack(columns)


def body(fine_input, fine_weight, fine_bias, cotangent, halo_index):
    owners = lax.axis_size("patch")
    regions = lax.axis_size("region")
    owner_id = lax.axis_index("patch")
    region_id = lax.axis_index("region")
    ks = steps_of(owners)
    blocks = 1 if regions == 2 else 2
    x = fine_input.reshape(SIDE, SIDE * CHANNELS)
    cot = cotangent.reshape(SIDE, SIDE * CHANNELS)
    pair = ((ROWS + SIDE, LANES), BF16)

    rows, cols = call(
        rim_kernel, [((SIDE, LANES), BF16)] * 2, x, scratch=[pltpu.VMEM((SIDE, LANES), F32)]
    )
    if regions == 2:
        cols = swap(cols, "region", 1)
    else:
        cols = jnp.concatenate([shift(cols, "region", 1), shift(cols, "region", -1)], axis=0)
    for k in ks:
        rows = jnp.concatenate([rows, swap(rows, "patch", k)], axis=0)

    forward, backward, columns = weights_of(fine_weight)
    bias_pair = jnp.broadcast_to(jnp.tile(fine_bias, 2)[None], (8, LANES))
    p0, p1, p2, signal = call(
        before_kernel, [pair, pair, pair, ((ROWS, LANES), F32)], x, forward, bias_pair,
        flops=2 * ROWS * 768 * 128, moved=4 * 2**20,
    )

    own = lax.dynamic_index_in_dim(halo_index, owner_id, 0, keepdims=False)
    source, within = own // (4 * SIDE), own % (4 * SIDE)
    is_row = within < 2 * SIDE
    slot = slot_of((source % owners) ^ owner_id, ks)
    after = (source // owners - region_id) % regions == 1
    column_row = within % SIDE + (0 if blocks == 1 else jnp.where(after, SIDE, 0))
    column_half = (within - 2 * SIDE) // SIDE
    place = jnp.where(is_row, slot * SIDE + within // 2, owners * SIDE + column_row)
    half = jnp.where(is_row, within % 2, column_half)

    def cells_of(v, fill):
        def padded(u):
            return jnp.concatenate([u, jnp.full((40 - PAIRS - 1,), fill, v.dtype)])

        top, bottom = v[0 : SIDE + 2], v[SIDE + 2 : 2 * SIDE + 4]
        return jnp.concatenate(
            [padded(top[0::2]), padded(top[1::2]), padded(bottom[0::2]), padded(bottom[1::2]), v[2 * SIDE + 4 :]]
        )

    hot = (cells_of(place, -1)[:, None] == jnp.arange((owners + blocks) * SIDE)[None]).astype(BF16)
    half_mask = jnp.broadcast_to(cells_of(half, 0).astype(F32)[:, None], (hot.shape[0], LANES))

    def ring(v, fill):
        edge = 2 * SIDE + 4
        pad = jnp.full((80 - SIDE - 2,), fill, v.dtype)
        left = jnp.concatenate([v[0:1], v[edge : edge + SIDE], v[SIDE + 2 : SIDE + 3], pad])
        right = jnp.concatenate([v[SIDE + 1 : SIDE + 2], v[edge + SIDE :], v[edge - 1 : edge], pad])
        return left, right

    scatter = []
    for row_of, half_of in zip(ring(column_row, -1), ring(column_half, 0)):
        for s in range(2):
            scatter.append(
                (jnp.arange(blocks * SIDE)[:, None] == jnp.where(half_of == s, row_of, -1)[None]).astype(BF16)
            )
    scatter = jnp.concatenate(scatter, axis=0)

    wanted = jnp.concatenate([halo_index[:, 1 : SIDE + 1], halo_index[:, SIDE + 3 : 2 * SIDE + 3]], axis=1)
    wanted = jnp.take(wanted, owner_id ^ owner_of(jnp.arange(owners), ks), axis=0)
    wanted = wanted - (region_id * owners + owner_id) * 4 * SIDE
    wanted = wanted.reshape(owners * SIDE, 2)
    pick = jnp.concatenate(
        [
            ((2 * jnp.arange(SIDE) + e)[:, None] == wanted[:, s][None]).astype(BF16)
            for e in range(2)
            for s in range(2)
        ],
        axis=0,
    )

    line = pltpu.VMEM((40, LANES), F32)
    grad, message, own_rows, sums = call(
        middle_kernel,
        [((ROWS, LANES), BF16), ((WROWS, LANES), BF16), ((SIDE, LANES), BF16), ((blocks * SIDE, LANES), BF16)],
        signal, cot, p0, p1, p2, rows, cols, hot, half_mask, forward, backward, columns, scatter,
        scratch=[pltpu.VMEM((ROWS, LANES), F32), line, line, line, line, pltpu.VMEM((96, LANES), F32)],
        flops=2 * ROWS * 768 * 128, moved=4 * 2**20,
    )

    if regions == 2:
        sides = [swap(sums, "region", 1)]
    else:
        sides = [shift(sums[SIDE:], "region", 1), shift(sums[:SIDE], "region", -1)]
    inner = call(
        inner_kernel, [((ROWS, LANES), F32)], grad, backward,
        scratch=[pltpu.VMEM((ROWS + SIDE, LANES), BF16)] * 3,
        flops=2 * ROWS * 768 * 128, moved=4 * 2**20,
    )[0]

    region_ks = steps_of(regions)
    for k in region_ks:
        extra = (own_rows,) if k == region_ks[-1] else ()
        size = (WROWS + SIDE * len(extra), LANES)
        message = call(join_kernel, [(size, BF16)], message, swap(message, "region", k), *extra)[0]
    for k in ks[:-1]:
        size = (2 * message.shape[0] - WROWS, LANES)
        message = call(join_kernel, [(size, BF16)], message, swap(message, "patch", k))[0]
    other = swap(message, "patch", ks[-1])
    scale = 1.0 / math.sqrt(regions * owners * SIDE * SIDE)
    kernel = functools.partial(last_kernel, scale)
    if len(sides) == 1:
        kernel = functools.partial(last_one_side, scale)
    input_grad, weight_grad, bias_grad = call(
        kernel,
        [((SIDE, SIDE * CHANNELS), BF16), ((CHANNELS, 9 * CHANNELS), F32), ((8, LANES), F32)],
        message, other, inner, pick, *sides,
    )
    return input_grad.reshape(1, SIDE, SIDE * CHANNELS), weight_grad.T, bias_grad[0, :CHANNELS]


def last_one_side(scale, mine, other, inner, pick, side_a, grad_ref, wt_ref, bias_ref):
    last_kernel(scale, mine, other, inner, pick, side_a, None, grad_ref, wt_ref, bias_ref)


def solution(mesh):
    placed = (
        P(("region", "patch"), None, None),
        P(),
        P(),
        P(("region", "patch"), None, None),
        P("region", None),
    )
    return jax.shard_map(
        body,
        mesh=mesh,
        in_specs=placed,
        out_specs=(P(("region", "patch"), None, None), P(), P()),
        check_vma=False,
    )
```

profile of v0, /device:TPU:0, one launch (start us, length us, event | category | flops | bytes accessed | tf_op | source)
XLA Modules:
  0.0 62.9 jit_solution(10317187437564250205)
XLA Ops:
  0.6 1.0 %copy-done.1 = bf16[1,64,4096]{2,1,0:T(8,128)(2,1)S(1)} copy-done((bf16[1,64,4096]{2,1,0:T(8,128)(2,1)S(1)}, bf16[1,64,4096]{2,1,0:T(8,128)(2,1)}, u32[]{:S(2)}) %copy-start.1) | copy-done | bytes 524312
  1.7 4.1 %collective-permute-start = (bf16[64,128]{1,0:T(8,128)(2,1)S(1)}, bf16[64,128]{1,0:T(8,128)(2,1)S(1)}, u32[]{:S(2)}, u32[]{:S(2)}) collective-permute-start(bf16[64,128]{1,0:T(8,128)(2,1)S(1)} %get-tuple-element.20), channel_id=1, source_target_pairs={{0,8},{1,9},{2,10},{3,11},{4,12},{5,13},{6,14},{7,15},{8,0},{9,1},... | collective-permute-start | bytes 49160 | tf_op jit(solution)/shard_map/ppermute | solution.py:293
  5.8 0.7 %dynamic-slice_reduce_fusion = s32[260]{0:T(512)S(1)} fusion(s32[16,260]{1,0:T(8,128)} %param.9, s32[]{:T(128)S(6)} %select_n.160), kind=kLoop, calls=%fused_computation.136 | loop fusion | bytes 2084 | tf_op jit(solution)/shard_map/jit(dynamic_index_in_dim)/dynamic_slice | solution.py:381
  6.6 0.7 %fusion.64 = (s32[1]{0:T(128)}, s32[1]{0:T(128)}, s32[1]{0:T(128)}, s32[1]{0:T(128)}, s32[1]{0:T(128)}, /*index=5*/s32[1]{0:T(128)}, s32[1]{0:T(128)}, s32[1]{0:T(128)}) fusion(s32[260]{0:T(512)S(1)} %get-tuple-element.69, s32[260]{0:T(512)S(1)} %get-tuple-element.70), kind=kLoop, calls=%fused_computation.175 | loop fusion | bytes 64 | tf_op jit(solution)/shard_map/slice | solution.py:406
  8.0 1.0 %reshape.381 = bf16[64,3,192]{2,1,0:T(4,128)(2,1)S(1)} reshape(bf16[64,576]{1,0:T(8,128)(2,1)} %bitcast.59) | data formatting | bytes 147456 | tf_op jit(solution)/shard_map/reshape | solution.py:325
  9.8 5.1 %compare_select_fusion.13 = (s32[80]{0:T(128)S(1)}, s32[80]{0:T(128)S(1)}, s32[80]{0:T(128)S(1)}, s32[80]{0:T(128)S(1)}, s32[80]{0:T(128)S(1)}, /*index=5*/s32[80]{0:T(128)S(1)}) fusion(s32[14]{0:T(128)S(1)} %concatenate.203, s32[1]{0:T(128)} %get-tuple-element.88, s32[64]{0:T(128)S(1)} %get-tuple-element.92, s32[1]{0:T(128)} %get-tuple-element.90, ...), kind=kLoop, calls=%fused_computation.135 | loop fusion | flops 1280 | bytes 3088 | tf_op jit(solution)/shard_map/jit(_where)/select_n | solution.py:414
  16.9 1.6 %collective-permute-start.1 = (bf16[128,128]{1,0:T(8,128)(2,1)S(1)}, bf16[128,128]{1,0:T(8,128)(2,1)S(1)}, u32[]{:S(2)}, u32[]{:S(2)}) collective-permute-start(bf16[128,128]{1,0:T(8,128)(2,1)S(1)} %pad_maximum_fusion.11), channel_id=1, source_target_pairs={{0,4},{1,5},{2,6},{3,7},{4,0},{5,1},{6,2},{7,3},{8,12},{9,13},{10,... | collective-permute-start | bytes 98312 | tf_op jit(solution)/shard_map/ppermute | solution.py:293
  18.5 3.6 %shard_map.76 = (bf16[2112,128]{1,0:T(8,128)(2,1)S(1)}, bf16[2112,128]{1,0:T(8,128)(2,1)S(1)}, bf16[2112,128]{1,0:T(8,128)(2,1)S(1)}, f32[2048,128]{1,0:T(8,128)S(1)}) custom-call(bf16[64,4096]{1,0:T(8,128)(2,1)S(1)} %bitcast.55, bf16[3,128,256]{2,1,0:T(8,128)(2,1)S(1)} %pad_maximum_fusion.w_ref, f32[8,128]{1,0:T(8,128)S(1)} %broadcast_in_dim.82.bias_ref), custom_call_target="tpu_custom_call" | custom-call | flops 402653184 | bytes 4194304 | tf_op jit(solution)/shard_map/pallas_call | solution.py:24
  22.2 1.6 %collective-permute-start.2 = (bf16[256,128]{1,0:T(8,128)(2,1)S(1)}, bf16[256,128]{1,0:T(8,128)(2,1)S(1)}, u32[]{:S(2)}, u32[]{:S(2)}) collective-permute-start(bf16[256,128]{1,0:T(8,128)(2,1)S(1)} %pad_maximum_fusion.10), channel_id=1, source_target_pairs={{0,2},{1,3},{2,0},{3,1},{4,6},{5,7},{6,4},{7,5},{8,10},{9,11},{10,... | collective-permute-start | bytes 196616 | tf_op jit(solution)/shard_map/ppermute | solution.py:293
  23.8 2.7 %collective-permute-done.2 = bf16[256,128]{1,0:T(8,128)(2,1)S(1)} collective-permute-done((bf16[256,128]{1,0:T(8,128)(2,1)S(1)}, bf16[256,128]{1,0:T(8,128)(2,1)S(1)}, u32[]{:S(2)}, u32[]{:S(2)}) %collective-permute-start.2) | collective-permute-done | bytes 65568 | tf_op jit(solution)/shard_map/ppermute | solution.py:293
  26.5 1.6 %collective-permute-start.3 = (bf16[512,128]{1,0:T(8,128)(2,1)S(1)}, bf16[512,128]{1,0:T(8,128)(2,1)S(1)}, u32[]{:S(2)}, u32[]{:S(2)}) collective-permute-start(bf16[512,128]{1,0:T(8,128)(2,1)S(1)} %pad_maximum_fusion.2), channel_id=1, source_target_pairs={{0,1},{1,0},{2,3},{3,2},{4,5},{5,4},{6,7},{7,6},{8,9},{9,8},{10,11... | collective-permute-start | bytes 393224 | tf_op jit(solution)/shard_map/ppermute | solution.py:293
  28.1 3.5 %collective-permute-done.3 = bf16[512,128]{1,0:T(8,128)(2,1)S(1)} collective-permute-done((bf16[512,128]{1,0:T(8,128)(2,1)S(1)}, bf16[512,128]{1,0:T(8,128)(2,1)S(1)}, u32[]{:S(2)}, u32[]{:S(2)}) %collective-permute-start.3) | collective-permute-done | bytes 131104 | tf_op jit(solution)/shard_map/ppermute | solution.py:293
  31.7 3.8 %shard_map.78 = (bf16[2048,128]{1,0:T(8,128)(2,1)S(1)}, bf16[320,128]{1,0:T(8,128)(2,1)S(1)}, bf16[64,128]{1,0:T(8,128)(2,1)S(1)}, bf16[64,128]{1,0:T(8,128)(2,1)S(1)}) custom-call(f32[2048,128]{1,0:T(8,128)S(1)} %get-tuple-element.16.s_in, bf16[64,4096]{1,0:T(8,128)(2,1)S(1)} %bitcast.53, bf16[2112,128]{1,0:T(8,128)(2,1)S(1)} %get-tuple-element.17.p0, ...), custom_call_target="tpu_custom_call" | custom-call | flops 402653184 | bytes 4194304 | tf_op jit(solution)/shard_map/pallas_call | solution.py:24
  35.6 0.6 gather_fusion
  37.4 7.4 %collective-permute-done.6.other = bf16[384,128]{1,0:T(8,128)(2,1)S(1)} collective-permute-done((bf16[384,128]{1,0:T(8,128)(2,1)S(1)}, bf16[384,128]{1,0:T(8,128)(2,1)S(1)}, u32[]{:S(2)}, u32[]{:S(2)}) %collective-permute-start.6) | collective-permute-done | bytes 98336 | tf_op jit(solution)/shard_map/ppermute | solution.py:293
  45.1 4.9 %collective-permute-done.7.other = bf16[448,128]{1,0:T(8,128)(2,1)S(1)} collective-permute-done((bf16[448,128]{1,0:T(8,128)(2,1)S(1)}, bf16[448,128]{1,0:T(8,128)(2,1)S(1)}, u32[]{:S(2)}, u32[]{:S(2)}) %collective-permute-start.7) | collective-permute-done | bytes 114720 | tf_op jit(solution)/shard_map/ppermute | solution.py:293
  50.0 1.6 %collective-permute-start.8 = (bf16[576,128]{1,0:T(8,128)(2,1)S(1)}, bf16[576,128]{1,0:T(8,128)(2,1)S(1)}, u32[]{:S(2)}, u32[]{:S(2)}) collective-permute-start(bf16[576,128]{1,0:T(8,128)(2,1)S(1)} %shard_map.81.mine), channel_id=1, source_target_pairs={{0,2},{1,3},{2,0},{3,1},{4,6},{5,7},{6,4},{7,5},{8,10},{9,11},{10,... | collective-permute-start | bytes 442376 | tf_op jit(solution)/shard_map/ppermute | solution.py:293
  51.6 0.5 slice_reduce_fusion.1
  52.1 3.1 %collective-permute-done.8.other = bf16[576,128]{1,0:T(8,128)(2,1)S(1)} collective-permute-done((bf16[576,128]{1,0:T(8,128)(2,1)S(1)}, bf16[576,128]{1,0:T(8,128)(2,1)S(1)}, u32[]{:S(2)}, u32[]{:S(2)}) %collective-permute-start.8) | collective-permute-done | bytes 147488 | tf_op jit(solution)/shard_map/ppermute | solution.py:293
  55.3 1.6 %collective-permute-start.9 = (bf16[832,128]{1,0:T(8,128)(2,1)S(1)}, bf16[832,128]{1,0:T(8,128)(2,1)S(1)}, u32[]{:S(2)}, u32[]{:S(2)}) collective-permute-start(bf16[832,128]{1,0:T(8,128)(2,1)S(1)} %shard_map.82.mine), channel_id=1, source_target_pairs={{0,1},{1,0},{2,3},{3,2},{4,5},{5,4},{6,7},{7,6},{8,9},{9,8},{10,11... | collective-permute-start | bytes 638984 | tf_op jit(solution)/shard_map/ppermute | solution.py:293
  57.2 3.5 %shard_map.83.inner = f32[2048,128]{1,0:T(8,128)S(1)} custom-call(bf16[2048,128]{1,0:T(8,128)(2,1)S(1)} %get-tuple-element.24.g_ref, bf16[3,256,128]{2,1,0:T(8,128)(2,1)S(1)} %pad_maximum_fusion.1.wb_ref), custom_call_target="tpu_custom_call" | custom-call | flops 402653184 | bytes 4194304 | tf_op jit(solution)/shard_map/pallas_call | solution.py:24
  60.7 0.5 collective-permute-done.9.other
  61.2 1.2 %shard_map.84 = (bf16[64,4096]{1,0:T(8,128)(2,1)}, f32[64,576]{1,0:T(8,128)}, f32[8,128]{1,0:T(8,128)S(1)}) custom-call(bf16[832,128]{1,0:T(8,128)(2,1)S(1)} %shard_map.82.mine, bf16[832,128]{1,0:T(8,128)(2,1)S(1)} %collective-permute-done.9.other, f32[2048,128]{1,0:T(8,128)S(1)} %shard_map.83.inner, bf16[256,1024]{1,0:T(8,128)(2,1)S(1)} %add_convert_fusion.pick, ...), custom_call_target="tpu_custom_call" | custom-call | tf_op jit(solution)/shard_map/pallas_call | solution.py:24
  62.4 0.5 slice_bitcast_fusion
  (103 shorter events, 5.6 us)
Async XLA Ops:
  0.6 1.0 %copy-start.1 = (bf16[1,64,4096]{2,1,0:T(8,128)(2,1)S(1)}, bf16[1,64,4096]{2,1,0:T(8,128)(2,1)}, u32[]{:S(2)}) copy-start(bf16[1,64,4096]{2,1,0:T(8,128)(2,1)} %param.5) | copy-start | bytes 1572868
  1.7 8.0 %copy-start.3 = (s32[16,260]{1,0:T(8,128)S(1)}, s32[16,260]{1,0:T(8,128)}, u32[]{:S(2)}) copy-start(s32[16,260]{1,0:T(8,128)} %param.9) | copy-start | bytes 49924
  1.7 15.2 %collective-permute-start = (bf16[64,128]{1,0:T(8,128)(2,1)S(1)}, bf16[64,128]{1,0:T(8,128)(2,1)S(1)}, u32[]{:S(2)}, u32[]{:S(2)}) collective-permute-start(bf16[64,128]{1,0:T(8,128)(2,1)S(1)} %get-tuple-element.20), channel_id=1, source_target_pairs={{0,8},{1,9},{2,10},{3,11},{4,12},{5,13},{6,14},{7,15},{8,0},{9,1},... | collective-permute-start | bytes 49160 | tf_op jit(solution)/shard_map/ppermute | solution.py:293
  5.8 25.8 %collective-permute-start.4 = (bf16[64,128]{1,0:T(8,128)(2,1)S(1)}, bf16[64,128]{1,0:T(8,128)(2,1)S(1)}, u32[]{:S(2)}, u32[]{:S(2)}) collective-permute-start(bf16[64,128]{1,0:T(8,128)(2,1)S(1)} %get-tuple-element.21), channel_id=1, source_target_pairs={{0,16},{16,0},{1,17},{17,1},{2,18},{18,2},{3,19},{19,3},{4,20},{20... | collective-permute-start | bytes 49160 | tf_op jit(solution)/shard_map/ppermute | solution.py:293
  9.3 6.1 %copy-start.4 = (pred[128]{0:T(512)(128)(4,1)S(1)}, pred[128]{0:T(512)(128)(4,1)}, u32[]{:S(2)}) copy-start(pred[128]{0:T(512)(128)(4,1)} %constant.136.clone.1) | copy-start | bytes 388
  15.4 1.4 %copy-start.5 = (f32[64]{0:T(128)S(1)}, f32[64]{0:T(128)}, u32[]{:S(2)}) copy-start(f32[64]{0:T(128)} %param.7) | copy-start | bytes 772
  15.4 3.1 %copy-start.2 = (bf16[1,64,4096]{2,1,0:T(8,128)(2,1)S(1)}, bf16[1,64,4096]{2,1,0:T(8,128)(2,1)}, u32[]{:S(2)}) copy-start(bf16[1,64,4096]{2,1,0:T(8,128)(2,1)} %param.5) | copy-start | bytes 1572868
  16.9 5.3 %collective-permute-start.1 = (bf16[128,128]{1,0:T(8,128)(2,1)S(1)}, bf16[128,128]{1,0:T(8,128)(2,1)S(1)}, u32[]{:S(2)}, u32[]{:S(2)}) collective-permute-start(bf16[128,128]{1,0:T(8,128)(2,1)S(1)} %pad_maximum_fusion.11), channel_id=1, source_target_pairs={{0,4},{1,5},{2,6},{3,7},{4,0},{5,1},{6,2},{7,3},{8,12},{9,13},{10,... | collective-permute-start | bytes 98312 | tf_op jit(solution)/shard_map/ppermute | solution.py:293
  18.5 13.2 %copy-start = (bf16[1,64,4096]{2,1,0:T(8,128)(2,1)S(1)}, bf16[1,64,4096]{2,1,0:T(8,128)(2,1)}, u32[]{:S(2)}) copy-start(bf16[1,64,4096]{2,1,0:T(8,128)(2,1)} %param.8) | copy-start | bytes 1572868
  22.2 4.3 %collective-permute-start.2 = (bf16[256,128]{1,0:T(8,128)(2,1)S(1)}, bf16[256,128]{1,0:T(8,128)(2,1)S(1)}, u32[]{:S(2)}, u32[]{:S(2)}) collective-permute-start(bf16[256,128]{1,0:T(8,128)(2,1)S(1)} %pad_maximum_fusion.10), channel_id=1, source_target_pairs={{0,2},{1,3},{2,0},{3,1},{4,6},{5,7},{6,4},{7,5},{8,10},{9,11},{10,... | collective-permute-start | bytes 196616 | tf_op jit(solution)/shard_map/ppermute | solution.py:293
  26.5 5.0 %collective-permute-start.3 = (bf16[512,128]{1,0:T(8,128)(2,1)S(1)}, bf16[512,128]{1,0:T(8,128)(2,1)S(1)}, u32[]{:S(2)}, u32[]{:S(2)}) collective-permute-start(bf16[512,128]{1,0:T(8,128)(2,1)S(1)} %pad_maximum_fusion.2), channel_id=1, source_target_pairs={{0,1},{1,0},{2,3},{3,2},{4,5},{5,4},{6,7},{7,6},{8,9},{9,8},{10,11... | collective-permute-start | bytes 393224 | tf_op jit(solution)/shard_map/ppermute | solution.py:293
  35.5 1.3 %collective-permute-start.5 = (bf16[320,128]{1,0:T(8,128)(2,1)S(1)}, bf16[320,128]{1,0:T(8,128)(2,1)S(1)}, u32[]{:S(2)}, u32[]{:S(2)}) collective-permute-start(bf16[320,128]{1,0:T(8,128)(2,1)S(1)} %get-tuple-element.22.mine), channel_id=1, source_target_pairs={{0,16},{16,0},{1,17},{17,1},{2,18},{18,2},{3,19},{19,3},{4,20},{20... | collective-permute-start | bytes 245768 | tf_op jit(solution)/shard_map/ppermute | solution.py:293
  36.8 8.0 %collective-permute-start.6 = (bf16[384,128]{1,0:T(8,128)(2,1)S(1)}, bf16[384,128]{1,0:T(8,128)(2,1)S(1)}, u32[]{:S(2)}, u32[]{:S(2)}) collective-permute-start(bf16[384,128]{1,0:T(8,128)(2,1)S(1)} %shard_map.79.mine), channel_id=1, source_target_pairs={{0,8},{1,9},{2,10},{3,11},{4,12},{5,13},{6,14},{7,15},{8,0},{9,1},... | collective-permute-start | bytes 294920 | tf_op jit(solution)/shard_map/ppermute | solution.py:293
  44.8 5.2 %collective-permute-start.7 = (bf16[448,128]{1,0:T(8,128)(2,1)S(1)}, bf16[448,128]{1,0:T(8,128)(2,1)S(1)}, u32[]{:S(2)}, u32[]{:S(2)}) collective-permute-start(bf16[448,128]{1,0:T(8,128)(2,1)S(1)} %shard_map.80.mine), channel_id=1, source_target_pairs={{0,4},{1,5},{2,6},{3,7},{4,0},{5,1},{6,2},{7,3},{8,12},{9,13},{10,... | collective-permute-start | bytes 344072 | tf_op jit(solution)/shard_map/ppermute | solution.py:293
  50.0 5.2 %collective-permute-start.8 = (bf16[576,128]{1,0:T(8,128)(2,1)S(1)}, bf16[576,128]{1,0:T(8,128)(2,1)S(1)}, u32[]{:S(2)}, u32[]{:S(2)}) collective-permute-start(bf16[576,128]{1,0:T(8,128)(2,1)S(1)} %shard_map.81.mine), channel_id=1, source_target_pairs={{0,2},{1,3},{2,0},{3,1},{4,6},{5,7},{6,4},{7,5},{8,10},{9,11},{10,... | collective-permute-start | bytes 442376 | tf_op jit(solution)/shard_map/ppermute | solution.py:293
  55.3 5.9 %collective-permute-start.9 = (bf16[832,128]{1,0:T(8,128)(2,1)S(1)}, bf16[832,128]{1,0:T(8,128)(2,1)S(1)}, u32[]{:S(2)}, u32[]{:S(2)}) collective-permute-start(bf16[832,128]{1,0:T(8,128)(2,1)S(1)} %shard_map.82.mine), channel_id=1, source_target_pairs={{0,1},{1,0},{2,3},{3,2},{4,5},{5,4},{6,7},{7,6},{8,9},{9,8},{10,11... | collective-permute-start | bytes 638984 | tf_op jit(solution)/shard_map/ppermute | solution.py:293
  57.1 3.6 %collective-permute-start.10 = (bf16[64,128]{1,0:T(8,128)(2,1)S(1)}, bf16[64,128]{1,0:T(8,128)(2,1)S(1)}, u32[]{:S(2)}, u32[]{:S(2)}) collective-permute-start(bf16[64,128]{1,0:T(8,128)(2,1)S(1)} %get-tuple-element.25), channel_id=1, source_target_pairs={{0,16},{16,0},{1,17},{17,1},{2,18},{18,2},{3,19},{19,3},{4,20},{20... | collective-permute-start | bytes 49160 | tf_op jit(solution)/shard_map/ppermute | solution.py:293
where the time goes:
time: 63.2 us; the launch traced here: 62.9 us
  waiting for transfers between devices  22.3 us (35%)
  starting transfers between devices  12.6 us (20%)
  Pallas kernels  12.2 us (19%)
  local copies, waits for them, and re-layouts  7.92 us (13%)
  other arithmetic  6.79 us (11%)
  between operations  1.08 us (2%)
    ppermute x11, waiting for transfers between devices, swap(): return lax.ppermute(x, axis, [(i, i ^ k) for i in range(n)])  22.3 us
    ppermute x11, starting transfers between devices, swap(): return lax.ppermute(x, axis, [(i, i ^ k) for i in range(n)])  12.6 us
    pallas_call x9, Pallas kernels, call(): pl.pallas_call(kernel, out_shape=shapes, in_specs=[whole] * len(args), ou...  12.2 us
    select_n x3, other arithmetic, body(): jnp.where(half_of == s, row_of, -1)[None]  5.14 us
  transfers between devices with their start and end apart: 11, of which 7 were waited for; matrix products, arithmetic and copies ran while one was open for 21% of the time, Pallas kernels for 11%

commit v1 on v0

--- a/solution.py
+++ b/solution.py
@@ -97,16 +97,100 @@
     rows_ref[...] = scr[...].astype(BF16)
     first = x_ref[:, 0:LANES].astype(F32)
     last = x_ref[:, (PAIRS - 1) * LANES :].astype(F32)
-    cols_ref[...] = jnp.where(low((SIDE, LANES)), first, last).astype(BF16)
-
-
-def before_kernel(x_ref, w_ref, bias_ref, p0, p1, p2, s_ref):
+    cols_ref[...] = halves(first, last).astype(BF16)
+
+
+def bits_moved(v, pairs):
+    result = jnp.zeros_like(v)
+    for from_bit, to_bit in pairs:
+        result = result | (((v >> from_bit) & 1) << to_bit)
+    return result
+
+
+def plan_kernel(owners, regions, blocks, index_ref, hot_ref, half_ref, scr):
+    owner = lax.axis_index("patch")
+    region = lax.axis_index("region")
+    bits = owners.bit_length() - 1
+    index = index_ref[pl.ds(owner, 1), :]
+    source, within = index >> 8, index & 255
+    slot = bits_moved((source & (owners - 1)) ^ owner, slot_bits(owners))
+    row = within & (SIDE - 1)
+    if blocks == 2:
+        row = row + jnp.where((((source >> bits) - region + regions) & (regions - 1)) == 1, SIDE, 0)
+    is_row = within < 2 * SIDE
+    place = jnp.where(is_row, slot * SIDE + (within >> 1), owners * SIDE + row)
+    half = jnp.where(is_row, within & 1, (within >> 6) & 1)
+    count = index.shape[1]
+    scr[...] = jnp.full(scr.shape, -1.0, F32)
+    scr[0:1, 0:count] = place.astype(F32)
+    scr[1:2, 0:count] = half.astype(F32)
+    column = jnp.transpose(scr[...])[0 : hot_ref.shape[0]]
+    half_ref[...] = jnp.broadcast_to(column[:, 1:2], half_ref.shape)
+    place = column[:, 0:1].astype(jnp.int32)
+    for c in range(0, hot_ref.shape[1], LANES):
+        n = min(LANES, hot_ref.shape[1] - c)
+        hot_ref[:, c : c + n] = (place == iota((hot_ref.shape[0], n), 1) + c).astype(F32).astype(BF16)
+
+
+def pick_kernel(owners, index_ref, pick_ref):
+    owner = lax.axis_index("patch")
+    base = (lax.axis_index("region") * owners + owner) * 4 * SIDE
+    back = [(b, a) for a, b in slot_bits(owners)]
+    want = 2 * iota((SIDE, LANES), 0)
+    is_low = low((1, LANES))
+    for t in range(owners // 2):
+        pair = []
+        for slot in (2 * t, 2 * t + 1):
+            k = sum(1 << to for frm, to in back if (slot >> frm) & 1)
+            line = index_ref[pl.ds(owner ^ k, 1), :]
+            pair.append((line[:, 1 : SIDE + 1], line[:, SIDE + 3 : 2 * SIDE + 3]))
+        for s in range(2):
+            both = jnp.concatenate([pair[0][s], pair[1][s]], axis=1) - base
+            for e in range(2):
+                hit = (both == want + e).astype(F32).astype(BF16)
+                n = 2 * e + s
+                pick_ref[n * SIDE : (n + 1) * SIDE, t * LANES : (t + 1) * LANES] = hit
+
+
+def weights_kernel(wt_ref, w_ref, wb_ref, wc_ref):
+    wide = [wt_ref[:, t * LANES : (t + 1) * LANES].astype(F32) for t in range(4)]
+    tail = wt_ref[:, 4 * LANES :].astype(F32)
+    wide.append(jnp.concatenate([tail, tail], axis=1))
+
+    def at(a, b, high):
+        m = 3 * a + b
+        v = wide[m // 2]
+        return v if m == 8 or (m % 2 == 1) == high else turn(v)
+
+    def pair(a, left, right):
+        zero = jnp.zeros((CHANNELS, LANES), F32)
+        lo = zero if left is None else at(a, left, False)
+        hi = zero if right is None else at(a, right, True)
+        return halves(lo, hi).astype(BF16)
+
+    c = CHANNELS
+    for a in range(3):
+        w_ref[a, 0:c, 0:LANES] = pair(a, 0, 1)
+        w_ref[a, 0:c, LANES:] = pair(a, 2, None)
+        w_ref[a, c:, 0:LANES] = pair(a, None, 0)
+        w_ref[a, c:, LANES:] = pair(a, 1, 2)
+        for w, (left, right) in enumerate(((2, None), (1, 2), (0, 1), (None, 0))):
+            wb_ref[2 - a, w * c : (w + 1) * c, :] = pair(a, left, right)
+        wc_ref[a, 0:c, :] = pair(a, 0, None)
+        wc_ref[a, c:, :] = pair(a, None, 2)
+
+
+def copies_kernel(x_ref, p0, p1, p2):
     shifted_copies(lambda q: x_ref[:, tile(q)].astype(F32), p0, p1, p2)
+
+
+def signal_kernel(p0, p1, p2, w_ref, bias_ref, s_ref):
     n = 4 * SIDE
+    bias = jnp.concatenate([bias_ref[...], bias_ref[...]], axis=1)
 
     def step(c, carry):
         start = pl.multiple_of(c * n, n)
-        s_ref[pl.ds(start, n), :] = product(p0, p1, p2, w_ref, start, n, NT) + bias_ref[0:1, :]
+        s_ref[pl.ds(start, n), :] = product(p0, p1, p2, w_ref, start, n, NT) + bias
         return carry
 
     lax.fori_loop(0, ROWS // n, step, 0)
@@ -122,22 +206,30 @@
 
 
 def middle_kernel(
-    s_in, cot_ref, p0, p1, p2, rows_ref, cols_ref, hot_ref, half_ref, w_ref, wb_ref, wc_ref, scat_ref,
-    g_ref, msg_ref, own_ref, sums_ref, s_ref, ht, hb, gt, gb, gc,
+    s_in, cot_ref, p0, p1, p2, rows_ref, cols_ref, hot_ref, half_ref, w_ref, wb_ref, wc_ref,
+    g_ref, msg_ref, own_ref, sums_ref, s_ref, cell_scr, gt, gb, gc, own_scr,
 ):
     many = rows_ref.shape[0]
     cells = dot(hot_ref[:, :many], rows_ref[...]) + dot(hot_ref[:, many:], cols_ref[...])
     other = turn(cells)
     upper = half_ref[...] > 0.5
+    edge = 2 * SIDE + 4
     as_low = jnp.where(upper, other, cells)
     as_high = jnp.where(upper, cells, other)
-    ht[...] = halves(as_low[0:40], as_high[40:80])
-    hb[...] = halves(as_low[80:120], as_high[120:160])
-    sides = halves(as_low[160:224], as_high[224:288])
+    sides = halves(as_low[edge : edge + SIDE], as_high[edge + SIDE : edge + 2 * SIDE])
+    odd = iota(cells.shape, 0) % 2 == 1
+    cell_scr[...] = jnp.where(odd, as_high, as_low)
+
+    def line_of(start):
+        even_cells = cell_scr[pl.ds(start, PAIRS + 1, stride=2), :]
+        odd_cells = cell_scr[pl.ds(start + 1, PAIRS + 1, stride=2), :]
+        both = halves(even_cells, odd_cells)
+        return jnp.concatenate([both[0:PAIRS], both[1 : PAIRS + 1]], axis=1).astype(BF16)
+
     is_low = low((SIDE, LANES))
     row = iota((SIDE, LANES), 0)
-    top = jnp.concatenate([ht[0:PAIRS, :], ht[1 : PAIRS + 1, :]], axis=1).astype(BF16)
-    bottom = jnp.concatenate([hb[0:PAIRS, :], hb[1 : PAIRS + 1, :]], axis=1).astype(BF16)
+    top = line_of(0)
+    bottom = line_of(SIDE + 2)
     s_ref[...] = s_in[...]
     first = pl.ds(0, PAIRS, stride=SIDE)
     final = pl.ds(SIDE - 1, PAIRS, stride=SIDE)
@@ -210,23 +302,37 @@
             high = jnp.where(row == 0, coarse, jnp.where(row == 1, fine, 0.0))
         msg_ref[t * SIDE : (t + 1) * SIDE, :] = halves(tap(2 * t, False), high).astype(BF16)
 
-    for dest, src, tap_row in ((0, gt, 2), (1, gb, 0)):
+    lines = []
+    for src, tap_row in ((gt, 2), (gb, 0)):
         window = jnp.concatenate([src[0:PAIRS, :], src[1 : PAIRS + 1, :]], axis=1).astype(BF16)
-        own_ref[dest * PAIRS : (dest + 1) * PAIRS, :] = dot(window, wb_ref[tap_row]).astype(BF16)
+        lines.append(dot(window, wb_ref[tap_row]))
+    own_scr[pl.ds(0, PAIRS, stride=2), :] = halves(lines[0], turn(lines[1]))
+    own_scr[pl.ds(1, PAIRS, stride=2), :] = halves(turn(lines[0]), lines[1])
+    own_ref[...] = own_scr[...].astype(BF16)
 
     gc[...] = jnp.zeros(gc.shape, F32)
     gc[8 : 8 + SIDE, :] = jnp.where(is_low, s_ref[0:SIDE, :], s_ref[ROWS - SIDE : ROWS, :])
     grads = dot(gc[8:88, :].astype(BF16), wc_ref[0])
     grads = grads + dot(gc[7:87, :].astype(BF16), wc_ref[1])
     grads = grads + dot(gc[6:86, :].astype(BF16), wc_ref[2])
-    spread = dot(scat_ref[...], grads.astype(BF16))
-    n = spread.shape[0] // 4
-    l0, l1, r0, r1 = (spread[i * n : (i + 1) * n] for i in range(4))
-    sums_ref[...] = halves(l0 + turn(r0), turn(l1) + r1).astype(BF16)
-
-
-def inner_kernel(g_ref, wb_ref, out_ref, p0, p1, p2):
+    other = turn(grads)
+    lefts = halves(grads, other)
+    rights = halves(other, grads)
+    cell_scr[...] = jnp.zeros(cell_scr.shape, F32)
+    for at, src, first_row, n in (
+        (0, lefts, 0, 1), (SIDE + 1, rights, 0, 1), (SIDE + 2, lefts, SIDE + 1, 1), (edge - 1, rights, SIDE + 1, 1),
+        (edge, lefts, 1, SIDE), (edge + SIDE, rights, 1, SIDE),
+    ):
+        cell_scr[at : at + n, :] = src[first_row : first_row + n]
+    placed = jnp.where(upper == low(cells.shape), 0.0, cell_scr[...]).astype(BF16)
+    sums_ref[...] = dot(hot_ref[:, many:], placed, TN).astype(BF16)
+
+
+def grad_copies_kernel(g_ref, p0, p1, p2):
     shifted_copies(lambda q: g_ref[block(q), :].astype(F32), p0, p1, p2)
+
+
+def inner_kernel(p0, p1, p2, wb_ref, out_ref):
     n = 4 * SIDE
 
     def step(c, carry):
@@ -268,7 +374,7 @@
     for t in range(4):
         wt_ref[:, t * LANES : (t + 1) * LANES] = total[t * SIDE : (t + 1) * SIDE] * scale
     wt_ref[:, 4 * LANES :] = tail[:, :CHANNELS] * scale
-    bias_ref[...] = turn(whole)[0:8] * scale
+    bias_ref[...] = turn(whole)[0:1, :CHANNELS] * scale
     n = mine.shape[0] - WROWS
     got = dot(pick[:, :n], mine[WROWS:, :]) + dot(pick[:, n:], other[WROWS:, :])
     a, b, c, d = (got[i * SIDE : (i + 1) * SIDE] for i in range(4))
@@ -307,47 +413,9 @@
     return ks
 
 
-def slot_of(relative, ks):
-    slot = jnp.zeros_like(relative)
-    for bit, k in enumerate(ks):
-        slot = slot + jnp.where((relative & k) != 0, 1 << bit, 0)
-    return slot
-
-
-def owner_of(slot, ks):
-    result = jnp.zeros_like(slot)
-    for bit, k in enumerate(ks):
-        result = result + jnp.where((slot >> bit) & 1 != 0, k, 0)
-    return result
-
-
-def weights_of(fine_weight):
-    wt = fine_weight.T.reshape(CHANNELS, 3, 3 * CHANNELS)
-    zero = jnp.zeros((CHANNELS, CHANNELS), BF16)
-    forward, backward, columns = [], [], []
-    for a in range(3):
-        rows = wt[:, a]
-        forward.append(
-            jnp.concatenate(
-                [jnp.concatenate([rows, zero], axis=1), jnp.concatenate([zero, rows], axis=1)], axis=0
-            )
-        )
-        taps = [wt[:, 2 - a, b * CHANNELS : (b + 1) * CHANNELS] for b in (2, 1, 0)]
-        backward.append(
-            jnp.concatenate(
-                [jnp.concatenate(taps + [zero], axis=0), jnp.concatenate([zero] + taps, axis=0)], axis=1
-            )
-        )
-        columns.append(
-            jnp.concatenate(
-                [
-                    jnp.concatenate([rows[:, :CHANNELS], zero], axis=1),
-                    jnp.concatenate([zero, rows[:, 2 * CHANNELS :]], axis=1),
-                ],
-                axis=0,
-            )
-        )
-    return jnp.stack(forward), jnp.stack(backward), jnp.stack(columns)
+def slot_bits(owners):
+    bits = owners.bit_length() - 1
+    return [(bits - 1 - i, i) for i in range(bits)]
 
 
 def body(fine_input, fine_weight, fine_bias, cotangent, halo_index):
@@ -371,69 +439,32 @@
     for k in ks:
         rows = jnp.concatenate([rows, swap(rows, "patch", k)], axis=0)
 
-    forward, backward, columns = weights_of(fine_weight)
-    bias_pair = jnp.broadcast_to(jnp.tile(fine_bias, 2)[None], (8, LANES))
-    p0, p1, p2, signal = call(
-        before_kernel, [pair, pair, pair, ((ROWS, LANES), F32)], x, forward, bias_pair,
-        flops=2 * ROWS * 768 * 128, moved=4 * 2**20,
-    )
-
-    own = lax.dynamic_index_in_dim(halo_index, owner_id, 0, keepdims=False)
-    source, within = own // (4 * SIDE), own % (4 * SIDE)
-    is_row = within < 2 * SIDE
-    slot = slot_of((source % owners) ^ owner_id, ks)
-    after = (source // owners - region_id) % regions == 1
-    column_row = within % SIDE + (0 if blocks == 1 else jnp.where(after, SIDE, 0))
-    column_half = (within - 2 * SIDE) // SIDE
-    place = jnp.where(is_row, slot * SIDE + within // 2, owners * SIDE + column_row)
-    half = jnp.where(is_row, within % 2, column_half)
-
-    def cells_of(v, fill):
-        def padded(u):
-            return jnp.concatenate([u, jnp.full((40 - PAIRS - 1,), fill, v.dtype)])
-
-        top, bottom = v[0 : SIDE + 2], v[SIDE + 2 : 2 * SIDE + 4]
-        return jnp.concatenate(
-            [padded(top[0::2]), padded(top[1::2]), padded(bottom[0::2]), padded(bottom[1::2]), v[2 * SIDE + 4 :]]
-        )
-
-    hot = (cells_of(place, -1)[:, None] == jnp.arange((owners + blocks) * SIDE)[None]).astype(BF16)
-    half_mask = jnp.broadcast_to(cells_of(half, 0).astype(F32)[:, None], (hot.shape[0], LANES))
-
-    def ring(v, fill):
-        edge = 2 * SIDE + 4
-        pad = jnp.full((80 - SIDE - 2,), fill, v.dtype)
-        left = jnp.concatenate([v[0:1], v[edge : edge + SIDE], v[SIDE + 2 : SIDE + 3], pad])
-        right = jnp.concatenate([v[SIDE + 1 : SIDE + 2], v[edge + SIDE :], v[edge - 1 : edge], pad])
-        return left, right
-
-    scatter = []
-    for row_of, half_of in zip(ring(column_row, -1), ring(column_half, 0)):
-        for s in range(2):
-            scatter.append(
-                (jnp.arange(blocks * SIDE)[:, None] == jnp.where(half_of == s, row_of, -1)[None]).astype(BF16)
-            )
-    scatter = jnp.concatenate(scatter, axis=0)
-
-    wanted = jnp.concatenate([halo_index[:, 1 : SIDE + 1], halo_index[:, SIDE + 3 : 2 * SIDE + 3]], axis=1)
-    wanted = jnp.take(wanted, owner_id ^ owner_of(jnp.arange(owners), ks), axis=0)
-    wanted = wanted - (region_id * owners + owner_id) * 4 * SIDE
-    wanted = wanted.reshape(owners * SIDE, 2)
-    pick = jnp.concatenate(
-        [
-            ((2 * jnp.arange(SIDE) + e)[:, None] == wanted[:, s][None]).astype(BF16)
-            for e in range(2)
-            for s in range(2)
-        ],
-        axis=0,
-    )
+    cells = 272
+    hot, half_mask = call(
+        functools.partial(plan_kernel, owners, regions, blocks),
+        [((cells, (owners + blocks) * SIDE), BF16), ((cells, LANES), F32)],
+        halo_index, scratch=[pltpu.VMEM((8, 384), F32)],
+    )
+    forward, backward, columns = call(
+        weights_kernel,
+        [((3, LANES, 2 * LANES), BF16), ((3, 2 * LANES, LANES), BF16), ((3, LANES, LANES), BF16)],
+        fine_weight.T,
+    )
+    copies = call(copies_kernel, [pair] * 3, x, moved=2 * 2**20)
+    signal = call(
+        signal_kernel, [((ROWS, LANES), F32)], *copies, forward, fine_bias.reshape(1, CHANNELS),
+        flops=2 * ROWS * 768 * 128, moved=3 * 2**20,
+    )[0]
 
     line = pltpu.VMEM((40, LANES), F32)
     grad, message, own_rows, sums = call(
         middle_kernel,
         [((ROWS, LANES), BF16), ((WROWS, LANES), BF16), ((SIDE, LANES), BF16), ((blocks * SIDE, LANES), BF16)],
-        signal, cot, p0, p1, p2, rows, cols, hot, half_mask, forward, backward, columns, scatter,
-        scratch=[pltpu.VMEM((ROWS, LANES), F32), line, line, line, line, pltpu.VMEM((96, LANES), F32)],
+        signal, cot, *copies, rows, cols, hot, half_mask, forward, backward, columns,
+        scratch=[
+            pltpu.VMEM((ROWS, LANES), F32), pltpu.VMEM((cells, LANES), F32), line, line,
+            pltpu.VMEM((96, LANES), F32), pltpu.VMEM((SIDE, LANES), F32),
+        ],
         flops=2 * ROWS * 768 * 128, moved=4 * 2**20,
     )
 
@@ -441,10 +472,12 @@
         sides = [swap(sums, "region", 1)]
     else:
         sides = [shift(sums[SIDE:], "region", 1), shift(sums[:SIDE], "region", -1)]
+    pick = call(
+        functools.partial(pick_kernel, owners), [((4 * SIDE, owners * SIDE), BF16)], halo_index
+    )[0]
+    grad_copies = call(grad_copies_kernel, [pair] * 3, grad, moved=2 * 2**20)
     inner = call(
-        inner_kernel, [((ROWS, LANES), F32)], grad, backward,
-        scratch=[pltpu.VMEM((ROWS + SIDE, LANES), BF16)] * 3,
-        flops=2 * ROWS * 768 * 128, moved=4 * 2**20,
+        inner_kernel, [((ROWS, LANES), F32)], *grad_copies, backward, flops=2 * ROWS * 768 * 128, moved=3 * 2**20
     )[0]
 
     region_ks = steps_of(regions)
@@ -462,10 +495,10 @@
         kernel = functools.partial(last_one_side, scale)
     input_grad, weight_grad, bias_grad = call(
         kernel,
-        [((SIDE, SIDE * CHANNELS), BF16), ((CHANNELS, 9 * CHANNELS), F32), ((8, LANES), F32)],
+        [((SIDE, SIDE * CHANNELS), BF16), ((CHANNELS, 9 * CHANNELS), F32), ((1, CHANNELS), F32)],
         message, other, inner, pick, *sides,
     )
-    return input_grad.reshape(1, SIDE, SIDE * CHANNELS), weight_grad.T, bias_grad[0, :CHANNELS]
+    return input_grad.reshape(1, SIDE, SIDE * CHANNELS), weight_grad.T, bias_grad.reshape(CHANNELS)
 
 
 def last_one_side(scale, mine, other, inner, pick, side_a, grad_ref, wt_ref, bias_ref):

time: 63.2 us -> 53.1 us (0.84)
  other arithmetic: 6.79 us -> 0.02 us
  local copies, waits for them, and re-layouts: 7.92 us -> 2.37 us
  starting transfers between devices: 12.6 us -> 14.4 us
  Pallas kernels: 12.2 us -> 13.1 us
    select_n x5 -> x0, other arithmetic: 5.18 us -> none  [the longest x3 5.14 us: body(): jnp.where(half_of == s, row_of, -1)[None]]
    slice x20 -> x0, local copies, waits for them, and re-layouts: 2.96 us -> none  [the longest x1 0.69 us: ring(): v[0:1]]
    ppermute x11, starting transfers between devices: 12.6 us -> 14.4 us  [swap(): return lax.ppermute(x, axis, [(i, i ^ k) for i in range(n)])]
    unnamed x18 -> x14, local copies, waits for them, and re-layouts: 1.11 us -> 2.36 us
    gather x2 -> x0, local copies, waits for them, and re-layouts: 1.03 us -> none  [body(): jnp.take(wanted, owner_id ^ owner_of(jnp.arange(owners), ks), axis=0)]
    reshape x1 -> x0, local copies, waits for them, and re-layouts: 1 us -> none  [weights_of(): wt = fine_weight.T.reshape(CHANNELS, 3, 3 * CHANNELS)]
    pallas_call x9 -> x14, Pallas kernels: 12.2 us -> 13.1 us  [call(): pl.pallas_call(kernel, out_shape=shapes, in_specs=[whole] * len(args), ou...]
    another operation x11 -> x0, other arithmetic: 0.75 us -> none  [weights_of(): return (jnp.stack(forward), jnp.stack(backward), jnp.stack(columns))]
  transfers between devices with their start and end apart: 11 -> 11, of which waited for: 7 -> 7; matrix products, arithmetic and copies ran while one was open for 21% -> 0% of each run, Pallas kernels for 11% -> 15%
where the time goes in v1:
time: 53.1 us; the launch traced here: 52.8 us
  waiting for transfers between devices  22.2 us (42%)
  starting transfers between devices  14.4 us (27%)
  Pallas kernels  13.1 us (25%)
  local copies, waits for them, and re-layouts  2.37 us (4%)
  between operations  0.82 us (2%)
    ppermute x11, waiting for transfers between devices, swap(): return lax.ppermute(x, axis, [(i, i ^ k) for i in range(n)])  22.2 us
    ppermute x11, starting transfers between devices, swap(): return lax.ppermute(x, axis, [(i, i ^ k) for i in range(n)])  14.4 us
    pallas_call x14, Pallas kernels, call(): pl.pallas_call(kernel, out_shape=shapes, in_specs=[whole] * len(args), ou...  13.1 us
    unnamed x14, local copies, waits for them, and re-layouts  2.36 us
  transfers between devices with their start and end apart: 11, of which 7 were waited for; matrix products, arithmetic and copies ran while one was open for 0% of the time, Pallas kernels for 15%

profile of v1, /device:TPU:0, one launch (start us, length us, event | category | flops | bytes accessed | tf_op | source)
XLA Modules:
  0.0 52.8 jit_solution(1737366771205181174)
XLA Ops:
  0.6 1.0 %copy-done = bf16[1,64,4096]{2,1,0:T(8,128)(2,1)S(1)} copy-done((bf16[1,64,4096]{2,1,0:T(8,128)(2,1)S(1)}, bf16[1,64,4096]{2,1,0:T(8,128)(2,1)}, u32[]{:S(2)}) %copy-start) | copy-done | bytes 524312
  1.7 4.1 %collective-permute-start = (bf16[64,128]{1,0:T(8,128)(2,1)S(1)}, bf16[64,128]{1,0:T(8,128)(2,1)S(1)}, u32[]{:S(2)}, u32[]{:S(2)}) collective-permute-start(bf16[64,128]{1,0:T(8,128)(2,1)S(1)} %get-tuple-element.27), channel_id=1, source_target_pairs={{0,8},{1,9},{2,10},{3,11},{4,12},{5,13},{6,14},{7,15},{8,0},{9,1},... | collective-permute-start | bytes 49160 | tf_op jit(solution)/shard_map/ppermute | solution.py:399
  5.8 1.5 %shard_map.76 = (bf16[2112,128]{1,0:T(8,128)(2,1)S(1)}, bf16[2112,128]{1,0:T(8,128)(2,1)S(1)}, bf16[2112,128]{1,0:T(8,128)(2,1)S(1)}) custom-call(bf16[64,4096]{1,0:T(8,128)(2,1)S(1)} %bitcast.8), custom_call_target="tpu_custom_call" | custom-call | bytes 2097152 | tf_op jit(solution)/shard_map/pallas_call | solution.py:24
  7.4 0.6 %copy-done.2 = s32[16,260]{1,0:T(8,128)S(1)} copy-done((s32[16,260]{1,0:T(8,128)S(1)}, s32[16,260]{1,0:T(8,128)}, u32[]{:S(2)}) %copy-start.2) | copy-done | bytes 16664
  8.0 0.3 shard_map.80
  8.4 1.6 %collective-permute-start.1 = (bf16[128,128]{1,0:T(8,128)(2,1)S(1)}, bf16[128,128]{1,0:T(8,128)(2,1)S(1)}, u32[]{:S(2)}, u32[]{:S(2)}) collective-permute-start(bf16[128,128]{1,0:T(8,128)(2,1)S(1)} %pad_maximum_fusion.2), channel_id=1, source_target_pairs={{0,4},{1,5},{2,6},{3,7},{4,0},{5,1},{6,2},{7,3},{8,12},{9,13},{10,... | collective-permute-start | bytes 98312 | tf_op jit(solution)/shard_map/ppermute | solution.py:399
  10.0 0.7 %copy-done.4 = f32[64]{0:T(128)S(1)} copy-done((f32[64]{0:T(128)S(1)}, f32[64]{0:T(128)}, u32[]{:S(2)}) %copy-start.4) | copy-done | bytes 280
  10.7 2.2 %shard_map.78.s_in = f32[2048,128]{1,0:T(8,128)S(1)} custom-call(bf16[2112,128]{1,0:T(8,128)(2,1)S(1)} %get-tuple-element.23.p0, bf16[2112,128]{1,0:T(8,128)(2,1)S(1)} %get-tuple-element.24.p1, bf16[2112,128]{1,0:T(8,128)(2,1)S(1)} %get-tuple-element.25.p2, bf16[3,128,256]{2,1,0:T(8,128)(2,1)S(1)} %get-tuple-element.26.w_ref, f32[1,64]{1,0:T(1,128)S(1)} %bitcast.11), custom_call_target="tpu_custom_call" | custom-call | flops 402653184 | bytes 3145728 | tf_op jit(solution)/shard_map/pallas_call | solution.py:24
  12.9 1.6 %collective-permute-start.2 = (bf16[256,128]{1,0:T(8,128)(2,1)S(1)}, bf16[256,128]{1,0:T(8,128)(2,1)S(1)}, u32[]{:S(2)}, u32[]{:S(2)}) collective-permute-start(bf16[256,128]{1,0:T(8,128)(2,1)S(1)} %pad_maximum_fusion.1), channel_id=1, source_target_pairs={{0,2},{1,3},{2,0},{3,1},{4,6},{5,7},{6,4},{7,5},{8,10},{9,11},{10,... | collective-permute-start | bytes 196616 | tf_op jit(solution)/shard_map/ppermute | solution.py:399
  14.5 2.7 %collective-permute-done.2 = bf16[256,128]{1,0:T(8,128)(2,1)S(1)} collective-permute-done((bf16[256,128]{1,0:T(8,128)(2,1)S(1)}, bf16[256,128]{1,0:T(8,128)(2,1)S(1)}, u32[]{:S(2)}, u32[]{:S(2)}) %collective-permute-start.2) | collective-permute-done | bytes 65568 | tf_op jit(solution)/shard_map/ppermute | solution.py:399
  17.3 1.6 %collective-permute-start.3 = (bf16[512,128]{1,0:T(8,128)(2,1)S(1)}, bf16[512,128]{1,0:T(8,128)(2,1)S(1)}, u32[]{:S(2)}, u32[]{:S(2)}) collective-permute-start(bf16[512,128]{1,0:T(8,128)(2,1)S(1)} %pad_maximum_fusion), channel_id=1, source_target_pairs={{0,1},{1,0},{2,3},{3,2},{4,5},{5,4},{6,7},{7,6},{8,9},{9,8},{10,11... | collective-permute-start | bytes 393224 | tf_op jit(solution)/shard_map/ppermute | solution.py:399
  18.9 3.4 %collective-permute-done.3 = bf16[512,128]{1,0:T(8,128)(2,1)S(1)} collective-permute-done((bf16[512,128]{1,0:T(8,128)(2,1)S(1)}, bf16[512,128]{1,0:T(8,128)(2,1)S(1)}, u32[]{:S(2)}, u32[]{:S(2)}) %collective-permute-start.3) | collective-permute-done | bytes 131104 | tf_op jit(solution)/shard_map/ppermute | solution.py:399
  22.4 3.9 %shard_map.81 = (bf16[2048,128]{1,0:T(8,128)(2,1)S(1)}, bf16[320,128]{1,0:T(8,128)(2,1)S(1)}, bf16[64,128]{1,0:T(8,128)(2,1)S(1)}, bf16[64,128]{1,0:T(8,128)(2,1)S(1)}) custom-call(f32[2048,128]{1,0:T(8,128)S(1)} %shard_map.78.s_in, bf16[64,4096]{1,0:T(8,128)(2,1)S(1)} %bitcast.9, bf16[2112,128]{1,0:T(8,128)(2,1)S(1)} %get-tuple-element.23.p0, ...), custom_call_target="tpu_custom_call" | custom-call | flops 402653184 | bytes 4194304 | tf_op jit(solution)/shard_map/pallas_call | solution.py:24
  26.3 1.3 %collective-permute-done.5.other = bf16[320,128]{1,0:T(8,128)(2,1)S(1)} collective-permute-done((bf16[320,128]{1,0:T(8,128)(2,1)S(1)}, bf16[320,128]{1,0:T(8,128)(2,1)S(1)}, u32[]{:S(2)}, u32[]{:S(2)}) %collective-permute-start.5) | collective-permute-done | bytes 81952 | tf_op jit(solution)/shard_map/ppermute | solution.py:399
  27.6 2.1 %collective-permute-start.6 = (bf16[384,128]{1,0:T(8,128)(2,1)S(1)}, bf16[384,128]{1,0:T(8,128)(2,1)S(1)}, u32[]{:S(2)}, u32[]{:S(2)}) collective-permute-start(bf16[384,128]{1,0:T(8,128)(2,1)S(1)} %shard_map.82.mine), channel_id=1, source_target_pairs={{0,8},{1,9},{2,10},{3,11},{4,12},{5,13},{6,14},{7,15},{8,0},{9,1},... | collective-permute-start | bytes 294920 | tf_op jit(solution)/shard_map/ppermute | solution.py:399
  29.8 5.8 %collective-permute-done.6.other = bf16[384,128]{1,0:T(8,128)(2,1)S(1)} collective-permute-done((bf16[384,128]{1,0:T(8,128)(2,1)S(1)}, bf16[384,128]{1,0:T(8,128)(2,1)S(1)}, u32[]{:S(2)}, u32[]{:S(2)}) %collective-permute-start.6) | collective-permute-done | bytes 98336 | tf_op jit(solution)/shard_map/ppermute | solution.py:399
  35.7 4.8 %collective-permute-done.7.other = bf16[448,128]{1,0:T(8,128)(2,1)S(1)} collective-permute-done((bf16[448,128]{1,0:T(8,128)(2,1)S(1)}, bf16[448,128]{1,0:T(8,128)(2,1)S(1)}, u32[]{:S(2)}, u32[]{:S(2)}) %collective-permute-start.7) | collective-permute-done | bytes 114720 | tf_op jit(solution)/shard_map/ppermute | solution.py:399
  40.5 1.6 %collective-permute-start.8 = (bf16[576,128]{1,0:T(8,128)(2,1)S(1)}, bf16[576,128]{1,0:T(8,128)(2,1)S(1)}, u32[]{:S(2)}, u32[]{:S(2)}) collective-permute-start(bf16[576,128]{1,0:T(8,128)(2,1)S(1)} %shard_map.84.mine), channel_id=1, source_target_pairs={{0,2},{1,3},{2,0},{3,1},{4,6},{5,7},{6,4},{7,5},{8,10},{9,11},{10,... | collective-permute-start | bytes 442376 | tf_op jit(solution)/shard_map/ppermute | solution.py:399
  42.1 3.6 %collective-permute-done.8.other = bf16[576,128]{1,0:T(8,128)(2,1)S(1)} collective-permute-done((bf16[576,128]{1,0:T(8,128)(2,1)S(1)}, bf16[576,128]{1,0:T(8,128)(2,1)S(1)}, u32[]{:S(2)}, u32[]{:S(2)}) %collective-permute-start.8) | collective-permute-done | bytes 147488 | tf_op jit(solution)/shard_map/ppermute | solution.py:399
  45.7 1.6 %collective-permute-start.9 = (bf16[832,128]{1,0:T(8,128)(2,1)S(1)}, bf16[832,128]{1,0:T(8,128)(2,1)S(1)}, u32[]{:S(2)}, u32[]{:S(2)}) collective-permute-start(bf16[832,128]{1,0:T(8,128)(2,1)S(1)} %shard_map.85.mine), channel_id=1, source_target_pairs={{0,1},{1,0},{2,3},{3,2},{4,5},{5,4},{6,7},{7,6},{8,9},{9,8},{10,11... | collective-permute-start | bytes 638984 | tf_op jit(solution)/shard_map/ppermute | solution.py:399
  47.5 1.5 %shard_map.86 = (bf16[2112,128]{1,0:T(8,128)(2,1)S(1)}, bf16[2112,128]{1,0:T(8,128)(2,1)S(1)}, bf16[2112,128]{1,0:T(8,128)(2,1)S(1)}) custom-call(bf16[2048,128]{1,0:T(8,128)(2,1)S(1)} %get-tuple-element.35.g_ref), custom_call_target="tpu_custom_call" | custom-call | bytes 2097152 | tf_op jit(solution)/shard_map/pallas_call | solution.py:24
  49.1 2.0 %shard_map.87.inner = f32[2048,128]{1,0:T(8,128)S(1)} custom-call(bf16[2112,128]{1,0:T(8,128)(2,1)S(1)} %get-tuple-element.36.p0, bf16[2112,128]{1,0:T(8,128)(2,1)S(1)} %get-tuple-element.37.p1, bf16[2112,128]{1,0:T(8,128)(2,1)S(1)} %get-tuple-element.38.p2, bf16[3,256,128]{2,1,0:T(8,128)(2,1)S(1)} %get-tuple-element.31.wb_ref), custom_call_target="tpu_custom_call" | custom-call | flops 402653184 | bytes 3145728 | tf_op jit(solution)/shard_map/pallas_call | solution.py:24
  51.1 0.5 collective-permute-done.9.other
  51.6 1.2 %shard_map.89 = (bf16[64,4096]{1,0:T(8,128)(2,1)}, f32[64,576]{1,0:T(8,128)}, f32[1,64]{1,0:T(1,128)}) custom-call(bf16[832,128]{1,0:T(8,128)(2,1)S(1)} %shard_map.85.mine, bf16[832,128]{1,0:T(8,128)(2,1)S(1)} %collective-permute-done.9.other, f32[2048,128]{1,0:T(8,128)S(1)} %shard_map.87.inner, bf16[256,1024]{1,0:T(8,128)(2,1)S(1)} %shard_map.88.pick, ...), custom_call_target="tpu_custom_call" | custom-call | tf_op jit(solution)/shard_map/pallas_call | solution.py:24
  (30 shorter events, 0.8 us)
Async XLA Ops:
  0.6 1.0 %copy-start = (bf16[1,64,4096]{2,1,0:T(8,128)(2,1)S(1)}, bf16[1,64,4096]{2,1,0:T(8,128)(2,1)}, u32[]{:S(2)}) copy-start(bf16[1,64,4096]{2,1,0:T(8,128)(2,1)} %param.5) | copy-start | bytes 1572868
  1.7 6.7 %collective-permute-start = (bf16[64,128]{1,0:T(8,128)(2,1)S(1)}, bf16[64,128]{1,0:T(8,128)(2,1)S(1)}, u32[]{:S(2)}, u32[]{:S(2)}) collective-permute-start(bf16[64,128]{1,0:T(8,128)(2,1)S(1)} %get-tuple-element.27), channel_id=1, source_target_pairs={{0,8},{1,9},{2,10},{3,11},{4,12},{5,13},{6,14},{7,15},{8,0},{9,1},... | collective-permute-start | bytes 49160 | tf_op jit(solution)/shard_map/ppermute | solution.py:399
  5.8 16.5 %collective-permute-start.4 = (bf16[64,128]{1,0:T(8,128)(2,1)S(1)}, bf16[64,128]{1,0:T(8,128)(2,1)S(1)}, u32[]{:S(2)}, u32[]{:S(2)}) collective-permute-start(bf16[64,128]{1,0:T(8,128)(2,1)S(1)} %get-tuple-element.28), channel_id=1, source_target_pairs={{0,16},{16,0},{1,17},{17,1},{2,18},{18,2},{3,19},{19,3},{4,20},{20... | collective-permute-start | bytes 49160 | tf_op jit(solution)/shard_map/ppermute | solution.py:399
  5.8 1.5 %copy-start.3 = (bf16[576,64]{0,1:T(8,128)(2,1)S(1)}, bf16[576,64]{0,1:T(8,128)(2,1)}, u32[]{:S(2)}) copy-start(bf16[576,64]{0,1:T(8,128)(2,1)} %param.6) | copy-start | bytes 221188
  7.3 0.7 %copy-start.2 = (s32[16,260]{1,0:T(8,128)S(1)}, s32[16,260]{1,0:T(8,128)}, u32[]{:S(2)}) copy-start(s32[16,260]{1,0:T(8,128)} %index_ref.3) | copy-start | bytes 49924
  8.4 4.5 %collective-permute-start.1 = (bf16[128,128]{1,0:T(8,128)(2,1)S(1)}, bf16[128,128]{1,0:T(8,128)(2,1)S(1)}, u32[]{:S(2)}, u32[]{:S(2)}) collective-permute-start(bf16[128,128]{1,0:T(8,128)(2,1)S(1)} %pad_maximum_fusion.2), channel_id=1, source_target_pairs={{0,4},{1,5},{2,6},{3,7},{4,0},{5,1},{6,2},{7,3},{8,12},{9,13},{10,... | collective-permute-start | bytes 98312 | tf_op jit(solution)/shard_map/ppermute | solution.py:399
  10.0 0.7 %copy-start.4 = (f32[64]{0:T(128)S(1)}, f32[64]{0:T(128)}, u32[]{:S(2)}) copy-start(f32[64]{0:T(128)} %param.7) | copy-start | bytes 772
  12.9 9.4 %copy-start.1 = (bf16[1,64,4096]{2,1,0:T(8,128)(2,1)S(1)}, bf16[1,64,4096]{2,1,0:T(8,128)(2,1)}, u32[]{:S(2)}) copy-start(bf16[1,64,4096]{2,1,0:T(8,128)(2,1)} %param.8) | copy-start | bytes 1572868
  12.9 4.3 %collective-permute-start.2 = (bf16[256,128]{1,0:T(8,128)(2,1)S(1)}, bf16[256,128]{1,0:T(8,128)(2,1)S(1)}, u32[]{:S(2)}, u32[]{:S(2)}) collective-permute-start(bf16[256,128]{1,0:T(8,128)(2,1)S(1)} %pad_maximum_fusion.1), channel_id=1, source_target_pairs={{0,2},{1,3},{2,0},{3,1},{4,6},{5,7},{6,4},{7,5},{8,10},{9,11},{10,... | collective-permute-start | bytes 196616 | tf_op jit(solution)/shard_map/ppermute | solution.py:399
  17.3 5.0 %collective-permute-start.3 = (bf16[512,128]{1,0:T(8,128)(2,1)S(1)}, bf16[512,128]{1,0:T(8,128)(2,1)S(1)}, u32[]{:S(2)}, u32[]{:S(2)}) collective-permute-start(bf16[512,128]{1,0:T(8,128)(2,1)S(1)} %pad_maximum_fusion), channel_id=1, source_target_pairs={{0,1},{1,0},{2,3},{3,2},{4,5},{5,4},{6,7},{7,6},{8,9},{9,8},{10,11... | collective-permute-start | bytes 393224 | tf_op jit(solution)/shard_map/ppermute | solution.py:399
  26.3 1.3 %collective-permute-start.5 = (bf16[320,128]{1,0:T(8,128)(2,1)S(1)}, bf16[320,128]{1,0:T(8,128)(2,1)S(1)}, u32[]{:S(2)}, u32[]{:S(2)}) collective-permute-start(bf16[320,128]{1,0:T(8,128)(2,1)S(1)} %get-tuple-element.33.mine), channel_id=1, source_target_pairs={{0,16},{16,0},{1,17},{17,1},{2,18},{18,2},{3,19},{19,3},{4,20},{20... | collective-permute-start | bytes 245768 | tf_op jit(solution)/shard_map/ppermute | solution.py:399
  27.6 7.9 %collective-permute-start.6 = (bf16[384,128]{1,0:T(8,128)(2,1)S(1)}, bf16[384,128]{1,0:T(8,128)(2,1)S(1)}, u32[]{:S(2)}, u32[]{:S(2)}) collective-permute-start(bf16[384,128]{1,0:T(8,128)(2,1)S(1)} %shard_map.82.mine), channel_id=1, source_target_pairs={{0,8},{1,9},{2,10},{3,11},{4,12},{5,13},{6,14},{7,15},{8,0},{9,1},... | collective-permute-start | bytes 294920 | tf_op jit(solution)/shard_map/ppermute | solution.py:399
  35.6 4.9 %collective-permute-start.7 = (bf16[448,128]{1,0:T(8,128)(2,1)S(1)}, bf16[448,128]{1,0:T(8,128)(2,1)S(1)}, u32[]{:S(2)}, u32[]{:S(2)}) collective-permute-start(bf16[448,128]{1,0:T(8,128)(2,1)S(1)} %shard_map.83.mine), channel_id=1, source_target_pairs={{0,4},{1,5},{2,6},{3,7},{4,0},{5,1},{6,2},{7,3},{8,12},{9,13},{10,... | collective-permute-start | bytes 344072 | tf_op jit(solution)/shard_map/ppermute | solution.py:399
  40.5 5.2 %collective-permute-start.8 = (bf16[576,128]{1,0:T(8,128)(2,1)S(1)}, bf16[576,128]{1,0:T(8,128)(2,1)S(1)}, u32[]{:S(2)}, u32[]{:S(2)}) collective-permute-start(bf16[576,128]{1,0:T(8,128)(2,1)S(1)} %shard_map.84.mine), channel_id=1, source_target_pairs={{0,2},{1,3},{2,0},{3,1},{4,6},{5,7},{6,4},{7,5},{8,10},{9,11},{10,... | collective-permute-start | bytes 442376 | tf_op jit(solution)/shard_map/ppermute | solution.py:399
  45.7 5.9 %collective-permute-start.9 = (bf16[832,128]{1,0:T(8,128)(2,1)S(1)}, bf16[832,128]{1,0:T(8,128)(2,1)S(1)}, u32[]{:S(2)}, u32[]{:S(2)}) collective-permute-start(bf16[832,128]{1,0:T(8,128)(2,1)S(1)} %shard_map.85.mine), channel_id=1, source_target_pairs={{0,1},{1,0},{2,3},{3,2},{4,5},{5,4},{6,7},{7,6},{8,9},{9,8},{10,11... | collective-permute-start | bytes 638984 | tf_op jit(solution)/shard_map/ppermute | solution.py:399
  49.0 2.1 %collective-permute-start.10 = (bf16[64,128]{1,0:T(8,128)(2,1)S(1)}, bf16[64,128]{1,0:T(8,128)(2,1)S(1)}, u32[]{:S(2)}, u32[]{:S(2)}) collective-permute-start(bf16[64,128]{1,0:T(8,128)(2,1)S(1)} %get-tuple-element.39), channel_id=1, source_target_pairs={{0,16},{16,0},{1,17},{17,1},{2,18},{18,2},{3,19},{19,3},{4,20},{20... | collective-permute-start | bytes 49160 | tf_op jit(solution)/shard_map/ppermute | solution.py:399

commit v2 on v1

--- a/solution.py
+++ b/solution.py
@@ -13,18 +13,18 @@
 PAIRS = SIDE // 2
 LANES = 2 * CHANNELS
 ROWS = PAIRS * SIDE
-WROWS = 5 * CHANNELS
+WROWS = 5 * CHANNELS // 2
 F32 = jnp.float32
 BF16 = jnp.bfloat16
 
 
-def call(kernel, outs, *args, scratch=(), flops=0, moved=0):
+def call(kernel, outs, *args, scratch=(), flops=0, moved=0, space=pltpu.VMEM):
     whole = pl.BlockSpec(memory_space=pltpu.VMEM)
     shapes = [jax.ShapeDtypeStruct(s, d) for s, d in outs]
     return pl.pallas_call(
         kernel,
         out_shape=shapes,
-        in_specs=[whole] * len(args),
+        in_specs=[pl.BlockSpec(memory_space=space)] * len(args),
         out_specs=[whole] * len(outs),
         scratch_shapes=list(scratch),
         compiler_params=pltpu.CompilerParams(vmem_limit_bytes=48 * 2**20),
@@ -89,15 +89,23 @@
     return total
 
 
-def rim_kernel(x_ref, rows_ref, cols_ref, scr):
+def rim_kernel(x_hbm, rows_ref, cols_ref, top, bottom, left, right, scr, sems):
+    copies = [
+        pltpu.make_async_copy(x_hbm.at[0:16, :], top, sems.at[0]),
+        pltpu.make_async_copy(x_hbm.at[SIDE - 16 : SIDE, :], bottom, sems.at[1]),
+        pltpu.make_async_copy(x_hbm.at[:, 0:LANES], left, sems.at[2]),
+        pltpu.make_async_copy(x_hbm.at[:, (PAIRS - 1) * LANES :], right, sems.at[3]),
+    ]
+    for copy in copies:
+        copy.start()
+    for copy in copies:
+        copy.wait()
     for q in range(PAIRS):
         lanes = slice(q * LANES, (q + 1) * LANES)
-        scr[q : q + 1, :] = x_ref[0:16, lanes].astype(F32)[0:1]
-        scr[PAIRS + q : PAIRS + q + 1, :] = x_ref[SIDE - 16 : SIDE, lanes].astype(F32)[15:16]
+        scr[q : q + 1, :] = top[:, lanes].astype(F32)[0:1]
+        scr[PAIRS + q : PAIRS + q + 1, :] = bottom[:, lanes].astype(F32)[15:16]
     rows_ref[...] = scr[...].astype(BF16)
-    first = x_ref[:, 0:LANES].astype(F32)
-    last = x_ref[:, (PAIRS - 1) * LANES :].astype(F32)
-    cols_ref[...] = halves(first, last).astype(BF16)
+    cols_ref[...] = halves(left[...].astype(F32), right[...].astype(F32)).astype(BF16)
 
 
 def bits_moved(v, pairs):
@@ -113,7 +121,9 @@
     bits = owners.bit_length() - 1
     index = index_ref[pl.ds(owner, 1), :]
     source, within = index >> 8, index & 255
-    slot = bits_moved((source & (owners - 1)) ^ owner, slot_bits(owners))
+    relative = (source & (owners - 1)) ^ owner
+    even, odd = (bits_moved(relative, slot_bits(owners, core)) for core in range(2))
+    slot = jnp.where((region & 1) == 1, odd, even)
     row = within & (SIDE - 1)
     if blocks == 2:
         row = row + jnp.where((((source >> bits) - region + regions) & (regions - 1)) == 1, SIDE, 0)
@@ -133,16 +143,16 @@
 
 
 def pick_kernel(owners, index_ref, pick_ref):
-    owner = lax.axis_index("patch")
-    base = (lax.axis_index("region") * owners + owner) * 4 * SIDE
-    back = [(b, a) for a, b in slot_bits(owners)]
+    owner, region = lax.axis_index("patch"), lax.axis_index("region")
+    base = (region * owners + owner) * 4 * SIDE
     want = 2 * iota((SIDE, LANES), 0)
-    is_low = low((1, LANES))
     for t in range(owners // 2):
         pair = []
         for slot in (2 * t, 2 * t + 1):
-            k = sum(1 << to for frm, to in back if (slot >> frm) & 1)
-            line = index_ref[pl.ds(owner ^ k, 1), :]
+            even, odd = (
+                sum(1 << frm for frm, to in slot_bits(owners, core) if (slot >> to) & 1) for core in range(2)
+            )
+            line = index_ref[pl.ds(owner ^ jnp.where((region & 1) == 1, odd, even), 1), :]
             pair.append((line[:, 1 : SIDE + 1], line[:, SIDE + 3 : 2 * SIDE + 3]))
         for s in range(2):
             both = jnp.concatenate([pair[0][s], pair[1][s]], axis=1) - base
@@ -207,7 +217,7 @@
 
 def middle_kernel(
     s_in, cot_ref, p0, p1, p2, rows_ref, cols_ref, hot_ref, half_ref, w_ref, wb_ref, wc_ref,
-    g_ref, msg_ref, own_ref, sums_ref, s_ref, cell_scr, gt, gb, gc, own_scr,
+    g_ref, keep_ref, send_ref, own_ref, sums_ref, s_ref, cell_scr, gt, gb, gc, own_scr, msg,
 ):
     many = rows_ref.shape[0]
     cells = dot(hot_ref[:, :many], rows_ref[...]) + dot(hot_ref[:, many:], cols_ref[...])
@@ -300,7 +310,10 @@
             high = tap(2 * t + 1, True)
         else:
             high = jnp.where(row == 0, coarse, jnp.where(row == 1, fine, 0.0))
-        msg_ref[t * SIDE : (t + 1) * SIDE, :] = halves(tap(2 * t, False), high).astype(BF16)
+        msg[t * SIDE : (t + 1) * SIDE, :] = halves(tap(2 * t, False), high)
+    core = lax.axis_index("region") & 1
+    keep_ref[...] = msg[pl.ds(pl.multiple_of(core * WROWS, WROWS), WROWS), :].astype(BF16)
+    send_ref[...] = msg[pl.ds(pl.multiple_of((1 - core) * WROWS, WROWS), WROWS), :].astype(BF16)
 
     lines = []
     for src, tap_row in ((gt, 2), (gb, 0)):
@@ -346,20 +359,24 @@
 def added_weights(mine, other):
     total = mine[0:WROWS, :].astype(F32) + other[0:WROWS, :].astype(F32)
     tail = total[WROWS - SIDE :]
-    whole = tail + pltpu.roll(tail, SIDE - 1, 0)
-    return total[: WROWS - SIDE], tail, whole
+    return total, tail + pltpu.roll(tail, SIDE - 1, 0)
+
+
+def bias_lanes(shape):
+    return jnp.logical_and(jnp.logical_not(low(shape)), (lax.axis_index("region") & 1) == 1)
 
 
 def join_kernel(mine, other, *rest):
     extra, out = rest[:-1], rest[-1]
-    total, tail, whole = added_weights(mine, other)
-    out[0 : WROWS - SIDE, :] = total.astype(BF16)
-    row = iota(tail.shape, 0)
+    total, whole = added_weights(mine, other)
+    out[0 : WROWS - SIDE, :] = total[: WROWS - SIDE].astype(BF16)
+    row = iota(whole.shape, 0)
     coarse = whole.astype(BF16).astype(F32)
     fine = pltpu.roll(whole - coarse, 1, 0)
-    is_low = low(tail.shape)
     out[WROWS - SIDE : WROWS, :] = jnp.where(
-        is_low, tail, jnp.where(row == 0, coarse, jnp.where(row == 1, fine, 0.0))
+        bias_lanes(whole.shape),
+        jnp.where(row == 0, coarse, jnp.where(row == 1, fine, 0.0)),
+        total[WROWS - SIDE :],
     ).astype(BF16)
     n = mine.shape[0] - WROWS
     if n:
@@ -369,19 +386,31 @@
         out[WROWS:, :] = extra[0][...]
 
 
-def last_kernel(scale, mine, other, inner, pick, side_a, side_b, grad_ref, wt_ref, bias_ref):
-    total, tail, whole = added_weights(mine, other)
+def close_kernel(scale, mine, other, out):
+    total, whole = added_weights(mine, other)
+    out[0 : WROWS - SIDE, :] = total[: WROWS - SIDE] * scale
+    out[WROWS - SIDE :, :] = jnp.where(bias_lanes(whole.shape), whole, total[WROWS - SIDE :]) * scale
+
+
+def weight_kernel(mine, other, wt_ref, bias_ref):
+    odd = (lax.axis_index("region") & 1) == 1
+    a, b = mine[...], other[...]
+    full = jnp.concatenate([jnp.where(odd, b, a), jnp.where(odd, a, b)], axis=0)
     for t in range(4):
-        wt_ref[:, t * LANES : (t + 1) * LANES] = total[t * SIDE : (t + 1) * SIDE] * scale
-    wt_ref[:, 4 * LANES :] = tail[:, :CHANNELS] * scale
-    bias_ref[...] = turn(whole)[0:1, :CHANNELS] * scale
+        wt_ref[:, t * LANES : (t + 1) * LANES] = full[t * SIDE : (t + 1) * SIDE]
+    wt_ref[:, 4 * LANES :] = full[4 * SIDE :, :CHANNELS]
+    bias_ref[...] = turn(full[4 * SIDE : 4 * SIDE + 8])[0:1, :CHANNELS]
+
+
+def last_kernel(mine, other, inner, pick, *rest):
+    side_refs, grad_ref = rest[:-1], rest[-1]
     n = mine.shape[0] - WROWS
     got = dot(pick[:, :n], mine[WROWS:, :]) + dot(pick[:, n:], other[WROWS:, :])
     a, b, c, d = (got[i * SIDE : (i + 1) * SIDE] for i in range(4))
     rims = halves(a + turn(b), turn(c) + d)
-    sides = side_a[...].astype(F32)
-    if side_b is not None:
-        sides = sides + side_b[...].astype(F32)
+    sides = side_refs[0][...].astype(F32)
+    for ref in side_refs[1:]:
+        sides = sides + ref[...].astype(F32)
     row = iota((SIDE, LANES), 0)
     is_low = low((SIDE, LANES))
     for q in range(PAIRS):
@@ -413,31 +442,50 @@
     return ks
 
 
-def slot_bits(owners):
-    bits = owners.bit_length() - 1
-    return [(bits - 1 - i, i) for i in range(bits)]
+def order_of(owners, core):
+    bits = list(range(owners.bit_length() - 1))[::-1]
+    return bits if core == 0 else bits[-1:] + bits[:-1]
+
+
+def slot_bits(owners, core):
+    return [(bit, step) for step, bit in enumerate(order_of(owners, core))]
+
+
+def exchange(x, step):
+    regions, owners = lax.axis_size("region"), lax.axis_size("patch")
+    pairs = []
+    for r in range(regions):
+        k = 1 << order_of(owners, r % 2)[step]
+        pairs += [(r * owners + i, r * owners + (i ^ k)) for i in range(owners)]
+    return lax.ppermute(x, ("region", "patch"), pairs)
 
 
 def body(fine_input, fine_weight, fine_bias, cotangent, halo_index):
     owners = lax.axis_size("patch")
     regions = lax.axis_size("region")
-    owner_id = lax.axis_index("patch")
-    region_id = lax.axis_index("region")
-    ks = steps_of(owners)
+    steps = owners.bit_length() - 1
     blocks = 1 if regions == 2 else 2
     x = fine_input.reshape(SIDE, SIDE * CHANNELS)
     cot = cotangent.reshape(SIDE, SIDE * CHANNELS)
     pair = ((ROWS + SIDE, LANES), BF16)
 
     rows, cols = call(
-        rim_kernel, [((SIDE, LANES), BF16)] * 2, x, scratch=[pltpu.VMEM((SIDE, LANES), F32)]
+        rim_kernel,
+        [((SIDE, LANES), BF16)] * 2,
+        x,
+        scratch=[
+            pltpu.VMEM((16, SIDE * CHANNELS), BF16), pltpu.VMEM((16, SIDE * CHANNELS), BF16),
+            pltpu.VMEM((SIDE, LANES), BF16), pltpu.VMEM((SIDE, LANES), BF16),
+            pltpu.VMEM((SIDE, LANES), F32), pltpu.SemaphoreType.DMA((4,)),
+        ],
+        space=pl.ANY,
     )
     if regions == 2:
         cols = swap(cols, "region", 1)
     else:
         cols = jnp.concatenate([shift(cols, "region", 1), shift(cols, "region", -1)], axis=0)
-    for k in ks:
-        rows = jnp.concatenate([rows, swap(rows, "patch", k)], axis=0)
+    for step in range(steps):
+        rows = jnp.concatenate([rows, exchange(rows, step)], axis=0)
 
     cells = 272
     hot, half_mask = call(
@@ -457,13 +505,13 @@
     )[0]
 
     line = pltpu.VMEM((40, LANES), F32)
-    grad, message, own_rows, sums = call(
+    grad, message, sent, own_rows, sums = call(
         middle_kernel,
-        [((ROWS, LANES), BF16), ((WROWS, LANES), BF16), ((SIDE, LANES), BF16), ((blocks * SIDE, LANES), BF16)],
+        [((ROWS, LANES), BF16), ((WROWS, LANES), BF16), ((WROWS, LANES), BF16), ((SIDE, LANES), BF16), ((blocks * SIDE, LANES), BF16)],
         signal, cot, *copies, rows, cols, hot, half_mask, forward, backward, columns,
         scratch=[
             pltpu.VMEM((ROWS, LANES), F32), pltpu.VMEM((cells, LANES), F32), line, line,
-            pltpu.VMEM((96, LANES), F32), pltpu.VMEM((SIDE, LANES), F32),
+            pltpu.VMEM((96, LANES), F32), pltpu.VMEM((SIDE, LANES), F32), pltpu.VMEM((2 * WROWS, LANES), F32),
         ],
         flops=2 * ROWS * 768 * 128, moved=4 * 2**20,
     )
@@ -480,29 +528,26 @@
         inner_kernel, [((ROWS, LANES), F32)], *grad_copies, backward, flops=2 * ROWS * 768 * 128, moved=3 * 2**20
     )[0]
 
-    region_ks = steps_of(regions)
+    region_ks = [1] + [k for k in steps_of(regions) if k > 1]
     for k in region_ks:
         extra = (own_rows,) if k == region_ks[-1] else ()
         size = (WROWS + SIDE * len(extra), LANES)
-        message = call(join_kernel, [(size, BF16)], message, swap(message, "region", k), *extra)[0]
-    for k in ks[:-1]:
+        other = swap(sent if k == 1 else message, "region", k)
+        message = call(join_kernel, [(size, BF16)], message, other, *extra)[0]
+    for step in range(steps - 1):
         size = (2 * message.shape[0] - WROWS, LANES)
-        message = call(join_kernel, [(size, BF16)], message, swap(message, "patch", k))[0]
-    other = swap(message, "patch", ks[-1])
+        message = call(join_kernel, [(size, BF16)], message, exchange(message, step))[0]
+    other = exchange(message, steps - 1)
     scale = 1.0 / math.sqrt(regions * owners * SIDE * SIDE)
-    kernel = functools.partial(last_kernel, scale)
-    if len(sides) == 1:
-        kernel = functools.partial(last_one_side, scale)
-    input_grad, weight_grad, bias_grad = call(
-        kernel,
-        [((SIDE, SIDE * CHANNELS), BF16), ((CHANNELS, 9 * CHANNELS), F32), ((1, CHANNELS), F32)],
-        message, other, inner, pick, *sides,
+    part = call(functools.partial(close_kernel, scale), [((WROWS, LANES), F32)], message, other)[0]
+    other_part = swap(part, "region", 1)
+    input_grad = call(
+        last_kernel, [((SIDE, SIDE * CHANNELS), BF16)], message, other, inner, pick, *sides, moved=2 * 2**20
+    )[0]
+    weight_grad, bias_grad = call(
+        weight_kernel, [((CHANNELS, 9 * CHANNELS), F32), ((1, CHANNELS), F32)], part, other_part
     )
     return input_grad.reshape(1, SIDE, SIDE * CHANNELS), weight_grad.T, bias_grad.reshape(CHANNELS)
-
-
-def last_one_side(scale, mine, other, inner, pick, side_a, grad_ref, wt_ref, bias_ref):
-    last_kernel(scale, mine, other, inner, pick, side_a, None, grad_ref, wt_ref, bias_ref)
 
 
 def solution(mesh):

time: 53.1 us -> 55.4 us (1.043)
  Pallas kernels: 13.1 us -> 14.1 us
  starting transfers between devices: 14.4 us -> 15.3 us
    ppermute x0 -> x8, waiting for transfers between devices: none -> 21.3 us  [exchange(): return lax.ppermute(x, ('region', 'patch'), pairs)]
    ppermute x11 -> x4, waiting for transfers between devices: 22.2 us -> 1.21 us  [swap(): return lax.ppermute(x, axis, [(i, i ^ k) for i in range(n)])]
    ppermute x0 -> x8, starting transfers between devices: none -> 14.6 us  [exchange(): return lax.ppermute(x, ('region', 'patch'), pairs)]
    ppermute x11 -> x4, starting transfers between devices: 14.4 us -> 0.7 us  [swap(): return lax.ppermute(x, axis, [(i, i ^ k) for i in range(n)])]
    pallas_call x14 -> x16, Pallas kernels: 13.1 us -> 14.1 us  [call(): pl.pallas_call(kernel, out_shape=shapes, in_specs=[pl.BlockSpec(memory_sp...]
  transfers between devices with their start and end apart: 11 -> 12, of which waited for: 7 -> 7; matrix products, arithmetic and copies ran while one was open for 0% -> 0% of each run, Pallas kernels for 15% -> 16%
where the time goes in v2:
time: 55.4 us; the launch traced here: 55.2 us
  waiting for transfers between devices  22.5 us (41%)
  starting transfers between devices  15.3 us (28%)
  Pallas kernels  14.1 us (25%)
  local copies, waits for them, and re-layouts  2.37 us (4%)
  between operations  0.83 us (1%)
    ppermute x8, waiting for transfers between devices, exchange(): return lax.ppermute(x, ('region', 'patch'), pairs)  21.3 us
    ppermute x8, starting transfers between devices, exchange(): return lax.ppermute(x, ('region', 'patch'), pairs)  14.6 us
    pallas_call x16, Pallas kernels, call(): pl.pallas_call(kernel, out_shape=shapes, in_specs=[pl.BlockSpec(memory_sp...  14.1 us
    unnamed x14, local copies, waits for them, and re-layouts  2.36 us
    ppermute x4, waiting for transfers between devices, swap(): return lax.ppermute(x, axis, [(i, i ^ k) for i in range(n)])  1.21 us
  transfers between devices with their start and end apart: 12, of which 7 were waited for; matrix products, arithmetic and copies ran while one was open for 0% of the time, Pallas kernels for 16%

profile of v2, /device:TPU:0, one launch (start us, length us, event | category | flops | bytes accessed | tf_op | source)
XLA Modules:
  0.0 55.2 jit_solution(13822205052864680178)
XLA Ops:
  0.6 1.0 %copy-done = bf16[1,64,4096]{2,1,0:T(8,128)(2,1)S(1)} copy-done((bf16[1,64,4096]{2,1,0:T(8,128)(2,1)S(1)}, bf16[1,64,4096]{2,1,0:T(8,128)(2,1)}, u32[]{:S(2)}) %copy-start) | copy-done | bytes 524312
  2.1 4.1 %collective-permute-start = (bf16[64,128]{1,0:T(8,128)(2,1)S(1)}, bf16[64,128]{1,0:T(8,128)(2,1)S(1)}, u32[]{:S(2)}, u32[]{:S(2)}) collective-permute-start(bf16[64,128]{1,0:T(8,128)(2,1)S(1)} %get-tuple-element.27), channel_id=1, source_target_pairs={{0,8},{1,9},{2,10},{3,11},{4,12},{5,13},{6,14},{7,15},{8,0},{9,1},... | collective-permute-start | bytes 49160 | tf_op jit(solution)/shard_map/ppermute | solution.py:460
  6.2 1.5 %shard_map.76 = (bf16[2112,128]{1,0:T(8,128)(2,1)S(1)}, bf16[2112,128]{1,0:T(8,128)(2,1)S(1)}, bf16[2112,128]{1,0:T(8,128)(2,1)S(1)}) custom-call(bf16[64,4096]{1,0:T(8,128)(2,1)S(1)} %bitcast.8), custom_call_target="tpu_custom_call" | custom-call | bytes 2097152 | tf_op jit(solution)/shard_map/pallas_call | solution.py:24
  7.8 0.6 %copy-done.2 = s32[16,260]{1,0:T(8,128)S(1)} copy-done((s32[16,260]{1,0:T(8,128)S(1)}, s32[16,260]{1,0:T(8,128)}, u32[]{:S(2)}) %copy-start.2) | copy-done | bytes 16664
  8.7 1.6 %collective-permute-start.1 = (bf16[128,128]{1,0:T(8,128)(2,1)S(1)}, bf16[128,128]{1,0:T(8,128)(2,1)S(1)}, u32[]{:S(2)}, u32[]{:S(2)}) collective-permute-start(bf16[128,128]{1,0:T(8,128)(2,1)S(1)} %pad_maximum_fusion.2), channel_id=1, source_target_pairs={{0,4},{1,5},{2,6},{3,7},{4,0},{5,1},{6,2},{7,3},{8,12},{9,13},{10,... | collective-permute-start | bytes 98312 | tf_op jit(solution)/shard_map/ppermute | solution.py:460
  10.4 0.7 %copy-done.4 = f32[64]{0:T(128)S(1)} copy-done((f32[64]{0:T(128)S(1)}, f32[64]{0:T(128)}, u32[]{:S(2)}) %copy-start.4) | copy-done | bytes 280
  11.0 2.2 %shard_map.78.s_in = f32[2048,128]{1,0:T(8,128)S(1)} custom-call(bf16[2112,128]{1,0:T(8,128)(2,1)S(1)} %get-tuple-element.23.p0, bf16[2112,128]{1,0:T(8,128)(2,1)S(1)} %get-tuple-element.24.p1, bf16[2112,128]{1,0:T(8,128)(2,1)S(1)} %get-tuple-element.25.p2, bf16[3,128,256]{2,1,0:T(8,128)(2,1)S(1)} %get-tuple-element.26.w_ref, f32[1,64]{1,0:T(1,128)S(1)} %bitcast.11), custom_call_target="tpu_custom_call" | custom-call | flops 402653184 | bytes 3145728 | tf_op jit(solution)/shard_map/pallas_call | solution.py:24
  13.3 1.6 %collective-permute-start.2 = (bf16[256,128]{1,0:T(8,128)(2,1)S(1)}, bf16[256,128]{1,0:T(8,128)(2,1)S(1)}, u32[]{:S(2)}, u32[]{:S(2)}) collective-permute-start(bf16[256,128]{1,0:T(8,128)(2,1)S(1)} %pad_maximum_fusion.1), channel_id=1, source_target_pairs={{0,2},{1,3},{2,0},{3,1},{4,6},{5,7},{6,4},{7,5},{8,10},{9,11},{10,... | collective-permute-start | bytes 196616 | tf_op jit(solution)/shard_map/ppermute | solution.py:460
  14.9 2.7 %collective-permute-done.2 = bf16[256,128]{1,0:T(8,128)(2,1)S(1)} collective-permute-done((bf16[256,128]{1,0:T(8,128)(2,1)S(1)}, bf16[256,128]{1,0:T(8,128)(2,1)S(1)}, u32[]{:S(2)}, u32[]{:S(2)}) %collective-permute-start.2) | collective-permute-done | bytes 65568 | tf_op jit(solution)/shard_map/ppermute | solution.py:460
  17.7 1.6 %collective-permute-start.3 = (bf16[512,128]{1,0:T(8,128)(2,1)S(1)}, bf16[512,128]{1,0:T(8,128)(2,1)S(1)}, u32[]{:S(2)}, u32[]{:S(2)}) collective-permute-start(bf16[512,128]{1,0:T(8,128)(2,1)S(1)} %pad_maximum_fusion), channel_id=1, source_target_pairs={{0,1},{1,0},{2,3},{3,2},{4,5},{5,4},{6,7},{7,6},{8,9},{9,8},{10,11... | collective-permute-start | bytes 393224 | tf_op jit(solution)/shard_map/ppermute | solution.py:460
  19.2 3.5 %collective-permute-done.3 = bf16[512,128]{1,0:T(8,128)(2,1)S(1)} collective-permute-done((bf16[512,128]{1,0:T(8,128)(2,1)S(1)}, bf16[512,128]{1,0:T(8,128)(2,1)S(1)}, u32[]{:S(2)}, u32[]{:S(2)}) %collective-permute-start.3) | collective-permute-done | bytes 131104 | tf_op jit(solution)/shard_map/ppermute | solution.py:460
  22.7 3.9 %shard_map.81 = (bf16[2048,128]{1,0:T(8,128)(2,1)S(1)}, bf16[160,128]{1,0:T(8,128)(2,1)S(1)}, bf16[160,128]{1,0:T(8,128)(2,1)S(1)}, bf16[64,128]{1,0:T(8,128)(2,1)S(1)}, bf16[64,128]{1,0:T(8,128)(2,1)S(1)}) custom-call(f32[2048,128]{1,0:T(8,128)S(1)} %shard_map.78.s_in, bf16[64,4096]{1,0:T(8,128)(2,1)S(1)} %bitcast.9, ...), custom_call_target="tpu_custom_call" | custom-call | flops 402653184 | bytes 4194304 | tf_op jit(solution)/shard_map/pallas_call | solution.py:24
  26.7 1.2 %collective-permute-done.5.other = bf16[160,128]{1,0:T(8,128)(2,1)S(1)} collective-permute-done((bf16[160,128]{1,0:T(8,128)(2,1)S(1)}, bf16[160,128]{1,0:T(8,128)(2,1)S(1)}, u32[]{:S(2)}, u32[]{:S(2)}) %collective-permute-start.5) | collective-permute-done | bytes 40992 | tf_op jit(solution)/shard_map/ppermute | solution.py:428
  27.9 2.1 %collective-permute-start.6 = (bf16[224,128]{1,0:T(8,128)(2,1)S(1)}, bf16[224,128]{1,0:T(8,128)(2,1)S(1)}, u32[]{:S(2)}, u32[]{:S(2)}) collective-permute-start(bf16[224,128]{1,0:T(8,128)(2,1)S(1)} %shard_map.82.mine), channel_id=1, source_target_pairs={{0,8},{1,9},{2,10},{3,11},{4,12},{5,13},{6,14},{7,15},{8,0},{9,1},... | collective-permute-start | bytes 172040 | tf_op jit(solution)/shard_map/ppermute | solution.py:460
  30.1 3.6 %collective-permute-done.6.other = bf16[224,128]{1,0:T(8,128)(2,1)S(1)} collective-permute-done((bf16[224,128]{1,0:T(8,128)(2,1)S(1)}, bf16[224,128]{1,0:T(8,128)(2,1)S(1)}, u32[]{:S(2)}, u32[]{:S(2)}) %collective-permute-start.6) | collective-permute-done | bytes 57376 | tf_op jit(solution)/shard_map/ppermute | solution.py:460
  34.2 3.9 %collective-permute-done.7.other = bf16[288,128]{1,0:T(8,128)(2,1)S(1)} collective-permute-done((bf16[288,128]{1,0:T(8,128)(2,1)S(1)}, bf16[288,128]{1,0:T(8,128)(2,1)S(1)}, u32[]{:S(2)}, u32[]{:S(2)}) %collective-permute-start.7) | collective-permute-done | bytes 73760 | tf_op jit(solution)/shard_map/ppermute | solution.py:460
  38.2 1.6 %collective-permute-start.8 = (bf16[416,128]{1,0:T(8,128)(2,1)S(1)}, bf16[416,128]{1,0:T(8,128)(2,1)S(1)}, u32[]{:S(2)}, u32[]{:S(2)}) collective-permute-start(bf16[416,128]{1,0:T(8,128)(2,1)S(1)} %shard_map.84.mine), channel_id=1, source_target_pairs={{0,2},{1,3},{2,0},{3,1},{4,6},{5,7},{6,4},{7,5},{8,10},{9,11},{10,... | collective-permute-start | bytes 319496 | tf_op jit(solution)/shard_map/ppermute | solution.py:460
  39.8 3.6 %collective-permute-done.8.other = bf16[416,128]{1,0:T(8,128)(2,1)S(1)} collective-permute-done((bf16[416,128]{1,0:T(8,128)(2,1)S(1)}, bf16[416,128]{1,0:T(8,128)(2,1)S(1)}, u32[]{:S(2)}, u32[]{:S(2)}) %collective-permute-start.8) | collective-permute-done | bytes 106528 | tf_op jit(solution)/shard_map/ppermute | solution.py:460
  43.4 1.6 %collective-permute-start.9 = (bf16[672,128]{1,0:T(8,128)(2,1)S(1)}, bf16[672,128]{1,0:T(8,128)(2,1)S(1)}, u32[]{:S(2)}, u32[]{:S(2)}) collective-permute-start(bf16[672,128]{1,0:T(8,128)(2,1)S(1)} %shard_map.85.mine), channel_id=1, source_target_pairs={{0,1},{1,0},{2,3},{3,2},{4,5},{5,4},{6,7},{7,6},{8,9},{9,8},{10,11... | collective-permute-start | bytes 516104 | tf_op jit(solution)/shard_map/ppermute | solution.py:460
  45.0 3.9 %collective-permute-done.9.other = bf16[672,128]{1,0:T(8,128)(2,1)S(1)} collective-permute-done((bf16[672,128]{1,0:T(8,128)(2,1)S(1)}, bf16[672,128]{1,0:T(8,128)(2,1)S(1)}, u32[]{:S(2)}, u32[]{:S(2)}) %collective-permute-start.9) | collective-permute-done | bytes 172064 | tf_op jit(solution)/shard_map/ppermute | solution.py:460
  49.2 1.5 %shard_map.86 = (bf16[2112,128]{1,0:T(8,128)(2,1)S(1)}, bf16[2112,128]{1,0:T(8,128)(2,1)S(1)}, bf16[2112,128]{1,0:T(8,128)(2,1)S(1)}) custom-call(bf16[2048,128]{1,0:T(8,128)(2,1)S(1)} %get-tuple-element.36.g_ref), custom_call_target="tpu_custom_call" | custom-call | bytes 2097152 | tf_op jit(solution)/shard_map/pallas_call | solution.py:24
  51.3 2.0 %shard_map.87.inner = f32[2048,128]{1,0:T(8,128)S(1)} custom-call(bf16[2112,128]{1,0:T(8,128)(2,1)S(1)} %get-tuple-element.37.p0, bf16[2112,128]{1,0:T(8,128)(2,1)S(1)} %get-tuple-element.38.p1, bf16[2112,128]{1,0:T(8,128)(2,1)S(1)} %get-tuple-element.39.p2, bf16[3,256,128]{2,1,0:T(8,128)(2,1)S(1)} %get-tuple-element.31.wb_ref), custom_call_target="tpu_custom_call" | custom-call | flops 402653184 | bytes 3145728 | tf_op jit(solution)/shard_map/pallas_call | solution.py:24
  53.3 1.2 %shard_map.89 = bf16[64,4096]{1,0:T(8,128)(2,1)} custom-call(bf16[672,128]{1,0:T(8,128)(2,1)S(1)} %shard_map.85.mine, bf16[672,128]{1,0:T(8,128)(2,1)S(1)} %collective-permute-done.9.other, f32[2048,128]{1,0:T(8,128)S(1)} %shard_map.87.inner, bf16[256,1024]{1,0:T(8,128)(2,1)S(1)} %shard_map.88.pick, bf16[64,128]{1,0:T(8,128)(2,1)S(1)} %collective-permute-done.10.rest_0_), custom_call_target="tpu_custom_call" | custom-call | bytes 2097152 | tf_op jit(solution)/shard_map/pallas_call | solution.py:24
  54.5 0.7 %shard_map.91 = (f32[64,576]{1,0:T(8,128)}, f32[1,64]{1,0:T(1,128)}) custom-call(f32[160,128]{1,0:T(8,128)S(1)} %shard_map.90.mine, f32[160,128]{1,0:T(8,128)S(1)} %collective-permute-done.11.other), custom_call_target="tpu_custom_call" | custom-call | tf_op jit(solution)/shard_map/pallas_call | solution.py:24
  (34 shorter events, 2.4 us)
Async XLA Ops:
  0.6 1.0 %copy-start = (bf16[1,64,4096]{2,1,0:T(8,128)(2,1)S(1)}, bf16[1,64,4096]{2,1,0:T(8,128)(2,1)}, u32[]{:S(2)}) copy-start(bf16[1,64,4096]{2,1,0:T(8,128)(2,1)} %param.5) | copy-start | bytes 1572868
  2.1 6.7 %collective-permute-start = (bf16[64,128]{1,0:T(8,128)(2,1)S(1)}, bf16[64,128]{1,0:T(8,128)(2,1)S(1)}, u32[]{:S(2)}, u32[]{:S(2)}) collective-permute-start(bf16[64,128]{1,0:T(8,128)(2,1)S(1)} %get-tuple-element.27), channel_id=1, source_target_pairs={{0,8},{1,9},{2,10},{3,11},{4,12},{5,13},{6,14},{7,15},{8,0},{9,1},... | collective-permute-start | bytes 49160 | tf_op jit(solution)/shard_map/ppermute | solution.py:460
  6.2 16.6 %collective-permute-start.4 = (bf16[64,128]{1,0:T(8,128)(2,1)S(1)}, bf16[64,128]{1,0:T(8,128)(2,1)S(1)}, u32[]{:S(2)}, u32[]{:S(2)}) collective-permute-start(bf16[64,128]{1,0:T(8,128)(2,1)S(1)} %get-tuple-element.28), channel_id=1, source_target_pairs={{0,16},{16,0},{1,17},{17,1},{2,18},{18,2},{3,19},{19,3},{4,20},{20... | collective-permute-start | bytes 49160 | tf_op jit(solution)/shard_map/ppermute | solution.py:428
  6.2 1.5 %copy-start.3 = (bf16[576,64]{0,1:T(8,128)(2,1)S(1)}, bf16[576,64]{0,1:T(8,128)(2,1)}, u32[]{:S(2)}) copy-start(bf16[576,64]{0,1:T(8,128)(2,1)} %param.6) | copy-start | bytes 221188
  7.7 0.7 %copy-start.2 = (s32[16,260]{1,0:T(8,128)S(1)}, s32[16,260]{1,0:T(8,128)}, u32[]{:S(2)}) copy-start(s32[16,260]{1,0:T(8,128)} %index_ref.3) | copy-start | bytes 49924
  8.7 4.5 %collective-permute-start.1 = (bf16[128,128]{1,0:T(8,128)(2,1)S(1)}, bf16[128,128]{1,0:T(8,128)(2,1)S(1)}, u32[]{:S(2)}, u32[]{:S(2)}) collective-permute-start(bf16[128,128]{1,0:T(8,128)(2,1)S(1)} %pad_maximum_fusion.2), channel_id=1, source_target_pairs={{0,4},{1,5},{2,6},{3,7},{4,0},{5,1},{6,2},{7,3},{8,12},{9,13},{10,... | collective-permute-start | bytes 98312 | tf_op jit(solution)/shard_map/ppermute | solution.py:460
  10.4 0.7 %copy-start.4 = (f32[64]{0:T(128)S(1)}, f32[64]{0:T(128)}, u32[]{:S(2)}) copy-start(f32[64]{0:T(128)} %param.7) | copy-start | bytes 772
  13.3 9.4 %copy-start.1 = (bf16[1,64,4096]{2,1,0:T(8,128)(2,1)S(1)}, bf16[1,64,4096]{2,1,0:T(8,128)(2,1)}, u32[]{:S(2)}) copy-start(bf16[1,64,4096]{2,1,0:T(8,128)(2,1)} %param.8) | copy-start | bytes 1572868
  13.3 4.3 %collective-permute-start.2 = (bf16[256,128]{1,0:T(8,128)(2,1)S(1)}, bf16[256,128]{1,0:T(8,128)(2,1)S(1)}, u32[]{:S(2)}, u32[]{:S(2)}) collective-permute-start(bf16[256,128]{1,0:T(8,128)(2,1)S(1)} %pad_maximum_fusion.1), channel_id=1, source_target_pairs={{0,2},{1,3},{2,0},{3,1},{4,6},{5,7},{6,4},{7,5},{8,10},{9,11},{10,... | collective-permute-start | bytes 196616 | tf_op jit(solution)/shard_map/ppermute | solution.py:460
  17.7 5.0 %collective-permute-start.3 = (bf16[512,128]{1,0:T(8,128)(2,1)S(1)}, bf16[512,128]{1,0:T(8,128)(2,1)S(1)}, u32[]{:S(2)}, u32[]{:S(2)}) collective-permute-start(bf16[512,128]{1,0:T(8,128)(2,1)S(1)} %pad_maximum_fusion), channel_id=1, source_target_pairs={{0,1},{1,0},{2,3},{3,2},{4,5},{5,4},{6,7},{7,6},{8,9},{9,8},{10,11... | collective-permute-start | bytes 393224 | tf_op jit(solution)/shard_map/ppermute | solution.py:460
  26.6 1.3 %collective-permute-start.5 = (bf16[160,128]{1,0:T(8,128)(2,1)S(1)}, bf16[160,128]{1,0:T(8,128)(2,1)S(1)}, u32[]{:S(2)}, u32[]{:S(2)}) collective-permute-start(bf16[160,128]{1,0:T(8,128)(2,1)S(1)} %get-tuple-element.34), channel_id=1, source_target_pairs={{0,16},{16,0},{1,17},{17,1},{2,18},{18,2},{3,19},{19,3},{4,20},{20... | collective-permute-start | bytes 122888 | tf_op jit(solution)/shard_map/ppermute | solution.py:428
  27.9 5.8 %collective-permute-start.6 = (bf16[224,128]{1,0:T(8,128)(2,1)S(1)}, bf16[224,128]{1,0:T(8,128)(2,1)S(1)}, u32[]{:S(2)}, u32[]{:S(2)}) collective-permute-start(bf16[224,128]{1,0:T(8,128)(2,1)S(1)} %shard_map.82.mine), channel_id=1, source_target_pairs={{0,8},{1,9},{2,10},{3,11},{4,12},{5,13},{6,14},{7,15},{8,0},{9,1},... | collective-permute-start | bytes 172040 | tf_op jit(solution)/shard_map/ppermute | solution.py:460
  33.7 4.4 %collective-permute-start.7 = (bf16[288,128]{1,0:T(8,128)(2,1)S(1)}, bf16[288,128]{1,0:T(8,128)(2,1)S(1)}, u32[]{:S(2)}, u32[]{:S(2)}) collective-permute-start(bf16[288,128]{1,0:T(8,128)(2,1)S(1)} %shard_map.83.mine), channel_id=1, source_target_pairs={{0,4},{1,5},{2,6},{3,7},{4,0},{5,1},{6,2},{7,3},{8,12},{9,13},{10,... | collective-permute-start | bytes 221192 | tf_op jit(solution)/shard_map/ppermute | solution.py:460
  38.2 5.2 %collective-permute-start.8 = (bf16[416,128]{1,0:T(8,128)(2,1)S(1)}, bf16[416,128]{1,0:T(8,128)(2,1)S(1)}, u32[]{:S(2)}, u32[]{:S(2)}) collective-permute-start(bf16[416,128]{1,0:T(8,128)(2,1)S(1)} %shard_map.84.mine), channel_id=1, source_target_pairs={{0,2},{1,3},{2,0},{3,1},{4,6},{5,7},{6,4},{7,5},{8,10},{9,11},{10,... | collective-permute-start | bytes 319496 | tf_op jit(solution)/shard_map/ppermute | solution.py:460
  43.4 5.5 %collective-permute-start.9 = (bf16[672,128]{1,0:T(8,128)(2,1)S(1)}, bf16[672,128]{1,0:T(8,128)(2,1)S(1)}, u32[]{:S(2)}, u32[]{:S(2)}) collective-permute-start(bf16[672,128]{1,0:T(8,128)(2,1)S(1)} %shard_map.85.mine), channel_id=1, source_target_pairs={{0,1},{1,0},{2,3},{3,2},{4,5},{5,4},{6,7},{7,6},{8,9},{9,8},{10,11... | collective-permute-start | bytes 516104 | tf_op jit(solution)/shard_map/ppermute | solution.py:460
  48.9 5.6 %collective-permute-start.11 = (f32[160,128]{1,0:T(8,128)S(1)}, f32[160,128]{1,0:T(8,128)S(1)}, u32[]{:S(2)}, u32[]{:S(2)}) collective-permute-start(f32[160,128]{1,0:T(8,128)S(1)} %shard_map.90.mine), channel_id=1, source_target_pairs={{0,16},{16,0},{1,17},{17,1},{2,18},{18,2},{3,19},{19,3},{4,20},{20... | collective-permute-start | bytes 245768 | tf_op jit(solution)/shard_map/ppermute | solution.py:428
  50.7 2.6 %collective-permute-start.10 = (bf16[64,128]{1,0:T(8,128)(2,1)S(1)}, bf16[64,128]{1,0:T(8,128)(2,1)S(1)}, u32[]{:S(2)}, u32[]{:S(2)}) collective-permute-start(bf16[64,128]{1,0:T(8,128)(2,1)S(1)} %get-tuple-element.40), channel_id=1, source_target_pairs={{0,16},{16,0},{1,17},{17,1},{2,18},{18,2},{3,19},{19,3},{4,20},{20... | collective-permute-start | bytes 49160 | tf_op jit(solution)/shard_map/ppermute | solution.py:428

commit v3 on v2

--- a/solution.py
+++ b/solution.py
@@ -18,7 +18,7 @@
 BF16 = jnp.bfloat16
 
 
-def call(kernel, outs, *args, scratch=(), flops=0, moved=0, space=pltpu.VMEM):
+def call(kernel, outs, *args, scratch=(), flops=0, moved=0, space=pltpu.VMEM, limit=48):
     whole = pl.BlockSpec(memory_space=pltpu.VMEM)
     shapes = [jax.ShapeDtypeStruct(s, d) for s, d in outs]
     return pl.pallas_call(
@@ -27,7 +27,7 @@
         in_specs=[pl.BlockSpec(memory_space=space)] * len(args),
         out_specs=[whole] * len(outs),
         scratch_shapes=list(scratch),
-        compiler_params=pltpu.CompilerParams(vmem_limit_bytes=48 * 2**20),
+        compiler_params=pltpu.CompilerParams(vmem_limit_bytes=limit * 2**20),
         cost_estimate=pl.CostEstimate(flops=flops, bytes_accessed=moved, transcendentals=0),
     )(*args)
 
@@ -217,7 +217,7 @@
 
 def middle_kernel(
     s_in, cot_ref, p0, p1, p2, rows_ref, cols_ref, hot_ref, half_ref, w_ref, wb_ref, wc_ref,
-    g_ref, keep_ref, send_ref, own_ref, sums_ref, s_ref, cell_scr, gt, gb, gc, own_scr, msg,
+    g_ref, keep_ref, send_ref, own_ref, s_ref, cell_scr, gt, gb, gc, own_scr, msg,
 ):
     many = rows_ref.shape[0]
     cells = dot(hot_ref[:, :many], rows_ref[...]) + dot(hot_ref[:, many:], cols_ref[...])
@@ -313,7 +313,7 @@
         msg[t * SIDE : (t + 1) * SIDE, :] = halves(tap(2 * t, False), high)
     core = lax.axis_index("region") & 1
     keep_ref[...] = msg[pl.ds(pl.multiple_of(core * WROWS, WROWS), WROWS), :].astype(BF16)
-    send_ref[...] = msg[pl.ds(pl.multiple_of((1 - core) * WROWS, WROWS), WROWS), :].astype(BF16)
+    send_ref[0:WROWS, :] = msg[pl.ds(pl.multiple_of((1 - core) * WROWS, WROWS), WROWS), :].astype(BF16)
 
     lines = []
     for src, tap_row in ((gt, 2), (gb, 0)):
@@ -338,7 +338,7 @@
     ):
         cell_scr[at : at + n, :] = src[first_row : first_row + n]
     placed = jnp.where(upper == low(cells.shape), 0.0, cell_scr[...]).astype(BF16)
-    sums_ref[...] = dot(hot_ref[:, many:], placed, TN).astype(BF16)
+    send_ref[WROWS:, :] = dot(hot_ref[:, many:], placed, TN).astype(BF16)
 
 
 def grad_copies_kernel(g_ref, p0, p1, p2):
@@ -408,7 +408,7 @@
     got = dot(pick[:, :n], mine[WROWS:, :]) + dot(pick[:, n:], other[WROWS:, :])
     a, b, c, d = (got[i * SIDE : (i + 1) * SIDE] for i in range(4))
     rims = halves(a + turn(b), turn(c) + d)
-    sides = side_refs[0][...].astype(F32)
+    sides = side_refs[0][side_refs[0].shape[0] - SIDE :, :].astype(F32)
     for ref in side_refs[1:]:
         sides = sides + ref[...].astype(F32)
     row = iota((SIDE, LANES), 0)
@@ -479,70 +479,82 @@
             pltpu.VMEM((SIDE, LANES), F32), pltpu.SemaphoreType.DMA((4,)),
         ],
         space=pl.ANY,
+        limit=60,
     )
     if regions == 2:
         cols = swap(cols, "region", 1)
     else:
         cols = jnp.concatenate([shift(cols, "region", 1), shift(cols, "region", -1)], axis=0)
-    for step in range(steps):
-        rows = jnp.concatenate([rows, exchange(rows, step)], axis=0)
-
-    cells = 272
-    hot, half_mask = call(
-        functools.partial(plan_kernel, owners, regions, blocks),
-        [((cells, (owners + blocks) * SIDE), BF16), ((cells, LANES), F32)],
-        halo_index, scratch=[pltpu.VMEM((8, 384), F32)],
-    )
+    count = 272
+    both = ((ROWS, LANES), F32)
+    work = dict(flops=2 * ROWS * 768 * 128, moved=3 * 2**20)
+
+    other = exchange(rows, 0)
+    copies = call(copies_kernel, [pair] * 3, x, moved=2 * 2**20)
     forward, backward, columns = call(
         weights_kernel,
         [((3, LANES, 2 * LANES), BF16), ((3, 2 * LANES, LANES), BF16), ((3, LANES, LANES), BF16)],
         fine_weight.T,
     )
-    copies = call(copies_kernel, [pair] * 3, x, moved=2 * 2**20)
-    signal = call(
-        signal_kernel, [((ROWS, LANES), F32)], *copies, forward, fine_bias.reshape(1, CHANNELS),
-        flops=2 * ROWS * 768 * 128, moved=3 * 2**20,
-    )[0]
+    other, copies, forward = lax.optimization_barrier((other, copies, forward))
+    rows = jnp.concatenate([rows, other], axis=0)
+    other = exchange(rows, 1)
+    signal = call(signal_kernel, [both], *copies, forward, fine_bias.reshape(1, CHANNELS), **work)[0]
+    other, signal, index = lax.optimization_barrier((other, signal, halo_index))
+    rows = jnp.concatenate([rows, other], axis=0)
+    other = exchange(rows, 2)
+    hot, half_mask = call(
+        functools.partial(plan_kernel, owners, regions, blocks),
+        [((count, (owners + blocks) * SIDE), BF16), ((count, LANES), F32)],
+        index, scratch=[pltpu.VMEM((8, 384), F32)],
+    )
+    pick = call(functools.partial(pick_kernel, owners), [((4 * SIDE, owners * SIDE), BF16)], index)[0]
+    other, hot, half_mask, pick = lax.optimization_barrier((other, hot, half_mask, pick))
+    rows = jnp.concatenate([rows, other], axis=0)
+    for step in range(3, steps):
+        rows = jnp.concatenate([rows, exchange(rows, step)], axis=0)
 
     line = pltpu.VMEM((40, LANES), F32)
-    grad, message, sent, own_rows, sums = call(
+    grad, message, sent, own_rows = call(
         middle_kernel,
-        [((ROWS, LANES), BF16), ((WROWS, LANES), BF16), ((WROWS, LANES), BF16), ((SIDE, LANES), BF16), ((blocks * SIDE, LANES), BF16)],
+        [((ROWS, LANES), BF16), ((WROWS, LANES), BF16), ((WROWS + blocks * SIDE, LANES), BF16), ((SIDE, LANES), BF16)],
         signal, cot, *copies, rows, cols, hot, half_mask, forward, backward, columns,
         scratch=[
-            pltpu.VMEM((ROWS, LANES), F32), pltpu.VMEM((cells, LANES), F32), line, line,
+            pltpu.VMEM((ROWS, LANES), F32), pltpu.VMEM((count, LANES), F32), line, line,
             pltpu.VMEM((96, LANES), F32), pltpu.VMEM((SIDE, LANES), F32), pltpu.VMEM((2 * WROWS, LANES), F32),
         ],
-        flops=2 * ROWS * 768 * 128, moved=4 * 2**20,
-    )
-
+        **work,
+    )
+
+    if regions > 2:
+        upper, lower = sent[WROWS + SIDE :], sent[WROWS : WROWS + SIDE]
+        sides = [shift(upper, "region", 1), shift(lower, "region", -1)]
+        sent = sent[:WROWS]
+    other = swap(sent, "region", 1)
     if regions == 2:
-        sides = [swap(sums, "region", 1)]
-    else:
-        sides = [shift(sums[SIDE:], "region", 1), shift(sums[:SIDE], "region", -1)]
-    pick = call(
-        functools.partial(pick_kernel, owners), [((4 * SIDE, owners * SIDE), BF16)], halo_index
-    )[0]
-    grad_copies = call(grad_copies_kernel, [pair] * 3, grad, moved=2 * 2**20)
-    inner = call(
-        inner_kernel, [((ROWS, LANES), F32)], *grad_copies, backward, flops=2 * ROWS * 768 * 128, moved=3 * 2**20
-    )[0]
-
-    region_ks = [1] + [k for k in steps_of(regions) if k > 1]
-    for k in region_ks:
-        extra = (own_rows,) if k == region_ks[-1] else ()
+        sides = [other]
+    far = [k for k in steps_of(regions) if k > 1]
+    for k in [1] + far:
+        extra = () if k != ([1] + far)[-1] else (own_rows,)
         size = (WROWS + SIDE * len(extra), LANES)
-        other = swap(sent if k == 1 else message, "region", k)
-        message = call(join_kernel, [(size, BF16)], message, other, *extra)[0]
-    for step in range(steps - 1):
-        size = (2 * message.shape[0] - WROWS, LANES)
-        message = call(join_kernel, [(size, BF16)], message, exchange(message, step))[0]
-    other = exchange(message, steps - 1)
+        message = call(join_kernel, [(size, BF16)], message, other if k == 1 else swap(message, "region", k), *extra)[0]
+    beside = grad
+    for step in range(steps):
+        message, beside = lax.optimization_barrier((message, beside))
+        other = exchange(message, step)
+        if step == 0:
+            beside = call(grad_copies_kernel, [pair] * 3, beside, moved=2 * 2**20)
+        if step == 1:
+            beside = call(inner_kernel, [both], *beside, backward, **work)[0]
+        other, beside = lax.optimization_barrier((other, beside))
+        if step < steps - 1:
+            size = (2 * message.shape[0] - WROWS, LANES)
+            message = call(join_kernel, [(size, BF16)], message, other)[0]
     scale = 1.0 / math.sqrt(regions * owners * SIDE * SIDE)
     part = call(functools.partial(close_kernel, scale), [((WROWS, LANES), F32)], message, other)[0]
     other_part = swap(part, "region", 1)
     input_grad = call(
-        last_kernel, [((SIDE, SIDE * CHANNELS), BF16)], message, other, inner, pick, *sides, moved=2 * 2**20
+        last_kernel, [((SIDE, SIDE * CHANNELS), BF16)], message, other, beside, pick, *sides, moved=2 * 2**20
     )[0]
     weight_grad, bias_grad = call(
         weight_kernel, [((CHANNELS, 9 * CHANNELS), F32), ((1, CHANNELS), F32)], part, other_part

time: 55.4 us -> 51 us (0.921)
  waiting for transfers between devices: 22.5 us -> 17.2 us
  Pallas kernels: 14.1 us -> 15.4 us
  local copies, waits for them, and re-layouts: 2.37 us -> 1.41 us
    ppermute x8, waiting for transfers between devices: 21.3 us -> 15.9 us  [exchange(): return lax.ppermute(x, ('region', 'patch'), pairs)]
    pallas_call x16, Pallas kernels: 14.1 us -> 15.4 us  [call(): pl.pallas_call(kernel, out_shape=shapes, in_specs=[pl.BlockSpec(memory_sp...]
    unnamed x14 -> x16, local copies, waits for them, and re-layouts: 2.36 us -> 1.39 us
    ppermute x4 -> x3, waiting for transfers between devices: 1.21 us -> 1.32 us  [swap(): return lax.ppermute(x, axis, [(i, i ^ k) for i in range(n)])]
  transfers between devices with their start and end apart: 12 -> 11, of which waited for: 7 -> 9; matrix products, arithmetic and copies ran while one was open for 0% -> 2% of each run, Pallas kernels for 16% -> 18%
where the time goes in v3:
time: 51 us; the launch traced here: 50.7 us
  waiting for transfers between devices  17.2 us (34%)
  starting transfers between devices  15.8 us (31%)
  Pallas kernels  15.4 us (30%)
  local copies, waits for them, and re-layouts  1.41 us (3%)
  between operations  0.79 us (2%)
    ppermute x8, waiting for transfers between devices, exchange(): return lax.ppermute(x, ('region', 'patch'), pairs)  15.9 us
    pallas_call x16, Pallas kernels, call(): pl.pallas_call(kernel, out_shape=shapes, in_specs=[pl.BlockSpec(memory_sp...  15.4 us
    ppermute x8, starting transfers between devices, exchange(): return lax.ppermute(x, ('region', 'patch'), pairs)  15.2 us
    unnamed x16, local copies, waits for them, and re-layouts  1.39 us
    ppermute x3, waiting for transfers between devices, swap(): return lax.ppermute(x, axis, [(i, i ^ k) for i in range(n)])  1.32 us
  transfers between devices with their start and end apart: 11, of which 9 were waited for; matrix products, arithmetic and copies ran while one was open for 2% of the time, Pallas kernels for 18%

profile of v3, /device:TPU:0, one launch (start us, length us, event | category | flops | bytes accessed | tf_op | source)
XLA Modules:
  0.0 50.7 jit_solution(904227619862479990)
XLA Ops:
  0.6 1.7 %shard_map.76 = (bf16[64,128]{1,0:T(8,128)(2,1)}, bf16[64,128]{1,0:T(8,128)(2,1)}) custom-call(bf16[64,4096]{1,0:T(8,128)(2,1)} %bitcast.7), custom_call_target="tpu_custom_call" | custom-call | tf_op jit(solution)/shard_map/pallas_call | solution.py:24
  2.9 3.7 %collective-permute-start = (bf16[64,128]{1,0:T(8,128)(2,1)}, bf16[64,128]{1,0:T(8,128)(2,1)S(1)}, u32[]{:S(2)}, u32[]{:S(2)}) collective-permute-start(bf16[64,128]{1,0:T(8,128)(2,1)} %get-tuple-element.54), channel_id=1, source_target_pairs={{0,8},{1,9},{2,10},{3,11},{4,12},{5,13},{6,14},{7,15},{8,0},{9,1},... | collective-permute-start | bytes 49160 | tf_op jit(solution)/shard_map/ppermute | solution.py:460
  6.5 0.8 %constant_dynamic-update-slice_fusion.4 = bf16[1024,128]{1,0:T(8,128)(2,1)S(1)} fusion(bf16[64,128]{1,0:T(8,128)(2,1)} %get-tuple-element.54), kind=kLoop, calls=%fused_computation.7 | loop fusion | bytes 32768
  7.3 1.5 %shard_map.77 = (bf16[2112,128]{1,0:T(8,128)(2,1)S(1)}, bf16[2112,128]{1,0:T(8,128)(2,1)S(1)}, bf16[2112,128]{1,0:T(8,128)(2,1)S(1)}) custom-call(bf16[64,4096]{1,0:T(8,128)(2,1)S(1)} %bitcast.8), custom_call_target="tpu_custom_call" | custom-call | bytes 2097152 | tf_op jit(solution)/shard_map/pallas_call | solution.py:24
  9.5 1.6 %collective-permute-start.1 = (bf16[128,128]{1,0:T(8,128)(2,1)S(1)}, bf16[128,128]{1,0:T(8,128)(2,1)S(1)}, u32[]{:S(2)}, u32[]{:S(2)}) collective-permute-start(bf16[128,128]{1,0:T(8,128)(2,1)S(1)} %pad_maximum_fusion.2), channel_id=1, source_target_pairs={{0,4},{1,5},{2,6},{3,7},{4,0},{5,1},{6,2},{7,3},{8,12},{9,13},{10,... | collective-permute-start | bytes 98312 | tf_op jit(solution)/shard_map/ppermute | solution.py:460
  11.1 2.2 %shard_map.79.s_in = f32[2048,128]{1,0:T(8,128)S(1)} custom-call(bf16[2112,128]{1,0:T(8,128)(2,1)S(1)} %get-tuple-element.60.p0, bf16[2112,128]{1,0:T(8,128)(2,1)S(1)} %get-tuple-element.61.p1, bf16[2112,128]{1,0:T(8,128)(2,1)S(1)} %get-tuple-element.62.p2, bf16[3,128,256]{2,1,0:T(8,128)(2,1)S(1)} %get-tuple-element.63.w_ref, f32[1,64]{1,0:T(1,128)S(1)} %bitcast.11), custom_call_target="tpu_custom_call" | custom-call | flops 402653184 | bytes 3145728 | tf_op jit(solution)/shard_map/pallas_call | solution.py:24
  13.4 1.6 %collective-permute-start.2 = (bf16[256,128]{1,0:T(8,128)(2,1)S(1)}, bf16[256,128]{1,0:T(8,128)(2,1)S(1)}, u32[]{:S(2)}, u32[]{:S(2)}) collective-permute-start(bf16[256,128]{1,0:T(8,128)(2,1)S(1)} %pad_maximum_fusion.1), channel_id=1, source_target_pairs={{0,2},{1,3},{2,0},{3,1},{4,6},{5,7},{6,4},{7,5},{8,10},{9,11},{10,... | collective-permute-start | bytes 196616 | tf_op jit(solution)/shard_map/ppermute | solution.py:460
  15.6 2.2 %collective-permute-done.2 = bf16[256,128]{1,0:T(8,128)(2,1)S(1)} collective-permute-done((bf16[256,128]{1,0:T(8,128)(2,1)S(1)}, bf16[256,128]{1,0:T(8,128)(2,1)S(1)}, u32[]{:S(2)}, u32[]{:S(2)}) %collective-permute-start.2) | collective-permute-done | bytes 65568 | tf_op jit(solution)/shard_map/ppermute | solution.py:460
  17.8 1.6 %collective-permute-start.3 = (bf16[512,128]{1,0:T(8,128)(2,1)S(1)}, bf16[512,128]{1,0:T(8,128)(2,1)S(1)}, u32[]{:S(2)}, u32[]{:S(2)}) collective-permute-start(bf16[512,128]{1,0:T(8,128)(2,1)S(1)} %pad_maximum_fusion), channel_id=1, source_target_pairs={{0,1},{1,0},{2,3},{3,2},{4,5},{5,4},{6,7},{7,6},{8,9},{9,8},{10,11... | collective-permute-start | bytes 393224 | tf_op jit(solution)/shard_map/ppermute | solution.py:460
  19.3 3.5 %collective-permute-done.3 = bf16[512,128]{1,0:T(8,128)(2,1)S(1)} collective-permute-done((bf16[512,128]{1,0:T(8,128)(2,1)S(1)}, bf16[512,128]{1,0:T(8,128)(2,1)S(1)}, u32[]{:S(2)}, u32[]{:S(2)}) %collective-permute-start.3) | collective-permute-done | bytes 131104 | tf_op jit(solution)/shard_map/ppermute | solution.py:460
  22.8 3.9 %shard_map.82 = (bf16[2048,128]{1,0:T(8,128)(2,1)S(1)}, bf16[160,128]{1,0:T(8,128)(2,1)S(1)}, bf16[224,128]{1,0:T(8,128)(2,1)S(1)}, bf16[64,128]{1,0:T(8,128)(2,1)S(1)}) custom-call(f32[2048,128]{1,0:T(8,128)S(1)} %shard_map.79.s_in, bf16[64,4096]{1,0:T(8,128)(2,1)S(1)} %bitcast.9, bf16[2112,128]{1,0:T(8,128)(2,1)S(1)} %get-tuple-element.60.p0, ...), custom_call_target="tpu_custom_call" | custom-call | flops 402653184 | bytes 3145728 | tf_op jit(solution)/shard_map/pallas_call | solution.py:24
  26.8 1.2 %collective-permute-done.5.other.rest_0_ = bf16[224,128]{1,0:T(8,128)(2,1)S(1)} collective-permute-done((bf16[224,128]{1,0:T(8,128)(2,1)S(1)}, bf16[224,128]{1,0:T(8,128)(2,1)S(1)}, u32[]{:S(2)}, u32[]{:S(2)}) %collective-permute-start.5) | collective-permute-done | bytes 57376 | tf_op jit(solution)/shard_map/ppermute | solution.py:428
  28.1 2.0 %collective-permute-start.6 = (bf16[224,128]{1,0:T(8,128)(2,1)S(1)}, bf16[224,128]{1,0:T(8,128)(2,1)S(1)}, u32[]{:S(2)}, u32[]{:S(2)}) collective-permute-start(bf16[224,128]{1,0:T(8,128)(2,1)S(1)} %shard_map.83.mine), channel_id=1, source_target_pairs={{0,8},{1,9},{2,10},{3,11},{4,12},{5,13},{6,14},{7,15},{8,0},{9,1},... | collective-permute-start | bytes 172040 | tf_op jit(solution)/shard_map/ppermute | solution.py:460
  30.1 1.5 %shard_map.84 = (bf16[2112,128]{1,0:T(8,128)(2,1)S(1)}, bf16[2112,128]{1,0:T(8,128)(2,1)S(1)}, bf16[2112,128]{1,0:T(8,128)(2,1)S(1)}) custom-call(bf16[2048,128]{1,0:T(8,128)(2,1)S(1)} %get-tuple-element.80.g_ref), custom_call_target="tpu_custom_call" | custom-call | bytes 2097152 | tf_op jit(solution)/shard_map/pallas_call | solution.py:24
  31.6 1.6 %collective-permute-done.6.other = bf16[224,128]{1,0:T(8,128)(2,1)S(1)} collective-permute-done((bf16[224,128]{1,0:T(8,128)(2,1)S(1)}, bf16[224,128]{1,0:T(8,128)(2,1)S(1)}, u32[]{:S(2)}, u32[]{:S(2)}) %collective-permute-start.6) | collective-permute-done | bytes 57376 | tf_op jit(solution)/shard_map/ppermute | solution.py:460
  33.3 1.6 %collective-permute-start.7 = (bf16[288,128]{1,0:T(8,128)(2,1)S(1)}, bf16[288,128]{1,0:T(8,128)(2,1)S(1)}, u32[]{:S(2)}, u32[]{:S(2)}) collective-permute-start(bf16[288,128]{1,0:T(8,128)(2,1)S(1)} %shard_map.85.mine), channel_id=1, source_target_pairs={{0,4},{1,5},{2,6},{3,7},{4,0},{5,1},{6,2},{7,3},{8,12},{9,13},{10,... | collective-permute-start | bytes 221192 | tf_op jit(solution)/shard_map/ppermute | solution.py:460
  34.9 2.0 %shard_map.86.inner = f32[2048,128]{1,0:T(8,128)S(1)} custom-call(bf16[2112,128]{1,0:T(8,128)(2,1)S(1)} %get-tuple-element.89.p0, bf16[2112,128]{1,0:T(8,128)(2,1)S(1)} %get-tuple-element.90.p1, bf16[2112,128]{1,0:T(8,128)(2,1)S(1)} %get-tuple-element.91.p2, bf16[3,256,128]{2,1,0:T(8,128)(2,1)S(1)} %get-tuple-element.73.wb_ref), custom_call_target="tpu_custom_call" | custom-call | flops 402653184 | bytes 3145728 | tf_op jit(solution)/shard_map/pallas_call | solution.py:24
  36.9 0.8 %collective-permute-done.7.other = bf16[288,128]{1,0:T(8,128)(2,1)S(1)} collective-permute-done((bf16[288,128]{1,0:T(8,128)(2,1)S(1)}, bf16[288,128]{1,0:T(8,128)(2,1)S(1)}, u32[]{:S(2)}, u32[]{:S(2)}) %collective-permute-start.7) | collective-permute-done | bytes 73760 | tf_op jit(solution)/shard_map/ppermute | solution.py:460
  37.7 1.6 %collective-permute-start.8 = (bf16[416,128]{1,0:T(8,128)(2,1)S(1)}, bf16[416,128]{1,0:T(8,128)(2,1)S(1)}, u32[]{:S(2)}, u32[]{:S(2)}) collective-permute-start(bf16[416,128]{1,0:T(8,128)(2,1)S(1)} %shard_map.87.mine), channel_id=1, source_target_pairs={{0,2},{1,3},{2,0},{3,1},{4,6},{5,7},{6,4},{7,5},{8,10},{9,11},{10,... | collective-permute-start | bytes 319496 | tf_op jit(solution)/shard_map/ppermute | solution.py:460
  39.3 3.9 %collective-permute-done.8.other = bf16[416,128]{1,0:T(8,128)(2,1)S(1)} collective-permute-done((bf16[416,128]{1,0:T(8,128)(2,1)S(1)}, bf16[416,128]{1,0:T(8,128)(2,1)S(1)}, u32[]{:S(2)}, u32[]{:S(2)}) %collective-permute-start.8) | collective-permute-done | bytes 106528 | tf_op jit(solution)/shard_map/ppermute | solution.py:460
  43.2 1.6 %collective-permute-start.9 = (bf16[672,128]{1,0:T(8,128)(2,1)S(1)}, bf16[672,128]{1,0:T(8,128)(2,1)S(1)}, u32[]{:S(2)}, u32[]{:S(2)}) collective-permute-start(bf16[672,128]{1,0:T(8,128)(2,1)S(1)} %shard_map.88.mine), channel_id=1, source_target_pairs={{0,1},{1,0},{2,3},{3,2},{4,5},{5,4},{6,7},{7,6},{8,9},{9,8},{10,11... | collective-permute-start | bytes 516104 | tf_op jit(solution)/shard_map/ppermute | solution.py:460
  44.7 3.9 %collective-permute-done.9.other = bf16[672,128]{1,0:T(8,128)(2,1)S(1)} collective-permute-done((bf16[672,128]{1,0:T(8,128)(2,1)S(1)}, bf16[672,128]{1,0:T(8,128)(2,1)S(1)}, u32[]{:S(2)}, u32[]{:S(2)}) %collective-permute-start.9) | collective-permute-done | bytes 172064 | tf_op jit(solution)/shard_map/ppermute | solution.py:460
  48.7 1.2 %shard_map.89 = bf16[64,4096]{1,0:T(8,128)(2,1)} custom-call(bf16[672,128]{1,0:T(8,128)(2,1)S(1)} %shard_map.88.mine, bf16[672,128]{1,0:T(8,128)(2,1)S(1)} %collective-permute-done.9.other, f32[2048,128]{1,0:T(8,128)S(1)} %shard_map.86.inner, bf16[256,1024]{1,0:T(8,128)(2,1)S(1)} %shard_map.81.pick, bf16[224,128]{1,0:T(8,128)(2,1)S(1)} %collective-permute-done.5.other.rest_0_), custom_call_target="tpu_custom_call" | custom-call | bytes 2097152 | tf_op jit(solution)/shard_map/pallas_call | solution.py:24
  50.0 0.7 %shard_map.91 = (f32[64,576]{1,0:T(8,128)}, f32[1,64]{1,0:T(1,128)}) custom-call(f32[160,128]{1,0:T(8,128)S(1)} %shard_map.90.mine, f32[160,128]{1,0:T(8,128)S(1)} %collective-permute-done.10.other), custom_call_target="tpu_custom_call" | custom-call | tf_op jit(solution)/shard_map/pallas_call | solution.py:24
  (34 shorter events, 2.3 us)
Async XLA Ops:
  0.6 6.7 %copy-start = (bf16[1,64,4096]{2,1,0:T(8,128)(2,1)S(1)}, bf16[1,64,4096]{2,1,0:T(8,128)(2,1)}, u32[]{:S(2)}) copy-start(bf16[1,64,4096]{2,1,0:T(8,128)(2,1)} %param.5) | copy-start | bytes 1572868
  2.3 20.5 %collective-permute-start.4 = (bf16[64,128]{1,0:T(8,128)(2,1)}, bf16[64,128]{1,0:T(8,128)(2,1)S(1)}, u32[]{:S(2)}, u32[]{:S(2)}) collective-permute-start(bf16[64,128]{1,0:T(8,128)(2,1)} %get-tuple-element.70), channel_id=1, source_target_pairs={{0,16},{16,0},{1,17},{17,1},{2,18},{18,2},{3,19},{19,3},{4,20},{20... | collective-permute-start | bytes 49160 | tf_op jit(solution)/shard_map/ppermute | solution.py:428
  2.9 6.0 %collective-permute-start = (bf16[64,128]{1,0:T(8,128)(2,1)}, bf16[64,128]{1,0:T(8,128)(2,1)S(1)}, u32[]{:S(2)}, u32[]{:S(2)}) collective-permute-start(bf16[64,128]{1,0:T(8,128)(2,1)} %get-tuple-element.54), channel_id=1, source_target_pairs={{0,8},{1,9},{2,10},{3,11},{4,12},{5,13},{6,14},{7,15},{8,0},{9,1},... | collective-permute-start | bytes 49160 | tf_op jit(solution)/shard_map/ppermute | solution.py:460
  7.3 1.5 %copy-start.3 = (bf16[576,64]{0,1:T(8,128)(2,1)S(1)}, bf16[576,64]{0,1:T(8,128)(2,1)}, u32[]{:S(2)}) copy-start(bf16[576,64]{0,1:T(8,128)(2,1)} %param.6) | copy-start | bytes 221188
  8.8 0.7 %copy-start.5 = (bf16[64,128]{1,0:T(8,128)(2,1)S(1)}, bf16[64,128]{1,0:T(8,128)(2,1)}, u32[]{:S(2)}) copy-start(bf16[64,128]{1,0:T(8,128)(2,1)} %get-tuple-element.54) | copy-start | bytes 49156
  9.5 1.6 %copy-start.4 = (f32[64]{0:T(128)S(1)}, f32[64]{0:T(128)}, u32[]{:S(2)}) copy-start(f32[64]{0:T(128)} %param.7) | copy-start | bytes 772
  9.5 3.9 %collective-permute-start.1 = (bf16[128,128]{1,0:T(8,128)(2,1)S(1)}, bf16[128,128]{1,0:T(8,128)(2,1)S(1)}, u32[]{:S(2)}, u32[]{:S(2)}) collective-permute-start(bf16[128,128]{1,0:T(8,128)(2,1)S(1)} %pad_maximum_fusion.2), channel_id=1, source_target_pairs={{0,4},{1,5},{2,6},{3,7},{4,0},{5,1},{6,2},{7,3},{8,12},{9,13},{10,... | collective-permute-start | bytes 98312 | tf_op jit(solution)/shard_map/ppermute | solution.py:460
  13.4 1.6 %copy-start.2 = (s32[16,260]{1,0:T(8,128)S(1)}, s32[16,260]{1,0:T(8,128)}, u32[]{:S(2)}) copy-start(s32[16,260]{1,0:T(8,128)} %index_ref.1) | copy-start | bytes 49924
  13.4 4.3 %collective-permute-start.2 = (bf16[256,128]{1,0:T(8,128)(2,1)S(1)}, bf16[256,128]{1,0:T(8,128)(2,1)S(1)}, u32[]{:S(2)}, u32[]{:S(2)}) collective-permute-start(bf16[256,128]{1,0:T(8,128)(2,1)S(1)} %pad_maximum_fusion.1), channel_id=1, source_target_pairs={{0,2},{1,3},{2,0},{3,1},{4,6},{5,7},{6,4},{7,5},{8,10},{9,11},{10,... | collective-permute-start | bytes 196616 | tf_op jit(solution)/shard_map/ppermute | solution.py:460
  15.0 7.8 %copy-start.1 = (bf16[1,64,4096]{2,1,0:T(8,128)(2,1)S(1)}, bf16[1,64,4096]{2,1,0:T(8,128)(2,1)}, u32[]{:S(2)}) copy-start(bf16[1,64,4096]{2,1,0:T(8,128)(2,1)} %param.8) | copy-start | bytes 1572868
  17.8 5.0 %collective-permute-start.3 = (bf16[512,128]{1,0:T(8,128)(2,1)S(1)}, bf16[512,128]{1,0:T(8,128)(2,1)S(1)}, u32[]{:S(2)}, u32[]{:S(2)}) collective-permute-start(bf16[512,128]{1,0:T(8,128)(2,1)S(1)} %pad_maximum_fusion), channel_id=1, source_target_pairs={{0,1},{1,0},{2,3},{3,2},{4,5},{5,4},{6,7},{7,6},{8,9},{9,8},{10,11... | collective-permute-start | bytes 393224 | tf_op jit(solution)/shard_map/ppermute | solution.py:460
  26.8 1.3 %collective-permute-start.5 = (bf16[224,128]{1,0:T(8,128)(2,1)S(1)}, bf16[224,128]{1,0:T(8,128)(2,1)S(1)}, u32[]{:S(2)}, u32[]{:S(2)}) collective-permute-start(bf16[224,128]{1,0:T(8,128)(2,1)S(1)} %get-tuple-element.76), channel_id=1, source_target_pairs={{0,16},{16,0},{1,17},{17,1},{2,18},{18,2},{3,19},{19,3},{4,20},{20... | collective-permute-start | bytes 172040 | tf_op jit(solution)/shard_map/ppermute | solution.py:428
  28.1 5.1 %collective-permute-start.6 = (bf16[224,128]{1,0:T(8,128)(2,1)S(1)}, bf16[224,128]{1,0:T(8,128)(2,1)S(1)}, u32[]{:S(2)}, u32[]{:S(2)}) collective-permute-start(bf16[224,128]{1,0:T(8,128)(2,1)S(1)} %shard_map.83.mine), channel_id=1, source_target_pairs={{0,8},{1,9},{2,10},{3,11},{4,12},{5,13},{6,14},{7,15},{8,0},{9,1},... | collective-permute-start | bytes 172040 | tf_op jit(solution)/shard_map/ppermute | solution.py:460
  33.3 4.4 %collective-permute-start.7 = (bf16[288,128]{1,0:T(8,128)(2,1)S(1)}, bf16[288,128]{1,0:T(8,128)(2,1)S(1)}, u32[]{:S(2)}, u32[]{:S(2)}) collective-permute-start(bf16[288,128]{1,0:T(8,128)(2,1)S(1)} %shard_map.85.mine), channel_id=1, source_target_pairs={{0,4},{1,5},{2,6},{3,7},{4,0},{5,1},{6,2},{7,3},{8,12},{9,13},{10,... | collective-permute-start | bytes 221192 | tf_op jit(solution)/shard_map/ppermute | solution.py:460
  37.7 5.4 %collective-permute-start.8 = (bf16[416,128]{1,0:T(8,128)(2,1)S(1)}, bf16[416,128]{1,0:T(8,128)(2,1)S(1)}, u32[]{:S(2)}, u32[]{:S(2)}) collective-permute-start(bf16[416,128]{1,0:T(8,128)(2,1)S(1)} %shard_map.87.mine), channel_id=1, source_target_pairs={{0,2},{1,3},{2,0},{3,1},{4,6},{5,7},{6,4},{7,5},{8,10},{9,11},{10,... | collective-permute-start | bytes 319496 | tf_op jit(solution)/shard_map/ppermute | solution.py:460
  43.2 5.5 %collective-permute-start.9 = (bf16[672,128]{1,0:T(8,128)(2,1)S(1)}, bf16[672,128]{1,0:T(8,128)(2,1)S(1)}, u32[]{:S(2)}, u32[]{:S(2)}) collective-permute-start(bf16[672,128]{1,0:T(8,128)(2,1)S(1)} %shard_map.88.mine), channel_id=1, source_target_pairs={{0,1},{1,0},{2,3},{3,2},{4,5},{5,4},{6,7},{7,6},{8,9},{9,8},{10,11... | collective-permute-start | bytes 516104 | tf_op jit(solution)/shard_map/ppermute | solution.py:460
  48.7 1.3 %collective-permute-start.10 = (f32[160,128]{1,0:T(8,128)S(1)}, f32[160,128]{1,0:T(8,128)S(1)}, u32[]{:S(2)}, u32[]{:S(2)}) collective-permute-start(f32[160,128]{1,0:T(8,128)S(1)} %shard_map.90.mine), channel_id=1, source_target_pairs={{0,16},{16,0},{1,17},{17,1},{2,18},{18,2},{3,19},{19,3},{4,20},{20... | collective-permute-start | bytes 245768 | tf_op jit(solution)/shard_map/ppermute | solution.py:428

commit v4 on v3

--- a/solution.py
+++ b/solution.py
@@ -89,23 +89,21 @@
     return total
 
 
-def rim_kernel(x_hbm, rows_ref, cols_ref, top, bottom, left, right, scr, sems):
-    copies = [
-        pltpu.make_async_copy(x_hbm.at[0:16, :], top, sems.at[0]),
-        pltpu.make_async_copy(x_hbm.at[SIDE - 16 : SIDE, :], bottom, sems.at[1]),
-        pltpu.make_async_copy(x_hbm.at[:, 0:LANES], left, sems.at[2]),
-        pltpu.make_async_copy(x_hbm.at[:, (PAIRS - 1) * LANES :], right, sems.at[3]),
-    ]
-    for copy in copies:
-        copy.start()
-    for copy in copies:
-        copy.wait()
+def rim_kernel(x_ref, rows_ref, cols_ref, scr):
     for q in range(PAIRS):
         lanes = slice(q * LANES, (q + 1) * LANES)
-        scr[q : q + 1, :] = top[:, lanes].astype(F32)[0:1]
-        scr[PAIRS + q : PAIRS + q + 1, :] = bottom[:, lanes].astype(F32)[15:16]
+        scr[q : q + 1, :] = x_ref[0:16, lanes].astype(F32)[0:1]
+        scr[PAIRS + q : PAIRS + q + 1, :] = x_ref[SIDE - 16 : SIDE, lanes].astype(F32)[15:16]
     rows_ref[...] = scr[...].astype(BF16)
-    cols_ref[...] = halves(left[...].astype(F32), right[...].astype(F32)).astype(BF16)
+    first = x_ref[:, 0:LANES].astype(F32)
+    last = x_ref[:, (PAIRS - 1) * LANES :].astype(F32)
+    cols_ref[...] = halves(first, last).astype(BF16)
+
+
+def rows_kernel(mine, other, out):
+    n = mine.shape[0]
+    out[0:n, :] = mine[...]
+    out[n:, :] = other[...]
 
 
 def bits_moved(v, pairs):
@@ -121,9 +119,7 @@
     bits = owners.bit_length() - 1
     index = index_ref[pl.ds(owner, 1), :]
     source, within = index >> 8, index & 255
-    relative = (source & (owners - 1)) ^ owner
-    even, odd = (bits_moved(relative, slot_bits(owners, core)) for core in range(2))
-    slot = jnp.where((region & 1) == 1, odd, even)
+    slot = bits_moved((source & (owners - 1)) ^ owner, slot_bits(owners))
     row = within & (SIDE - 1)
     if blocks == 2:
         row = row + jnp.where((((source >> bits) - region + regions) & (regions - 1)) == 1, SIDE, 0)
@@ -149,10 +145,8 @@
     for t in range(owners // 2):
         pair = []
         for slot in (2 * t, 2 * t + 1):
-            even, odd = (
-                sum(1 << frm for frm, to in slot_bits(owners, core) if (slot >> to) & 1) for core in range(2)
-            )
-            line = index_ref[pl.ds(owner ^ jnp.where((region & 1) == 1, odd, even), 1), :]
+            relative = sum(1 << bit for bit, to in slot_bits(owners) if (slot >> to) & 1)
+            line = index_ref[pl.ds(owner ^ relative, 1), :]
             pair.append((line[:, 1 : SIDE + 1], line[:, SIDE + 3 : 2 * SIDE + 3]))
         for s in range(2):
             both = jnp.concatenate([pair[0][s], pair[1][s]], axis=1) - base
@@ -216,11 +210,14 @@
 
 
 def middle_kernel(
-    s_in, cot_ref, p0, p1, p2, rows_ref, cols_ref, hot_ref, half_ref, w_ref, wb_ref, wc_ref,
+    s_in, cot_ref, p0, p1, p2, rows_a, rows_b, rows_c, rows_d, cols_ref, hot_ref, half_ref, w_ref, wb_ref, wc_ref,
     g_ref, keep_ref, send_ref, own_ref, s_ref, cell_scr, gt, gb, gc, own_scr, msg,
 ):
-    many = rows_ref.shape[0]
-    cells = dot(hot_ref[:, :many], rows_ref[...]) + dot(hot_ref[:, many:], cols_ref[...])
+    n = rows_a.shape[0]
+    many = 4 * n
+    cells = dot(hot_ref[:, many:], cols_ref[...])
+    for i, ref in enumerate((rows_a, rows_b, rows_c, rows_d)):
+        cells = cells + dot(hot_ref[:, i * n : (i + 1) * n], ref[...])
     other = turn(cells)
     upper = half_ref[...] > 0.5
     edge = 2 * SIDE + 4
@@ -386,8 +383,12 @@
         out[WROWS:, :] = extra[0][...]
 
 
-def close_kernel(scale, mine, other, out):
-    total, whole = added_weights(mine, other)
+def close_kernel(scale, a, b, c, d, out):
+    left, _ = added_weights(a, b)
+    right, _ = added_weights(c, d)
+    total = left + right
+    tail = total[WROWS - SIDE :]
+    whole = tail + pltpu.roll(tail, SIDE - 1, 0)
     out[0 : WROWS - SIDE, :] = total[: WROWS - SIDE] * scale
     out[WROWS - SIDE :, :] = jnp.where(bias_lanes(whole.shape), whole, total[WROWS - SIDE :]) * scale
 
@@ -402,10 +403,12 @@
     bias_ref[...] = turn(full[4 * SIDE : 4 * SIDE + 8])[0:1, :CHANNELS]
 
 
-def last_kernel(mine, other, inner, pick, *rest):
+def last_kernel(row_a, row_b, row_c, row_d, inner, pick, *rest):
     side_refs, grad_ref = rest[:-1], rest[-1]
-    n = mine.shape[0] - WROWS
-    got = dot(pick[:, :n], mine[WROWS:, :]) + dot(pick[:, n:], other[WROWS:, :])
+    n = row_a.shape[0] - WROWS
+    got = 0.0
+    for i, ref in enumerate((row_a, row_b, row_c, row_d)):
+        got = got + dot(pick[:, i * n : (i + 1) * n], ref[WROWS:, :])
     a, b, c, d = (got[i * SIDE : (i + 1) * SIDE] for i in range(4))
     rims = halves(a + turn(b), turn(c) + d)
     sides = side_refs[0][side_refs[0].shape[0] - SIDE :, :].astype(F32)
@@ -442,45 +445,31 @@
     return ks
 
 
-def order_of(owners, core):
-    bits = list(range(owners.bit_length() - 1))[::-1]
-    return bits if core == 0 else bits[-1:] + bits[:-1]
-
-
-def slot_bits(owners, core):
-    return [(bit, step) for step, bit in enumerate(order_of(owners, core))]
-
-
-def exchange(x, step):
-    regions, owners = lax.axis_size("region"), lax.axis_size("patch")
-    pairs = []
-    for r in range(regions):
-        k = 1 << order_of(owners, r % 2)[step]
-        pairs += [(r * owners + i, r * owners + (i ^ k)) for i in range(owners)]
-    return lax.ppermute(x, ("region", "patch"), pairs)
+def slot_bits(owners):
+    high = range(2, owners.bit_length() - 1)
+    count = len(high)
+    return [(bit, step) for step, bit in enumerate(high)] + [(0, count), (1, count + 1)]
+
+
+def exchange(x, k):
+    return swap(x, "patch", k)
+
+
+def three_partners(x):
+    got = {k: exchange(x, k) for k in (3, 2, 1)}
+    return [got[k] for k in (1, 2, 3)]
 
 
 def body(fine_input, fine_weight, fine_bias, cotangent, halo_index):
     owners = lax.axis_size("patch")
     regions = lax.axis_size("region")
-    steps = owners.bit_length() - 1
+    high = [1 << bit for bit in range(2, owners.bit_length() - 1)]
     blocks = 1 if regions == 2 else 2
     x = fine_input.reshape(SIDE, SIDE * CHANNELS)
     cot = cotangent.reshape(SIDE, SIDE * CHANNELS)
     pair = ((ROWS + SIDE, LANES), BF16)
 
-    rows, cols = call(
-        rim_kernel,
-        [((SIDE, LANES), BF16)] * 2,
-        x,
-        scratch=[
-            pltpu.VMEM((16, SIDE * CHANNELS), BF16), pltpu.VMEM((16, SIDE * CHANNELS), BF16),
-            pltpu.VMEM((SIDE, LANES), BF16), pltpu.VMEM((SIDE, LANES), BF16),
-            pltpu.VMEM((SIDE, LANES), F32), pltpu.SemaphoreType.DMA((4,)),
-        ],
-        space=pl.ANY,
-        limit=60,
-    )
+    rows, cols = call(rim_kernel, [((SIDE, LANES), BF16)] * 2, x, scratch=[pltpu.VMEM((SIDE, LANES), F32)])
     if regions == 2:
         cols = swap(cols, "region", 1)
     else:
@@ -489,7 +478,10 @@
     both = ((ROWS, LANES), F32)
     work = dict(flops=2 * ROWS * 768 * 128, moved=3 * 2**20)
 
-    other = exchange(rows, 0)
+    def joined(rows, other):
+        return call(rows_kernel, [((2 * rows.shape[0], LANES), BF16)], rows, other)[0]
+
+    other = exchange(rows, high[0])
     copies = call(copies_kernel, [pair] * 3, x, moved=2 * 2**20)
     forward, backward, columns = call(
         weights_kernel,
@@ -497,28 +489,27 @@
         fine_weight.T,
     )
     other, copies, forward = lax.optimization_barrier((other, copies, forward))
-    rows = jnp.concatenate([rows, other], axis=0)
-    other = exchange(rows, 1)
+    rows = joined(rows, other)
+    other = exchange(rows, high[1])
     signal = call(signal_kernel, [both], *copies, forward, fine_bias.reshape(1, CHANNELS), **work)[0]
     other, signal, index = lax.optimization_barrier((other, signal, halo_index))
-    rows = jnp.concatenate([rows, other], axis=0)
-    other = exchange(rows, 2)
+    rows = joined(rows, other)
+    for k in high[2:]:
+        rows = joined(rows, exchange(rows, k))
+    others = three_partners(rows)
     hot, half_mask = call(
         functools.partial(plan_kernel, owners, regions, blocks),
         [((count, (owners + blocks) * SIDE), BF16), ((count, LANES), F32)],
         index, scratch=[pltpu.VMEM((8, 384), F32)],
     )
     pick = call(functools.partial(pick_kernel, owners), [((4 * SIDE, owners * SIDE), BF16)], index)[0]
-    other, hot, half_mask, pick = lax.optimization_barrier((other, hot, half_mask, pick))
-    rows = jnp.concatenate([rows, other], axis=0)
-    for step in range(3, steps):
-        rows = jnp.concatenate([rows, exchange(rows, step)], axis=0)
+    others, hot, half_mask, pick = lax.optimization_barrier((others, hot, half_mask, pick))
 
     line = pltpu.VMEM((40, LANES), F32)
     grad, message, sent, own_rows = call(
         middle_kernel,
         [((ROWS, LANES), BF16), ((WROWS, LANES), BF16), ((WROWS + blocks * SIDE, LANES), BF16), ((SIDE, LANES), BF16)],
-        signal, cot, *copies, rows, cols, hot, half_mask, forward, backward, columns,
+        signal, cot, *copies, rows, *others, cols, hot, half_mask, forward, backward, columns,
         scratch=[
             pltpu.VMEM((ROWS, LANES), F32), pltpu.VMEM((count, LANES), F32), line, line,
             pltpu.VMEM((96, LANES), F32), pltpu.VMEM((SIDE, LANES), F32), pltpu.VMEM((2 * WROWS, LANES), F32),
@@ -539,22 +530,23 @@
         size = (WROWS + SIDE * len(extra), LANES)
         message = call(join_kernel, [(size, BF16)], message, other if k == 1 else swap(message, "region", k), *extra)[0]
     beside = grad
-    for step in range(steps):
+    for step, k in enumerate(high):
         message, beside = lax.optimization_barrier((message, beside))
-        other = exchange(message, step)
-        if step == 0:
+        other = exchange(message, k)
+        if step == 1:
             beside = call(grad_copies_kernel, [pair] * 3, beside, moved=2 * 2**20)
-        if step == 1:
-            beside = call(inner_kernel, [both], *beside, backward, **work)[0]
         other, beside = lax.optimization_barrier((other, beside))
-        if step < steps - 1:
-            size = (2 * message.shape[0] - WROWS, LANES)
-            message = call(join_kernel, [(size, BF16)], message, other)[0]
+        size = (2 * message.shape[0] - WROWS, LANES)
+        message = call(join_kernel, [(size, BF16)], message, other)[0]
+    message, beside = lax.optimization_barrier((message, beside))
+    others = three_partners(message)
+    beside = call(inner_kernel, [both], *beside, backward, **work)[0]
+    others, beside = lax.optimization_barrier((others, beside))
     scale = 1.0 / math.sqrt(regions * owners * SIDE * SIDE)
-    part = call(functools.partial(close_kernel, scale), [((WROWS, LANES), F32)], message, other)[0]
+    part = call(functools.partial(close_kernel, scale), [((WROWS, LANES), F32)], message, *others)[0]
     other_part = swap(part, "region", 1)
     input_grad = call(
-        last_kernel, [((SIDE, SIDE * CHANNELS), BF16)], message, other, beside, pick, *sides, moved=2 * 2**20
+        last_kernel, [((SIDE, SIDE * CHANNELS), BF16)], message, *others, beside, pick, *sides, moved=2 * 2**20
     )[0]
     weight_grad, bias_grad = call(
         weight_kernel, [((CHANNELS, 9 * CHANNELS), F32), ((1, CHANNELS), F32)], part, other_part

time: 51 us -> 43.2 us (0.85)
  waiting for transfers between devices: 17.2 us -> 9.82 us
  starting transfers between devices: 15.8 us -> 17.6 us
  Pallas kernels: 15.4 us -> 13.8 us
    ppermute x3 -> x13, starting transfers between devices: 0.66 us -> 17.6 us  [swap(): return lax.ppermute(x, axis, [(i, i ^ k) for i in range(n)])]
    ppermute x8 -> x0, waiting for transfers between devices: 15.9 us -> none  [exchange(): return lax.ppermute(x, ('region', 'patch'), pairs)]
    ppermute x8 -> x0, starting transfers between devices: 15.2 us -> none  [exchange(): return lax.ppermute(x, ('region', 'patch'), pairs)]
    ppermute x3 -> x13, waiting for transfers between devices: 1.32 us -> 9.82 us  [swap(): return lax.ppermute(x, axis, [(i, i ^ k) for i in range(n)])]
    pallas_call x16 -> x17, Pallas kernels: 15.4 us -> 13.8 us  [call(): pl.pallas_call(kernel, out_shape=shapes, in_specs=[pl.BlockSpec(memory_sp...]
    unnamed x16 -> x10, local copies, waits for them, and re-layouts: 1.39 us -> 1.05 us
  transfers between devices with their start and end apart: 11 -> 13, of which waited for: 9 -> 11; matrix products, arithmetic and copies ran while one was open for 2% -> 0% of each run, Pallas kernels for 18% -> 21%
where the time goes in v4:
time: 43.2 us; the launch traced here: 43.1 us
  starting transfers between devices  17.6 us (41%)
  Pallas kernels  13.8 us (32%)
  waiting for transfers between devices  9.82 us (23%)
  local copies, waits for them, and re-layouts  1.05 us (2%)
  between operations  0.77 us (2%)
    ppermute x13, starting transfers between devices, swap(): return lax.ppermute(x, axis, [(i, i ^ k) for i in range(n)])  17.6 us
    pallas_call x17, Pallas kernels, call(): pl.pallas_call(kernel, out_shape=shapes, in_specs=[pl.BlockSpec(memory_sp...  13.8 us
    ppermute x13, waiting for transfers between devices, swap(): return lax.ppermute(x, axis, [(i, i ^ k) for i in range(n)])  9.82 us
    unnamed x10, local copies, waits for them, and re-layouts  1.05 us
  transfers between devices with their start and end apart: 13, of which 11 were waited for; matrix products, arithmetic and copies ran while one was open for 0% of the time, Pallas kernels for 21%

profile of v4, /device:TPU:0, one launch (start us, length us, event | category | flops | bytes accessed | tf_op | source)
XLA Modules:
  0.0 43.1 jit_solution(7009736907647891688)
XLA Ops:
  0.6 1.0 %copy-done = bf16[1,64,4096]{2,1,0:T(8,128)(2,1)S(1)} copy-done((bf16[1,64,4096]{2,1,0:T(8,128)(2,1)S(1)}, bf16[1,64,4096]{2,1,0:T(8,128)(2,1)}, u32[]{:S(2)}) %copy-start) | copy-done | bytes 524312
  1.7 3.1 %collective-permute-start = (bf16[64,128]{1,0:T(8,128)(2,1)S(1)}, bf16[64,128]{1,0:T(8,128)(2,1)S(1)}, u32[]{:S(2)}, u32[]{:S(2)}) collective-permute-start(bf16[64,128]{1,0:T(8,128)(2,1)S(1)} %get-tuple-element.54.mine), channel_id=1, source_target_pairs={{0,4},{1,5},{2,6},{3,7},{4,0},{5,1},{6,2},{7,3},{8,12},{9,13},{10,... | collective-permute-start | bytes 49160 | tf_op jit(solution)/shard_map/ppermute | solution.py:431
  4.8 1.5 %shard_map.77 = (bf16[2112,128]{1,0:T(8,128)(2,1)S(1)}, bf16[2112,128]{1,0:T(8,128)(2,1)S(1)}, bf16[2112,128]{1,0:T(8,128)(2,1)S(1)}) custom-call(bf16[64,4096]{1,0:T(8,128)(2,1)S(1)} %bitcast.8), custom_call_target="tpu_custom_call" | custom-call | bytes 2097152 | tf_op jit(solution)/shard_map/pallas_call | solution.py:24
  6.5 3.0 %collective-permute-start.1 = (bf16[128,128]{1,0:T(8,128)(2,1)S(1)}, bf16[128,128]{1,0:T(8,128)(2,1)S(1)}, u32[]{:S(2)}, u32[]{:S(2)}) collective-permute-start(bf16[128,128]{1,0:T(8,128)(2,1)S(1)} %shard_map.79.mine), channel_id=1, source_target_pairs={{0,8},{1,9},{2,10},{3,11},{4,12},{5,13},{6,14},{7,15},{8,0},{9,1},... | collective-permute-start | bytes 98312 | tf_op jit(solution)/shard_map/ppermute | solution.py:431
  9.6 2.2 %shard_map.80.s_in = f32[2048,128]{1,0:T(8,128)S(1)} custom-call(bf16[2112,128]{1,0:T(8,128)(2,1)S(1)} %get-tuple-element.60.p0, bf16[2112,128]{1,0:T(8,128)(2,1)S(1)} %get-tuple-element.61.p1, bf16[2112,128]{1,0:T(8,128)(2,1)S(1)} %get-tuple-element.62.p2, bf16[3,128,256]{2,1,0:T(8,128)(2,1)S(1)} %get-tuple-element.63.w_ref, f32[1,64]{1,0:T(1,128)S(1)} %bitcast.11), custom_call_target="tpu_custom_call" | custom-call | flops 402653184 | bytes 3145728 | tf_op jit(solution)/shard_map/pallas_call | solution.py:24
  11.8 2.5 %collective-permute-start.4 = (bf16[256,128]{1,0:T(8,128)(2,1)S(1)}, bf16[256,128]{1,0:T(8,128)(2,1)S(1)}, u32[]{:S(2)}, u32[]{:S(2)}) collective-permute-start(bf16[256,128]{1,0:T(8,128)(2,1)S(1)} %shard_map.81.rows_a), channel_id=1, source_target_pairs={{0,3},{1,2},{2,1},{3,0},{4,7},{5,6},{6,5},{7,4},{8,11},{9,10},{10,... | collective-permute-start | bytes 196616 | tf_op jit(solution)/shard_map/ppermute | solution.py:431
  14.3 0.5 %collective-permute-start.3 = (bf16[256,128]{1,0:T(8,128)(2,1)S(1)}, bf16[256,128]{1,0:T(8,128)(2,1)S(1)}, u32[]{:S(2)}, u32[]{:S(2)}) collective-permute-start(bf16[256,128]{1,0:T(8,128)(2,1)S(1)} %shard_map.81.rows_a), channel_id=1, source_target_pairs={{0,2},{1,3},{2,0},{3,1},{4,6},{5,7},{6,4},{7,5},{8,10},{9,11},{10,... | collective-permute-start | bytes 196616 | tf_op jit(solution)/shard_map/ppermute | solution.py:431
  14.8 0.5 %collective-permute-start.2 = (bf16[256,128]{1,0:T(8,128)(2,1)S(1)}, bf16[256,128]{1,0:T(8,128)(2,1)S(1)}, u32[]{:S(2)}, u32[]{:S(2)}) collective-permute-start(bf16[256,128]{1,0:T(8,128)(2,1)S(1)} %shard_map.81.rows_a), channel_id=1, source_target_pairs={{0,1},{1,0},{2,3},{3,2},{4,5},{5,4},{6,7},{7,6},{8,9},{9,8},{10,11... | collective-permute-start | bytes 196616 | tf_op jit(solution)/shard_map/ppermute | solution.py:431
  15.9 1.5 %collective-permute-done.4.rows_d = bf16[256,128]{1,0:T(8,128)(2,1)S(1)} collective-permute-done((bf16[256,128]{1,0:T(8,128)(2,1)S(1)}, bf16[256,128]{1,0:T(8,128)(2,1)S(1)}, u32[]{:S(2)}, u32[]{:S(2)}) %collective-permute-start.4) | collective-permute-done | bytes 65568 | tf_op jit(solution)/shard_map/ppermute | solution.py:431
  17.5 1.1 %collective-permute-done.3.rows_c = bf16[256,128]{1,0:T(8,128)(2,1)S(1)} collective-permute-done((bf16[256,128]{1,0:T(8,128)(2,1)S(1)}, bf16[256,128]{1,0:T(8,128)(2,1)S(1)}, u32[]{:S(2)}, u32[]{:S(2)}) %collective-permute-start.3) | collective-permute-done | bytes 65568 | tf_op jit(solution)/shard_map/ppermute | solution.py:431
  19.1 4.0 %shard_map.84 = (bf16[2048,128]{1,0:T(8,128)(2,1)S(1)}, bf16[160,128]{1,0:T(8,128)(2,1)S(1)}, bf16[224,128]{1,0:T(8,128)(2,1)S(1)}, bf16[64,128]{1,0:T(8,128)(2,1)S(1)}) custom-call(f32[2048,128]{1,0:T(8,128)S(1)} %shard_map.80.s_in, bf16[64,4096]{1,0:T(8,128)(2,1)S(1)} %bitcast.9, bf16[2112,128]{1,0:T(8,128)(2,1)S(1)} %get-tuple-element.60.p0, ...), custom_call_target="tpu_custom_call" | custom-call | flops 402653184 | bytes 3145728 | tf_op jit(solution)/shard_map/pallas_call | solution.py:24
  23.2 1.2 %collective-permute-done.6.other.rest_0_ = bf16[224,128]{1,0:T(8,128)(2,1)S(1)} collective-permute-done((bf16[224,128]{1,0:T(8,128)(2,1)S(1)}, bf16[224,128]{1,0:T(8,128)(2,1)S(1)}, u32[]{:S(2)}, u32[]{:S(2)}) %collective-permute-start.6) | collective-permute-done | bytes 57376 | tf_op jit(solution)/shard_map/ppermute | solution.py:431
  24.5 1.6 %collective-permute-start.7 = (bf16[224,128]{1,0:T(8,128)(2,1)S(1)}, bf16[224,128]{1,0:T(8,128)(2,1)S(1)}, u32[]{:S(2)}, u32[]{:S(2)}) collective-permute-start(bf16[224,128]{1,0:T(8,128)(2,1)S(1)} %shard_map.85.mine), channel_id=1, source_target_pairs={{0,4},{1,5},{2,6},{3,7},{4,0},{5,1},{6,2},{7,3},{8,12},{9,13},{10,... | collective-permute-start | bytes 172040 | tf_op jit(solution)/shard_map/ppermute | solution.py:431
  26.1 2.6 %collective-permute-done.7.other = bf16[224,128]{1,0:T(8,128)(2,1)S(1)} collective-permute-done((bf16[224,128]{1,0:T(8,128)(2,1)S(1)}, bf16[224,128]{1,0:T(8,128)(2,1)S(1)}, u32[]{:S(2)}, u32[]{:S(2)}) %collective-permute-start.7) | collective-permute-done | bytes 57376 | tf_op jit(solution)/shard_map/ppermute | solution.py:431
  28.7 2.6 %collective-permute-start.8 = (bf16[288,128]{1,0:T(8,128)(2,1)S(1)}, bf16[288,128]{1,0:T(8,128)(2,1)S(1)}, u32[]{:S(2)}, u32[]{:S(2)}) collective-permute-start(bf16[288,128]{1,0:T(8,128)(2,1)S(1)} %shard_map.86.mine), channel_id=1, source_target_pairs={{0,8},{1,9},{2,10},{3,11},{4,12},{5,13},{6,14},{7,15},{8,0},{9,1},... | collective-permute-start | bytes 221192 | tf_op jit(solution)/shard_map/ppermute | solution.py:431
  31.3 1.5 %shard_map.87 = (bf16[2112,128]{1,0:T(8,128)(2,1)S(1)}, bf16[2112,128]{1,0:T(8,128)(2,1)S(1)}, bf16[2112,128]{1,0:T(8,128)(2,1)S(1)}) custom-call(bf16[2048,128]{1,0:T(8,128)(2,1)S(1)} %get-tuple-element.86.g_ref), custom_call_target="tpu_custom_call" | custom-call | bytes 2097152 | tf_op jit(solution)/shard_map/pallas_call | solution.py:24
  32.8 1.3 %collective-permute-done.8.other = bf16[288,128]{1,0:T(8,128)(2,1)S(1)} collective-permute-done((bf16[288,128]{1,0:T(8,128)(2,1)S(1)}, bf16[288,128]{1,0:T(8,128)(2,1)S(1)}, u32[]{:S(2)}, u32[]{:S(2)}) %collective-permute-start.8) | collective-permute-done | bytes 73760 | tf_op jit(solution)/shard_map/ppermute | solution.py:431
  34.1 1.6 %collective-permute-start.11 = (bf16[416,128]{1,0:T(8,128)(2,1)S(1)}, bf16[416,128]{1,0:T(8,128)(2,1)S(1)}, u32[]{:S(2)}, u32[]{:S(2)}) collective-permute-start(bf16[416,128]{1,0:T(8,128)(2,1)S(1)} %shard_map.88.row_a.a), channel_id=1, source_target_pairs={{0,3},{1,2},{2,1},{3,0},{4,7},{5,6},{6,5},{7,4},{8,11},{9,10},{10,... | collective-permute-start | bytes 319496 | tf_op jit(solution)/shard_map/ppermute | solution.py:431
  35.6 0.5 %collective-permute-start.10 = (bf16[416,128]{1,0:T(8,128)(2,1)S(1)}, bf16[416,128]{1,0:T(8,128)(2,1)S(1)}, u32[]{:S(2)}, u32[]{:S(2)}) collective-permute-start(bf16[416,128]{1,0:T(8,128)(2,1)S(1)} %shard_map.88.row_a.a), channel_id=1, source_target_pairs={{0,2},{1,3},{2,0},{3,1},{4,6},{5,7},{6,4},{7,5},{8,10},{9,11},{10,... | collective-permute-start | bytes 319496 | tf_op jit(solution)/shard_map/ppermute | solution.py:431
  36.1 1.5 %collective-permute-start.9 = (bf16[416,128]{1,0:T(8,128)(2,1)S(1)}, bf16[416,128]{1,0:T(8,128)(2,1)S(1)}, u32[]{:S(2)}, u32[]{:S(2)}) collective-permute-start(bf16[416,128]{1,0:T(8,128)(2,1)S(1)} %shard_map.88.row_a.a), channel_id=1, source_target_pairs={{0,1},{1,0},{2,3},{3,2},{4,5},{5,4},{6,7},{7,6},{8,9},{9,8},{10,11... | collective-permute-start | bytes 319496 | tf_op jit(solution)/shard_map/ppermute | solution.py:431
  37.6 2.0 %shard_map.89.inner = f32[2048,128]{1,0:T(8,128)S(1)} custom-call(bf16[2112,128]{1,0:T(8,128)(2,1)S(1)} %get-tuple-element.95.p0, bf16[2112,128]{1,0:T(8,128)(2,1)S(1)} %get-tuple-element.96.p1, bf16[2112,128]{1,0:T(8,128)(2,1)S(1)} %get-tuple-element.97.p2, bf16[3,256,128]{2,1,0:T(8,128)(2,1)S(1)} %get-tuple-element.75.wb_ref), custom_call_target="tpu_custom_call" | custom-call | flops 402653184 | bytes 3145728 | tf_op jit(solution)/shard_map/pallas_call | solution.py:24
  39.8 1.1 %collective-permute-done.10.row_c.c = bf16[416,128]{1,0:T(8,128)(2,1)S(1)} collective-permute-done((bf16[416,128]{1,0:T(8,128)(2,1)S(1)}, bf16[416,128]{1,0:T(8,128)(2,1)S(1)}, u32[]{:S(2)}, u32[]{:S(2)}) %collective-permute-start.10) | collective-permute-done | bytes 106528 | tf_op jit(solution)/shard_map/ppermute | solution.py:431
  41.1 1.2 %shard_map.90 = bf16[64,4096]{1,0:T(8,128)(2,1)} custom-call(bf16[416,128]{1,0:T(8,128)(2,1)S(1)} %shard_map.88.row_a.a, bf16[416,128]{1,0:T(8,128)(2,1)S(1)} %collective-permute-done.9.row_b.b, bf16[416,128]{1,0:T(8,128)(2,1)S(1)} %collective-permute-done.10.row_c.c, bf16[416,128]{1,0:T(8,128)(2,1)S(1)} %collective-permute-done.11.row_d.d, ...), custom_call_target="tpu_custom_call" | custom-call | bytes 2097152 | tf_op jit(solution)/shard_map/pallas_call | solution.py:24
  42.4 0.7 %shard_map.92 = (f32[64,576]{1,0:T(8,128)}, f32[1,64]{1,0:T(1,128)}) custom-call(f32[160,128]{1,0:T(8,128)S(1)} %shard_map.91.mine, f32[160,128]{1,0:T(8,128)S(1)} %collective-permute-done.12.other), custom_call_target="tpu_custom_call" | custom-call | tf_op jit(solution)/shard_map/pallas_call | solution.py:24
  (29 shorter events, 1.9 us)
Async XLA Ops:
  0.6 1.0 %copy-start = (bf16[1,64,4096]{2,1,0:T(8,128)(2,1)S(1)}, bf16[1,64,4096]{2,1,0:T(8,128)(2,1)}, u32[]{:S(2)}) copy-start(bf16[1,64,4096]{2,1,0:T(8,128)(2,1)} %param.5) | copy-start | bytes 1572868
  1.7 4.6 %copy-start.3 = (bf16[576,64]{0,1:T(8,128)(2,1)S(1)}, bf16[576,64]{0,1:T(8,128)(2,1)}, u32[]{:S(2)}) copy-start(bf16[576,64]{0,1:T(8,128)(2,1)} %param.6) | copy-start | bytes 221188
  1.7 4.8 %collective-permute-start = (bf16[64,128]{1,0:T(8,128)(2,1)S(1)}, bf16[64,128]{1,0:T(8,128)(2,1)S(1)}, u32[]{:S(2)}, u32[]{:S(2)}) collective-permute-start(bf16[64,128]{1,0:T(8,128)(2,1)S(1)} %get-tuple-element.54.mine), channel_id=1, source_target_pairs={{0,4},{1,5},{2,6},{3,7},{4,0},{5,1},{6,2},{7,3},{8,12},{9,13},{10,... | collective-permute-start | bytes 49160 | tf_op jit(solution)/shard_map/ppermute | solution.py:431
  6.5 3.0 %copy-start.4 = (f32[64]{0:T(128)S(1)}, f32[64]{0:T(128)}, u32[]{:S(2)}) copy-start(f32[64]{0:T(128)} %param.7) | copy-start | bytes 772
  6.5 5.3 %collective-permute-start.1 = (bf16[128,128]{1,0:T(8,128)(2,1)S(1)}, bf16[128,128]{1,0:T(8,128)(2,1)S(1)}, u32[]{:S(2)}, u32[]{:S(2)}) collective-permute-start(bf16[128,128]{1,0:T(8,128)(2,1)S(1)} %shard_map.79.mine), channel_id=1, source_target_pairs={{0,8},{1,9},{2,10},{3,11},{4,12},{5,13},{6,14},{7,15},{8,0},{9,1},... | collective-permute-start | bytes 98312 | tf_op jit(solution)/shard_map/ppermute | solution.py:431
  9.6 5.8 %copy-start.2 = (s32[16,260]{1,0:T(8,128)S(1)}, s32[16,260]{1,0:T(8,128)}, u32[]{:S(2)}) copy-start(s32[16,260]{1,0:T(8,128)} %index_ref.1) | copy-start | bytes 49924
  11.8 7.3 %copy-start.1 = (bf16[1,64,4096]{2,1,0:T(8,128)(2,1)S(1)}, bf16[1,64,4096]{2,1,0:T(8,128)(2,1)}, u32[]{:S(2)}) copy-start(bf16[1,64,4096]{2,1,0:T(8,128)(2,1)} %param.8) | copy-start | bytes 1572868
  11.8 5.7 %collective-permute-start.4 = (bf16[256,128]{1,0:T(8,128)(2,1)S(1)}, bf16[256,128]{1,0:T(8,128)(2,1)S(1)}, u32[]{:S(2)}, u32[]{:S(2)}) collective-permute-start(bf16[256,128]{1,0:T(8,128)(2,1)S(1)} %shard_map.81.rows_a), channel_id=1, source_target_pairs={{0,3},{1,2},{2,1},{3,0},{4,7},{5,6},{6,5},{7,4},{8,11},{9,10},{10,... | collective-permute-start | bytes 196616 | tf_op jit(solution)/shard_map/ppermute | solution.py:431
  14.3 4.3 %collective-permute-start.3 = (bf16[256,128]{1,0:T(8,128)(2,1)S(1)}, bf16[256,128]{1,0:T(8,128)(2,1)S(1)}, u32[]{:S(2)}, u32[]{:S(2)}) collective-permute-start(bf16[256,128]{1,0:T(8,128)(2,1)S(1)} %shard_map.81.rows_a), channel_id=1, source_target_pairs={{0,2},{1,3},{2,0},{3,1},{4,6},{5,7},{6,4},{7,5},{8,10},{9,11},{10,... | collective-permute-start | bytes 196616 | tf_op jit(solution)/shard_map/ppermute | solution.py:431
  14.8 4.3 %collective-permute-start.2 = (bf16[256,128]{1,0:T(8,128)(2,1)S(1)}, bf16[256,128]{1,0:T(8,128)(2,1)S(1)}, u32[]{:S(2)}, u32[]{:S(2)}) collective-permute-start(bf16[256,128]{1,0:T(8,128)(2,1)S(1)} %shard_map.81.rows_a), channel_id=1, source_target_pairs={{0,1},{1,0},{2,3},{3,2},{4,5},{5,4},{6,7},{7,6},{8,9},{9,8},{10,11... | collective-permute-start | bytes 196616 | tf_op jit(solution)/shard_map/ppermute | solution.py:431
  15.4 3.7 %collective-permute-start.5 = (bf16[64,128]{1,0:T(8,128)(2,1)S(1)}, bf16[64,128]{1,0:T(8,128)(2,1)S(1)}, u32[]{:S(2)}, u32[]{:S(2)}) collective-permute-start(bf16[64,128]{1,0:T(8,128)(2,1)S(1)} %get-tuple-element.72), channel_id=1, source_target_pairs={{0,16},{16,0},{1,17},{17,1},{2,18},{18,2},{3,19},{19,3},{4,20},{20... | collective-permute-start | bytes 49160 | tf_op jit(solution)/shard_map/ppermute | solution.py:431
  23.1 1.3 %collective-permute-start.6 = (bf16[224,128]{1,0:T(8,128)(2,1)S(1)}, bf16[224,128]{1,0:T(8,128)(2,1)S(1)}, u32[]{:S(2)}, u32[]{:S(2)}) collective-permute-start(bf16[224,128]{1,0:T(8,128)(2,1)S(1)} %get-tuple-element.78), channel_id=1, source_target_pairs={{0,16},{16,0},{1,17},{17,1},{2,18},{18,2},{3,19},{19,3},{4,20},{20... | collective-permute-start | bytes 172040 | tf_op jit(solution)/shard_map/ppermute | solution.py:431
  24.5 4.2 %collective-permute-start.7 = (bf16[224,128]{1,0:T(8,128)(2,1)S(1)}, bf16[224,128]{1,0:T(8,128)(2,1)S(1)}, u32[]{:S(2)}, u32[]{:S(2)}) collective-permute-start(bf16[224,128]{1,0:T(8,128)(2,1)S(1)} %shard_map.85.mine), channel_id=1, source_target_pairs={{0,4},{1,5},{2,6},{3,7},{4,0},{5,1},{6,2},{7,3},{8,12},{9,13},{10,... | collective-permute-start | bytes 172040 | tf_op jit(solution)/shard_map/ppermute | solution.py:431
  28.7 5.3 %collective-permute-start.8 = (bf16[288,128]{1,0:T(8,128)(2,1)S(1)}, bf16[288,128]{1,0:T(8,128)(2,1)S(1)}, u32[]{:S(2)}, u32[]{:S(2)}) collective-permute-start(bf16[288,128]{1,0:T(8,128)(2,1)S(1)} %shard_map.86.mine), channel_id=1, source_target_pairs={{0,8},{1,9},{2,10},{3,11},{4,12},{5,13},{6,14},{7,15},{8,0},{9,1},... | collective-permute-start | bytes 221192 | tf_op jit(solution)/shard_map/ppermute | solution.py:431
  34.1 5.7 %collective-permute-start.11 = (bf16[416,128]{1,0:T(8,128)(2,1)S(1)}, bf16[416,128]{1,0:T(8,128)(2,1)S(1)}, u32[]{:S(2)}, u32[]{:S(2)}) collective-permute-start(bf16[416,128]{1,0:T(8,128)(2,1)S(1)} %shard_map.88.row_a.a), channel_id=1, source_target_pairs={{0,3},{1,2},{2,1},{3,0},{4,7},{5,6},{6,5},{7,4},{8,11},{9,10},{10,... | collective-permute-start | bytes 319496 | tf_op jit(solution)/shard_map/ppermute | solution.py:431
  35.6 5.3 %collective-permute-start.10 = (bf16[416,128]{1,0:T(8,128)(2,1)S(1)}, bf16[416,128]{1,0:T(8,128)(2,1)S(1)}, u32[]{:S(2)}, u32[]{:S(2)}) collective-permute-start(bf16[416,128]{1,0:T(8,128)(2,1)S(1)} %shard_map.88.row_a.a), channel_id=1, source_target_pairs={{0,2},{1,3},{2,0},{3,1},{4,6},{5,7},{6,4},{7,5},{8,10},{9,11},{10,... | collective-permute-start | bytes 319496 | tf_op jit(solution)/shard_map/ppermute | solution.py:431
  36.1 4.9 %collective-permute-start.9 = (bf16[416,128]{1,0:T(8,128)(2,1)S(1)}, bf16[416,128]{1,0:T(8,128)(2,1)S(1)}, u32[]{:S(2)}, u32[]{:S(2)}) collective-permute-start(bf16[416,128]{1,0:T(8,128)(2,1)S(1)} %shard_map.88.row_a.a), channel_id=1, source_target_pairs={{0,1},{1,0},{2,3},{3,2},{4,5},{5,4},{6,7},{7,6},{8,9},{9,8},{10,11... | collective-permute-start | bytes 319496 | tf_op jit(solution)/shard_map/ppermute | solution.py:431
  41.0 1.3 %collective-permute-start.12 = (f32[160,128]{1,0:T(8,128)S(1)}, f32[160,128]{1,0:T(8,128)S(1)}, u32[]{:S(2)}, u32[]{:S(2)}) collective-permute-start(f32[160,128]{1,0:T(8,128)S(1)} %shard_map.91.mine), channel_id=1, source_target_pairs={{0,16},{16,0},{1,17},{17,1},{2,18},{18,2},{3,19},{19,3},{4,20},{20... | collective-permute-start | bytes 245768 | tf_op jit(solution)/shard_map/ppermute | solution.py:431

commit v5 on v4

--- a/solution.py
+++ b/solution.py
@@ -60,13 +60,16 @@
 TN = ((0,), (0,))
 
 
-def shifted_copies(load, p0, p1, p2):
+def shifted_copies(load, p0, p1, p2, lines=None):
     is_low = low((SIDE, LANES))
     row = iota((SIDE, LANES), 0)
 
     def put(q, before, now):
         v = jnp.where(is_low, before, now)
         p1[block(q), :] = v.astype(BF16)
+        if lines is not None:
+            for i, r in enumerate((0, 1, SIDE - 2, SIDE - 1)):
+                lines[i, pl.ds(q, 1), :] = v[r : r + 1]
         p0[block(q), :] = jnp.where(row == 0, 0.0, pltpu.roll(v, 1, 0)).astype(BF16)
         p2[block(q), :] = jnp.where(row == SIDE - 1, 0.0, pltpu.roll(v, SIDE - 1, 0)).astype(BF16)
 
@@ -184,8 +187,8 @@
         wc_ref[a, c:, :] = pair(a, None, 2)
 
 
-def copies_kernel(x_ref, p0, p1, p2):
-    shifted_copies(lambda q: x_ref[:, tile(q)].astype(F32), p0, p1, p2)
+def copies_kernel(x_ref, p0, p1, p2, lines):
+    shifted_copies(lambda q: x_ref[:, tile(q)].astype(F32), p0, p1, p2, lines)
 
 
 def signal_kernel(p0, p1, p2, w_ref, bias_ref, s_ref):
@@ -209,9 +212,33 @@
     return jnp.where(low(even.shape), even, odd)
 
 
+def inside_kernel(s_ref, cot_ref, p0, p1, p2, g_ref, terms_ref, bias_ref, cot_lines):
+    row = iota((SIDE, LANES), 0)
+    border = jnp.logical_or(row == 0, row == SIDE - 1)
+
+    def step(q, bias):
+        upstream = cot_ref[:, tile(q)].astype(F32)
+        g = jnp.where(border, 0.0, slope_times(s_ref[block(q), :], upstream)).astype(BF16)
+        g_ref[block(q), :] = g
+        cot_lines[pl.ds(q, 1), :] = upstream[0:1]
+        cot_lines[pl.ds(PAIRS + q, 1), :] = upstream[SIDE - 1 :]
+        return bias + jnp.sum(g.astype(F32).reshape(8, 8, LANES), axis=0)
+
+    cot_lines[...] = jnp.zeros(cot_lines.shape, F32)
+    bias_ref[...] = lax.fori_loop(1, PAIRS - 1, step, jnp.zeros((8, LANES), F32), unroll=2)
+    g_ref[0:SIDE, :] = jnp.zeros((SIDE, LANES), BF16)
+    g_ref[ROWS - SIDE :, :] = jnp.zeros((SIDE, LANES), BF16)
+    g = g_ref[SIDE : ROWS - SIDE, :]
+    for a, p in enumerate((p0, p1, p2)):
+        for shift in (0, 1):
+            start = (1 + shift) * SIDE
+            terms_ref[a, :, shift * LANES : (shift + 1) * LANES] = dot(g, p[start : start + ROWS - 2 * SIDE, :], TN)
+
+
 def middle_kernel(
-    s_in, cot_ref, p0, p1, p2, rows_a, rows_b, rows_c, rows_d, cols_ref, hot_ref, half_ref, w_ref, wb_ref, wc_ref,
-    g_ref, keep_ref, send_ref, own_ref, s_ref, cell_scr, gt, gb, gc, own_scr, msg,
+    s_ref, cot_ref, p0, p1, p2, lines, terms_ref, bias_ref, cot_lines, rows_a, rows_b, rows_c, rows_d, cols_ref,
+    hot_ref, half_ref, w_ref, wb_ref, wc_ref,
+    g_lines, g_sides, keep_ref, send_ref, own_ref, cell_scr, gt, gb, gc, own_scr, msg,
 ):
     n = rows_a.shape[0]
     many = 4 * n
@@ -227,67 +254,92 @@
     odd = iota(cells.shape, 0) % 2 == 1
     cell_scr[...] = jnp.where(odd, as_high, as_low)
 
+    def windows(both):
+        return jnp.concatenate([both[0:PAIRS], both[1 : PAIRS + 1]], axis=1)
+
     def line_of(start):
         even_cells = cell_scr[pl.ds(start, PAIRS + 1, stride=2), :]
         odd_cells = cell_scr[pl.ds(start + 1, PAIRS + 1, stride=2), :]
-        both = halves(even_cells, odd_cells)
-        return jnp.concatenate([both[0:PAIRS], both[1 : PAIRS + 1]], axis=1).astype(BF16)
+        return windows(halves(even_cells, odd_cells))
 
     is_low = low((SIDE, LANES))
     row = iota((SIDE, LANES), 0)
     top = line_of(0)
     bottom = line_of(SIDE + 2)
-    s_ref[...] = s_in[...]
-    first = pl.ds(0, PAIRS, stride=SIDE)
-    final = pl.ds(SIDE - 1, PAIRS, stride=SIDE)
-    s_ref[first, :] += dot(top, w_ref[0], NT)
-    s_ref[final, :] += dot(bottom, w_ref[2], NT)
     moved = (
         jnp.where(row == 0, 0.0, pltpu.roll(sides, 1, 0)),
         sides,
         jnp.where(row == SIDE - 1, 0.0, pltpu.roll(sides, SIDE - 1, 0)),
     )
-    lefts = [jnp.where(is_low, m, 0.0).astype(BF16) for m in moved]
-    rights = [jnp.where(is_low, 0.0, m).astype(BF16) for m in moved]
-    for a in range(3):
-        s_ref[0:SIDE, :] += dot(lefts[a], w_ref[a, :, 0:LANES], NT)
-        s_ref[ROWS - SIDE : ROWS, :] += dot(rights[a], w_ref[a, :, LANES:], NT)
-
-    def step(q, carry):
-        bias, before = carry
-        g = slope_times(s_ref[block(q), :], cot_ref[:, tile(q)].astype(F32)).astype(BF16)
-        g_ref[block(q), :] = g
-        wide = g.astype(F32)
-        now = turn(wide)
-        pair = jnp.where(is_low, before, now)
-        gt[pl.ds(q, 1), :] = pair[0:1]
-        gb[pl.ds(q, 1), :] = pair[SIDE - 1 :]
-        s_ref[block(q), :] = wide
-        return bias + jnp.sum(wide.reshape(8, 8, LANES), axis=0), now
-
-    zero = jnp.zeros((SIDE, LANES), F32)
-    bias, last = lax.fori_loop(0, PAIRS, step, (jnp.zeros((8, LANES), F32), zero), unroll=2)
-    pair = jnp.where(is_low, last, 0.0)
-    gt[PAIRS : PAIRS + 1, :] = pair[0:1]
-    gb[PAIRS : PAIRS + 1, :] = pair[SIDE - 1 :]
-
-    g = g_ref[...]
-    g_first = s_ref[first, :].astype(BF16)
-    g_final = s_ref[final, :].astype(BF16)
+    lefts = [jnp.where(is_low, m, 0.0) for m in moved]
+    rights = [jnp.where(is_low, 0.0, m) for m in moved]
+    top_signal = dot(top.astype(BF16), w_ref[0], NT)
+    bottom_signal = dot(bottom.astype(BF16), w_ref[2], NT)
+
+    def side_grad(q, columns, lanes):
+        signal = s_ref[q * SIDE : (q + 1) * SIDE, :]
+        for a in range(3):
+            signal = signal + dot(columns[a].astype(BF16), w_ref[a, :, lanes], NT)
+        signal = signal + jnp.where(row == 0, top_signal[q : q + 1], 0.0)
+        signal = signal + jnp.where(row == SIDE - 1, bottom_signal[q : q + 1], 0.0)
+        upstream = cot_ref[:, q * LANES : (q + 1) * LANES].astype(F32)
+        return slope_times(signal, upstream).astype(BF16).astype(F32)
+
+    end = PAIRS - 1
+    g_left = side_grad(0, lefts, slice(0, LANES))
+    g_right = side_grad(end, rights, slice(LANES, 2 * LANES))
+    pair = iota((PAIRS, LANES), 0)
+    ends = jnp.logical_or(pair == 0, pair == end)
+
+    def line_grad(first_row, halo_signal):
+        signal = s_ref[pl.ds(first_row, PAIRS, stride=SIDE), :] + halo_signal
+        upstream = cot_lines[0:PAIRS, :] if first_row == 0 else cot_lines[PAIRS:, :]
+        g = jnp.where(ends, 0.0, slope_times(signal, upstream)).astype(BF16).astype(F32)
+        r = slice(first_row, first_row + 1)
+        return g, jnp.where(pair == 0, g_left[r], jnp.where(pair == end, g_right[r], g))
+
+    inner_top, all_top = line_grad(0, top_signal)
+    inner_bottom, all_bottom = line_grad(SIDE - 1, bottom_signal)
+    g_lines[0:PAIRS, :] = all_top
+    g_lines[PAIRS:, :] = all_bottom
+    g_sides[0:SIDE, :] = g_left.astype(BF16)
+    g_sides[SIDE:, :] = g_right.astype(BF16)
+    border = jnp.concatenate([inner_top, inner_bottom, g_left, g_right], axis=0)
+    bias = jnp.sum(bias_ref[...], axis=0, keepdims=True) + jnp.sum(border, axis=0, keepdims=True)
+    border = border.astype(BF16)
+    kept = [windows(lines[i]) for i in range(4)]
+    none = jnp.zeros((SIDE, LANES), F32)
+    wide_row = iota((SIDE, 2 * LANES), 0)
+
+    def side_window(a, p, q, columns):
+        parts = [p[(q + i) * SIDE : (q + i + 1) * SIDE, :].astype(F32) for i in range(2)]
+        window = jnp.concatenate(parts, axis=1) + columns
+        if a == 0:
+            window = window + jnp.where(wide_row == 0, top[q : q + 1], 0.0)
+        if a == 2:
+            window = window + jnp.where(wide_row == SIDE - 1, bottom[q : q + 1], 0.0)
+        return window
+
     terms = []
+    over = (top, kept[0], kept[1])
+    under = (kept[2], kept[3], bottom)
     for a, p in enumerate((p0, p1, p2)):
-        for shift in (0, 1):
-            t = dot(g, p[shift * SIDE : shift * SIDE + ROWS, :], TN)
-            lanes = slice(shift * LANES, (shift + 1) * LANES)
-            if a == 0:
-                t += dot(g_first, top[:, lanes], TN)
-            if a == 2:
-                t += dot(g_final, bottom[:, lanes], TN)
-            if shift == 0:
-                t += dot(g[0:SIDE], lefts[a], TN)
-            else:
-                t += dot(g[ROWS - SIDE :], rights[a], TN)
-            terms.append(t)
+        window = jnp.concatenate(
+            [
+                over[a],
+                under[a],
+                side_window(a, p, 0, jnp.concatenate([lefts[a], none], axis=1)),
+                side_window(a, p, end, jnp.concatenate([none, rights[a]], axis=1)),
+            ],
+            axis=0,
+        ).astype(BF16)
+        t = terms_ref[a] + dot(border, window, TN)
+        terms += [t[:, :LANES], t[:, LANES:]]
+    for scr, line in ((gt, all_top), (gb, all_bottom)):
+        turned = turn(line)
+        scr[...] = jnp.zeros(scr.shape, F32)
+        scr[1 : PAIRS + 1, :] = jnp.where(low(line.shape), turned, 0.0)
+        scr[0:PAIRS, :] += jnp.where(low(line.shape), 0.0, turned)
 
     def tap(m, high):
         a, b = m // 3, m % 3
@@ -298,8 +350,7 @@
             result = result + (part if (w % 2 == 1) == high else turn(part))
         return result
 
-    total = jnp.sum(bias, axis=0, keepdims=True)
-    total = total + turn(total)
+    total = bias + turn(bias)
     coarse = total.astype(BF16).astype(F32)
     fine = total - coarse
     for t in range(5):
@@ -321,7 +372,7 @@
     own_ref[...] = own_scr[...].astype(BF16)
 
     gc[...] = jnp.zeros(gc.shape, F32)
-    gc[8 : 8 + SIDE, :] = jnp.where(is_low, s_ref[0:SIDE, :], s_ref[ROWS - SIDE : ROWS, :])
+    gc[8 : 8 + SIDE, :] = halves(g_left, g_right)
     grads = dot(gc[8:88, :].astype(BF16), wc_ref[0])
     grads = grads + dot(gc[7:87, :].astype(BF16), wc_ref[1])
     grads = grads + dot(gc[6:86, :].astype(BF16), wc_ref[2])
@@ -338,8 +389,18 @@
     send_ref[WROWS:, :] = dot(hot_ref[:, many:], placed, TN).astype(BF16)
 
 
-def grad_copies_kernel(g_ref, p0, p1, p2):
-    shifted_copies(lambda q: g_ref[block(q), :].astype(F32), p0, p1, p2)
+def grad_copies_kernel(g_ref, g_lines, g_sides, p0, p1, p2):
+    row = iota((SIDE, LANES), 0)
+    left = g_sides[0:SIDE, :].astype(F32)
+    right = g_sides[SIDE:, :].astype(F32)
+
+    def load(q):
+        g = g_ref[block(q), :].astype(F32)
+        g = jnp.where(row == 0, g_lines[pl.ds(q, 1), :], g)
+        g = jnp.where(row == SIDE - 1, g_lines[pl.ds(PAIRS + q, 1), :], g)
+        return jnp.where(q == 0, left, jnp.where(q == PAIRS - 1, right, g))
+
+    shifted_copies(load, p0, p1, p2)
 
 
 def inner_kernel(p0, p1, p2, wb_ref, out_ref):
@@ -482,13 +543,13 @@
         return call(rows_kernel, [((2 * rows.shape[0], LANES), BF16)], rows, other)[0]
 
     other = exchange(rows, high[0])
-    copies = call(copies_kernel, [pair] * 3, x, moved=2 * 2**20)
+    *copies, lines = call(copies_kernel, [pair] * 3 + [((4, 40, LANES), F32)], x, moved=2 * 2**20)
     forward, backward, columns = call(
         weights_kernel,
         [((3, LANES, 2 * LANES), BF16), ((3, 2 * LANES, LANES), BF16), ((3, LANES, LANES), BF16)],
         fine_weight.T,
     )
-    other, copies, forward = lax.optimization_barrier((other, copies, forward))
+    other, copies, lines, forward = lax.optimization_barrier((other, copies, lines, forward))
     rows = joined(rows, other)
     other = exchange(rows, high[1])
     signal = call(signal_kernel, [both], *copies, forward, fine_bias.reshape(1, CHANNELS), **work)[0]
@@ -503,18 +564,27 @@
         index, scratch=[pltpu.VMEM((8, 384), F32)],
     )
     pick = call(functools.partial(pick_kernel, owners), [((4 * SIDE, owners * SIDE), BF16)], index)[0]
-    others, hot, half_mask, pick = lax.optimization_barrier((others, hot, half_mask, pick))
+    inside = call(
+        inside_kernel,
+        [((ROWS, LANES), BF16), ((3, LANES, 2 * LANES), F32), ((8, LANES), F32), ((SIDE, LANES), F32)],
+        signal, cot, *copies, **work,
+    )
+    others, hot, half_mask, pick, inside = lax.optimization_barrier((others, hot, half_mask, pick, inside))
+    grad, *inside = inside
 
     line = pltpu.VMEM((40, LANES), F32)
-    grad, message, sent, own_rows = call(
+    g_lines, g_sides, message, sent, own_rows = call(
         middle_kernel,
-        [((ROWS, LANES), BF16), ((WROWS, LANES), BF16), ((WROWS + blocks * SIDE, LANES), BF16), ((SIDE, LANES), BF16)],
-        signal, cot, *copies, rows, *others, cols, hot, half_mask, forward, backward, columns,
+        [
+            ((SIDE, LANES), F32), ((2 * SIDE, LANES), BF16),
+            ((WROWS, LANES), BF16), ((WROWS + blocks * SIDE, LANES), BF16), ((SIDE, LANES), BF16),
+        ],
+        signal, cot, *copies, lines, *inside, rows, *others, cols, hot, half_mask, forward, backward, columns,
         scratch=[
-            pltpu.VMEM((ROWS, LANES), F32), pltpu.VMEM((count, LANES), F32), line, line,
+            pltpu.VMEM((count, LANES), F32), line, line,
             pltpu.VMEM((96, LANES), F32), pltpu.VMEM((SIDE, LANES), F32), pltpu.VMEM((2 * WROWS, LANES), F32),
         ],
-        **work,
+        moved=2**20,
     )
 
     if regions > 2:
@@ -529,12 +599,12 @@
         extra = () if k != ([1] + far)[-1] else (own_rows,)
         size = (WROWS + SIDE * len(extra), LANES)
         message = call(join_kernel, [(size, BF16)], message, other if k == 1 else swap(message, "region", k), *extra)[0]
-    beside = grad
+    beside = [grad, g_lines, g_sides]
     for step, k in enumerate(high):
         message, beside = lax.optimization_barrier((message, beside))
         other = exchange(message, k)
         if step == 1:
-            beside = call(grad_copies_kernel, [pair] * 3, beside, moved=2 * 2**20)
+            beside = call(grad_copies_kernel, [pair] * 3, *beside, moved=2 * 2**20)
         other, beside = lax.optimization_barrier((other, beside))
         size = (2 * message.shape[0] - WROWS, LANES)
         message = call(join_kernel, [(size, BF16)], message, other)[0]

time: 43.2 us -> 40.6 us (0.940)
  waiting for transfers between devices: 9.82 us -> 8.14 us
  Pallas kernels: 13.8 us -> 12.9 us
    ppermute x13, waiting for transfers between devices: 9.82 us -> 8.14 us  [swap(): return lax.ppermute(x, axis, [(i, i ^ k) for i in range(n)])]
    pallas_call x17 -> x18, Pallas kernels: 13.8 us -> 12.9 us  [call(): pl.pallas_call(kernel, out_shape=shapes, in_specs=[pl.BlockSpec(memory_sp...]
  transfers between devices with their start and end apart: 13 -> 13, of which waited for: 11 -> 10; matrix products, arithmetic and copies ran while one was open for 0% -> 0% of each run, Pallas kernels for 21% -> 26%
where the time goes in v5:
time: 40.6 us; the launch traced here: 40.5 us
  starting transfers between devices  17.6 us (43%)
  Pallas kernels  12.9 us (32%)
  waiting for transfers between devices  8.14 us (20%)
  local copies, waits for them, and re-layouts  1.05 us (3%)
  between operations  0.78 us (2%)
    ppermute x13, starting transfers between devices, swap(): return lax.ppermute(x, axis, [(i, i ^ k) for i in range(n)])  17.6 us
    pallas_call x18, Pallas kernels, call(): pl.pallas_call(kernel, out_shape=shapes, in_specs=[pl.BlockSpec(memory_sp...  12.9 us
    ppermute x13, waiting for transfers between devices, swap(): return lax.ppermute(x, axis, [(i, i ^ k) for i in range(n)])  8.14 us
    unnamed x10, local copies, waits for them, and re-layouts  1.05 us
  transfers between devices with their start and end apart: 13, of which 10 were waited for; matrix products, arithmetic and copies ran while one was open for 0% of the time, Pallas kernels for 26%

profile of v5, /device:TPU:0, one launch (start us, length us, event | category | flops | bytes accessed | tf_op | source)
XLA Modules:
  0.0 40.5 jit_solution(5489956026115085636)
XLA Ops:
  0.6 1.0 %copy-done.1 = bf16[1,64,4096]{2,1,0:T(8,128)(2,1)S(1)} copy-done((bf16[1,64,4096]{2,1,0:T(8,128)(2,1)S(1)}, bf16[1,64,4096]{2,1,0:T(8,128)(2,1)}, u32[]{:S(2)}) %copy-start.1) | copy-done | bytes 524312
  1.7 3.1 %collective-permute-start = (bf16[64,128]{1,0:T(8,128)(2,1)S(1)}, bf16[64,128]{1,0:T(8,128)(2,1)S(1)}, u32[]{:S(2)}, u32[]{:S(2)}) collective-permute-start(bf16[64,128]{1,0:T(8,128)(2,1)S(1)} %get-tuple-element.71.mine), channel_id=1, source_target_pairs={{0,4},{1,5},{2,6},{3,7},{4,0},{5,1},{6,2},{7,3},{8,12},{9,13},{10,... | collective-permute-start | bytes 49160 | tf_op jit(solution)/shard_map/ppermute | solution.py:492
  4.8 1.5 %shard_map.77 = (bf16[2112,128]{1,0:T(8,128)(2,1)S(1)}, bf16[2112,128]{1,0:T(8,128)(2,1)S(1)}, bf16[2112,128]{1,0:T(8,128)(2,1)S(1)}, f32[4,40,128]{2,1,0:T(8,128)S(1)}) custom-call(bf16[64,4096]{1,0:T(8,128)(2,1)S(1)} %bitcast.10), custom_call_target="tpu_custom_call" | custom-call | bytes 2097152 | tf_op jit(solution)/shard_map/pallas_call | solution.py:24
  6.5 3.0 %collective-permute-start.1 = (bf16[128,128]{1,0:T(8,128)(2,1)S(1)}, bf16[128,128]{1,0:T(8,128)(2,1)S(1)}, u32[]{:S(2)}, u32[]{:S(2)}) collective-permute-start(bf16[128,128]{1,0:T(8,128)(2,1)S(1)} %shard_map.79.mine), channel_id=1, source_target_pairs={{0,8},{1,9},{2,10},{3,11},{4,12},{5,13},{6,14},{7,15},{8,0},{9,1},... | collective-permute-start | bytes 98312 | tf_op jit(solution)/shard_map/ppermute | solution.py:492
  9.6 2.2 %shard_map.80.s_ref = f32[2048,128]{1,0:T(8,128)S(1)} custom-call(bf16[2112,128]{1,0:T(8,128)(2,1)S(1)} %get-tuple-element.78.p0, bf16[2112,128]{1,0:T(8,128)(2,1)S(1)} %get-tuple-element.79.p1, bf16[2112,128]{1,0:T(8,128)(2,1)S(1)} %get-tuple-element.80.p2, bf16[3,128,256]{2,1,0:T(8,128)(2,1)S(1)} %get-tuple-element.81.w_ref, f32[1,64]{1,0:T(1,128)S(1)} %bitcast.12), custom_call_target="tpu_custom_call" | custom-call | flops 402653184 | bytes 3145728 | tf_op jit(solution)/shard_map/pallas_call | solution.py:24
  11.8 2.5 %collective-permute-start.4 = (bf16[256,128]{1,0:T(8,128)(2,1)S(1)}, bf16[256,128]{1,0:T(8,128)(2,1)S(1)}, u32[]{:S(2)}, u32[]{:S(2)}) collective-permute-start(bf16[256,128]{1,0:T(8,128)(2,1)S(1)} %shard_map.81.rows_a), channel_id=1, source_target_pairs={{0,3},{1,2},{2,1},{3,0},{4,7},{5,6},{6,5},{7,4},{8,11},{9,10},{10,... | collective-permute-start | bytes 196616 | tf_op jit(solution)/shard_map/ppermute | solution.py:492
  14.3 0.5 %collective-permute-start.3 = (bf16[256,128]{1,0:T(8,128)(2,1)S(1)}, bf16[256,128]{1,0:T(8,128)(2,1)S(1)}, u32[]{:S(2)}, u32[]{:S(2)}) collective-permute-start(bf16[256,128]{1,0:T(8,128)(2,1)S(1)} %shard_map.81.rows_a), channel_id=1, source_target_pairs={{0,2},{1,3},{2,0},{3,1},{4,6},{5,7},{6,4},{7,5},{8,10},{9,11},{10,... | collective-permute-start | bytes 196616 | tf_op jit(solution)/shard_map/ppermute | solution.py:492
  14.8 0.5 %collective-permute-start.2 = (bf16[256,128]{1,0:T(8,128)(2,1)S(1)}, bf16[256,128]{1,0:T(8,128)(2,1)S(1)}, u32[]{:S(2)}, u32[]{:S(2)}) collective-permute-start(bf16[256,128]{1,0:T(8,128)(2,1)S(1)} %shard_map.81.rows_a), channel_id=1, source_target_pairs={{0,1},{1,0},{2,3},{3,2},{4,5},{5,4},{6,7},{7,6},{8,9},{9,8},{10,11... | collective-permute-start | bytes 196616 | tf_op jit(solution)/shard_map/ppermute | solution.py:492
  15.4 1.6 %shard_map.84 = (bf16[2048,128]{1,0:T(8,128)(2,1)S(1)}, f32[3,128,256]{2,1,0:T(8,128)S(1)}, f32[8,128]{1,0:T(8,128)S(1)}, f32[64,128]{1,0:T(8,128)S(1)}) custom-call(f32[2048,128]{1,0:T(8,128)S(1)} %shard_map.80.s_ref, bf16[64,4096]{1,0:T(8,128)(2,1)S(1)} %bitcast.7, bf16[2112,128]{1,0:T(8,128)(2,1)S(1)} %get-tuple-element.78.p0, ...), custom_call_target="tpu_custom_call" | custom-call | flops 402653184 | bytes 3145728 | tf_op jit(solution)/shard_map/pallas_call | solution.py:24
  17.6 1.0 %collective-permute-done.3.rows_c = bf16[256,128]{1,0:T(8,128)(2,1)S(1)} collective-permute-done((bf16[256,128]{1,0:T(8,128)(2,1)S(1)}, bf16[256,128]{1,0:T(8,128)(2,1)S(1)}, u32[]{:S(2)}, u32[]{:S(2)}) %collective-permute-start.3) | collective-permute-done | bytes 65568 | tf_op jit(solution)/shard_map/ppermute | solution.py:492
  18.6 0.5 %collective-permute-done.2.rows_b = bf16[256,128]{1,0:T(8,128)(2,1)S(1)} collective-permute-done((bf16[256,128]{1,0:T(8,128)(2,1)S(1)}, bf16[256,128]{1,0:T(8,128)(2,1)S(1)}, u32[]{:S(2)}, u32[]{:S(2)}) %collective-permute-start.2) | collective-permute-done | bytes 65568 | tf_op jit(solution)/shard_map/ppermute | solution.py:492
  19.1 1.4 %shard_map.85 = (f32[64,128]{1,0:T(8,128)S(1)}, bf16[128,128]{1,0:T(8,128)(2,1)S(1)}, bf16[160,128]{1,0:T(8,128)(2,1)S(1)}, bf16[224,128]{1,0:T(8,128)(2,1)S(1)}, bf16[64,128]{1,0:T(8,128)(2,1)S(1)}) custom-call(f32[2048,128]{1,0:T(8,128)S(1)} %shard_map.80.s_ref, bf16[64,4096]{1,0:T(8,128)(2,1)S(1)} %bitcast.8, bf16[2112,128]{1,0:T(8,128)(2,1)S(1)} %get-tuple-element.78.p0, ...), custom_call_target="tpu_custom_call" | custom-call | bytes 1048576 | tf_op jit(solution)/shard_map/pallas_call | solution.py:24
  20.6 1.2 %collective-permute-done.6.other.rest_0_ = bf16[224,128]{1,0:T(8,128)(2,1)S(1)} collective-permute-done((bf16[224,128]{1,0:T(8,128)(2,1)S(1)}, bf16[224,128]{1,0:T(8,128)(2,1)S(1)}, u32[]{:S(2)}, u32[]{:S(2)}) %collective-permute-start.6) | collective-permute-done | bytes 57376 | tf_op jit(solution)/shard_map/ppermute | solution.py:492
  21.9 1.6 %collective-permute-start.7 = (bf16[224,128]{1,0:T(8,128)(2,1)S(1)}, bf16[224,128]{1,0:T(8,128)(2,1)S(1)}, u32[]{:S(2)}, u32[]{:S(2)}) collective-permute-start(bf16[224,128]{1,0:T(8,128)(2,1)S(1)} %shard_map.86.mine), channel_id=1, source_target_pairs={{0,4},{1,5},{2,6},{3,7},{4,0},{5,1},{6,2},{7,3},{8,12},{9,13},{10,... | collective-permute-start | bytes 172040 | tf_op jit(solution)/shard_map/ppermute | solution.py:492
  23.5 2.6 %collective-permute-done.7.other = bf16[224,128]{1,0:T(8,128)(2,1)S(1)} collective-permute-done((bf16[224,128]{1,0:T(8,128)(2,1)S(1)}, bf16[224,128]{1,0:T(8,128)(2,1)S(1)}, u32[]{:S(2)}, u32[]{:S(2)}) %collective-permute-start.7) | collective-permute-done | bytes 57376 | tf_op jit(solution)/shard_map/ppermute | solution.py:492
  26.1 2.6 %collective-permute-start.8 = (bf16[288,128]{1,0:T(8,128)(2,1)S(1)}, bf16[288,128]{1,0:T(8,128)(2,1)S(1)}, u32[]{:S(2)}, u32[]{:S(2)}) collective-permute-start(bf16[288,128]{1,0:T(8,128)(2,1)S(1)} %shard_map.87.mine), channel_id=1, source_target_pairs={{0,8},{1,9},{2,10},{3,11},{4,12},{5,13},{6,14},{7,15},{8,0},{9,1},... | collective-permute-start | bytes 221192 | tf_op jit(solution)/shard_map/ppermute | solution.py:492
  28.7 1.5 %shard_map.88 = (bf16[2112,128]{1,0:T(8,128)(2,1)S(1)}, bf16[2112,128]{1,0:T(8,128)(2,1)S(1)}, bf16[2112,128]{1,0:T(8,128)(2,1)S(1)}) custom-call(bf16[2048,128]{1,0:T(8,128)(2,1)S(1)} %get-tuple-element.118.g_ref, f32[64,128]{1,0:T(8,128)S(1)} %get-tuple-element.119.g_lines, bf16[128,128]{1,0:T(8,128)(2,1)S(1)} %get-tuple-element.120.g_sides), custom_call_target="tpu_custom_call" | custom-call | bytes 2097152 | tf_op jit(solution)/shard_map/pallas_call | solution.py:24
  30.2 1.2 %collective-permute-done.8.other = bf16[288,128]{1,0:T(8,128)(2,1)S(1)} collective-permute-done((bf16[288,128]{1,0:T(8,128)(2,1)S(1)}, bf16[288,128]{1,0:T(8,128)(2,1)S(1)}, u32[]{:S(2)}, u32[]{:S(2)}) %collective-permute-start.8) | collective-permute-done | bytes 73760 | tf_op jit(solution)/shard_map/ppermute | solution.py:492
  31.5 1.6 %collective-permute-start.11 = (bf16[416,128]{1,0:T(8,128)(2,1)S(1)}, bf16[416,128]{1,0:T(8,128)(2,1)S(1)}, u32[]{:S(2)}, u32[]{:S(2)}) collective-permute-start(bf16[416,128]{1,0:T(8,128)(2,1)S(1)} %shard_map.89.row_a.a), channel_id=1, source_target_pairs={{0,3},{1,2},{2,1},{3,0},{4,7},{5,6},{6,5},{7,4},{8,11},{9,10},{10,... | collective-permute-start | bytes 319496 | tf_op jit(solution)/shard_map/ppermute | solution.py:492
  33.5 1.5 %collective-permute-start.9 = (bf16[416,128]{1,0:T(8,128)(2,1)S(1)}, bf16[416,128]{1,0:T(8,128)(2,1)S(1)}, u32[]{:S(2)}, u32[]{:S(2)}) collective-permute-start(bf16[416,128]{1,0:T(8,128)(2,1)S(1)} %shard_map.89.row_a.a), channel_id=1, source_target_pairs={{0,1},{1,0},{2,3},{3,2},{4,5},{5,4},{6,7},{7,6},{8,9},{9,8},{10,11... | collective-permute-start | bytes 319496 | tf_op jit(solution)/shard_map/ppermute | solution.py:492
  35.0 2.0 %shard_map.90.inner = f32[2048,128]{1,0:T(8,128)S(1)} custom-call(bf16[2112,128]{1,0:T(8,128)(2,1)S(1)} %get-tuple-element.129.p0, bf16[2112,128]{1,0:T(8,128)(2,1)S(1)} %get-tuple-element.130.p1, bf16[2112,128]{1,0:T(8,128)(2,1)S(1)} %get-tuple-element.131.p2, bf16[3,256,128]{2,1,0:T(8,128)(2,1)S(1)} %get-tuple-element.101.wb_ref), custom_call_target="tpu_custom_call" | custom-call | flops 402653184 | bytes 3145728 | tf_op jit(solution)/shard_map/pallas_call | solution.py:24
  37.2 1.1 %collective-permute-done.10.row_c.c = bf16[416,128]{1,0:T(8,128)(2,1)S(1)} collective-permute-done((bf16[416,128]{1,0:T(8,128)(2,1)S(1)}, bf16[416,128]{1,0:T(8,128)(2,1)S(1)}, u32[]{:S(2)}, u32[]{:S(2)}) %collective-permute-start.10) | collective-permute-done | bytes 106528 | tf_op jit(solution)/shard_map/ppermute | solution.py:492
  38.5 1.2 %shard_map.91 = bf16[64,4096]{1,0:T(8,128)(2,1)} custom-call(bf16[416,128]{1,0:T(8,128)(2,1)S(1)} %shard_map.89.row_a.a, bf16[416,128]{1,0:T(8,128)(2,1)S(1)} %collective-permute-done.9.row_b.b, bf16[416,128]{1,0:T(8,128)(2,1)S(1)} %collective-permute-done.10.row_c.c, bf16[416,128]{1,0:T(8,128)(2,1)S(1)} %collective-permute-done.11.row_d.d, ...), custom_call_target="tpu_custom_call" | custom-call | bytes 2097152 | tf_op jit(solution)/shard_map/pallas_call | solution.py:24
  39.8 0.7 %shard_map.93 = (f32[64,576]{1,0:T(8,128)}, f32[1,64]{1,0:T(1,128)}) custom-call(f32[160,128]{1,0:T(8,128)S(1)} %shard_map.92.mine, f32[160,128]{1,0:T(8,128)S(1)} %collective-permute-done.12.other), custom_call_target="tpu_custom_call" | custom-call | tf_op jit(solution)/shard_map/pallas_call | solution.py:24
  (30 shorter events, 1.9 us)
Async XLA Ops:
  0.6 1.0 %copy-start.1 = (bf16[1,64,4096]{2,1,0:T(8,128)(2,1)S(1)}, bf16[1,64,4096]{2,1,0:T(8,128)(2,1)}, u32[]{:S(2)}) copy-start(bf16[1,64,4096]{2,1,0:T(8,128)(2,1)} %param.5) | copy-start | bytes 1572868
  1.7 4.6 %copy-start.3 = (bf16[576,64]{0,1:T(8,128)(2,1)S(1)}, bf16[576,64]{0,1:T(8,128)(2,1)}, u32[]{:S(2)}) copy-start(bf16[576,64]{0,1:T(8,128)(2,1)} %param.6) | copy-start | bytes 221188
  1.7 4.8 %collective-permute-start = (bf16[64,128]{1,0:T(8,128)(2,1)S(1)}, bf16[64,128]{1,0:T(8,128)(2,1)S(1)}, u32[]{:S(2)}, u32[]{:S(2)}) collective-permute-start(bf16[64,128]{1,0:T(8,128)(2,1)S(1)} %get-tuple-element.71.mine), channel_id=1, source_target_pairs={{0,4},{1,5},{2,6},{3,7},{4,0},{5,1},{6,2},{7,3},{8,12},{9,13},{10,... | collective-permute-start | bytes 49160 | tf_op jit(solution)/shard_map/ppermute | solution.py:492
  6.5 3.0 %copy-start.4 = (f32[64]{0:T(128)S(1)}, f32[64]{0:T(128)}, u32[]{:S(2)}) copy-start(f32[64]{0:T(128)} %param.7) | copy-start | bytes 772
  6.5 5.3 %collective-permute-start.1 = (bf16[128,128]{1,0:T(8,128)(2,1)S(1)}, bf16[128,128]{1,0:T(8,128)(2,1)S(1)}, u32[]{:S(2)}, u32[]{:S(2)}) collective-permute-start(bf16[128,128]{1,0:T(8,128)(2,1)S(1)} %shard_map.79.mine), channel_id=1, source_target_pairs={{0,8},{1,9},{2,10},{3,11},{4,12},{5,13},{6,14},{7,15},{8,0},{9,1},... | collective-permute-start | bytes 98312 | tf_op jit(solution)/shard_map/ppermute | solution.py:492
  9.6 5.8 %copy-start = (bf16[1,64,4096]{2,1,0:T(8,128)(2,1)S(1)}, bf16[1,64,4096]{2,1,0:T(8,128)(2,1)}, u32[]{:S(2)}) copy-start(bf16[1,64,4096]{2,1,0:T(8,128)(2,1)} %param.8) | copy-start | bytes 1572868
  11.8 5.8 %collective-permute-start.4 = (bf16[256,128]{1,0:T(8,128)(2,1)S(1)}, bf16[256,128]{1,0:T(8,128)(2,1)S(1)}, u32[]{:S(2)}, u32[]{:S(2)}) collective-permute-start(bf16[256,128]{1,0:T(8,128)(2,1)S(1)} %shard_map.81.rows_a), channel_id=1, source_target_pairs={{0,3},{1,2},{2,1},{3,0},{4,7},{5,6},{6,5},{7,4},{8,11},{9,10},{10,... | collective-permute-start | bytes 196616 | tf_op jit(solution)/shard_map/ppermute | solution.py:492
  14.3 4.3 %collective-permute-start.3 = (bf16[256,128]{1,0:T(8,128)(2,1)S(1)}, bf16[256,128]{1,0:T(8,128)(2,1)S(1)}, u32[]{:S(2)}, u32[]{:S(2)}) collective-permute-start(bf16[256,128]{1,0:T(8,128)(2,1)S(1)} %shard_map.81.rows_a), channel_id=1, source_target_pairs={{0,2},{1,3},{2,0},{3,1},{4,6},{5,7},{6,4},{7,5},{8,10},{9,11},{10,... | collective-permute-start | bytes 196616 | tf_op jit(solution)/shard_map/ppermute | solution.py:492
  14.8 4.3 %collective-permute-start.2 = (bf16[256,128]{1,0:T(8,128)(2,1)S(1)}, bf16[256,128]{1,0:T(8,128)(2,1)S(1)}, u32[]{:S(2)}, u32[]{:S(2)}) collective-permute-start(bf16[256,128]{1,0:T(8,128)(2,1)S(1)} %shard_map.81.rows_a), channel_id=1, source_target_pairs={{0,1},{1,0},{2,3},{3,2},{4,5},{5,4},{6,7},{7,6},{8,9},{9,8},{10,11... | collective-permute-start | bytes 196616 | tf_op jit(solution)/shard_map/ppermute | solution.py:492
  15.4 3.7 %collective-permute-start.5 = (bf16[64,128]{1,0:T(8,128)(2,1)S(1)}, bf16[64,128]{1,0:T(8,128)(2,1)S(1)}, u32[]{:S(2)}, u32[]{:S(2)}) collective-permute-start(bf16[64,128]{1,0:T(8,128)(2,1)S(1)} %get-tuple-element.98), channel_id=1, source_target_pairs={{0,16},{16,0},{1,17},{17,1},{2,18},{18,2},{3,19},{19,3},{4,20},{20... | collective-permute-start | bytes 49160 | tf_op jit(solution)/shard_map/ppermute | solution.py:492
  15.4 1.7 %copy-start.2 = (s32[16,260]{1,0:T(8,128)S(1)}, s32[16,260]{1,0:T(8,128)}, u32[]{:S(2)}) copy-start(s32[16,260]{1,0:T(8,128)} %index_ref.1) | copy-start | bytes 49924
  20.5 1.3 %collective-permute-start.6 = (bf16[224,128]{1,0:T(8,128)(2,1)S(1)}, bf16[224,128]{1,0:T(8,128)(2,1)S(1)}, u32[]{:S(2)}, u32[]{:S(2)}) collective-permute-start(bf16[224,128]{1,0:T(8,128)(2,1)S(1)} %get-tuple-element.104), channel_id=1, source_target_pairs={{0,16},{16,0},{1,17},{17,1},{2,18},{18,2},{3,19},{19,3},{4,20},{20... | collective-permute-start | bytes 172040 | tf_op jit(solution)/shard_map/ppermute | solution.py:492
  21.9 4.2 %collective-permute-start.7 = (bf16[224,128]{1,0:T(8,128)(2,1)S(1)}, bf16[224,128]{1,0:T(8,128)(2,1)S(1)}, u32[]{:S(2)}, u32[]{:S(2)}) collective-permute-start(bf16[224,128]{1,0:T(8,128)(2,1)S(1)} %shard_map.86.mine), channel_id=1, source_target_pairs={{0,4},{1,5},{2,6},{3,7},{4,0},{5,1},{6,2},{7,3},{8,12},{9,13},{10,... | collective-permute-start | bytes 172040 | tf_op jit(solution)/shard_map/ppermute | solution.py:492
  26.1 5.3 %collective-permute-start.8 = (bf16[288,128]{1,0:T(8,128)(2,1)S(1)}, bf16[288,128]{1,0:T(8,128)(2,1)S(1)}, u32[]{:S(2)}, u32[]{:S(2)}) collective-permute-start(bf16[288,128]{1,0:T(8,128)(2,1)S(1)} %shard_map.87.mine), channel_id=1, source_target_pairs={{0,8},{1,9},{2,10},{3,11},{4,12},{5,13},{6,14},{7,15},{8,0},{9,1},... | collective-permute-start | bytes 221192 | tf_op jit(solution)/shard_map/ppermute | solution.py:492
  31.5 5.7 %collective-permute-start.11 = (bf16[416,128]{1,0:T(8,128)(2,1)S(1)}, bf16[416,128]{1,0:T(8,128)(2,1)S(1)}, u32[]{:S(2)}, u32[]{:S(2)}) collective-permute-start(bf16[416,128]{1,0:T(8,128)(2,1)S(1)} %shard_map.89.row_a.a), channel_id=1, source_target_pairs={{0,3},{1,2},{2,1},{3,0},{4,7},{5,6},{6,5},{7,4},{8,11},{9,10},{10,... | collective-permute-start | bytes 319496 | tf_op jit(solution)/shard_map/ppermute | solution.py:492
  33.0 5.2 %collective-permute-start.10 = (bf16[416,128]{1,0:T(8,128)(2,1)S(1)}, bf16[416,128]{1,0:T(8,128)(2,1)S(1)}, u32[]{:S(2)}, u32[]{:S(2)}) collective-permute-start(bf16[416,128]{1,0:T(8,128)(2,1)S(1)} %shard_map.89.row_a.a), channel_id=1, source_target_pairs={{0,2},{1,3},{2,0},{3,1},{4,6},{5,7},{6,4},{7,5},{8,10},{9,11},{10,... | collective-permute-start | bytes 319496 | tf_op jit(solution)/shard_map/ppermute | solution.py:492
  33.5 4.9 %collective-permute-start.9 = (bf16[416,128]{1,0:T(8,128)(2,1)S(1)}, bf16[416,128]{1,0:T(8,128)(2,1)S(1)}, u32[]{:S(2)}, u32[]{:S(2)}) collective-permute-start(bf16[416,128]{1,0:T(8,128)(2,1)S(1)} %shard_map.89.row_a.a), channel_id=1, source_target_pairs={{0,1},{1,0},{2,3},{3,2},{4,5},{5,4},{6,7},{7,6},{8,9},{9,8},{10,11... | collective-permute-start | bytes 319496 | tf_op jit(solution)/shard_map/ppermute | solution.py:492
  38.4 1.3 %collective-permute-start.12 = (f32[160,128]{1,0:T(8,128)S(1)}, f32[160,128]{1,0:T(8,128)S(1)}, u32[]{:S(2)}, u32[]{:S(2)}) collective-permute-start(f32[160,128]{1,0:T(8,128)S(1)} %shard_map.92.mine), channel_id=1, source_target_pairs={{0,16},{16,0},{1,17},{17,1},{2,18},{18,2},{3,19},{19,3},{4,20},{20... | collective-permute-start | bytes 245768 | tf_op jit(solution)/shard_map/ppermute | solution.py:492

commit v6 on v5

--- a/solution.py
+++ b/solution.py
@@ -103,10 +103,11 @@
     cols_ref[...] = halves(first, last).astype(BF16)
 
 
-def rows_kernel(mine, other, out):
-    n = mine.shape[0]
-    out[0:n, :] = mine[...]
-    out[n:, :] = other[...]
+def rows_kernel(*refs):
+    parts, out = refs[:-1], refs[-1]
+    n = parts[0].shape[0]
+    for i, part in enumerate(parts):
+        out[i * n : (i + 1) * n, :] = part[...]
 
 
 def bits_moved(v, pairs):
@@ -414,19 +415,20 @@
     lax.fori_loop(0, ROWS // n, step, 0)
 
 
-def added_weights(mine, other):
-    total = mine[0:WROWS, :].astype(F32) + other[0:WROWS, :].astype(F32)
-    tail = total[WROWS - SIDE :]
-    return total, tail + pltpu.roll(tail, SIDE - 1, 0)
+def added_weights(parts):
+    terms = [part[0:WROWS, :].astype(F32) for part in parts]
+    while len(terms) > 1:
+        terms = [terms[i] + terms[i + 1] for i in range(0, len(terms), 2)]
+    tail = terms[0][WROWS - SIDE :]
+    return terms[0], tail + pltpu.roll(tail, SIDE - 1, 0)
 
 
 def bias_lanes(shape):
     return jnp.logical_and(jnp.logical_not(low(shape)), (lax.axis_index("region") & 1) == 1)
 
 
-def join_kernel(mine, other, *rest):
-    extra, out = rest[:-1], rest[-1]
-    total, whole = added_weights(mine, other)
+def put_weights(parts, out):
+    total, whole = added_weights(parts)
     out[0 : WROWS - SIDE, :] = total[: WROWS - SIDE].astype(BF16)
     row = iota(whole.shape, 0)
     coarse = whole.astype(BF16).astype(F32)
@@ -436,20 +438,26 @@
         jnp.where(row == 0, coarse, jnp.where(row == 1, fine, 0.0)),
         total[WROWS - SIDE :],
     ).astype(BF16)
-    n = mine.shape[0] - WROWS
-    if n:
-        out[WROWS : WROWS + n, :] = mine[WROWS:, :]
-        out[WROWS + n :, :] = other[WROWS:, :]
+
+
+def first_join_kernel(mine, other, *rest):
+    extra, out = rest[:-1], rest[-1]
+    put_weights((mine, other), out)
     if extra:
         out[WROWS:, :] = extra[0][...]
 
 
-def close_kernel(scale, a, b, c, d, out):
-    left, _ = added_weights(a, b)
-    right, _ = added_weights(c, d)
-    total = left + right
-    tail = total[WROWS - SIDE :]
-    whole = tail + pltpu.roll(tail, SIDE - 1, 0)
+def join_kernel(*refs):
+    parts, out = refs[:-1], refs[-1]
+    put_weights(parts, out)
+    n = parts[0].shape[0] - WROWS
+    for i, part in enumerate(parts):
+        out[WROWS + i * n : WROWS + (i + 1) * n, :] = part[WROWS:, :]
+
+
+def close_kernel(scale, *refs):
+    parts, out = refs[:-1], refs[-1]
+    total, whole = added_weights(parts)
     out[0 : WROWS - SIDE, :] = total[: WROWS - SIDE] * scale
     out[WROWS - SIDE :, :] = jnp.where(bias_lanes(whole.shape), whole, total[WROWS - SIDE :]) * scale
 
@@ -506,25 +514,30 @@
     return ks
 
 
+def rounds_of(owners):
+    count = owners.bit_length() - 1
+    pairs = [(bit, bit + 1) for bit in range(count % 2, count, 2)][::-1]
+    if count % 2:
+        pairs = [tuple(b - 1 for b in p) for p in pairs]
+        return [(count - 1,)] + pairs
+    return pairs
+
+
 def slot_bits(owners):
-    high = range(2, owners.bit_length() - 1)
-    count = len(high)
-    return [(bit, step) for step, bit in enumerate(high)] + [(0, count), (1, count + 1)]
-
-
-def exchange(x, k):
-    return swap(x, "patch", k)
-
-
-def three_partners(x):
-    got = {k: exchange(x, k) for k in (3, 2, 1)}
-    return [got[k] for k in (1, 2, 3)]
+    bits = [bit for bits in rounds_of(owners) for bit in bits]
+    return [(bit, to) for to, bit in enumerate(bits)]
+
+
+def exchange(x, bits):
+    ks = [sum(1 << bits[i] for i in range(len(bits)) if (n >> i) & 1) for n in range(1, 1 << len(bits))]
+    got = {k: swap(x, "patch", k) for k in ks[::-1]}
+    return [got[k] for k in ks]
 
 
 def body(fine_input, fine_weight, fine_bias, cotangent, halo_index):
     owners = lax.axis_size("patch")
     regions = lax.axis_size("region")
-    high = [1 << bit for bit in range(2, owners.bit_length() - 1)]
+    rounds = rounds_of(owners)
     blocks = 1 if regions == 2 else 2
     x = fine_input.reshape(SIDE, SIDE * CHANNELS)
     cot = cotangent.reshape(SIDE, SIDE * CHANNELS)
@@ -539,25 +552,19 @@
     both = ((ROWS, LANES), F32)
     work = dict(flops=2 * ROWS * 768 * 128, moved=3 * 2**20)
 
-    def joined(rows, other):
-        return call(rows_kernel, [((2 * rows.shape[0], LANES), BF16)], rows, other)[0]
-
-    other = exchange(rows, high[0])
+    others = exchange(rows, rounds[0])
     *copies, lines = call(copies_kernel, [pair] * 3 + [((4, 40, LANES), F32)], x, moved=2 * 2**20)
     forward, backward, columns = call(
         weights_kernel,
         [((3, LANES, 2 * LANES), BF16), ((3, 2 * LANES, LANES), BF16), ((3, LANES, LANES), BF16)],
         fine_weight.T,
     )
-    other, copies, lines, forward = lax.optimization_barrier((other, copies, lines, forward))
-    rows = joined(rows, other)
-    other = exchange(rows, high[1])
     signal = call(signal_kernel, [both], *copies, forward, fine_bias.reshape(1, CHANNELS), **work)[0]
-    other, signal, index = lax.optimization_barrier((other, signal, halo_index))
-    rows = joined(rows, other)
-    for k in high[2:]:
-        rows = joined(rows, exchange(rows, k))
-    others = three_partners(rows)
+    others, signal, index = lax.optimization_barrier((others, signal, halo_index))
+    for bits in rounds[1:]:
+        size = ((len(others) + 1) * rows.shape[0], LANES)
+        rows = call(rows_kernel, [(size, BF16)], rows, *others)[0]
+        others = exchange(rows, bits)
     hot, half_mask = call(
         functools.partial(plan_kernel, owners, regions, blocks),
         [((count, (owners + blocks) * SIDE), BF16), ((count, LANES), F32)],
@@ -598,18 +605,19 @@
     for k in [1] + far:
         extra = () if k != ([1] + far)[-1] else (own_rows,)
         size = (WROWS + SIDE * len(extra), LANES)
-        message = call(join_kernel, [(size, BF16)], message, other if k == 1 else swap(message, "region", k), *extra)[0]
+        got = other if k == 1 else swap(message, "region", k)
+        message = call(first_join_kernel, [(size, BF16)], message, got, *extra)[0]
     beside = [grad, g_lines, g_sides]
-    for step, k in enumerate(high):
+    for bits in rounds[:-1]:
         message, beside = lax.optimization_barrier((message, beside))
-        other = exchange(message, k)
-        if step == 1:
+        others = exchange(message, bits)
+        if bits == rounds[-2]:
             beside = call(grad_copies_kernel, [pair] * 3, *beside, moved=2 * 2**20)
-        other, beside = lax.optimization_barrier((other, beside))
-        size = (2 * message.shape[0] - WROWS, LANES)
-        message = call(join_kernel, [(size, BF16)], message, other)[0]
+        others, beside = lax.optimization_barrier((others, beside))
+        size = (WROWS + (len(others) + 1) * (message.shape[0] - WROWS), LANES)
+        message = call(join_kernel, [(size, BF16)], message, *others)[0]
     message, beside = lax.optimization_barrier((message, beside))
-    others = three_partners(message)
+    others = exchange(message, rounds[-1])
     beside = call(inner_kernel, [both], *beside, backward, **work)[0]
     others, beside = lax.optimization_barrier((others, beside))
     scale = 1.0 / math.sqrt(regions * owners * SIDE * SIDE)

time: 40.6 us -> 40.7 us (level)
  local copies, waits for them, and re-layouts: 1.05 us -> 1.7 us
  waiting for transfers between devices: 8.14 us -> 7.65 us
    unnamed x10, local copies, waits for them, and re-layouts: 1.05 us -> 1.7 us
    ppermute x13 -> x15, waiting for transfers between devices: 8.14 us -> 7.65 us  [swap(): return lax.ppermute(x, axis, [(i, i ^ k) for i in range(n)])]
    ppermute x13 -> x15, starting transfers between devices: 17.6 us -> 17.5 us  [swap(): return lax.ppermute(x, axis, [(i, i ^ k) for i in range(n)])]
    pallas_call x18 -> x16, Pallas kernels: 12.9 us -> 12.9 us  [call(): pl.pallas_call(kernel, out_shape=shapes, in_specs=[pl.BlockSpec(memory_sp...]
  transfers between devices with their start and end apart: 13 -> 15, of which waited for: 10 -> 9; matrix products, arithmetic and copies ran while one was open for 0% -> 0% of each run, Pallas kernels for 26% -> 26%
where the time goes in v6:
time: 40.7 us; the launch traced here: 40.5 us
  starting transfers between devices  17.5 us (43%)
  Pallas kernels  12.9 us (32%)
  waiting for transfers between devices  7.65 us (19%)
  local copies, waits for them, and re-layouts  1.7 us (4%)
  between operations  0.8 us (2%)
    ppermute x15, starting transfers between devices, swap(): return lax.ppermute(x, axis, [(i, i ^ k) for i in range(n)])  17.5 us
    pallas_call x16, Pallas kernels, call(): pl.pallas_call(kernel, out_shape=shapes, in_specs=[pl.BlockSpec(memory_sp...  12.9 us
    ppermute x15, waiting for transfers between devices, swap(): return lax.ppermute(x, axis, [(i, i ^ k) for i in range(n)])  7.65 us
    unnamed x10, local copies, waits for them, and re-layouts  1.7 us
  transfers between devices with their start and end apart: 15, of which 9 were waited for; matrix products, arithmetic and copies ran while one was open for 0% of the time, Pallas kernels for 26%

profile of v6, /device:TPU:0, one launch (start us, length us, event | category | flops | bytes accessed | tf_op | source)
XLA Modules:
  0.0 40.5 jit_solution(16328435094561726361)
XLA Ops:
  0.6 1.0 %copy-done.1 = bf16[1,64,4096]{2,1,0:T(8,128)(2,1)S(1)} copy-done((bf16[1,64,4096]{2,1,0:T(8,128)(2,1)S(1)}, bf16[1,64,4096]{2,1,0:T(8,128)(2,1)}, u32[]{:S(2)}) %copy-start.1) | copy-done | bytes 524312
  1.7 5.1 %collective-permute-start.2 = (bf16[64,128]{1,0:T(8,128)(2,1)S(1)}, bf16[64,128]{1,0:T(8,128)(2,1)S(1)}, u32[]{:S(2)}, u32[]{:S(2)}) collective-permute-start(bf16[64,128]{1,0:T(8,128)(2,1)S(1)} %get-tuple-element.61.refs_0_), channel_id=1, source_target_pairs={{0,12},{1,13},{2,14},{3,15},{4,8},{5,9},{6,10},{7,11},{8,4},{9,5},... | collective-permute-start | bytes 49160 | tf_op jit(solution)/shard_map/ppermute | solution.py:500
  6.8 0.6 %collective-permute-start = (bf16[64,128]{1,0:T(8,128)(2,1)S(1)}, bf16[64,128]{1,0:T(8,128)(2,1)S(1)}, u32[]{:S(2)}, u32[]{:S(2)}) collective-permute-start(bf16[64,128]{1,0:T(8,128)(2,1)S(1)} %get-tuple-element.61.refs_0_), channel_id=1, source_target_pairs={{0,4},{1,5},{2,6},{3,7},{4,0},{5,1},{6,2},{7,3},{8,12},{9,13},{10,... | collective-permute-start | bytes 49160 | tf_op jit(solution)/shard_map/ppermute | solution.py:500
  7.5 1.5 %shard_map.77 = (bf16[2112,128]{1,0:T(8,128)(2,1)S(1)}, bf16[2112,128]{1,0:T(8,128)(2,1)S(1)}, bf16[2112,128]{1,0:T(8,128)(2,1)S(1)}, f32[4,40,128]{2,1,0:T(8,128)S(1)}) custom-call(bf16[64,4096]{1,0:T(8,128)(2,1)S(1)} %bitcast.10), custom_call_target="tpu_custom_call" | custom-call | bytes 2097152 | tf_op jit(solution)/shard_map/pallas_call | solution.py:24
  9.1 0.6 %copy-done.4 = f32[64]{0:T(128)S(1)} copy-done((f32[64]{0:T(128)S(1)}, f32[64]{0:T(128)}, u32[]{:S(2)}) %copy-start.4) | copy-done | bytes 280
  9.7 2.2 %shard_map.79.s_ref = f32[2048,128]{1,0:T(8,128)S(1)} custom-call(bf16[2112,128]{1,0:T(8,128)(2,1)S(1)} %get-tuple-element.62.p0, bf16[2112,128]{1,0:T(8,128)(2,1)S(1)} %get-tuple-element.63.p1, bf16[2112,128]{1,0:T(8,128)(2,1)S(1)} %get-tuple-element.64.p2, bf16[3,128,256]{2,1,0:T(8,128)(2,1)S(1)} %get-tuple-element.65.w_ref, f32[1,64]{1,0:T(1,128)S(1)} %bitcast.12), custom_call_target="tpu_custom_call" | custom-call | flops 402653184 | bytes 3145728 | tf_op jit(solution)/shard_map/pallas_call | solution.py:24
  12.0 2.6 %collective-permute-start.5 = (bf16[256,128]{1,0:T(8,128)(2,1)S(1)}, bf16[256,128]{1,0:T(8,128)(2,1)S(1)}, u32[]{:S(2)}, u32[]{:S(2)}) collective-permute-start(bf16[256,128]{1,0:T(8,128)(2,1)S(1)} %shard_map.80.rows_a), channel_id=1, source_target_pairs={{0,3},{1,2},{2,1},{3,0},{4,7},{5,6},{6,5},{7,4},{8,11},{9,10},{10,... | collective-permute-start | bytes 196616 | tf_op jit(solution)/shard_map/ppermute | solution.py:500
  14.6 0.5 %collective-permute-start.4 = (bf16[256,128]{1,0:T(8,128)(2,1)S(1)}, bf16[256,128]{1,0:T(8,128)(2,1)S(1)}, u32[]{:S(2)}, u32[]{:S(2)}) collective-permute-start(bf16[256,128]{1,0:T(8,128)(2,1)S(1)} %shard_map.80.rows_a), channel_id=1, source_target_pairs={{0,2},{1,3},{2,0},{3,1},{4,6},{5,7},{6,4},{7,5},{8,10},{9,11},{10,... | collective-permute-start | bytes 196616 | tf_op jit(solution)/shard_map/ppermute | solution.py:500
  15.6 1.6 %shard_map.83 = (bf16[2048,128]{1,0:T(8,128)(2,1)S(1)}, f32[3,128,256]{2,1,0:T(8,128)S(1)}, f32[8,128]{1,0:T(8,128)S(1)}, f32[64,128]{1,0:T(8,128)S(1)}) custom-call(f32[2048,128]{1,0:T(8,128)S(1)} %shard_map.79.s_ref, bf16[64,4096]{1,0:T(8,128)(2,1)S(1)} %bitcast.7, bf16[2112,128]{1,0:T(8,128)(2,1)S(1)} %get-tuple-element.62.p0, ...), custom_call_target="tpu_custom_call" | custom-call | flops 402653184 | bytes 3145728 | tf_op jit(solution)/shard_map/pallas_call | solution.py:24
  17.8 1.1 %collective-permute-done.4.rows_c = bf16[256,128]{1,0:T(8,128)(2,1)S(1)} collective-permute-done((bf16[256,128]{1,0:T(8,128)(2,1)S(1)}, bf16[256,128]{1,0:T(8,128)(2,1)S(1)}, u32[]{:S(2)}, u32[]{:S(2)}) %collective-permute-start.4) | collective-permute-done | bytes 65568 | tf_op jit(solution)/shard_map/ppermute | solution.py:500
  19.4 1.4 %shard_map.84 = (f32[64,128]{1,0:T(8,128)S(1)}, bf16[128,128]{1,0:T(8,128)(2,1)S(1)}, bf16[160,128]{1,0:T(8,128)(2,1)S(1)}, bf16[224,128]{1,0:T(8,128)(2,1)S(1)}, bf16[64,128]{1,0:T(8,128)(2,1)S(1)}) custom-call(f32[2048,128]{1,0:T(8,128)S(1)} %shard_map.79.s_ref, bf16[64,4096]{1,0:T(8,128)(2,1)S(1)} %bitcast.8, bf16[2112,128]{1,0:T(8,128)(2,1)S(1)} %get-tuple-element.62.p0, ...), custom_call_target="tpu_custom_call" | custom-call | bytes 1048576 | tf_op jit(solution)/shard_map/pallas_call | solution.py:24
  20.9 1.2 %collective-permute-done.7.other.rest_0_ = bf16[224,128]{1,0:T(8,128)(2,1)S(1)} collective-permute-done((bf16[224,128]{1,0:T(8,128)(2,1)S(1)}, bf16[224,128]{1,0:T(8,128)(2,1)S(1)}, u32[]{:S(2)}, u32[]{:S(2)}) %collective-permute-start.7) | collective-permute-done | bytes 57376 | tf_op jit(solution)/shard_map/ppermute | solution.py:500
  22.1 3.7 %collective-permute-start.10 = (bf16[224,128]{1,0:T(8,128)(2,1)S(1)}, bf16[224,128]{1,0:T(8,128)(2,1)S(1)}, u32[]{:S(2)}, u32[]{:S(2)}) collective-permute-start(bf16[224,128]{1,0:T(8,128)(2,1)S(1)} %shard_map.85.refs_0_), channel_id=1, source_target_pairs={{0,12},{1,13},{2,14},{3,15},{4,8},{5,9},{6,10},{7,11},{8,4},{9,5},... | collective-permute-start | bytes 172040 | tf_op jit(solution)/shard_map/ppermute | solution.py:500
  25.9 0.7 %collective-permute-start.8 = (bf16[224,128]{1,0:T(8,128)(2,1)S(1)}, bf16[224,128]{1,0:T(8,128)(2,1)S(1)}, u32[]{:S(2)}, u32[]{:S(2)}) collective-permute-start(bf16[224,128]{1,0:T(8,128)(2,1)S(1)} %shard_map.85.refs_0_), channel_id=1, source_target_pairs={{0,4},{1,5},{2,6},{3,7},{4,0},{5,1},{6,2},{7,3},{8,12},{9,13},{10,... | collective-permute-start | bytes 172040 | tf_op jit(solution)/shard_map/ppermute | solution.py:500
  26.6 1.5 %shard_map.86 = (bf16[2112,128]{1,0:T(8,128)(2,1)S(1)}, bf16[2112,128]{1,0:T(8,128)(2,1)S(1)}, bf16[2112,128]{1,0:T(8,128)(2,1)S(1)}) custom-call(bf16[2048,128]{1,0:T(8,128)(2,1)S(1)} %get-tuple-element.96.g_ref, f32[64,128]{1,0:T(8,128)S(1)} %get-tuple-element.97.g_lines, bf16[128,128]{1,0:T(8,128)(2,1)S(1)} %get-tuple-element.98.g_sides), custom_call_target="tpu_custom_call" | custom-call | bytes 2097152 | tf_op jit(solution)/shard_map/pallas_call | solution.py:24
  28.1 0.5 %collective-permute-done.10.refs_3_ = bf16[224,128]{1,0:T(8,128)(2,1)S(1)} collective-permute-done((bf16[224,128]{1,0:T(8,128)(2,1)S(1)}, bf16[224,128]{1,0:T(8,128)(2,1)S(1)}, u32[]{:S(2)}, u32[]{:S(2)}) %collective-permute-start.10) | collective-permute-done | bytes 57376 | tf_op jit(solution)/shard_map/ppermute | solution.py:500
  28.6 2.4 %collective-permute-done.9.refs_2_ = bf16[224,128]{1,0:T(8,128)(2,1)S(1)} collective-permute-done((bf16[224,128]{1,0:T(8,128)(2,1)S(1)}, bf16[224,128]{1,0:T(8,128)(2,1)S(1)}, u32[]{:S(2)}, u32[]{:S(2)}) %collective-permute-start.9) | collective-permute-done | bytes 57376 | tf_op jit(solution)/shard_map/ppermute | solution.py:500
  31.3 1.6 %collective-permute-start.13 = (bf16[416,128]{1,0:T(8,128)(2,1)S(1)}, bf16[416,128]{1,0:T(8,128)(2,1)S(1)}, u32[]{:S(2)}, u32[]{:S(2)}) collective-permute-start(bf16[416,128]{1,0:T(8,128)(2,1)S(1)} %shard_map.87.row_a.refs_0_), channel_id=1, source_target_pairs={{0,3},{1,2},{2,1},{3,0},{4,7},{5,6},{6,5},{7,4},{8,11},{9,10},{10,... | collective-permute-start | bytes 319496 | tf_op jit(solution)/shard_map/ppermute | solution.py:500
  33.4 1.5 %collective-permute-start.11 = (bf16[416,128]{1,0:T(8,128)(2,1)S(1)}, bf16[416,128]{1,0:T(8,128)(2,1)S(1)}, u32[]{:S(2)}, u32[]{:S(2)}) collective-permute-start(bf16[416,128]{1,0:T(8,128)(2,1)S(1)} %shard_map.87.row_a.refs_0_), channel_id=1, source_target_pairs={{0,1},{1,0},{2,3},{3,2},{4,5},{5,4},{6,7},{7,6},{8,9},{9,8},{10,11... | collective-permute-start | bytes 319496 | tf_op jit(solution)/shard_map/ppermute | solution.py:500
  34.9 2.0 %shard_map.88.inner = f32[2048,128]{1,0:T(8,128)S(1)} custom-call(bf16[2112,128]{1,0:T(8,128)(2,1)S(1)} %get-tuple-element.109.p0, bf16[2112,128]{1,0:T(8,128)(2,1)S(1)} %get-tuple-element.110.p1, bf16[2112,128]{1,0:T(8,128)(2,1)S(1)} %get-tuple-element.111.p2, bf16[3,256,128]{2,1,0:T(8,128)(2,1)S(1)} %get-tuple-element.87.wb_ref), custom_call_target="tpu_custom_call" | custom-call | flops 402653184 | bytes 3145728 | tf_op jit(solution)/shard_map/pallas_call | solution.py:24
  36.9 0.6 %collective-permute-done.13.row_d.refs_3_ = bf16[416,128]{1,0:T(8,128)(2,1)S(1)} collective-permute-done((bf16[416,128]{1,0:T(8,128)(2,1)S(1)}, bf16[416,128]{1,0:T(8,128)(2,1)S(1)}, u32[]{:S(2)}, u32[]{:S(2)}) %collective-permute-start.13) | collective-permute-done | bytes 106528 | tf_op jit(solution)/shard_map/ppermute | solution.py:500
  37.5 0.9 %collective-permute-done.12.row_c.refs_2_ = bf16[416,128]{1,0:T(8,128)(2,1)S(1)} collective-permute-done((bf16[416,128]{1,0:T(8,128)(2,1)S(1)}, bf16[416,128]{1,0:T(8,128)(2,1)S(1)}, u32[]{:S(2)}, u32[]{:S(2)}) %collective-permute-start.12) | collective-permute-done | bytes 106528 | tf_op jit(solution)/shard_map/ppermute | solution.py:500
  38.5 1.2 %shard_map.89 = bf16[64,4096]{1,0:T(8,128)(2,1)} custom-call(bf16[416,128]{1,0:T(8,128)(2,1)S(1)} %shard_map.87.row_a.refs_0_, bf16[416,128]{1,0:T(8,128)(2,1)S(1)} %collective-permute-done.11.row_b.refs_1_, bf16[416,128]{1,0:T(8,128)(2,1)S(1)} %collective-permute-done.12.row_c.refs_2_, bf16[416,128]{1,0:T(8,128)(2,1)S(1)} %collective-permute-done.13.row_d.refs_3_, ...), custom_call_target="tpu_custom_call" | custom-call | bytes 2097152 | tf_op jit(solution)/shard_map/pallas_call | solution.py:24
  39.8 0.7 %shard_map.91 = (f32[64,576]{1,0:T(8,128)}, f32[1,64]{1,0:T(1,128)}) custom-call(f32[160,128]{1,0:T(8,128)S(1)} %shard_map.90.mine, f32[160,128]{1,0:T(8,128)S(1)} %collective-permute-done.14.other), custom_call_target="tpu_custom_call" | custom-call | tf_op jit(solution)/shard_map/pallas_call | solution.py:24
  (32 shorter events, 2.8 us)
Async XLA Ops:
  0.6 1.0 %copy-start.1 = (bf16[1,64,4096]{2,1,0:T(8,128)(2,1)S(1)}, bf16[1,64,4096]{2,1,0:T(8,128)(2,1)}, u32[]{:S(2)}) copy-start(bf16[1,64,4096]{2,1,0:T(8,128)(2,1)} %param.5) | copy-start | bytes 1572868
  1.7 7.3 %copy-start.3 = (bf16[576,64]{0,1:T(8,128)(2,1)S(1)}, bf16[576,64]{0,1:T(8,128)(2,1)}, u32[]{:S(2)}) copy-start(bf16[576,64]{0,1:T(8,128)(2,1)} %param.6) | copy-start | bytes 221188
  1.7 10.3 %collective-permute-start.2 = (bf16[64,128]{1,0:T(8,128)(2,1)S(1)}, bf16[64,128]{1,0:T(8,128)(2,1)S(1)}, u32[]{:S(2)}, u32[]{:S(2)}) collective-permute-start(bf16[64,128]{1,0:T(8,128)(2,1)S(1)} %get-tuple-element.61.refs_0_), channel_id=1, source_target_pairs={{0,12},{1,13},{2,14},{3,15},{4,8},{5,9},{6,10},{7,11},{8,4},{9,5},... | collective-permute-start | bytes 49160 | tf_op jit(solution)/shard_map/ppermute | solution.py:500
  6.8 5.1 %collective-permute-start.1 = (bf16[64,128]{1,0:T(8,128)(2,1)S(1)}, bf16[64,128]{1,0:T(8,128)(2,1)S(1)}, u32[]{:S(2)}, u32[]{:S(2)}) collective-permute-start(bf16[64,128]{1,0:T(8,128)(2,1)S(1)} %get-tuple-element.61.refs_0_), channel_id=1, source_target_pairs={{0,8},{1,9},{2,10},{3,11},{4,12},{5,13},{6,14},{7,15},{8,0},{9,1},... | collective-permute-start | bytes 49160 | tf_op jit(solution)/shard_map/ppermute | solution.py:500
  6.8 5.2 %collective-permute-start = (bf16[64,128]{1,0:T(8,128)(2,1)S(1)}, bf16[64,128]{1,0:T(8,128)(2,1)S(1)}, u32[]{:S(2)}, u32[]{:S(2)}) collective-permute-start(bf16[64,128]{1,0:T(8,128)(2,1)S(1)} %get-tuple-element.61.refs_0_), channel_id=1, source_target_pairs={{0,4},{1,5},{2,6},{3,7},{4,0},{5,1},{6,2},{7,3},{8,12},{9,13},{10,... | collective-permute-start | bytes 49160 | tf_op jit(solution)/shard_map/ppermute | solution.py:500
  9.1 0.7 %copy-start.4 = (f32[64]{0:T(128)S(1)}, f32[64]{0:T(128)}, u32[]{:S(2)}) copy-start(f32[64]{0:T(128)} %param.7) | copy-start | bytes 772
  9.7 5.8 %copy-start = (bf16[1,64,4096]{2,1,0:T(8,128)(2,1)S(1)}, bf16[1,64,4096]{2,1,0:T(8,128)(2,1)}, u32[]{:S(2)}) copy-start(bf16[1,64,4096]{2,1,0:T(8,128)(2,1)} %param.8) | copy-start | bytes 1572868
  12.0 5.8 %collective-permute-start.5 = (bf16[256,128]{1,0:T(8,128)(2,1)S(1)}, bf16[256,128]{1,0:T(8,128)(2,1)S(1)}, u32[]{:S(2)}, u32[]{:S(2)}) collective-permute-start(bf16[256,128]{1,0:T(8,128)(2,1)S(1)} %shard_map.80.rows_a), channel_id=1, source_target_pairs={{0,3},{1,2},{2,1},{3,0},{4,7},{5,6},{6,5},{7,4},{8,11},{9,10},{10,... | collective-permute-start | bytes 196616 | tf_op jit(solution)/shard_map/ppermute | solution.py:500
  14.6 4.3 %collective-permute-start.4 = (bf16[256,128]{1,0:T(8,128)(2,1)S(1)}, bf16[256,128]{1,0:T(8,128)(2,1)S(1)}, u32[]{:S(2)}, u32[]{:S(2)}) collective-permute-start(bf16[256,128]{1,0:T(8,128)(2,1)S(1)} %shard_map.80.rows_a), channel_id=1, source_target_pairs={{0,2},{1,3},{2,0},{3,1},{4,6},{5,7},{6,4},{7,5},{8,10},{9,11},{10,... | collective-permute-start | bytes 196616 | tf_op jit(solution)/shard_map/ppermute | solution.py:500
  15.1 4.3 %collective-permute-start.3 = (bf16[256,128]{1,0:T(8,128)(2,1)S(1)}, bf16[256,128]{1,0:T(8,128)(2,1)S(1)}, u32[]{:S(2)}, u32[]{:S(2)}) collective-permute-start(bf16[256,128]{1,0:T(8,128)(2,1)S(1)} %shard_map.80.rows_a), channel_id=1, source_target_pairs={{0,1},{1,0},{2,3},{3,2},{4,5},{5,4},{6,7},{7,6},{8,9},{9,8},{10,11... | collective-permute-start | bytes 196616 | tf_op jit(solution)/shard_map/ppermute | solution.py:500
  15.6 3.8 %collective-permute-start.6 = (bf16[64,128]{1,0:T(8,128)(2,1)S(1)}, bf16[64,128]{1,0:T(8,128)(2,1)S(1)}, u32[]{:S(2)}, u32[]{:S(2)}) collective-permute-start(bf16[64,128]{1,0:T(8,128)(2,1)S(1)} %get-tuple-element.84), channel_id=1, source_target_pairs={{0,16},{16,0},{1,17},{17,1},{2,18},{18,2},{3,19},{19,3},{4,20},{20... | collective-permute-start | bytes 49160 | tf_op jit(solution)/shard_map/ppermute | solution.py:500
  15.6 1.7 %copy-start.2 = (s32[16,260]{1,0:T(8,128)S(1)}, s32[16,260]{1,0:T(8,128)}, u32[]{:S(2)}) copy-start(s32[16,260]{1,0:T(8,128)} %index_ref.1) | copy-start | bytes 49924
  20.8 1.3 %collective-permute-start.7 = (bf16[224,128]{1,0:T(8,128)(2,1)S(1)}, bf16[224,128]{1,0:T(8,128)(2,1)S(1)}, u32[]{:S(2)}, u32[]{:S(2)}) collective-permute-start(bf16[224,128]{1,0:T(8,128)(2,1)S(1)} %get-tuple-element.90), channel_id=1, source_target_pairs={{0,16},{16,0},{1,17},{17,1},{2,18},{18,2},{3,19},{19,3},{4,20},{20... | collective-permute-start | bytes 172040 | tf_op jit(solution)/shard_map/ppermute | solution.py:500
  22.1 6.5 %collective-permute-start.10 = (bf16[224,128]{1,0:T(8,128)(2,1)S(1)}, bf16[224,128]{1,0:T(8,128)(2,1)S(1)}, u32[]{:S(2)}, u32[]{:S(2)}) collective-permute-start(bf16[224,128]{1,0:T(8,128)(2,1)S(1)} %shard_map.85.refs_0_), channel_id=1, source_target_pairs={{0,12},{1,13},{2,14},{3,15},{4,8},{5,9},{6,10},{7,11},{8,4},{9,5},... | collective-permute-start | bytes 172040 | tf_op jit(solution)/shard_map/ppermute | solution.py:500
  25.9 5.1 %collective-permute-start.9 = (bf16[224,128]{1,0:T(8,128)(2,1)S(1)}, bf16[224,128]{1,0:T(8,128)(2,1)S(1)}, u32[]{:S(2)}, u32[]{:S(2)}) collective-permute-start(bf16[224,128]{1,0:T(8,128)(2,1)S(1)} %shard_map.85.refs_0_), channel_id=1, source_target_pairs={{0,8},{1,9},{2,10},{3,11},{4,12},{5,13},{6,14},{7,15},{8,0},{9,1},... | collective-permute-start | bytes 172040 | tf_op jit(solution)/shard_map/ppermute | solution.py:500
  25.9 5.4 %collective-permute-start.8 = (bf16[224,128]{1,0:T(8,128)(2,1)S(1)}, bf16[224,128]{1,0:T(8,128)(2,1)S(1)}, u32[]{:S(2)}, u32[]{:S(2)}) collective-permute-start(bf16[224,128]{1,0:T(8,128)(2,1)S(1)} %shard_map.85.refs_0_), channel_id=1, source_target_pairs={{0,4},{1,5},{2,6},{3,7},{4,0},{5,1},{6,2},{7,3},{8,12},{9,13},{10,... | collective-permute-start | bytes 172040 | tf_op jit(solution)/shard_map/ppermute | solution.py:500
  31.3 6.2 %collective-permute-start.13 = (bf16[416,128]{1,0:T(8,128)(2,1)S(1)}, bf16[416,128]{1,0:T(8,128)(2,1)S(1)}, u32[]{:S(2)}, u32[]{:S(2)}) collective-permute-start(bf16[416,128]{1,0:T(8,128)(2,1)S(1)} %shard_map.87.row_a.refs_0_), channel_id=1, source_target_pairs={{0,3},{1,2},{2,1},{3,0},{4,7},{5,6},{6,5},{7,4},{8,11},{9,10},{10,... | collective-permute-start | bytes 319496 | tf_op jit(solution)/shard_map/ppermute | solution.py:500
  32.9 5.5 %collective-permute-start.12 = (bf16[416,128]{1,0:T(8,128)(2,1)S(1)}, bf16[416,128]{1,0:T(8,128)(2,1)S(1)}, u32[]{:S(2)}, u32[]{:S(2)}) collective-permute-start(bf16[416,128]{1,0:T(8,128)(2,1)S(1)} %shard_map.87.row_a.refs_0_), channel_id=1, source_target_pairs={{0,2},{1,3},{2,0},{3,1},{4,6},{5,7},{6,4},{7,5},{8,10},{9,11},{10,... | collective-permute-start | bytes 319496 | tf_op jit(solution)/shard_map/ppermute | solution.py:500
  33.4 5.1 %collective-permute-start.11 = (bf16[416,128]{1,0:T(8,128)(2,1)S(1)}, bf16[416,128]{1,0:T(8,128)(2,1)S(1)}, u32[]{:S(2)}, u32[]{:S(2)}) collective-permute-start(bf16[416,128]{1,0:T(8,128)(2,1)S(1)} %shard_map.87.row_a.refs_0_), channel_id=1, source_target_pairs={{0,1},{1,0},{2,3},{3,2},{4,5},{5,4},{6,7},{7,6},{8,9},{9,8},{10,11... | collective-permute-start | bytes 319496 | tf_op jit(solution)/shard_map/ppermute | solution.py:500
  38.5 1.3 %collective-permute-start.14 = (f32[160,128]{1,0:T(8,128)S(1)}, f32[160,128]{1,0:T(8,128)S(1)}, u32[]{:S(2)}, u32[]{:S(2)}) collective-permute-start(f32[160,128]{1,0:T(8,128)S(1)} %shard_map.90.mine), channel_id=1, source_target_pairs={{0,16},{16,0},{1,17},{17,1},{2,18},{18,2},{3,19},{19,3},{4,20},{20... | collective-permute-start | bytes 245768 | tf_op jit(solution)/shard_map/ppermute | solution.py:500

commit v7 on v6

--- a/solution.py
+++ b/solution.py
@@ -18,13 +18,13 @@
 BF16 = jnp.bfloat16
 
 
-def call(kernel, outs, *args, scratch=(), flops=0, moved=0, space=pltpu.VMEM, limit=48):
+def call(kernel, outs, *args, scratch=(), flops=0, moved=0, limit=48):
     whole = pl.BlockSpec(memory_space=pltpu.VMEM)
     shapes = [jax.ShapeDtypeStruct(s, d) for s, d in outs]
     return pl.pallas_call(
         kernel,
         out_shape=shapes,
-        in_specs=[pl.BlockSpec(memory_space=space)] * len(args),
+        in_specs=[whole] * len(args),
         out_specs=[whole] * len(outs),
         scratch_shapes=list(scratch),
         compiler_params=pltpu.CompilerParams(vmem_limit_bytes=limit * 2**20),
@@ -79,14 +79,14 @@
         return now
 
     zero = jnp.zeros((SIDE, LANES), F32)
-    last = lax.fori_loop(0, PAIRS, step, zero, unroll=2)
+    last = lax.fori_loop(0, PAIRS, step, zero, unroll=4)
     put(PAIRS, last, zero)
 
 
-def product(p0, p1, p2, w_ref, start, n, dims):
+def product(p0, p1, p2, w_ref, dims):
     total = None
     for a, p in enumerate((p0, p1, p2)):
-        window = jnp.concatenate([p[pl.ds(start, n), :], p[pl.ds(start + SIDE, n), :]], axis=1)
+        window = jnp.concatenate([p[0:ROWS, :], p[SIDE : ROWS + SIDE, :]], axis=1)
         term = dot(window, w_ref[a], dims)
         total = term if total is None else total + term
     return total
@@ -192,16 +192,8 @@
     shifted_copies(lambda q: x_ref[:, tile(q)].astype(F32), p0, p1, p2, lines)
 
 
-def signal_kernel(p0, p1, p2, w_ref, bias_ref, s_ref):
-    n = 4 * SIDE
-    bias = jnp.concatenate([bias_ref[...], bias_ref[...]], axis=1)
-
-    def step(c, carry):
-        start = pl.multiple_of(c * n, n)
-        s_ref[pl.ds(start, n), :] = product(p0, p1, p2, w_ref, start, n, NT) + bias
-        return carry
-
-    lax.fori_loop(0, ROWS // n, step, 0)
+def signal_kernel(p0, p1, p2, w_ref, s_ref):
+    s_ref[...] = product(p0, p1, p2, w_ref, NT)
 
 
 def slope_times(signal, upstream):
@@ -213,13 +205,14 @@
     return jnp.where(low(even.shape), even, odd)
 
 
-def inside_kernel(s_ref, cot_ref, p0, p1, p2, g_ref, terms_ref, bias_ref, cot_lines):
+def inside_kernel(s_ref, offset, cot_ref, p0, p1, p2, g_ref, terms_ref, bias_ref, cot_lines):
     row = iota((SIDE, LANES), 0)
     border = jnp.logical_or(row == 0, row == SIDE - 1)
+    added = jnp.concatenate([offset[...], offset[...]], axis=1)
 
     def step(q, bias):
         upstream = cot_ref[:, tile(q)].astype(F32)
-        g = jnp.where(border, 0.0, slope_times(s_ref[block(q), :], upstream)).astype(BF16)
+        g = jnp.where(border, 0.0, slope_times(s_ref[block(q), :] + added, upstream)).astype(BF16)
         g_ref[block(q), :] = g
         cot_lines[pl.ds(q, 1), :] = upstream[0:1]
         cot_lines[pl.ds(PAIRS + q, 1), :] = upstream[SIDE - 1 :]
@@ -237,10 +230,11 @@
 
 
 def middle_kernel(
-    s_ref, cot_ref, p0, p1, p2, lines, terms_ref, bias_ref, cot_lines, rows_a, rows_b, rows_c, rows_d, cols_ref,
+    s_ref, offset, cot_ref, p0, p1, p2, lines, terms_ref, bias_ref, cot_lines, rows_a, rows_b, rows_c, rows_d, cols_ref,
     hot_ref, half_ref, w_ref, wb_ref, wc_ref,
     g_lines, g_sides, keep_ref, send_ref, own_ref, cell_scr, gt, gb, gc, own_scr, msg,
 ):
+    added = jnp.concatenate([offset[...], offset[...]], axis=1)
     n = rows_a.shape[0]
     many = 4 * n
     cells = dot(hot_ref[:, many:], cols_ref[...])
@@ -278,7 +272,7 @@
     bottom_signal = dot(bottom.astype(BF16), w_ref[2], NT)
 
     def side_grad(q, columns, lanes):
-        signal = s_ref[q * SIDE : (q + 1) * SIDE, :]
+        signal = s_ref[q * SIDE : (q + 1) * SIDE, :] + added
         for a in range(3):
             signal = signal + dot(columns[a].astype(BF16), w_ref[a, :, lanes], NT)
         signal = signal + jnp.where(row == 0, top_signal[q : q + 1], 0.0)
@@ -293,7 +287,7 @@
     ends = jnp.logical_or(pair == 0, pair == end)
 
     def line_grad(first_row, halo_signal):
-        signal = s_ref[pl.ds(first_row, PAIRS, stride=SIDE), :] + halo_signal
+        signal = s_ref[pl.ds(first_row, PAIRS, stride=SIDE), :] + added + halo_signal
         upstream = cot_lines[0:PAIRS, :] if first_row == 0 else cot_lines[PAIRS:, :]
         g = jnp.where(ends, 0.0, slope_times(signal, upstream)).astype(BF16).astype(F32)
         r = slice(first_row, first_row + 1)
@@ -405,14 +399,7 @@
 
 
 def inner_kernel(p0, p1, p2, wb_ref, out_ref):
-    n = 4 * SIDE
-
-    def step(c, carry):
-        start = pl.multiple_of(c * n, n)
-        out_ref[pl.ds(start, n), :] = product(p0, p1, p2, wb_ref, start, n, ((1,), (0,)))
-        return carry
-
-    lax.fori_loop(0, ROWS // n, step, 0)
+    out_ref[...] = product(p0, p1, p2, wb_ref, ((1,), (0,)))
 
 
 def added_weights(parts):
@@ -559,8 +546,11 @@
         [((3, LANES, 2 * LANES), BF16), ((3, 2 * LANES, LANES), BF16), ((3, LANES, LANES), BF16)],
         fine_weight.T,
     )
-    signal = call(signal_kernel, [both], *copies, forward, fine_bias.reshape(1, CHANNELS), **work)[0]
-    others, signal, index = lax.optimization_barrier((others, signal, halo_index))
+    signal = call(
+        signal_kernel, [both], *copies, forward, **work,
+    )[0]
+    offset = fine_bias.reshape(1, CHANNELS)
+    others, signal, index, offset = lax.optimization_barrier((others, signal, halo_index, offset))
     for bits in rounds[1:]:
         size = ((len(others) + 1) * rows.shape[0], LANES)
         rows = call(rows_kernel, [(size, BF16)], rows, *others)[0]
@@ -570,13 +560,12 @@
         [((count, (owners + blocks) * SIDE), BF16), ((count, LANES), F32)],
         index, scratch=[pltpu.VMEM((8, 384), F32)],
     )
-    pick = call(functools.partial(pick_kernel, owners), [((4 * SIDE, owners * SIDE), BF16)], index)[0]
     inside = call(
         inside_kernel,
         [((ROWS, LANES), BF16), ((3, LANES, 2 * LANES), F32), ((8, LANES), F32), ((SIDE, LANES), F32)],
-        signal, cot, *copies, **work,
-    )
-    others, hot, half_mask, pick, inside = lax.optimization_barrier((others, hot, half_mask, pick, inside))
+        signal, offset, cot, *copies, **work,
+    )
+    others, hot, half_mask, inside = lax.optimization_barrier((others, hot, half_mask, inside))
     grad, *inside = inside
 
     line = pltpu.VMEM((40, LANES), F32)
@@ -586,7 +575,7 @@
             ((SIDE, LANES), F32), ((2 * SIDE, LANES), BF16),
             ((WROWS, LANES), BF16), ((WROWS + blocks * SIDE, LANES), BF16), ((SIDE, LANES), BF16),
         ],
-        signal, cot, *copies, lines, *inside, rows, *others, cols, hot, half_mask, forward, backward, columns,
+        signal, offset, cot, *copies, lines, *inside, rows, *others, cols, hot, half_mask, forward, backward, columns,
         scratch=[
             pltpu.VMEM((count, LANES), F32), line, line,
             pltpu.VMEM((96, LANES), F32), pltpu.VMEM((SIDE, LANES), F32), pltpu.VMEM((2 * WROWS, LANES), F32),
@@ -609,11 +598,12 @@
         message = call(first_join_kernel, [(size, BF16)], message, got, *extra)[0]
     beside = [grad, g_lines, g_sides]
     for bits in rounds[:-1]:
-        message, beside = lax.optimization_barrier((message, beside))
+        message, beside, index = lax.optimization_barrier((message, beside, index))
         others = exchange(message, bits)
         if bits == rounds[-2]:
+            pick = call(functools.partial(pick_kernel, owners), [((4 * SIDE, owners * SIDE), BF16)], index)[0]
             beside = call(grad_copies_kernel, [pair] * 3, *beside, moved=2 * 2**20)
-        others, beside = lax.optimization_barrier((others, beside))
+            others, beside, pick = lax.optimization_barrier((others, beside, pick))
         size = (WROWS + (len(others) + 1) * (message.shape[0] - WROWS), LANES)
         message = call(join_kernel, [(size, BF16)], message, *others)[0]
     message, beside = lax.optimization_barrier((message, beside))

time: 40.7 us -> 40.3 us (level)
  Pallas kernels: 12.9 us -> 9.57 us
  waiting for transfers between devices: 7.65 us -> 10.6 us
    pallas_call x16, Pallas kernels: 12.9 us -> 9.57 us  [call(): pl.pallas_call(kernel, out_shape=shapes, in_specs=[whole] * len(args), ou...]
    ppermute x15, waiting for transfers between devices: 7.65 us -> 10.6 us  [swap(): return lax.ppermute(x, axis, [(i, i ^ k) for i in range(n)])]
  transfers between devices with their start and end apart: 15 -> 15, of which waited for: 9 -> 10; matrix products, arithmetic and copies ran while one was open for 0% -> 0% of each run, Pallas kernels for 26% -> 18%
where the time goes in v7:
time: 40.3 us; the launch traced here: 40.1 us
  starting transfers between devices  17.5 us (43%)
  waiting for transfers between devices  10.6 us (26%)
  Pallas kernels  9.57 us (24%)
  local copies, waits for them, and re-layouts  1.7 us (4%)
  between operations  0.78 us (2%)
    ppermute x15, starting transfers between devices, swap(): return lax.ppermute(x, axis, [(i, i ^ k) for i in range(n)])  17.5 us
    ppermute x15, waiting for transfers between devices, swap(): return lax.ppermute(x, axis, [(i, i ^ k) for i in range(n)])  10.6 us
    pallas_call x16, Pallas kernels, call(): pl.pallas_call(kernel, out_shape=shapes, in_specs=[whole] * len(args), ou...  9.57 us
    unnamed x10, local copies, waits for them, and re-layouts  1.7 us
  transfers between devices with their start and end apart: 15, of which 10 were waited for; matrix products, arithmetic and copies ran while one was open for 0% of the time, Pallas kernels for 18%

profile of v7, /device:TPU:0, one launch (start us, length us, event | category | flops | bytes accessed | tf_op | source)
XLA Modules:
  0.0 40.1 jit_solution(12405553818539873476)
XLA Ops:
  0.6 1.0 %copy-done = bf16[1,64,4096]{2,1,0:T(8,128)(2,1)S(1)} copy-done((bf16[1,64,4096]{2,1,0:T(8,128)(2,1)S(1)}, bf16[1,64,4096]{2,1,0:T(8,128)(2,1)}, u32[]{:S(2)}) %copy-start) | copy-done | bytes 524312
  1.7 5.1 %collective-permute-start.2 = (bf16[64,128]{1,0:T(8,128)(2,1)S(1)}, bf16[64,128]{1,0:T(8,128)(2,1)S(1)}, u32[]{:S(2)}, u32[]{:S(2)}) collective-permute-start(bf16[64,128]{1,0:T(8,128)(2,1)S(1)} %get-tuple-element.63.refs_0_), channel_id=1, source_target_pairs={{0,12},{1,13},{2,14},{3,15},{4,8},{5,9},{6,10},{7,11},{8,4},{9,5},... | collective-permute-start | bytes 49160 | tf_op jit(solution)/shard_map/ppermute | solution.py:487
  6.8 0.6 %collective-permute-start = (bf16[64,128]{1,0:T(8,128)(2,1)S(1)}, bf16[64,128]{1,0:T(8,128)(2,1)S(1)}, u32[]{:S(2)}, u32[]{:S(2)}) collective-permute-start(bf16[64,128]{1,0:T(8,128)(2,1)S(1)} %get-tuple-element.63.refs_0_), channel_id=1, source_target_pairs={{0,4},{1,5},{2,6},{3,7},{4,0},{5,1},{6,2},{7,3},{8,12},{9,13},{10,... | collective-permute-start | bytes 49160 | tf_op jit(solution)/shard_map/ppermute | solution.py:487
  7.5 0.9 %shard_map.77 = (bf16[2112,128]{1,0:T(8,128)(2,1)S(1)}, bf16[2112,128]{1,0:T(8,128)(2,1)S(1)}, bf16[2112,128]{1,0:T(8,128)(2,1)S(1)}, f32[4,40,128]{2,1,0:T(8,128)S(1)}) custom-call(bf16[64,4096]{1,0:T(8,128)(2,1)S(1)} %bitcast.8), custom_call_target="tpu_custom_call" | custom-call | bytes 2097152 | tf_op jit(solution)/shard_map/pallas_call | solution.py:24
  8.5 1.0 %shard_map.79.s_ref = f32[2048,128]{1,0:T(8,128)S(1)} custom-call(bf16[2112,128]{1,0:T(8,128)(2,1)S(1)} %get-tuple-element.64.p0, bf16[2112,128]{1,0:T(8,128)(2,1)S(1)} %get-tuple-element.65.p1, bf16[2112,128]{1,0:T(8,128)(2,1)S(1)} %get-tuple-element.66.p2, bf16[3,128,256]{2,1,0:T(8,128)(2,1)S(1)} %get-tuple-element.67.w_ref), custom_call_target="tpu_custom_call" | custom-call | flops 402653184 | bytes 3145728 | tf_op jit(solution)/shard_map/pallas_call | solution.py:24
  9.5 2.0 %collective-permute-done.1.refs_2_ = bf16[64,128]{1,0:T(8,128)(2,1)S(1)} collective-permute-done((bf16[64,128]{1,0:T(8,128)(2,1)S(1)}, bf16[64,128]{1,0:T(8,128)(2,1)S(1)}, u32[]{:S(2)}, u32[]{:S(2)}) %collective-permute-start.1) | collective-permute-done | bytes 16416 | tf_op jit(solution)/shard_map/ppermute | solution.py:487
  11.5 2.5 %collective-permute-start.5 = (bf16[256,128]{1,0:T(8,128)(2,1)S(1)}, bf16[256,128]{1,0:T(8,128)(2,1)S(1)}, u32[]{:S(2)}, u32[]{:S(2)}) collective-permute-start(bf16[256,128]{1,0:T(8,128)(2,1)S(1)} %shard_map.80.rows_a), channel_id=1, source_target_pairs={{0,3},{1,2},{2,1},{3,0},{4,7},{5,6},{6,5},{7,4},{8,11},{9,10},{10,... | collective-permute-start | bytes 196616 | tf_op jit(solution)/shard_map/ppermute | solution.py:487
  14.5 0.5 %collective-permute-start.3 = (bf16[256,128]{1,0:T(8,128)(2,1)S(1)}, bf16[256,128]{1,0:T(8,128)(2,1)S(1)}, u32[]{:S(2)}, u32[]{:S(2)}) collective-permute-start(bf16[256,128]{1,0:T(8,128)(2,1)S(1)} %shard_map.80.rows_a), channel_id=1, source_target_pairs={{0,1},{1,0},{2,3},{3,2},{4,5},{5,4},{6,7},{7,6},{8,9},{9,8},{10,11... | collective-permute-start | bytes 196616 | tf_op jit(solution)/shard_map/ppermute | solution.py:487
  15.0 0.6 %copy-done.4 = f32[64]{0:T(128)S(1)} copy-done((f32[64]{0:T(128)S(1)}, f32[64]{0:T(128)}, u32[]{:S(2)}) %copy-start.4) | copy-done | bytes 280
  15.7 1.8 %shard_map.82 = (bf16[2048,128]{1,0:T(8,128)(2,1)S(1)}, f32[3,128,256]{2,1,0:T(8,128)S(1)}, f32[8,128]{1,0:T(8,128)S(1)}, f32[64,128]{1,0:T(8,128)S(1)}) custom-call(f32[2048,128]{1,0:T(8,128)S(1)} %shard_map.79.s_ref, f32[1,64]{1,0:T(1,128)S(1)} %bitcast.12, bf16[64,4096]{1,0:T(8,128)(2,1)S(1)} %bitcast.9, bf16[2112,128]{1,0:T(8,128)(2,1)S(1)} %get-tuple-element.64.p0, ...), custom_call_target="tpu_custom_call" | custom-call | flops 402653184 | bytes 3145728 | tf_op jit(solution)/shard_map/pallas_call | solution.py:24
  18.8 1.4 %shard_map.83 = (f32[64,128]{1,0:T(8,128)S(1)}, bf16[128,128]{1,0:T(8,128)(2,1)S(1)}, bf16[160,128]{1,0:T(8,128)(2,1)S(1)}, bf16[224,128]{1,0:T(8,128)(2,1)S(1)}, bf16[64,128]{1,0:T(8,128)(2,1)S(1)}) custom-call(f32[2048,128]{1,0:T(8,128)S(1)} %shard_map.79.s_ref, f32[1,64]{1,0:T(1,128)S(1)} %bitcast.13, bf16[64,4096]{1,0:T(8,128)(2,1)S(1)} %bitcast.10, ...), custom_call_target="tpu_custom_call" | custom-call | bytes 1048576 | tf_op jit(solution)/shard_map/pallas_call | solution.py:24
  20.3 1.2 %collective-permute-done.7.other.rest_0_ = bf16[224,128]{1,0:T(8,128)(2,1)S(1)} collective-permute-done((bf16[224,128]{1,0:T(8,128)(2,1)S(1)}, bf16[224,128]{1,0:T(8,128)(2,1)S(1)}, u32[]{:S(2)}, u32[]{:S(2)}) %collective-permute-start.7) | collective-permute-done | bytes 57376 | tf_op jit(solution)/shard_map/ppermute | solution.py:487
  21.5 1.8 %collective-permute-start.10 = (bf16[224,128]{1,0:T(8,128)(2,1)S(1)}, bf16[224,128]{1,0:T(8,128)(2,1)S(1)}, u32[]{:S(2)}, u32[]{:S(2)}) collective-permute-start(bf16[224,128]{1,0:T(8,128)(2,1)S(1)} %shard_map.84.refs_0_), channel_id=1, source_target_pairs={{0,12},{1,13},{2,14},{3,15},{4,8},{5,9},{6,10},{7,11},{8,4},{9,5},... | collective-permute-start | bytes 172040 | tf_op jit(solution)/shard_map/ppermute | solution.py:487
  23.6 2.4 %collective-permute-start.8 = (bf16[224,128]{1,0:T(8,128)(2,1)S(1)}, bf16[224,128]{1,0:T(8,128)(2,1)S(1)}, u32[]{:S(2)}, u32[]{:S(2)}) collective-permute-start(bf16[224,128]{1,0:T(8,128)(2,1)S(1)} %shard_map.84.refs_0_), channel_id=1, source_target_pairs={{0,4},{1,5},{2,6},{3,7},{4,0},{5,1},{6,2},{7,3},{8,12},{9,13},{10,... | collective-permute-start | bytes 172040 | tf_op jit(solution)/shard_map/ppermute | solution.py:487
  26.2 0.9 %shard_map.85 = (bf16[2112,128]{1,0:T(8,128)(2,1)S(1)}, bf16[2112,128]{1,0:T(8,128)(2,1)S(1)}, bf16[2112,128]{1,0:T(8,128)(2,1)S(1)}) custom-call(bf16[2048,128]{1,0:T(8,128)(2,1)S(1)} %get-tuple-element.99.g_ref, f32[64,128]{1,0:T(8,128)S(1)} %get-tuple-element.100.g_lines, bf16[128,128]{1,0:T(8,128)(2,1)S(1)} %get-tuple-element.101.g_sides), custom_call_target="tpu_custom_call" | custom-call | bytes 2097152 | tf_op jit(solution)/shard_map/pallas_call | solution.py:24
  27.1 1.1 %collective-permute-done.10.refs_3_ = bf16[224,128]{1,0:T(8,128)(2,1)S(1)} collective-permute-done((bf16[224,128]{1,0:T(8,128)(2,1)S(1)}, bf16[224,128]{1,0:T(8,128)(2,1)S(1)}, u32[]{:S(2)}, u32[]{:S(2)}) %collective-permute-start.10) | collective-permute-done | bytes 57376 | tf_op jit(solution)/shard_map/ppermute | solution.py:487
  28.2 1.6 %collective-permute-done.9.refs_2_ = bf16[224,128]{1,0:T(8,128)(2,1)S(1)} collective-permute-done((bf16[224,128]{1,0:T(8,128)(2,1)S(1)}, bf16[224,128]{1,0:T(8,128)(2,1)S(1)}, u32[]{:S(2)}, u32[]{:S(2)}) %collective-permute-start.9) | collective-permute-done | bytes 57376 | tf_op jit(solution)/shard_map/ppermute | solution.py:487
  29.9 1.6 %collective-permute-start.13 = (bf16[416,128]{1,0:T(8,128)(2,1)S(1)}, bf16[416,128]{1,0:T(8,128)(2,1)S(1)}, u32[]{:S(2)}, u32[]{:S(2)}) collective-permute-start(bf16[416,128]{1,0:T(8,128)(2,1)S(1)} %shard_map.87.row_a.refs_0_), channel_id=1, source_target_pairs={{0,3},{1,2},{2,1},{3,0},{4,7},{5,6},{6,5},{7,4},{8,11},{9,10},{10,... | collective-permute-start | bytes 319496 | tf_op jit(solution)/shard_map/ppermute | solution.py:487
  32.0 1.4 %collective-permute-start.11 = (bf16[416,128]{1,0:T(8,128)(2,1)S(1)}, bf16[416,128]{1,0:T(8,128)(2,1)S(1)}, u32[]{:S(2)}, u32[]{:S(2)}) collective-permute-start(bf16[416,128]{1,0:T(8,128)(2,1)S(1)} %shard_map.87.row_a.refs_0_), channel_id=1, source_target_pairs={{0,1},{1,0},{2,3},{3,2},{4,5},{5,4},{6,7},{7,6},{8,9},{9,8},{10,11... | collective-permute-start | bytes 319496 | tf_op jit(solution)/shard_map/ppermute | solution.py:487
  33.4 1.0 %shard_map.88.inner = f32[2048,128]{1,0:T(8,128)S(1)} custom-call(bf16[2112,128]{1,0:T(8,128)(2,1)S(1)} %get-tuple-element.113.p0, bf16[2112,128]{1,0:T(8,128)(2,1)S(1)} %get-tuple-element.114.p1, bf16[2112,128]{1,0:T(8,128)(2,1)S(1)} %get-tuple-element.115.p2, bf16[3,256,128]{2,1,0:T(8,128)(2,1)S(1)} %get-tuple-element.90.wb_ref), custom_call_target="tpu_custom_call" | custom-call | flops 402653184 | bytes 3145728 | tf_op jit(solution)/shard_map/pallas_call | solution.py:24
  34.4 2.0 %collective-permute-done.13.row_d.refs_3_ = bf16[416,128]{1,0:T(8,128)(2,1)S(1)} collective-permute-done((bf16[416,128]{1,0:T(8,128)(2,1)S(1)}, bf16[416,128]{1,0:T(8,128)(2,1)S(1)}, u32[]{:S(2)}, u32[]{:S(2)}) %collective-permute-start.13) | collective-permute-done | bytes 106528 | tf_op jit(solution)/shard_map/ppermute | solution.py:487
  36.4 1.5 %collective-permute-done.12.row_c.refs_2_ = bf16[416,128]{1,0:T(8,128)(2,1)S(1)} collective-permute-done((bf16[416,128]{1,0:T(8,128)(2,1)S(1)}, bf16[416,128]{1,0:T(8,128)(2,1)S(1)}, u32[]{:S(2)}, u32[]{:S(2)}) %collective-permute-start.12) | collective-permute-done | bytes 106528 | tf_op jit(solution)/shard_map/ppermute | solution.py:487
  38.2 1.2 %shard_map.89 = bf16[64,4096]{1,0:T(8,128)(2,1)} custom-call(bf16[416,128]{1,0:T(8,128)(2,1)S(1)} %shard_map.87.row_a.refs_0_, bf16[416,128]{1,0:T(8,128)(2,1)S(1)} %collective-permute-done.11.row_b.refs_1_, bf16[416,128]{1,0:T(8,128)(2,1)S(1)} %collective-permute-done.12.row_c.refs_2_, bf16[416,128]{1,0:T(8,128)(2,1)S(1)} %collective-permute-done.13.row_d.refs_3_, ...), custom_call_target="tpu_custom_call" | custom-call | bytes 2097152 | tf_op jit(solution)/shard_map/pallas_call | solution.py:24
  39.4 0.7 %shard_map.91 = (f32[64,576]{1,0:T(8,128)}, f32[1,64]{1,0:T(1,128)}) custom-call(f32[160,128]{1,0:T(8,128)S(1)} %shard_map.90.mine, f32[160,128]{1,0:T(8,128)S(1)} %collective-permute-done.14.other), custom_call_target="tpu_custom_call" | custom-call | tf_op jit(solution)/shard_map/pallas_call | solution.py:24
  (32 shorter events, 3.3 us)
Async XLA Ops:
  0.6 1.0 %copy-start = (bf16[1,64,4096]{2,1,0:T(8,128)(2,1)S(1)}, bf16[1,64,4096]{2,1,0:T(8,128)(2,1)}, u32[]{:S(2)}) copy-start(bf16[1,64,4096]{2,1,0:T(8,128)(2,1)} %param.5) | copy-start | bytes 1572868
  1.7 6.6 %copy-start.3 = (bf16[576,64]{0,1:T(8,128)(2,1)S(1)}, bf16[576,64]{0,1:T(8,128)(2,1)}, u32[]{:S(2)}) copy-start(bf16[576,64]{0,1:T(8,128)(2,1)} %param.6) | copy-start | bytes 221188
  1.7 7.8 %collective-permute-start.2 = (bf16[64,128]{1,0:T(8,128)(2,1)S(1)}, bf16[64,128]{1,0:T(8,128)(2,1)S(1)}, u32[]{:S(2)}, u32[]{:S(2)}) collective-permute-start(bf16[64,128]{1,0:T(8,128)(2,1)S(1)} %get-tuple-element.63.refs_0_), channel_id=1, source_target_pairs={{0,12},{1,13},{2,14},{3,15},{4,8},{5,9},{6,10},{7,11},{8,4},{9,5},... | collective-permute-start | bytes 49160 | tf_op jit(solution)/shard_map/ppermute | solution.py:487
  6.8 4.6 %collective-permute-start.1 = (bf16[64,128]{1,0:T(8,128)(2,1)S(1)}, bf16[64,128]{1,0:T(8,128)(2,1)S(1)}, u32[]{:S(2)}, u32[]{:S(2)}) collective-permute-start(bf16[64,128]{1,0:T(8,128)(2,1)S(1)} %get-tuple-element.63.refs_0_), channel_id=1, source_target_pairs={{0,8},{1,9},{2,10},{3,11},{4,12},{5,13},{6,14},{7,15},{8,0},{9,1},... | collective-permute-start | bytes 49160 | tf_op jit(solution)/shard_map/ppermute | solution.py:487
  6.8 4.6 %collective-permute-start = (bf16[64,128]{1,0:T(8,128)(2,1)S(1)}, bf16[64,128]{1,0:T(8,128)(2,1)S(1)}, u32[]{:S(2)}, u32[]{:S(2)}) collective-permute-start(bf16[64,128]{1,0:T(8,128)(2,1)S(1)} %get-tuple-element.63.refs_0_), channel_id=1, source_target_pairs={{0,4},{1,5},{2,6},{3,7},{4,0},{5,1},{6,2},{7,3},{8,12},{9,13},{10,... | collective-permute-start | bytes 49160 | tf_op jit(solution)/shard_map/ppermute | solution.py:487
  8.5 6.6 %copy-start.1 = (bf16[1,64,4096]{2,1,0:T(8,128)(2,1)S(1)}, bf16[1,64,4096]{2,1,0:T(8,128)(2,1)}, u32[]{:S(2)}) copy-start(bf16[1,64,4096]{2,1,0:T(8,128)(2,1)} %param.8) | copy-start | bytes 1572868
  11.5 6.4 %collective-permute-start.5 = (bf16[256,128]{1,0:T(8,128)(2,1)S(1)}, bf16[256,128]{1,0:T(8,128)(2,1)S(1)}, u32[]{:S(2)}, u32[]{:S(2)}) collective-permute-start(bf16[256,128]{1,0:T(8,128)(2,1)S(1)} %shard_map.80.rows_a), channel_id=1, source_target_pairs={{0,3},{1,2},{2,1},{3,0},{4,7},{5,6},{6,5},{7,4},{8,11},{9,10},{10,... | collective-permute-start | bytes 196616 | tf_op jit(solution)/shard_map/ppermute | solution.py:487
  14.0 4.3 %collective-permute-start.4 = (bf16[256,128]{1,0:T(8,128)(2,1)S(1)}, bf16[256,128]{1,0:T(8,128)(2,1)S(1)}, u32[]{:S(2)}, u32[]{:S(2)}) collective-permute-start(bf16[256,128]{1,0:T(8,128)(2,1)S(1)} %shard_map.80.rows_a), channel_id=1, source_target_pairs={{0,2},{1,3},{2,0},{3,1},{4,6},{5,7},{6,4},{7,5},{8,10},{9,11},{10,... | collective-permute-start | bytes 196616 | tf_op jit(solution)/shard_map/ppermute | solution.py:487
  14.5 4.3 %collective-permute-start.3 = (bf16[256,128]{1,0:T(8,128)(2,1)S(1)}, bf16[256,128]{1,0:T(8,128)(2,1)S(1)}, u32[]{:S(2)}, u32[]{:S(2)}) collective-permute-start(bf16[256,128]{1,0:T(8,128)(2,1)S(1)} %shard_map.80.rows_a), channel_id=1, source_target_pairs={{0,1},{1,0},{2,3},{3,2},{4,5},{5,4},{6,7},{7,6},{8,9},{9,8},{10,11... | collective-permute-start | bytes 196616 | tf_op jit(solution)/shard_map/ppermute | solution.py:487
  15.0 0.7 %copy-start.4 = (f32[64]{0:T(128)S(1)}, f32[64]{0:T(128)}, u32[]{:S(2)}) copy-start(f32[64]{0:T(128)} %param.7) | copy-start | bytes 772
  15.0 3.7 %collective-permute-start.6 = (bf16[64,128]{1,0:T(8,128)(2,1)S(1)}, bf16[64,128]{1,0:T(8,128)(2,1)S(1)}, u32[]{:S(2)}, u32[]{:S(2)}) collective-permute-start(bf16[64,128]{1,0:T(8,128)(2,1)S(1)} %get-tuple-element.87), channel_id=1, source_target_pairs={{0,16},{16,0},{1,17},{17,1},{2,18},{18,2},{3,19},{19,3},{4,20},{20... | collective-permute-start | bytes 49160 | tf_op jit(solution)/shard_map/ppermute | solution.py:487
  15.7 1.8 %copy-start.2 = (s32[16,260]{1,0:T(8,128)S(1)}, s32[16,260]{1,0:T(8,128)}, u32[]{:S(2)}) copy-start(s32[16,260]{1,0:T(8,128)} %index_ref.1) | copy-start | bytes 49924
  20.2 1.3 %collective-permute-start.7 = (bf16[224,128]{1,0:T(8,128)(2,1)S(1)}, bf16[224,128]{1,0:T(8,128)(2,1)S(1)}, u32[]{:S(2)}, u32[]{:S(2)}) collective-permute-start(bf16[224,128]{1,0:T(8,128)(2,1)S(1)} %get-tuple-element.93), channel_id=1, source_target_pairs={{0,16},{16,0},{1,17},{17,1},{2,18},{18,2},{3,19},{19,3},{4,20},{20... | collective-permute-start | bytes 172040 | tf_op jit(solution)/shard_map/ppermute | solution.py:487
  21.5 6.7 %collective-permute-start.10 = (bf16[224,128]{1,0:T(8,128)(2,1)S(1)}, bf16[224,128]{1,0:T(8,128)(2,1)S(1)}, u32[]{:S(2)}, u32[]{:S(2)}) collective-permute-start(bf16[224,128]{1,0:T(8,128)(2,1)S(1)} %shard_map.84.refs_0_), channel_id=1, source_target_pairs={{0,12},{1,13},{2,14},{3,15},{4,8},{5,9},{6,10},{7,11},{8,4},{9,5},... | collective-permute-start | bytes 172040 | tf_op jit(solution)/shard_map/ppermute | solution.py:487
  23.4 6.5 %collective-permute-start.9 = (bf16[224,128]{1,0:T(8,128)(2,1)S(1)}, bf16[224,128]{1,0:T(8,128)(2,1)S(1)}, u32[]{:S(2)}, u32[]{:S(2)}) collective-permute-start(bf16[224,128]{1,0:T(8,128)(2,1)S(1)} %shard_map.84.refs_0_), channel_id=1, source_target_pairs={{0,8},{1,9},{2,10},{3,11},{4,12},{5,13},{6,14},{7,15},{8,0},{9,1},... | collective-permute-start | bytes 172040 | tf_op jit(solution)/shard_map/ppermute | solution.py:487
  23.6 6.2 %collective-permute-start.8 = (bf16[224,128]{1,0:T(8,128)(2,1)S(1)}, bf16[224,128]{1,0:T(8,128)(2,1)S(1)}, u32[]{:S(2)}, u32[]{:S(2)}) collective-permute-start(bf16[224,128]{1,0:T(8,128)(2,1)S(1)} %shard_map.84.refs_0_), channel_id=1, source_target_pairs={{0,4},{1,5},{2,6},{3,7},{4,0},{5,1},{6,2},{7,3},{8,12},{9,13},{10,... | collective-permute-start | bytes 172040 | tf_op jit(solution)/shard_map/ppermute | solution.py:487
  29.9 6.6 %collective-permute-start.13 = (bf16[416,128]{1,0:T(8,128)(2,1)S(1)}, bf16[416,128]{1,0:T(8,128)(2,1)S(1)}, u32[]{:S(2)}, u32[]{:S(2)}) collective-permute-start(bf16[416,128]{1,0:T(8,128)(2,1)S(1)} %shard_map.87.row_a.refs_0_), channel_id=1, source_target_pairs={{0,3},{1,2},{2,1},{3,0},{4,7},{5,6},{6,5},{7,4},{8,11},{9,10},{10,... | collective-permute-start | bytes 319496 | tf_op jit(solution)/shard_map/ppermute | solution.py:487
  31.5 6.4 %collective-permute-start.12 = (bf16[416,128]{1,0:T(8,128)(2,1)S(1)}, bf16[416,128]{1,0:T(8,128)(2,1)S(1)}, u32[]{:S(2)}, u32[]{:S(2)}) collective-permute-start(bf16[416,128]{1,0:T(8,128)(2,1)S(1)} %shard_map.87.row_a.refs_0_), channel_id=1, source_target_pairs={{0,2},{1,3},{2,0},{3,1},{4,6},{5,7},{6,4},{7,5},{8,10},{9,11},{10,... | collective-permute-start | bytes 319496 | tf_op jit(solution)/shard_map/ppermute | solution.py:487
  32.0 6.0 %collective-permute-start.11 = (bf16[416,128]{1,0:T(8,128)(2,1)S(1)}, bf16[416,128]{1,0:T(8,128)(2,1)S(1)}, u32[]{:S(2)}, u32[]{:S(2)}) collective-permute-start(bf16[416,128]{1,0:T(8,128)(2,1)S(1)} %shard_map.87.row_a.refs_0_), channel_id=1, source_target_pairs={{0,1},{1,0},{2,3},{3,2},{4,5},{5,4},{6,7},{7,6},{8,9},{9,8},{10,11... | collective-permute-start | bytes 319496 | tf_op jit(solution)/shard_map/ppermute | solution.py:487
  38.1 1.3 %collective-permute-start.14 = (f32[160,128]{1,0:T(8,128)S(1)}, f32[160,128]{1,0:T(8,128)S(1)}, u32[]{:S(2)}, u32[]{:S(2)}) collective-permute-start(f32[160,128]{1,0:T(8,128)S(1)} %shard_map.90.mine), channel_id=1, source_target_pairs={{0,16},{16,0},{1,17},{17,1},{2,18},{18,2},{3,19},{19,3},{4,20},{20... | collective-permute-start | bytes 245768 | tf_op jit(solution)/shard_map/ppermute | solution.py:487

commit v8 on v7

--- a/solution.py
+++ b/solution.py
@@ -14,6 +14,8 @@
 LANES = 2 * CHANNELS
 ROWS = PAIRS * SIDE
 WROWS = 5 * CHANNELS // 2
+FAR_ORDER = (0, 2, 1)
+NEAR_ORDER = (0, 1, 2)
 F32 = jnp.float32
 BF16 = jnp.bfloat16
 
@@ -104,7 +106,7 @@
 
 
 def rows_kernel(*refs):
-    parts, out = refs[:-1], refs[-1]
+    parts, out = by_distance(refs[:-1], FAR_ORDER), refs[-1]
     n = parts[0].shape[0]
     for i, part in enumerate(parts):
         out[i * n : (i + 1) * n, :] = part[...]
@@ -231,14 +233,14 @@
 
 def middle_kernel(
     s_ref, offset, cot_ref, p0, p1, p2, lines, terms_ref, bias_ref, cot_lines, rows_a, rows_b, rows_c, rows_d, cols_ref,
-    hot_ref, half_ref, w_ref, wb_ref, wc_ref,
-    g_lines, g_sides, keep_ref, send_ref, own_ref, cell_scr, gt, gb, gc, own_scr, msg,
+    hot_ref, half_ref, w_ref, wc_ref,
+    g_lines, g_sides, keep_ref, send_ref, cell_scr, gc, msg,
 ):
     added = jnp.concatenate([offset[...], offset[...]], axis=1)
     n = rows_a.shape[0]
     many = 4 * n
     cells = dot(hot_ref[:, many:], cols_ref[...])
-    for i, ref in enumerate((rows_a, rows_b, rows_c, rows_d)):
+    for i, ref in enumerate(by_distance((rows_a, rows_b, rows_c, rows_d), NEAR_ORDER)):
         cells = cells + dot(hot_ref[:, i * n : (i + 1) * n], ref[...])
     other = turn(cells)
     upper = half_ref[...] > 0.5
@@ -330,12 +332,6 @@
         ).astype(BF16)
         t = terms_ref[a] + dot(border, window, TN)
         terms += [t[:, :LANES], t[:, LANES:]]
-    for scr, line in ((gt, all_top), (gb, all_bottom)):
-        turned = turn(line)
-        scr[...] = jnp.zeros(scr.shape, F32)
-        scr[1 : PAIRS + 1, :] = jnp.where(low(line.shape), turned, 0.0)
-        scr[0:PAIRS, :] += jnp.where(low(line.shape), 0.0, turned)
-
     def tap(m, high):
         a, b = m // 3, m % 3
         result = 0.0
@@ -357,14 +353,6 @@
     core = lax.axis_index("region") & 1
     keep_ref[...] = msg[pl.ds(pl.multiple_of(core * WROWS, WROWS), WROWS), :].astype(BF16)
     send_ref[0:WROWS, :] = msg[pl.ds(pl.multiple_of((1 - core) * WROWS, WROWS), WROWS), :].astype(BF16)
-
-    lines = []
-    for src, tap_row in ((gt, 2), (gb, 0)):
-        window = jnp.concatenate([src[0:PAIRS, :], src[1 : PAIRS + 1, :]], axis=1).astype(BF16)
-        lines.append(dot(window, wb_ref[tap_row]))
-    own_scr[pl.ds(0, PAIRS, stride=2), :] = halves(lines[0], turn(lines[1]))
-    own_scr[pl.ds(1, PAIRS, stride=2), :] = halves(turn(lines[0]), lines[1])
-    own_ref[...] = own_scr[...].astype(BF16)
 
     gc[...] = jnp.zeros(gc.shape, F32)
     gc[8 : 8 + SIDE, :] = halves(g_left, g_right)
@@ -384,6 +372,22 @@
     send_ref[WROWS:, :] = dot(hot_ref[:, many:], placed, TN).astype(BF16)
 
 
+def halo_rows_kernel(g_lines, wb_ref, own_ref, gt, gb, own_scr):
+    all_top, all_bottom = g_lines[0:PAIRS, :], g_lines[PAIRS:, :]
+    for scr, line in ((gt, all_top), (gb, all_bottom)):
+        turned = turn(line)
+        scr[...] = jnp.zeros(scr.shape, F32)
+        scr[1 : PAIRS + 1, :] = jnp.where(low(line.shape), turned, 0.0)
+        scr[0:PAIRS, :] += jnp.where(low(line.shape), 0.0, turned)
+    lines = []
+    for src, tap_row in ((gt, 2), (gb, 0)):
+        window = jnp.concatenate([src[0:PAIRS, :], src[1 : PAIRS + 1, :]], axis=1).astype(BF16)
+        lines.append(dot(window, wb_ref[tap_row]))
+    own_scr[pl.ds(0, PAIRS, stride=2), :] = halves(lines[0], turn(lines[1]))
+    own_scr[pl.ds(1, PAIRS, stride=2), :] = halves(turn(lines[0]), lines[1])
+    own_ref[...] = own_scr[...].astype(BF16)
+
+
 def grad_copies_kernel(g_ref, g_lines, g_sides, p0, p1, p2):
     row = iota((SIDE, LANES), 0)
     left = g_sides[0:SIDE, :].astype(F32)
@@ -435,7 +439,7 @@
 
 
 def join_kernel(*refs):
-    parts, out = refs[:-1], refs[-1]
+    parts, out = by_distance(refs[:-1], FAR_ORDER), refs[-1]
     put_weights(parts, out)
     n = parts[0].shape[0] - WROWS
     for i, part in enumerate(parts):
@@ -443,7 +447,7 @@
 
 
 def close_kernel(scale, *refs):
-    parts, out = refs[:-1], refs[-1]
+    parts, out = by_distance(refs[:-1], NEAR_ORDER), refs[-1]
     total, whole = added_weights(parts)
     out[0 : WROWS - SIDE, :] = total[: WROWS - SIDE] * scale
     out[WROWS - SIDE :, :] = jnp.where(bias_lanes(whole.shape), whole, total[WROWS - SIDE :]) * scale
@@ -463,7 +467,7 @@
     side_refs, grad_ref = rest[:-1], rest[-1]
     n = row_a.shape[0] - WROWS
     got = 0.0
-    for i, ref in enumerate((row_a, row_b, row_c, row_d)):
+    for i, ref in enumerate(by_distance((row_a, row_b, row_c, row_d), NEAR_ORDER)):
         got = got + dot(pick[:, i * n : (i + 1) * n], ref[WROWS:, :])
     a, b, c, d = (got[i * SIDE : (i + 1) * SIDE] for i in range(4))
     rims = halves(a + turn(b), turn(c) + d)
@@ -515,10 +519,14 @@
     return [(bit, to) for to, bit in enumerate(bits)]
 
 
-def exchange(x, bits):
+def exchange(x, bits, order):
     ks = [sum(1 << bits[i] for i in range(len(bits)) if (n >> i) & 1) for n in range(1, 1 << len(bits))]
-    got = {k: swap(x, "patch", k) for k in ks[::-1]}
-    return [got[k] for k in ks]
+    return [swap(x, "patch", ks[i]) for i in order if i < len(ks)]
+
+
+def by_distance(parts, order):
+    places = [i for i in order if i < len(parts) - 1]
+    return [parts[0]] + [parts[1 + places.index(i)] for i in range(len(places))]
 
 
 def body(fine_input, fine_weight, fine_bias, cotangent, halo_index):
@@ -539,7 +547,7 @@
     both = ((ROWS, LANES), F32)
     work = dict(flops=2 * ROWS * 768 * 128, moved=3 * 2**20)
 
-    others = exchange(rows, rounds[0])
+    others = exchange(rows, rounds[0], FAR_ORDER)
     *copies, lines = call(copies_kernel, [pair] * 3 + [((4, 40, LANES), F32)], x, moved=2 * 2**20)
     forward, backward, columns = call(
         weights_kernel,
@@ -554,7 +562,7 @@
     for bits in rounds[1:]:
         size = ((len(others) + 1) * rows.shape[0], LANES)
         rows = call(rows_kernel, [(size, BF16)], rows, *others)[0]
-        others = exchange(rows, bits)
+        others = exchange(rows, bits, NEAR_ORDER if bits == rounds[-1] else FAR_ORDER)
     hot, half_mask = call(
         functools.partial(plan_kernel, owners, regions, blocks),
         [((count, (owners + blocks) * SIDE), BF16), ((count, LANES), F32)],
@@ -569,16 +577,15 @@
     grad, *inside = inside
 
     line = pltpu.VMEM((40, LANES), F32)
-    g_lines, g_sides, message, sent, own_rows = call(
+    g_lines, g_sides, message, sent = call(
         middle_kernel,
         [
             ((SIDE, LANES), F32), ((2 * SIDE, LANES), BF16),
-            ((WROWS, LANES), BF16), ((WROWS + blocks * SIDE, LANES), BF16), ((SIDE, LANES), BF16),
+            ((WROWS, LANES), BF16), ((WROWS + blocks * SIDE, LANES), BF16),
         ],
-        signal, offset, cot, *copies, lines, *inside, rows, *others, cols, hot, half_mask, forward, backward, columns,
+        signal, offset, cot, *copies, lines, *inside, rows, *others, cols, hot, half_mask, forward, columns,
         scratch=[
-            pltpu.VMEM((count, LANES), F32), line, line,
-            pltpu.VMEM((96, LANES), F32), pltpu.VMEM((SIDE, LANES), F32), pltpu.VMEM((2 * WROWS, LANES), F32),
+            pltpu.VMEM((count, LANES), F32), pltpu.VMEM((96, LANES), F32), pltpu.VMEM((2 * WROWS, LANES), F32),
         ],
         moved=2**20,
     )
@@ -588,6 +595,11 @@
         sides = [shift(upper, "region", 1), shift(lower, "region", -1)]
         sent = sent[:WROWS]
     other = swap(sent, "region", 1)
+    own_rows = call(
+        halo_rows_kernel, [((SIDE, LANES), BF16)], g_lines, backward,
+        scratch=[line, line, pltpu.VMEM((SIDE, LANES), F32)],
+    )[0]
+    other, own_rows = lax.optimization_barrier((other, own_rows))
     if regions == 2:
         sides = [other]
     far = [k for k in steps_of(regions) if k > 1]
@@ -599,7 +611,7 @@
     beside = [grad, g_lines, g_sides]
     for bits in rounds[:-1]:
         message, beside, index = lax.optimization_barrier((message, beside, index))
-        others = exchange(message, bits)
+        others = exchange(message, bits, FAR_ORDER)
         if bits == rounds[-2]:
             pick = call(functools.partial(pick_kernel, owners), [((4 * SIDE, owners * SIDE), BF16)], index)[0]
             beside = call(grad_copies_kernel, [pair] * 3, *beside, moved=2 * 2**20)
@@ -607,7 +619,7 @@
         size = (WROWS + (len(others) + 1) * (message.shape[0] - WROWS), LANES)
         message = call(join_kernel, [(size, BF16)], message, *others)[0]
     message, beside = lax.optimization_barrier((message, beside))
-    others = exchange(message, rounds[-1])
+    others = exchange(message, rounds[-1], NEAR_ORDER)
     beside = call(inner_kernel, [both], *beside, backward, **work)[0]
     others, beside = lax.optimization_barrier((others, beside))
     scale = 1.0 / math.sqrt(regions * owners * SIDE * SIDE)

time: 40.3 us -> 39.8 us (0.988)
  starting transfers between devices: 17.5 us -> 16.5 us
    ppermute x15, starting transfers between devices: 17.5 us -> 16.5 us  [swap(): return lax.ppermute(x, axis, [(i, i ^ k) for i in range(n)])]
    pallas_call x16 -> x17, Pallas kernels: 9.57 us -> 9.76 us  [call(): pl.pallas_call(kernel, out_shape=shapes, in_specs=[whole] * len(args), ou...]
  transfers between devices with their start and end apart: 15 -> 15, of which waited for: 10 -> 11; matrix products, arithmetic and copies ran while one was open for 0% -> 0% of each run, Pallas kernels for 18% -> 19%
where the time goes in v8:
time: 39.8 us; the launch traced here: 39.6 us
  starting transfers between devices  16.5 us (41%)
  waiting for transfers between devices  10.9 us (27%)
  Pallas kernels  9.76 us (25%)
  local copies, waits for them, and re-layouts  1.7 us (4%)
  between operations  0.78 us (2%)
    ppermute x15, starting transfers between devices, swap(): return lax.ppermute(x, axis, [(i, i ^ k) for i in range(n)])  16.5 us
    ppermute x15, waiting for transfers between devices, swap(): return lax.ppermute(x, axis, [(i, i ^ k) for i in range(n)])  10.9 us
    pallas_call x17, Pallas kernels, call(): pl.pallas_call(kernel, out_shape=shapes, in_specs=[whole] * len(args), ou...  9.76 us
    unnamed x10, local copies, waits for them, and re-layouts  1.7 us
  transfers between devices with their start and end apart: 15, of which 11 were waited for; matrix products, arithmetic and copies ran while one was open for 0% of the time, Pallas kernels for 19%

profile of v8, /device:TPU:0, one launch (start us, length us, event | category | flops | bytes accessed | tf_op | source)
XLA Modules:
  0.0 39.6 jit_solution(15744699860410952278)
XLA Ops:
  0.6 1.0 %copy-done = bf16[1,64,4096]{2,1,0:T(8,128)(2,1)S(1)} copy-done((bf16[1,64,4096]{2,1,0:T(8,128)(2,1)S(1)}, bf16[1,64,4096]{2,1,0:T(8,128)(2,1)}, u32[]{:S(2)}) %copy-start) | copy-done | bytes 524312
  1.7 4.1 %collective-permute-start.2 = (bf16[64,128]{1,0:T(8,128)(2,1)S(1)}, bf16[64,128]{1,0:T(8,128)(2,1)S(1)}, u32[]{:S(2)}, u32[]{:S(2)}) collective-permute-start(bf16[64,128]{1,0:T(8,128)(2,1)S(1)} %get-tuple-element.64.refs_0_), channel_id=1, source_target_pairs={{0,8},{1,9},{2,10},{3,11},{4,12},{5,13},{6,14},{7,15},{8,0},{9,1},... | collective-permute-start | bytes 49160 | tf_op jit(solution)/shard_map/ppermute | solution.py:491
  5.8 1.3 %collective-permute-start.1 = (bf16[64,128]{1,0:T(8,128)(2,1)S(1)}, bf16[64,128]{1,0:T(8,128)(2,1)S(1)}, u32[]{:S(2)}, u32[]{:S(2)}) collective-permute-start(bf16[64,128]{1,0:T(8,128)(2,1)S(1)} %get-tuple-element.64.refs_0_), channel_id=1, source_target_pairs={{0,12},{1,13},{2,14},{3,15},{4,8},{5,9},{6,10},{7,11},{8,4},{9,5},... | collective-permute-start | bytes 49160 | tf_op jit(solution)/shard_map/ppermute | solution.py:491
  7.4 0.9 %shard_map.77 = (bf16[2112,128]{1,0:T(8,128)(2,1)S(1)}, bf16[2112,128]{1,0:T(8,128)(2,1)S(1)}, bf16[2112,128]{1,0:T(8,128)(2,1)S(1)}, f32[4,40,128]{2,1,0:T(8,128)S(1)}) custom-call(bf16[64,4096]{1,0:T(8,128)(2,1)S(1)} %bitcast.8), custom_call_target="tpu_custom_call" | custom-call | bytes 2097152 | tf_op jit(solution)/shard_map/pallas_call | solution.py:26
  8.4 1.0 %shard_map.79.s_ref = f32[2048,128]{1,0:T(8,128)S(1)} custom-call(bf16[2112,128]{1,0:T(8,128)(2,1)S(1)} %get-tuple-element.65.p0, bf16[2112,128]{1,0:T(8,128)(2,1)S(1)} %get-tuple-element.66.p1, bf16[2112,128]{1,0:T(8,128)(2,1)S(1)} %get-tuple-element.67.p2, bf16[3,128,256]{2,1,0:T(8,128)(2,1)S(1)} %get-tuple-element.68.w_ref), custom_call_target="tpu_custom_call" | custom-call | flops 402653184 | bytes 3145728 | tf_op jit(solution)/shard_map/pallas_call | solution.py:26
  9.4 2.0 %collective-permute-done.1.refs_2_ = bf16[64,128]{1,0:T(8,128)(2,1)S(1)} collective-permute-done((bf16[64,128]{1,0:T(8,128)(2,1)S(1)}, bf16[64,128]{1,0:T(8,128)(2,1)S(1)}, u32[]{:S(2)}, u32[]{:S(2)}) %collective-permute-start.1) | collective-permute-done | bytes 16416 | tf_op jit(solution)/shard_map/ppermute | solution.py:491
  11.4 2.5 %collective-permute-start.5 = (bf16[256,128]{1,0:T(8,128)(2,1)S(1)}, bf16[256,128]{1,0:T(8,128)(2,1)S(1)}, u32[]{:S(2)}, u32[]{:S(2)}) collective-permute-start(bf16[256,128]{1,0:T(8,128)(2,1)S(1)} %shard_map.80.rows_a), channel_id=1, source_target_pairs={{0,3},{1,2},{2,1},{3,0},{4,7},{5,6},{6,5},{7,4},{8,11},{9,10},{10,... | collective-permute-start | bytes 196616 | tf_op jit(solution)/shard_map/ppermute | solution.py:491
  14.9 0.6 %copy-done.4 = f32[64]{0:T(128)S(1)} copy-done((f32[64]{0:T(128)S(1)}, f32[64]{0:T(128)}, u32[]{:S(2)}) %copy-start.4) | copy-done | bytes 280
  15.6 1.8 %shard_map.82 = (bf16[2048,128]{1,0:T(8,128)(2,1)S(1)}, f32[3,128,256]{2,1,0:T(8,128)S(1)}, f32[8,128]{1,0:T(8,128)S(1)}, f32[64,128]{1,0:T(8,128)S(1)}) custom-call(f32[2048,128]{1,0:T(8,128)S(1)} %shard_map.79.s_ref, f32[1,64]{1,0:T(1,128)S(1)} %bitcast.12, bf16[64,4096]{1,0:T(8,128)(2,1)S(1)} %bitcast.9, bf16[2112,128]{1,0:T(8,128)(2,1)S(1)} %get-tuple-element.65.p0, ...), custom_call_target="tpu_custom_call" | custom-call | flops 402653184 | bytes 3145728 | tf_op jit(solution)/shard_map/pallas_call | solution.py:26
  18.7 1.3 %shard_map.83 = (f32[64,128]{1,0:T(8,128)S(1)}, bf16[128,128]{1,0:T(8,128)(2,1)S(1)}, bf16[160,128]{1,0:T(8,128)(2,1)S(1)}, bf16[224,128]{1,0:T(8,128)(2,1)S(1)}) custom-call(f32[2048,128]{1,0:T(8,128)S(1)} %shard_map.79.s_ref, f32[1,64]{1,0:T(1,128)S(1)} %bitcast.13, bf16[64,4096]{1,0:T(8,128)(2,1)S(1)} %bitcast.10, ...), custom_call_target="tpu_custom_call" | custom-call | bytes 1048576 | tf_op jit(solution)/shard_map/pallas_call | solution.py:26
  20.4 0.9 %collective-permute-done.7.other.rest_0_ = bf16[224,128]{1,0:T(8,128)(2,1)S(1)} collective-permute-done((bf16[224,128]{1,0:T(8,128)(2,1)S(1)}, bf16[224,128]{1,0:T(8,128)(2,1)S(1)}, u32[]{:S(2)}, u32[]{:S(2)}) %collective-permute-start.7) | collective-permute-done | bytes 57376 | tf_op jit(solution)/shard_map/ppermute | solution.py:491
  21.3 1.2 %collective-permute-start.10 = (bf16[224,128]{1,0:T(8,128)(2,1)S(1)}, bf16[224,128]{1,0:T(8,128)(2,1)S(1)}, u32[]{:S(2)}, u32[]{:S(2)}) collective-permute-start(bf16[224,128]{1,0:T(8,128)(2,1)S(1)} %shard_map.85.refs_0_), channel_id=1, source_target_pairs={{0,8},{1,9},{2,10},{3,11},{4,12},{5,13},{6,14},{7,15},{8,0},{9,1},... | collective-permute-start | bytes 172040 | tf_op jit(solution)/shard_map/ppermute | solution.py:491
  22.6 1.1 %collective-permute-start.9 = (bf16[224,128]{1,0:T(8,128)(2,1)S(1)}, bf16[224,128]{1,0:T(8,128)(2,1)S(1)}, u32[]{:S(2)}, u32[]{:S(2)}) collective-permute-start(bf16[224,128]{1,0:T(8,128)(2,1)S(1)} %shard_map.85.refs_0_), channel_id=1, source_target_pairs={{0,12},{1,13},{2,14},{3,15},{4,8},{5,9},{6,10},{7,11},{8,4},{9,5},... | collective-permute-start | bytes 172040 | tf_op jit(solution)/shard_map/ppermute | solution.py:491
  23.6 1.3 %collective-permute-start.8 = (bf16[224,128]{1,0:T(8,128)(2,1)S(1)}, bf16[224,128]{1,0:T(8,128)(2,1)S(1)}, u32[]{:S(2)}, u32[]{:S(2)}) collective-permute-start(bf16[224,128]{1,0:T(8,128)(2,1)S(1)} %shard_map.85.refs_0_), channel_id=1, source_target_pairs={{0,4},{1,5},{2,6},{3,7},{4,0},{5,1},{6,2},{7,3},{8,12},{9,13},{10,... | collective-permute-start | bytes 172040 | tf_op jit(solution)/shard_map/ppermute | solution.py:491
  25.1 0.9 %shard_map.86 = (bf16[2112,128]{1,0:T(8,128)(2,1)S(1)}, bf16[2112,128]{1,0:T(8,128)(2,1)S(1)}, bf16[2112,128]{1,0:T(8,128)(2,1)S(1)}) custom-call(bf16[2048,128]{1,0:T(8,128)(2,1)S(1)} %get-tuple-element.101.g_ref, f32[64,128]{1,0:T(8,128)S(1)} %get-tuple-element.102.g_lines, bf16[128,128]{1,0:T(8,128)(2,1)S(1)} %get-tuple-element.103.g_sides), custom_call_target="tpu_custom_call" | custom-call | bytes 2097152 | tf_op jit(solution)/shard_map/pallas_call | solution.py:26
  26.0 1.7 %collective-permute-done.10.refs_3_ = bf16[224,128]{1,0:T(8,128)(2,1)S(1)} collective-permute-done((bf16[224,128]{1,0:T(8,128)(2,1)S(1)}, bf16[224,128]{1,0:T(8,128)(2,1)S(1)}, u32[]{:S(2)}, u32[]{:S(2)}) %collective-permute-start.10) | collective-permute-done | bytes 57376 | tf_op jit(solution)/shard_map/ppermute | solution.py:491
  27.7 1.0 %collective-permute-done.9.refs_2_ = bf16[224,128]{1,0:T(8,128)(2,1)S(1)} collective-permute-done((bf16[224,128]{1,0:T(8,128)(2,1)S(1)}, bf16[224,128]{1,0:T(8,128)(2,1)S(1)}, u32[]{:S(2)}, u32[]{:S(2)}) %collective-permute-start.9) | collective-permute-done | bytes 57376 | tf_op jit(solution)/shard_map/ppermute | solution.py:491
  29.4 1.6 %collective-permute-start.13 = (bf16[416,128]{1,0:T(8,128)(2,1)S(1)}, bf16[416,128]{1,0:T(8,128)(2,1)S(1)}, u32[]{:S(2)}, u32[]{:S(2)}) collective-permute-start(bf16[416,128]{1,0:T(8,128)(2,1)S(1)} %shard_map.88.row_a.refs_0_), channel_id=1, source_target_pairs={{0,3},{1,2},{2,1},{3,0},{4,7},{5,6},{6,5},{7,4},{8,11},{9,10},{10,... | collective-permute-start | bytes 319496 | tf_op jit(solution)/shard_map/ppermute | solution.py:491
  31.5 1.4 %collective-permute-start.11 = (bf16[416,128]{1,0:T(8,128)(2,1)S(1)}, bf16[416,128]{1,0:T(8,128)(2,1)S(1)}, u32[]{:S(2)}, u32[]{:S(2)}) collective-permute-start(bf16[416,128]{1,0:T(8,128)(2,1)S(1)} %shard_map.88.row_a.refs_0_), channel_id=1, source_target_pairs={{0,1},{1,0},{2,3},{3,2},{4,5},{5,4},{6,7},{7,6},{8,9},{9,8},{10,11... | collective-permute-start | bytes 319496 | tf_op jit(solution)/shard_map/ppermute | solution.py:491
  32.9 1.0 %shard_map.89.inner = f32[2048,128]{1,0:T(8,128)S(1)} custom-call(bf16[2112,128]{1,0:T(8,128)(2,1)S(1)} %get-tuple-element.115.p0, bf16[2112,128]{1,0:T(8,128)(2,1)S(1)} %get-tuple-element.116.p1, bf16[2112,128]{1,0:T(8,128)(2,1)S(1)} %get-tuple-element.117.p2, bf16[3,256,128]{2,1,0:T(8,128)(2,1)S(1)} %get-tuple-element.95.wb_ref), custom_call_target="tpu_custom_call" | custom-call | flops 402653184 | bytes 3145728 | tf_op jit(solution)/shard_map/pallas_call | solution.py:26
  33.9 2.0 %collective-permute-done.13.row_d.refs_3_ = bf16[416,128]{1,0:T(8,128)(2,1)S(1)} collective-permute-done((bf16[416,128]{1,0:T(8,128)(2,1)S(1)}, bf16[416,128]{1,0:T(8,128)(2,1)S(1)}, u32[]{:S(2)}, u32[]{:S(2)}) %collective-permute-start.13) | collective-permute-done | bytes 106528 | tf_op jit(solution)/shard_map/ppermute | solution.py:491
  35.9 1.5 %collective-permute-done.12.row_c.refs_2_ = bf16[416,128]{1,0:T(8,128)(2,1)S(1)} collective-permute-done((bf16[416,128]{1,0:T(8,128)(2,1)S(1)}, bf16[416,128]{1,0:T(8,128)(2,1)S(1)}, u32[]{:S(2)}, u32[]{:S(2)}) %collective-permute-start.12) | collective-permute-done | bytes 106528 | tf_op jit(solution)/shard_map/ppermute | solution.py:491
  37.7 1.2 %shard_map.90 = bf16[64,4096]{1,0:T(8,128)(2,1)} custom-call(bf16[416,128]{1,0:T(8,128)(2,1)S(1)} %shard_map.88.row_a.refs_0_, bf16[416,128]{1,0:T(8,128)(2,1)S(1)} %collective-permute-done.11.row_b.refs_1_, bf16[416,128]{1,0:T(8,128)(2,1)S(1)} %collective-permute-done.12.row_c.refs_2_, bf16[416,128]{1,0:T(8,128)(2,1)S(1)} %collective-permute-done.13.row_d.refs_3_, ...), custom_call_target="tpu_custom_call" | custom-call | bytes 2097152 | tf_op jit(solution)/shard_map/pallas_call | solution.py:26
  38.9 0.7 %shard_map.92 = (f32[64,576]{1,0:T(8,128)}, f32[1,64]{1,0:T(1,128)}) custom-call(f32[160,128]{1,0:T(8,128)S(1)} %shard_map.91.mine, f32[160,128]{1,0:T(8,128)S(1)} %collective-permute-done.14.other), custom_call_target="tpu_custom_call" | custom-call | tf_op jit(solution)/shard_map/pallas_call | solution.py:26
  (33 shorter events, 4.7 us)
Async XLA Ops:
  0.6 1.0 %copy-start = (bf16[1,64,4096]{2,1,0:T(8,128)(2,1)S(1)}, bf16[1,64,4096]{2,1,0:T(8,128)(2,1)}, u32[]{:S(2)}) copy-start(bf16[1,64,4096]{2,1,0:T(8,128)(2,1)} %param.5) | copy-start | bytes 1572868
  1.7 6.6 %copy-start.3 = (bf16[576,64]{0,1:T(8,128)(2,1)S(1)}, bf16[576,64]{0,1:T(8,128)(2,1)}, u32[]{:S(2)}) copy-start(bf16[576,64]{0,1:T(8,128)(2,1)} %param.6) | copy-start | bytes 221188
  1.7 7.7 %collective-permute-start.2 = (bf16[64,128]{1,0:T(8,128)(2,1)S(1)}, bf16[64,128]{1,0:T(8,128)(2,1)S(1)}, u32[]{:S(2)}, u32[]{:S(2)}) collective-permute-start(bf16[64,128]{1,0:T(8,128)(2,1)S(1)} %get-tuple-element.64.refs_0_), channel_id=1, source_target_pairs={{0,8},{1,9},{2,10},{3,11},{4,12},{5,13},{6,14},{7,15},{8,0},{9,1},... | collective-permute-start | bytes 49160 | tf_op jit(solution)/shard_map/ppermute | solution.py:491
  5.8 5.5 %collective-permute-start.1 = (bf16[64,128]{1,0:T(8,128)(2,1)S(1)}, bf16[64,128]{1,0:T(8,128)(2,1)S(1)}, u32[]{:S(2)}, u32[]{:S(2)}) collective-permute-start(bf16[64,128]{1,0:T(8,128)(2,1)S(1)} %get-tuple-element.64.refs_0_), channel_id=1, source_target_pairs={{0,12},{1,13},{2,14},{3,15},{4,8},{5,9},{6,10},{7,11},{8,4},{9,5},... | collective-permute-start | bytes 49160 | tf_op jit(solution)/shard_map/ppermute | solution.py:491
  7.2 4.2 %collective-permute-start = (bf16[64,128]{1,0:T(8,128)(2,1)S(1)}, bf16[64,128]{1,0:T(8,128)(2,1)S(1)}, u32[]{:S(2)}, u32[]{:S(2)}) collective-permute-start(bf16[64,128]{1,0:T(8,128)(2,1)S(1)} %get-tuple-element.64.refs_0_), channel_id=1, source_target_pairs={{0,4},{1,5},{2,6},{3,7},{4,0},{5,1},{6,2},{7,3},{8,12},{9,13},{10,... | collective-permute-start | bytes 49160 | tf_op jit(solution)/shard_map/ppermute | solution.py:491
  8.4 6.5 %copy-start.1 = (bf16[1,64,4096]{2,1,0:T(8,128)(2,1)S(1)}, bf16[1,64,4096]{2,1,0:T(8,128)(2,1)}, u32[]{:S(2)}) copy-start(bf16[1,64,4096]{2,1,0:T(8,128)(2,1)} %param.8) | copy-start | bytes 1572868
  11.4 6.4 %collective-permute-start.5 = (bf16[256,128]{1,0:T(8,128)(2,1)S(1)}, bf16[256,128]{1,0:T(8,128)(2,1)S(1)}, u32[]{:S(2)}, u32[]{:S(2)}) collective-permute-start(bf16[256,128]{1,0:T(8,128)(2,1)S(1)} %shard_map.80.rows_a), channel_id=1, source_target_pairs={{0,3},{1,2},{2,1},{3,0},{4,7},{5,6},{6,5},{7,4},{8,11},{9,10},{10,... | collective-permute-start | bytes 196616 | tf_op jit(solution)/shard_map/ppermute | solution.py:491
  13.9 4.3 %collective-permute-start.4 = (bf16[256,128]{1,0:T(8,128)(2,1)S(1)}, bf16[256,128]{1,0:T(8,128)(2,1)S(1)}, u32[]{:S(2)}, u32[]{:S(2)}) collective-permute-start(bf16[256,128]{1,0:T(8,128)(2,1)S(1)} %shard_map.80.rows_a), channel_id=1, source_target_pairs={{0,2},{1,3},{2,0},{3,1},{4,6},{5,7},{6,4},{7,5},{8,10},{9,11},{10,... | collective-permute-start | bytes 196616 | tf_op jit(solution)/shard_map/ppermute | solution.py:491
  14.4 4.3 %collective-permute-start.3 = (bf16[256,128]{1,0:T(8,128)(2,1)S(1)}, bf16[256,128]{1,0:T(8,128)(2,1)S(1)}, u32[]{:S(2)}, u32[]{:S(2)}) collective-permute-start(bf16[256,128]{1,0:T(8,128)(2,1)S(1)} %shard_map.80.rows_a), channel_id=1, source_target_pairs={{0,1},{1,0},{2,3},{3,2},{4,5},{5,4},{6,7},{7,6},{8,9},{9,8},{10,11... | collective-permute-start | bytes 196616 | tf_op jit(solution)/shard_map/ppermute | solution.py:491
  14.9 0.7 %copy-start.4 = (f32[64]{0:T(128)S(1)}, f32[64]{0:T(128)}, u32[]{:S(2)}) copy-start(f32[64]{0:T(128)} %param.7) | copy-start | bytes 772
  14.9 3.7 %collective-permute-start.6 = (bf16[64,128]{1,0:T(8,128)(2,1)S(1)}, bf16[64,128]{1,0:T(8,128)(2,1)S(1)}, u32[]{:S(2)}, u32[]{:S(2)}) collective-permute-start(bf16[64,128]{1,0:T(8,128)(2,1)S(1)} %get-tuple-element.88), channel_id=1, source_target_pairs={{0,16},{16,0},{1,17},{17,1},{2,18},{18,2},{3,19},{19,3},{4,20},{20... | collective-permute-start | bytes 49160 | tf_op jit(solution)/shard_map/ppermute | solution.py:491
  15.6 1.8 %copy-start.2 = (s32[16,260]{1,0:T(8,128)S(1)}, s32[16,260]{1,0:T(8,128)}, u32[]{:S(2)}) copy-start(s32[16,260]{1,0:T(8,128)} %index_ref.1) | copy-start | bytes 49924
  20.0 1.3 %collective-permute-start.7 = (bf16[224,128]{1,0:T(8,128)(2,1)S(1)}, bf16[224,128]{1,0:T(8,128)(2,1)S(1)}, u32[]{:S(2)}, u32[]{:S(2)}) collective-permute-start(bf16[224,128]{1,0:T(8,128)(2,1)S(1)} %get-tuple-element.93), channel_id=1, source_target_pairs={{0,16},{16,0},{1,17},{17,1},{2,18},{18,2},{3,19},{19,3},{4,20},{20... | collective-permute-start | bytes 172040 | tf_op jit(solution)/shard_map/ppermute | solution.py:491
  21.3 6.4 %collective-permute-start.10 = (bf16[224,128]{1,0:T(8,128)(2,1)S(1)}, bf16[224,128]{1,0:T(8,128)(2,1)S(1)}, u32[]{:S(2)}, u32[]{:S(2)}) collective-permute-start(bf16[224,128]{1,0:T(8,128)(2,1)S(1)} %shard_map.85.refs_0_), channel_id=1, source_target_pairs={{0,8},{1,9},{2,10},{3,11},{4,12},{5,13},{6,14},{7,15},{8,0},{9,1},... | collective-permute-start | bytes 172040 | tf_op jit(solution)/shard_map/ppermute | solution.py:491
  22.6 6.2 %collective-permute-start.9 = (bf16[224,128]{1,0:T(8,128)(2,1)S(1)}, bf16[224,128]{1,0:T(8,128)(2,1)S(1)}, u32[]{:S(2)}, u32[]{:S(2)}) collective-permute-start(bf16[224,128]{1,0:T(8,128)(2,1)S(1)} %shard_map.85.refs_0_), channel_id=1, source_target_pairs={{0,12},{1,13},{2,14},{3,15},{4,8},{5,9},{6,10},{7,11},{8,4},{9,5},... | collective-permute-start | bytes 172040 | tf_op jit(solution)/shard_map/ppermute | solution.py:491
  23.6 5.7 %collective-permute-start.8 = (bf16[224,128]{1,0:T(8,128)(2,1)S(1)}, bf16[224,128]{1,0:T(8,128)(2,1)S(1)}, u32[]{:S(2)}, u32[]{:S(2)}) collective-permute-start(bf16[224,128]{1,0:T(8,128)(2,1)S(1)} %shard_map.85.refs_0_), channel_id=1, source_target_pairs={{0,4},{1,5},{2,6},{3,7},{4,0},{5,1},{6,2},{7,3},{8,12},{9,13},{10,... | collective-permute-start | bytes 172040 | tf_op jit(solution)/shard_map/ppermute | solution.py:491
  29.4 6.6 %collective-permute-start.13 = (bf16[416,128]{1,0:T(8,128)(2,1)S(1)}, bf16[416,128]{1,0:T(8,128)(2,1)S(1)}, u32[]{:S(2)}, u32[]{:S(2)}) collective-permute-start(bf16[416,128]{1,0:T(8,128)(2,1)S(1)} %shard_map.88.row_a.refs_0_), channel_id=1, source_target_pairs={{0,3},{1,2},{2,1},{3,0},{4,7},{5,6},{6,5},{7,4},{8,11},{9,10},{10,... | collective-permute-start | bytes 319496 | tf_op jit(solution)/shard_map/ppermute | solution.py:491
  31.0 6.5 %collective-permute-start.12 = (bf16[416,128]{1,0:T(8,128)(2,1)S(1)}, bf16[416,128]{1,0:T(8,128)(2,1)S(1)}, u32[]{:S(2)}, u32[]{:S(2)}) collective-permute-start(bf16[416,128]{1,0:T(8,128)(2,1)S(1)} %shard_map.88.row_a.refs_0_), channel_id=1, source_target_pairs={{0,2},{1,3},{2,0},{3,1},{4,6},{5,7},{6,4},{7,5},{8,10},{9,11},{10,... | collective-permute-start | bytes 319496 | tf_op jit(solution)/shard_map/ppermute | solution.py:491
  31.5 6.1 %collective-permute-start.11 = (bf16[416,128]{1,0:T(8,128)(2,1)S(1)}, bf16[416,128]{1,0:T(8,128)(2,1)S(1)}, u32[]{:S(2)}, u32[]{:S(2)}) collective-permute-start(bf16[416,128]{1,0:T(8,128)(2,1)S(1)} %shard_map.88.row_a.refs_0_), channel_id=1, source_target_pairs={{0,1},{1,0},{2,3},{3,2},{4,5},{5,4},{6,7},{7,6},{8,9},{9,8},{10,11... | collective-permute-start | bytes 319496 | tf_op jit(solution)/shard_map/ppermute | solution.py:491
  37.6 1.3 %collective-permute-start.14 = (f32[160,128]{1,0:T(8,128)S(1)}, f32[160,128]{1,0:T(8,128)S(1)}, u32[]{:S(2)}, u32[]{:S(2)}) collective-permute-start(f32[160,128]{1,0:T(8,128)S(1)} %shard_map.91.mine), channel_id=1, source_target_pairs={{0,16},{16,0},{1,17},{17,1},{2,18},{18,2},{3,19},{19,3},{4,20},{20... | collective-permute-start | bytes 245768 | tf_op jit(solution)/shard_map/ppermute | solution.py:491

commit v9 on v8

--- a/solution.py
+++ b/solution.py
@@ -94,15 +94,12 @@
     return total
 
 
-def rim_kernel(x_ref, rows_ref, cols_ref, scr):
+def rim_kernel(top, bottom, rows_ref, scr):
     for q in range(PAIRS):
         lanes = slice(q * LANES, (q + 1) * LANES)
-        scr[q : q + 1, :] = x_ref[0:16, lanes].astype(F32)[0:1]
-        scr[PAIRS + q : PAIRS + q + 1, :] = x_ref[SIDE - 16 : SIDE, lanes].astype(F32)[15:16]
+        scr[q : q + 1, :] = top[:, lanes].astype(F32)[0:1]
+        scr[PAIRS + q : PAIRS + q + 1, :] = bottom[:, lanes].astype(F32)[15:16]
     rows_ref[...] = scr[...].astype(BF16)
-    first = x_ref[:, 0:LANES].astype(F32)
-    last = x_ref[:, (PAIRS - 1) * LANES :].astype(F32)
-    cols_ref[...] = halves(first, last).astype(BF16)
 
 
 def rows_kernel(*refs):
@@ -190,7 +187,10 @@
         wc_ref[a, c:, :] = pair(a, None, 2)
 
 
-def copies_kernel(x_ref, p0, p1, p2, lines):
+def copies_kernel(x_ref, p0, p1, p2, lines, cols_ref):
+    first = x_ref[:, 0:LANES].astype(F32)
+    last = x_ref[:, (PAIRS - 1) * LANES :].astype(F32)
+    cols_ref[...] = halves(first, last).astype(BF16)
     shifted_copies(lambda q: x_ref[:, tile(q)].astype(F32), p0, p1, p2, lines)
 
 
@@ -538,17 +538,21 @@
     cot = cotangent.reshape(SIDE, SIDE * CHANNELS)
     pair = ((ROWS + SIDE, LANES), BF16)
 
-    rows, cols = call(rim_kernel, [((SIDE, LANES), BF16)] * 2, x, scratch=[pltpu.VMEM((SIDE, LANES), F32)])
+    rows = call(
+        rim_kernel, [((SIDE, LANES), BF16)], x[:16], x[SIDE - 16 :], scratch=[pltpu.VMEM((SIDE, LANES), F32)]
+    )[0]
+    count = 272
+    both = ((ROWS, LANES), F32)
+    work = dict(flops=2 * ROWS * 768 * 128, moved=3 * 2**20)
+
+    others = exchange(rows, rounds[0], FAR_ORDER)
+    *copies, lines, cols = call(
+        copies_kernel, [pair] * 3 + [((4, 40, LANES), F32), ((SIDE, LANES), BF16)], x, moved=2 * 2**20
+    )
     if regions == 2:
         cols = swap(cols, "region", 1)
     else:
         cols = jnp.concatenate([shift(cols, "region", 1), shift(cols, "region", -1)], axis=0)
-    count = 272
-    both = ((ROWS, LANES), F32)
-    work = dict(flops=2 * ROWS * 768 * 128, moved=3 * 2**20)
-
-    others = exchange(rows, rounds[0], FAR_ORDER)
-    *copies, lines = call(copies_kernel, [pair] * 3 + [((4, 40, LANES), F32)], x, moved=2 * 2**20)
     forward, backward, columns = call(
         weights_kernel,
         [((3, LANES, 2 * LANES), BF16), ((3, 2 * LANES, LANES), BF16), ((3, LANES, LANES), BF16)],

time: 39.8 us -> 39.8 us (level)
    slice x0 -> x1, local copies, waits for them, and re-layouts: none -> 1.04 us  [body(): x[SIDE - 16:]]
    unnamed x10, local copies, waits for them, and re-layouts: 1.7 us -> 0.67 us
where the time goes in v9:
time: 39.8 us; the launch traced here: 39.6 us
  starting transfers between devices  16.5 us (41%)
  waiting for transfers between devices  10.9 us (27%)
  Pallas kernels  9.77 us (25%)
  local copies, waits for them, and re-layouts  1.71 us (4%)
  between operations  0.79 us (2%)
    ppermute x15, starting transfers between devices, swap(): return lax.ppermute(x, axis, [(i, i ^ k) for i in range(n)])  16.5 us
    ppermute x15, waiting for transfers between devices, swap(): return lax.ppermute(x, axis, [(i, i ^ k) for i in range(n)])  10.9 us
    pallas_call x17, Pallas kernels, call(): pl.pallas_call(kernel, out_shape=shapes, in_specs=[whole] * len(args), ou...  9.77 us
    slice x1, local copies, waits for them, and re-layouts, body(): x[SIDE - 16:]  1.04 us
  transfers between devices with their start and end apart: 15, of which 11 were waited for; matrix products, arithmetic and copies ran while one was open for 0% of the time, Pallas kernels for 19%

profile of v9, /device:TPU:0, one launch (start us, length us, event | category | flops | bytes accessed | tf_op | source)
XLA Modules:
  0.0 39.6 jit_solution(9563461247851449796)
XLA Ops:
  0.6 1.0 %slice_bitcast_fusion = (bf16[16,4096]{1,0:T(8,128)(2,1)S(1)}, bf16[16,4096]{1,0:T(8,128)(2,1)S(1)}) fusion(bf16[1,64,4096]{2,1,0:T(8,128)(2,1)} %param.5), kind=kLoop, calls=%fused_computation | loop fusion | bytes 524288 | tf_op jit(solution)/shard_map/slice | solution.py:542
  1.7 4.1 %collective-permute-start.2 = (bf16[64,128]{1,0:T(8,128)(2,1)S(1)}, bf16[64,128]{1,0:T(8,128)(2,1)S(1)}, u32[]{:S(2)}, u32[]{:S(2)}) collective-permute-start(bf16[64,128]{1,0:T(8,128)(2,1)S(1)} %shard_map.76.refs_0_), channel_id=1, source_target_pairs={{0,8},{1,9},{2,10},{3,11},{4,12},{5,13},{6,14},{7,15},{8,0},{9,1},... | collective-permute-start | bytes 49160 | tf_op jit(solution)/shard_map/ppermute | solution.py:491
  5.8 1.3 %collective-permute-start.1 = (bf16[64,128]{1,0:T(8,128)(2,1)S(1)}, bf16[64,128]{1,0:T(8,128)(2,1)S(1)}, u32[]{:S(2)}, u32[]{:S(2)}) collective-permute-start(bf16[64,128]{1,0:T(8,128)(2,1)S(1)} %shard_map.76.refs_0_), channel_id=1, source_target_pairs={{0,12},{1,13},{2,14},{3,15},{4,8},{5,9},{6,10},{7,11},{8,4},{9,5},... | collective-permute-start | bytes 49160 | tf_op jit(solution)/shard_map/ppermute | solution.py:491
  7.5 0.9 %shard_map.77 = (bf16[2112,128]{1,0:T(8,128)(2,1)S(1)}, bf16[2112,128]{1,0:T(8,128)(2,1)S(1)}, bf16[2112,128]{1,0:T(8,128)(2,1)S(1)}, f32[4,40,128]{2,1,0:T(8,128)S(1)}, bf16[64,128]{1,0:T(8,128)(2,1)S(1)}) custom-call(bf16[64,4096]{1,0:T(8,128)(2,1)S(1)} %bitcast.13), custom_call_target="tpu_custom_call" | custom-call | bytes 2097152 | tf_op jit(solution)/shard_map/pallas_call | solution.py:26
  8.4 1.0 %shard_map.79.s_ref = f32[2048,128]{1,0:T(8,128)S(1)} custom-call(bf16[2112,128]{1,0:T(8,128)(2,1)S(1)} %get-tuple-element.63.p0, bf16[2112,128]{1,0:T(8,128)(2,1)S(1)} %get-tuple-element.64.p1, bf16[2112,128]{1,0:T(8,128)(2,1)S(1)} %get-tuple-element.65.p2, bf16[3,128,256]{2,1,0:T(8,128)(2,1)S(1)} %get-tuple-element.66.w_ref), custom_call_target="tpu_custom_call" | custom-call | flops 402653184 | bytes 3145728 | tf_op jit(solution)/shard_map/pallas_call | solution.py:26
  9.4 1.9 %collective-permute-done.1.refs_2_ = bf16[64,128]{1,0:T(8,128)(2,1)S(1)} collective-permute-done((bf16[64,128]{1,0:T(8,128)(2,1)S(1)}, bf16[64,128]{1,0:T(8,128)(2,1)S(1)}, u32[]{:S(2)}, u32[]{:S(2)}) %collective-permute-start.1) | collective-permute-done | bytes 16416 | tf_op jit(solution)/shard_map/ppermute | solution.py:491
  11.4 2.5 %collective-permute-start.5 = (bf16[256,128]{1,0:T(8,128)(2,1)S(1)}, bf16[256,128]{1,0:T(8,128)(2,1)S(1)}, u32[]{:S(2)}, u32[]{:S(2)}) collective-permute-start(bf16[256,128]{1,0:T(8,128)(2,1)S(1)} %shard_map.80.rows_a), channel_id=1, source_target_pairs={{0,3},{1,2},{2,1},{3,0},{4,7},{5,6},{6,5},{7,4},{8,11},{9,10},{10,... | collective-permute-start | bytes 196616 | tf_op jit(solution)/shard_map/ppermute | solution.py:491
  14.9 0.6 %copy-done.4 = f32[64]{0:T(128)S(1)} copy-done((f32[64]{0:T(128)S(1)}, f32[64]{0:T(128)}, u32[]{:S(2)}) %copy-start.4) | copy-done | bytes 280
  15.6 1.8 %shard_map.82 = (bf16[2048,128]{1,0:T(8,128)(2,1)S(1)}, f32[3,128,256]{2,1,0:T(8,128)S(1)}, f32[8,128]{1,0:T(8,128)S(1)}, f32[64,128]{1,0:T(8,128)S(1)}) custom-call(f32[2048,128]{1,0:T(8,128)S(1)} %shard_map.79.s_ref, f32[1,64]{1,0:T(1,128)S(1)} %bitcast.15, bf16[64,4096]{1,0:T(8,128)(2,1)S(1)} %bitcast.11, bf16[2112,128]{1,0:T(8,128)(2,1)S(1)} %get-tuple-element.63.p0, ...), custom_call_target="tpu_custom_call" | custom-call | flops 402653184 | bytes 3145728 | tf_op jit(solution)/shard_map/pallas_call | solution.py:26
  18.7 1.3 %shard_map.83 = (f32[64,128]{1,0:T(8,128)S(1)}, bf16[128,128]{1,0:T(8,128)(2,1)S(1)}, bf16[160,128]{1,0:T(8,128)(2,1)S(1)}, bf16[224,128]{1,0:T(8,128)(2,1)S(1)}) custom-call(f32[2048,128]{1,0:T(8,128)S(1)} %shard_map.79.s_ref, f32[1,64]{1,0:T(1,128)S(1)} %bitcast.16, bf16[64,4096]{1,0:T(8,128)(2,1)S(1)} %bitcast.12, ...), custom_call_target="tpu_custom_call" | custom-call | bytes 1048576 | tf_op jit(solution)/shard_map/pallas_call | solution.py:26
  20.4 0.9 %collective-permute-done.7.other.rest_0_ = bf16[224,128]{1,0:T(8,128)(2,1)S(1)} collective-permute-done((bf16[224,128]{1,0:T(8,128)(2,1)S(1)}, bf16[224,128]{1,0:T(8,128)(2,1)S(1)}, u32[]{:S(2)}, u32[]{:S(2)}) %collective-permute-start.7) | collective-permute-done | bytes 57376 | tf_op jit(solution)/shard_map/ppermute | solution.py:491
  21.3 1.2 %collective-permute-start.10 = (bf16[224,128]{1,0:T(8,128)(2,1)S(1)}, bf16[224,128]{1,0:T(8,128)(2,1)S(1)}, u32[]{:S(2)}, u32[]{:S(2)}) collective-permute-start(bf16[224,128]{1,0:T(8,128)(2,1)S(1)} %shard_map.85.refs_0_), channel_id=1, source_target_pairs={{0,8},{1,9},{2,10},{3,11},{4,12},{5,13},{6,14},{7,15},{8,0},{9,1},... | collective-permute-start | bytes 172040 | tf_op jit(solution)/shard_map/ppermute | solution.py:491
  22.6 1.1 %collective-permute-start.9 = (bf16[224,128]{1,0:T(8,128)(2,1)S(1)}, bf16[224,128]{1,0:T(8,128)(2,1)S(1)}, u32[]{:S(2)}, u32[]{:S(2)}) collective-permute-start(bf16[224,128]{1,0:T(8,128)(2,1)S(1)} %shard_map.85.refs_0_), channel_id=1, source_target_pairs={{0,12},{1,13},{2,14},{3,15},{4,8},{5,9},{6,10},{7,11},{8,4},{9,5},... | collective-permute-start | bytes 172040 | tf_op jit(solution)/shard_map/ppermute | solution.py:491
  23.6 1.3 %collective-permute-start.8 = (bf16[224,128]{1,0:T(8,128)(2,1)S(1)}, bf16[224,128]{1,0:T(8,128)(2,1)S(1)}, u32[]{:S(2)}, u32[]{:S(2)}) collective-permute-start(bf16[224,128]{1,0:T(8,128)(2,1)S(1)} %shard_map.85.refs_0_), channel_id=1, source_target_pairs={{0,4},{1,5},{2,6},{3,7},{4,0},{5,1},{6,2},{7,3},{8,12},{9,13},{10,... | collective-permute-start | bytes 172040 | tf_op jit(solution)/shard_map/ppermute | solution.py:491
  25.1 0.9 %shard_map.86 = (bf16[2112,128]{1,0:T(8,128)(2,1)S(1)}, bf16[2112,128]{1,0:T(8,128)(2,1)S(1)}, bf16[2112,128]{1,0:T(8,128)(2,1)S(1)}) custom-call(bf16[2048,128]{1,0:T(8,128)(2,1)S(1)} %get-tuple-element.99.g_ref, f32[64,128]{1,0:T(8,128)S(1)} %get-tuple-element.100.g_lines, bf16[128,128]{1,0:T(8,128)(2,1)S(1)} %get-tuple-element.101.g_sides), custom_call_target="tpu_custom_call" | custom-call | bytes 2097152 | tf_op jit(solution)/shard_map/pallas_call | solution.py:26
  26.0 1.7 %collective-permute-done.10.refs_3_ = bf16[224,128]{1,0:T(8,128)(2,1)S(1)} collective-permute-done((bf16[224,128]{1,0:T(8,128)(2,1)S(1)}, bf16[224,128]{1,0:T(8,128)(2,1)S(1)}, u32[]{:S(2)}, u32[]{:S(2)}) %collective-permute-start.10) | collective-permute-done | bytes 57376 | tf_op jit(solution)/shard_map/ppermute | solution.py:491
  27.7 1.0 %collective-permute-done.9.refs_2_ = bf16[224,128]{1,0:T(8,128)(2,1)S(1)} collective-permute-done((bf16[224,128]{1,0:T(8,128)(2,1)S(1)}, bf16[224,128]{1,0:T(8,128)(2,1)S(1)}, u32[]{:S(2)}, u32[]{:S(2)}) %collective-permute-start.9) | collective-permute-done | bytes 57376 | tf_op jit(solution)/shard_map/ppermute | solution.py:491
  29.4 1.6 %collective-permute-start.13 = (bf16[416,128]{1,0:T(8,128)(2,1)S(1)}, bf16[416,128]{1,0:T(8,128)(2,1)S(1)}, u32[]{:S(2)}, u32[]{:S(2)}) collective-permute-start(bf16[416,128]{1,0:T(8,128)(2,1)S(1)} %shard_map.88.row_a.refs_0_), channel_id=1, source_target_pairs={{0,3},{1,2},{2,1},{3,0},{4,7},{5,6},{6,5},{7,4},{8,11},{9,10},{10,... | collective-permute-start | bytes 319496 | tf_op jit(solution)/shard_map/ppermute | solution.py:491
  31.5 1.4 %collective-permute-start.11 = (bf16[416,128]{1,0:T(8,128)(2,1)S(1)}, bf16[416,128]{1,0:T(8,128)(2,1)S(1)}, u32[]{:S(2)}, u32[]{:S(2)}) collective-permute-start(bf16[416,128]{1,0:T(8,128)(2,1)S(1)} %shard_map.88.row_a.refs_0_), channel_id=1, source_target_pairs={{0,1},{1,0},{2,3},{3,2},{4,5},{5,4},{6,7},{7,6},{8,9},{9,8},{10,11... | collective-permute-start | bytes 319496 | tf_op jit(solution)/shard_map/ppermute | solution.py:491
  32.9 1.0 %shard_map.89.inner = f32[2048,128]{1,0:T(8,128)S(1)} custom-call(bf16[2112,128]{1,0:T(8,128)(2,1)S(1)} %get-tuple-element.113.p0, bf16[2112,128]{1,0:T(8,128)(2,1)S(1)} %get-tuple-element.114.p1, bf16[2112,128]{1,0:T(8,128)(2,1)S(1)} %get-tuple-element.115.p2, bf16[3,256,128]{2,1,0:T(8,128)(2,1)S(1)} %get-tuple-element.93.wb_ref), custom_call_target="tpu_custom_call" | custom-call | flops 402653184 | bytes 3145728 | tf_op jit(solution)/shard_map/pallas_call | solution.py:26
  33.9 2.0 %collective-permute-done.13.row_d.refs_3_ = bf16[416,128]{1,0:T(8,128)(2,1)S(1)} collective-permute-done((bf16[416,128]{1,0:T(8,128)(2,1)S(1)}, bf16[416,128]{1,0:T(8,128)(2,1)S(1)}, u32[]{:S(2)}, u32[]{:S(2)}) %collective-permute-start.13) | collective-permute-done | bytes 106528 | tf_op jit(solution)/shard_map/ppermute | solution.py:491
  36.0 1.5 %collective-permute-done.12.row_c.refs_2_ = bf16[416,128]{1,0:T(8,128)(2,1)S(1)} collective-permute-done((bf16[416,128]{1,0:T(8,128)(2,1)S(1)}, bf16[416,128]{1,0:T(8,128)(2,1)S(1)}, u32[]{:S(2)}, u32[]{:S(2)}) %collective-permute-start.12) | collective-permute-done | bytes 106528 | tf_op jit(solution)/shard_map/ppermute | solution.py:491
  37.7 1.2 %shard_map.90 = bf16[64,4096]{1,0:T(8,128)(2,1)} custom-call(bf16[416,128]{1,0:T(8,128)(2,1)S(1)} %shard_map.88.row_a.refs_0_, bf16[416,128]{1,0:T(8,128)(2,1)S(1)} %collective-permute-done.11.row_b.refs_1_, bf16[416,128]{1,0:T(8,128)(2,1)S(1)} %collective-permute-done.12.row_c.refs_2_, bf16[416,128]{1,0:T(8,128)(2,1)S(1)} %collective-permute-done.13.row_d.refs_3_, ...), custom_call_target="tpu_custom_call" | custom-call | bytes 2097152 | tf_op jit(solution)/shard_map/pallas_call | solution.py:26
  39.0 0.7 %shard_map.92 = (f32[64,576]{1,0:T(8,128)}, f32[1,64]{1,0:T(1,128)}) custom-call(f32[160,128]{1,0:T(8,128)S(1)} %shard_map.91.mine, f32[160,128]{1,0:T(8,128)S(1)} %collective-permute-done.14.other), custom_call_target="tpu_custom_call" | custom-call | tf_op jit(solution)/shard_map/pallas_call | solution.py:26
  (34 shorter events, 4.7 us)
Async XLA Ops:
  0.6 6.9 %copy-start.1 = (bf16[1,64,4096]{2,1,0:T(8,128)(2,1)S(1)}, bf16[1,64,4096]{2,1,0:T(8,128)(2,1)}, u32[]{:S(2)}) copy-start(bf16[1,64,4096]{2,1,0:T(8,128)(2,1)} %param.5) | copy-start | bytes 1572868
  1.7 5.7 %copy-start.3 = (bf16[576,64]{0,1:T(8,128)(2,1)S(1)}, bf16[576,64]{0,1:T(8,128)(2,1)}, u32[]{:S(2)}) copy-start(bf16[576,64]{0,1:T(8,128)(2,1)} %param.6) | copy-start | bytes 221188
  1.7 7.7 %collective-permute-start.2 = (bf16[64,128]{1,0:T(8,128)(2,1)S(1)}, bf16[64,128]{1,0:T(8,128)(2,1)S(1)}, u32[]{:S(2)}, u32[]{:S(2)}) collective-permute-start(bf16[64,128]{1,0:T(8,128)(2,1)S(1)} %shard_map.76.refs_0_), channel_id=1, source_target_pairs={{0,8},{1,9},{2,10},{3,11},{4,12},{5,13},{6,14},{7,15},{8,0},{9,1},... | collective-permute-start | bytes 49160 | tf_op jit(solution)/shard_map/ppermute | solution.py:491
  5.8 5.5 %collective-permute-start.1 = (bf16[64,128]{1,0:T(8,128)(2,1)S(1)}, bf16[64,128]{1,0:T(8,128)(2,1)S(1)}, u32[]{:S(2)}, u32[]{:S(2)}) collective-permute-start(bf16[64,128]{1,0:T(8,128)(2,1)S(1)} %shard_map.76.refs_0_), channel_id=1, source_target_pairs={{0,12},{1,13},{2,14},{3,15},{4,8},{5,9},{6,10},{7,11},{8,4},{9,5},... | collective-permute-start | bytes 49160 | tf_op jit(solution)/shard_map/ppermute | solution.py:491
  7.2 4.2 %collective-permute-start = (bf16[64,128]{1,0:T(8,128)(2,1)S(1)}, bf16[64,128]{1,0:T(8,128)(2,1)S(1)}, u32[]{:S(2)}, u32[]{:S(2)}) collective-permute-start(bf16[64,128]{1,0:T(8,128)(2,1)S(1)} %shard_map.76.refs_0_), channel_id=1, source_target_pairs={{0,4},{1,5},{2,6},{3,7},{4,0},{5,1},{6,2},{7,3},{8,12},{9,13},{10,... | collective-permute-start | bytes 49160 | tf_op jit(solution)/shard_map/ppermute | solution.py:491
  8.4 6.5 %copy-start = (bf16[1,64,4096]{2,1,0:T(8,128)(2,1)S(1)}, bf16[1,64,4096]{2,1,0:T(8,128)(2,1)}, u32[]{:S(2)}) copy-start(bf16[1,64,4096]{2,1,0:T(8,128)(2,1)} %param.8) | copy-start | bytes 1572868
  11.4 6.4 %collective-permute-start.5 = (bf16[256,128]{1,0:T(8,128)(2,1)S(1)}, bf16[256,128]{1,0:T(8,128)(2,1)S(1)}, u32[]{:S(2)}, u32[]{:S(2)}) collective-permute-start(bf16[256,128]{1,0:T(8,128)(2,1)S(1)} %shard_map.80.rows_a), channel_id=1, source_target_pairs={{0,3},{1,2},{2,1},{3,0},{4,7},{5,6},{6,5},{7,4},{8,11},{9,10},{10,... | collective-permute-start | bytes 196616 | tf_op jit(solution)/shard_map/ppermute | solution.py:491
  13.9 4.3 %collective-permute-start.4 = (bf16[256,128]{1,0:T(8,128)(2,1)S(1)}, bf16[256,128]{1,0:T(8,128)(2,1)S(1)}, u32[]{:S(2)}, u32[]{:S(2)}) collective-permute-start(bf16[256,128]{1,0:T(8,128)(2,1)S(1)} %shard_map.80.rows_a), channel_id=1, source_target_pairs={{0,2},{1,3},{2,0},{3,1},{4,6},{5,7},{6,4},{7,5},{8,10},{9,11},{10,... | collective-permute-start | bytes 196616 | tf_op jit(solution)/shard_map/ppermute | solution.py:491
  14.4 4.3 %collective-permute-start.3 = (bf16[256,128]{1,0:T(8,128)(2,1)S(1)}, bf16[256,128]{1,0:T(8,128)(2,1)S(1)}, u32[]{:S(2)}, u32[]{:S(2)}) collective-permute-start(bf16[256,128]{1,0:T(8,128)(2,1)S(1)} %shard_map.80.rows_a), channel_id=1, source_target_pairs={{0,1},{1,0},{2,3},{3,2},{4,5},{5,4},{6,7},{7,6},{8,9},{9,8},{10,11... | collective-permute-start | bytes 196616 | tf_op jit(solution)/shard_map/ppermute | solution.py:491
  14.9 0.7 %copy-start.4 = (f32[64]{0:T(128)S(1)}, f32[64]{0:T(128)}, u32[]{:S(2)}) copy-start(f32[64]{0:T(128)} %param.7) | copy-start | bytes 772
  14.9 3.7 %collective-permute-start.6 = (bf16[64,128]{1,0:T(8,128)(2,1)S(1)}, bf16[64,128]{1,0:T(8,128)(2,1)S(1)}, u32[]{:S(2)}, u32[]{:S(2)}) collective-permute-start(bf16[64,128]{1,0:T(8,128)(2,1)S(1)} %get-tuple-element.86), channel_id=1, source_target_pairs={{0,16},{16,0},{1,17},{17,1},{2,18},{18,2},{3,19},{19,3},{4,20},{20... | collective-permute-start | bytes 49160 | tf_op jit(solution)/shard_map/ppermute | solution.py:491
  15.6 1.8 %copy-start.2 = (s32[16,260]{1,0:T(8,128)S(1)}, s32[16,260]{1,0:T(8,128)}, u32[]{:S(2)}) copy-start(s32[16,260]{1,0:T(8,128)} %index_ref.1) | copy-start | bytes 49924
  20.0 1.3 %collective-permute-start.7 = (bf16[224,128]{1,0:T(8,128)(2,1)S(1)}, bf16[224,128]{1,0:T(8,128)(2,1)S(1)}, u32[]{:S(2)}, u32[]{:S(2)}) collective-permute-start(bf16[224,128]{1,0:T(8,128)(2,1)S(1)} %get-tuple-element.91), channel_id=1, source_target_pairs={{0,16},{16,0},{1,17},{17,1},{2,18},{18,2},{3,19},{19,3},{4,20},{20... | collective-permute-start | bytes 172040 | tf_op jit(solution)/shard_map/ppermute | solution.py:491
  21.3 6.4 %collective-permute-start.10 = (bf16[224,128]{1,0:T(8,128)(2,1)S(1)}, bf16[224,128]{1,0:T(8,128)(2,1)S(1)}, u32[]{:S(2)}, u32[]{:S(2)}) collective-permute-start(bf16[224,128]{1,0:T(8,128)(2,1)S(1)} %shard_map.85.refs_0_), channel_id=1, source_target_pairs={{0,8},{1,9},{2,10},{3,11},{4,12},{5,13},{6,14},{7,15},{8,0},{9,1},... | collective-permute-start | bytes 172040 | tf_op jit(solution)/shard_map/ppermute | solution.py:491
  22.6 6.2 %collective-permute-start.9 = (bf16[224,128]{1,0:T(8,128)(2,1)S(1)}, bf16[224,128]{1,0:T(8,128)(2,1)S(1)}, u32[]{:S(2)}, u32[]{:S(2)}) collective-permute-start(bf16[224,128]{1,0:T(8,128)(2,1)S(1)} %shard_map.85.refs_0_), channel_id=1, source_target_pairs={{0,12},{1,13},{2,14},{3,15},{4,8},{5,9},{6,10},{7,11},{8,4},{9,5},... | collective-permute-start | bytes 172040 | tf_op jit(solution)/shard_map/ppermute | solution.py:491
  23.6 5.7 %collective-permute-start.8 = (bf16[224,128]{1,0:T(8,128)(2,1)S(1)}, bf16[224,128]{1,0:T(8,128)(2,1)S(1)}, u32[]{:S(2)}, u32[]{:S(2)}) collective-permute-start(bf16[224,128]{1,0:T(8,128)(2,1)S(1)} %shard_map.85.refs_0_), channel_id=1, source_target_pairs={{0,4},{1,5},{2,6},{3,7},{4,0},{5,1},{6,2},{7,3},{8,12},{9,13},{10,... | collective-permute-start | bytes 172040 | tf_op jit(solution)/shard_map/ppermute | solution.py:491
  29.4 6.6 %collective-permute-start.13 = (bf16[416,128]{1,0:T(8,128)(2,1)S(1)}, bf16[416,128]{1,0:T(8,128)(2,1)S(1)}, u32[]{:S(2)}, u32[]{:S(2)}) collective-permute-start(bf16[416,128]{1,0:T(8,128)(2,1)S(1)} %shard_map.88.row_a.refs_0_), channel_id=1, source_target_pairs={{0,3},{1,2},{2,1},{3,0},{4,7},{5,6},{6,5},{7,4},{8,11},{9,10},{10,... | collective-permute-start | bytes 319496 | tf_op jit(solution)/shard_map/ppermute | solution.py:491
  31.0 6.5 %collective-permute-start.12 = (bf16[416,128]{1,0:T(8,128)(2,1)S(1)}, bf16[416,128]{1,0:T(8,128)(2,1)S(1)}, u32[]{:S(2)}, u32[]{:S(2)}) collective-permute-start(bf16[416,128]{1,0:T(8,128)(2,1)S(1)} %shard_map.88.row_a.refs_0_), channel_id=1, source_target_pairs={{0,2},{1,3},{2,0},{3,1},{4,6},{5,7},{6,4},{7,5},{8,10},{9,11},{10,... | collective-permute-start | bytes 319496 | tf_op jit(solution)/shard_map/ppermute | solution.py:491
  31.5 6.1 %collective-permute-start.11 = (bf16[416,128]{1,0:T(8,128)(2,1)S(1)}, bf16[416,128]{1,0:T(8,128)(2,1)S(1)}, u32[]{:S(2)}, u32[]{:S(2)}) collective-permute-start(bf16[416,128]{1,0:T(8,128)(2,1)S(1)} %shard_map.88.row_a.refs_0_), channel_id=1, source_target_pairs={{0,1},{1,0},{2,3},{3,2},{4,5},{5,4},{6,7},{7,6},{8,9},{9,8},{10,11... | collective-permute-start | bytes 319496 | tf_op jit(solution)/shard_map/ppermute | solution.py:491
  37.6 1.3 %collective-permute-start.14 = (f32[160,128]{1,0:T(8,128)S(1)}, f32[160,128]{1,0:T(8,128)S(1)}, u32[]{:S(2)}, u32[]{:S(2)}) collective-permute-start(f32[160,128]{1,0:T(8,128)S(1)} %shard_map.91.mine), channel_id=1, source_target_pairs={{0,16},{16,0},{1,17},{17,1},{2,18},{18,2},{3,19},{19,3},{4,20},{20... | collective-permute-start | bytes 245768 | tf_op jit(solution)/shard_map/ppermute | solution.py:491

commit v10 on v9

--- a/solution.py
+++ b/solution.py
@@ -221,7 +221,7 @@
         return bias + jnp.sum(g.astype(F32).reshape(8, 8, LANES), axis=0)
 
     cot_lines[...] = jnp.zeros(cot_lines.shape, F32)
-    bias_ref[...] = lax.fori_loop(1, PAIRS - 1, step, jnp.zeros((8, LANES), F32), unroll=2)
+    bias_ref[...] = lax.fori_loop(1, PAIRS - 1, step, jnp.zeros((8, LANES), F32), unroll=6)
     g_ref[0:SIDE, :] = jnp.zeros((SIDE, LANES), BF16)
     g_ref[ROWS - SIDE :, :] = jnp.zeros((SIDE, LANES), BF16)
     g = g_ref[SIDE : ROWS - SIDE, :]

time: 39.8 us -> 39.8 us (level)
  no operation moved by 1% of the time
where the time goes in v10:
time: 39.8 us; the launch traced here: 39.6 us
  starting transfers between devices  16.5 us (41%)
  waiting for transfers between devices  11 us (28%)
  Pallas kernels  9.65 us (24%)
  local copies, waits for them, and re-layouts  1.71 us (4%)
  between operations  0.79 us (2%)
    ppermute x15, starting transfers between devices, swap(): return lax.ppermute(x, axis, [(i, i ^ k) for i in range(n)])  16.5 us
    ppermute x15, waiting for transfers between devices, swap(): return lax.ppermute(x, axis, [(i, i ^ k) for i in range(n)])  11 us
    pallas_call x17, Pallas kernels, call(): pl.pallas_call(kernel, out_shape=shapes, in_specs=[whole] * len(args), ou...  9.65 us
    slice x1, local copies, waits for them, and re-layouts, body(): x[SIDE - 16:]  1.04 us
  transfers between devices with their start and end apart: 15, of which 11 were waited for; matrix products, arithmetic and copies ran while one was open for 0% of the time, Pallas kernels for 19%

profile of v10, /device:TPU:0, one launch (start us, length us, event | category | flops | bytes accessed | tf_op | source)
XLA Modules:
  0.0 39.6 jit_solution(6952489957173832255)
XLA Ops:
  0.6 1.0 %slice_bitcast_fusion = (bf16[16,4096]{1,0:T(8,128)(2,1)S(1)}, bf16[16,4096]{1,0:T(8,128)(2,1)S(1)}) fusion(bf16[1,64,4096]{2,1,0:T(8,128)(2,1)} %param.5), kind=kLoop, calls=%fused_computation | loop fusion | bytes 524288 | tf_op jit(solution)/shard_map/slice | solution.py:542
  1.7 4.1 %collective-permute-start.2 = (bf16[64,128]{1,0:T(8,128)(2,1)S(1)}, bf16[64,128]{1,0:T(8,128)(2,1)S(1)}, u32[]{:S(2)}, u32[]{:S(2)}) collective-permute-start(bf16[64,128]{1,0:T(8,128)(2,1)S(1)} %shard_map.76.refs_0_), channel_id=1, source_target_pairs={{0,8},{1,9},{2,10},{3,11},{4,12},{5,13},{6,14},{7,15},{8,0},{9,1},... | collective-permute-start | bytes 49160 | tf_op jit(solution)/shard_map/ppermute | solution.py:491
  5.8 1.3 %collective-permute-start.1 = (bf16[64,128]{1,0:T(8,128)(2,1)S(1)}, bf16[64,128]{1,0:T(8,128)(2,1)S(1)}, u32[]{:S(2)}, u32[]{:S(2)}) collective-permute-start(bf16[64,128]{1,0:T(8,128)(2,1)S(1)} %shard_map.76.refs_0_), channel_id=1, source_target_pairs={{0,12},{1,13},{2,14},{3,15},{4,8},{5,9},{6,10},{7,11},{8,4},{9,5},... | collective-permute-start | bytes 49160 | tf_op jit(solution)/shard_map/ppermute | solution.py:491
  7.5 0.9 %shard_map.77 = (bf16[2112,128]{1,0:T(8,128)(2,1)S(1)}, bf16[2112,128]{1,0:T(8,128)(2,1)S(1)}, bf16[2112,128]{1,0:T(8,128)(2,1)S(1)}, f32[4,40,128]{2,1,0:T(8,128)S(1)}, bf16[64,128]{1,0:T(8,128)(2,1)S(1)}) custom-call(bf16[64,4096]{1,0:T(8,128)(2,1)S(1)} %bitcast.13), custom_call_target="tpu_custom_call" | custom-call | bytes 2097152 | tf_op jit(solution)/shard_map/pallas_call | solution.py:26
  8.4 1.0 %shard_map.79.s_ref = f32[2048,128]{1,0:T(8,128)S(1)} custom-call(bf16[2112,128]{1,0:T(8,128)(2,1)S(1)} %get-tuple-element.63.p0, bf16[2112,128]{1,0:T(8,128)(2,1)S(1)} %get-tuple-element.64.p1, bf16[2112,128]{1,0:T(8,128)(2,1)S(1)} %get-tuple-element.65.p2, bf16[3,128,256]{2,1,0:T(8,128)(2,1)S(1)} %get-tuple-element.66.w_ref), custom_call_target="tpu_custom_call" | custom-call | flops 402653184 | bytes 3145728 | tf_op jit(solution)/shard_map/pallas_call | solution.py:26
  9.4 1.9 %collective-permute-done.1.refs_2_ = bf16[64,128]{1,0:T(8,128)(2,1)S(1)} collective-permute-done((bf16[64,128]{1,0:T(8,128)(2,1)S(1)}, bf16[64,128]{1,0:T(8,128)(2,1)S(1)}, u32[]{:S(2)}, u32[]{:S(2)}) %collective-permute-start.1) | collective-permute-done | bytes 16416 | tf_op jit(solution)/shard_map/ppermute | solution.py:491
  11.4 2.5 %collective-permute-start.5 = (bf16[256,128]{1,0:T(8,128)(2,1)S(1)}, bf16[256,128]{1,0:T(8,128)(2,1)S(1)}, u32[]{:S(2)}, u32[]{:S(2)}) collective-permute-start(bf16[256,128]{1,0:T(8,128)(2,1)S(1)} %shard_map.80.rows_a), channel_id=1, source_target_pairs={{0,3},{1,2},{2,1},{3,0},{4,7},{5,6},{6,5},{7,4},{8,11},{9,10},{10,... | collective-permute-start | bytes 196616 | tf_op jit(solution)/shard_map/ppermute | solution.py:491
  14.9 0.6 %copy-done.4 = f32[64]{0:T(128)S(1)} copy-done((f32[64]{0:T(128)S(1)}, f32[64]{0:T(128)}, u32[]{:S(2)}) %copy-start.4) | copy-done | bytes 280
  15.6 1.7 %shard_map.82 = (bf16[2048,128]{1,0:T(8,128)(2,1)S(1)}, f32[3,128,256]{2,1,0:T(8,128)S(1)}, f32[8,128]{1,0:T(8,128)S(1)}, f32[64,128]{1,0:T(8,128)S(1)}) custom-call(f32[2048,128]{1,0:T(8,128)S(1)} %shard_map.79.s_ref, f32[1,64]{1,0:T(1,128)S(1)} %bitcast.15, bf16[64,4096]{1,0:T(8,128)(2,1)S(1)} %bitcast.11, bf16[2112,128]{1,0:T(8,128)(2,1)S(1)} %get-tuple-element.63.p0, ...), custom_call_target="tpu_custom_call" | custom-call | flops 402653184 | bytes 3145728 | tf_op jit(solution)/shard_map/pallas_call | solution.py:26
  18.7 1.3 %shard_map.83 = (f32[64,128]{1,0:T(8,128)S(1)}, bf16[128,128]{1,0:T(8,128)(2,1)S(1)}, bf16[160,128]{1,0:T(8,128)(2,1)S(1)}, bf16[224,128]{1,0:T(8,128)(2,1)S(1)}) custom-call(f32[2048,128]{1,0:T(8,128)S(1)} %shard_map.79.s_ref, f32[1,64]{1,0:T(1,128)S(1)} %bitcast.16, bf16[64,4096]{1,0:T(8,128)(2,1)S(1)} %bitcast.12, ...), custom_call_target="tpu_custom_call" | custom-call | bytes 1048576 | tf_op jit(solution)/shard_map/pallas_call | solution.py:26
  20.4 0.9 %collective-permute-done.7.other.rest_0_ = bf16[224,128]{1,0:T(8,128)(2,1)S(1)} collective-permute-done((bf16[224,128]{1,0:T(8,128)(2,1)S(1)}, bf16[224,128]{1,0:T(8,128)(2,1)S(1)}, u32[]{:S(2)}, u32[]{:S(2)}) %collective-permute-start.7) | collective-permute-done | bytes 57376 | tf_op jit(solution)/shard_map/ppermute | solution.py:491
  21.3 1.2 %collective-permute-start.10 = (bf16[224,128]{1,0:T(8,128)(2,1)S(1)}, bf16[224,128]{1,0:T(8,128)(2,1)S(1)}, u32[]{:S(2)}, u32[]{:S(2)}) collective-permute-start(bf16[224,128]{1,0:T(8,128)(2,1)S(1)} %shard_map.85.refs_0_), channel_id=1, source_target_pairs={{0,8},{1,9},{2,10},{3,11},{4,12},{5,13},{6,14},{7,15},{8,0},{9,1},... | collective-permute-start | bytes 172040 | tf_op jit(solution)/shard_map/ppermute | solution.py:491
  22.6 1.1 %collective-permute-start.9 = (bf16[224,128]{1,0:T(8,128)(2,1)S(1)}, bf16[224,128]{1,0:T(8,128)(2,1)S(1)}, u32[]{:S(2)}, u32[]{:S(2)}) collective-permute-start(bf16[224,128]{1,0:T(8,128)(2,1)S(1)} %shard_map.85.refs_0_), channel_id=1, source_target_pairs={{0,12},{1,13},{2,14},{3,15},{4,8},{5,9},{6,10},{7,11},{8,4},{9,5},... | collective-permute-start | bytes 172040 | tf_op jit(solution)/shard_map/ppermute | solution.py:491
  23.6 1.3 %collective-permute-start.8 = (bf16[224,128]{1,0:T(8,128)(2,1)S(1)}, bf16[224,128]{1,0:T(8,128)(2,1)S(1)}, u32[]{:S(2)}, u32[]{:S(2)}) collective-permute-start(bf16[224,128]{1,0:T(8,128)(2,1)S(1)} %shard_map.85.refs_0_), channel_id=1, source_target_pairs={{0,4},{1,5},{2,6},{3,7},{4,0},{5,1},{6,2},{7,3},{8,12},{9,13},{10,... | collective-permute-start | bytes 172040 | tf_op jit(solution)/shard_map/ppermute | solution.py:491
  25.1 0.9 %shard_map.86 = (bf16[2112,128]{1,0:T(8,128)(2,1)S(1)}, bf16[2112,128]{1,0:T(8,128)(2,1)S(1)}, bf16[2112,128]{1,0:T(8,128)(2,1)S(1)}) custom-call(bf16[2048,128]{1,0:T(8,128)(2,1)S(1)} %get-tuple-element.99.g_ref, f32[64,128]{1,0:T(8,128)S(1)} %get-tuple-element.100.g_lines, bf16[128,128]{1,0:T(8,128)(2,1)S(1)} %get-tuple-element.101.g_sides), custom_call_target="tpu_custom_call" | custom-call | bytes 2097152 | tf_op jit(solution)/shard_map/pallas_call | solution.py:26
  26.0 1.7 %collective-permute-done.10.refs_3_ = bf16[224,128]{1,0:T(8,128)(2,1)S(1)} collective-permute-done((bf16[224,128]{1,0:T(8,128)(2,1)S(1)}, bf16[224,128]{1,0:T(8,128)(2,1)S(1)}, u32[]{:S(2)}, u32[]{:S(2)}) %collective-permute-start.10) | collective-permute-done | bytes 57376 | tf_op jit(solution)/shard_map/ppermute | solution.py:491
  27.7 1.0 %collective-permute-done.9.refs_2_ = bf16[224,128]{1,0:T(8,128)(2,1)S(1)} collective-permute-done((bf16[224,128]{1,0:T(8,128)(2,1)S(1)}, bf16[224,128]{1,0:T(8,128)(2,1)S(1)}, u32[]{:S(2)}, u32[]{:S(2)}) %collective-permute-start.9) | collective-permute-done | bytes 57376 | tf_op jit(solution)/shard_map/ppermute | solution.py:491
  29.4 1.6 %collective-permute-start.13 = (bf16[416,128]{1,0:T(8,128)(2,1)S(1)}, bf16[416,128]{1,0:T(8,128)(2,1)S(1)}, u32[]{:S(2)}, u32[]{:S(2)}) collective-permute-start(bf16[416,128]{1,0:T(8,128)(2,1)S(1)} %shard_map.88.row_a.refs_0_), channel_id=1, source_target_pairs={{0,3},{1,2},{2,1},{3,0},{4,7},{5,6},{6,5},{7,4},{8,11},{9,10},{10,... | collective-permute-start | bytes 319496 | tf_op jit(solution)/shard_map/ppermute | solution.py:491
  31.5 1.5 %collective-permute-start.11 = (bf16[416,128]{1,0:T(8,128)(2,1)S(1)}, bf16[416,128]{1,0:T(8,128)(2,1)S(1)}, u32[]{:S(2)}, u32[]{:S(2)}) collective-permute-start(bf16[416,128]{1,0:T(8,128)(2,1)S(1)} %shard_map.88.row_a.refs_0_), channel_id=1, source_target_pairs={{0,1},{1,0},{2,3},{3,2},{4,5},{5,4},{6,7},{7,6},{8,9},{9,8},{10,11... | collective-permute-start | bytes 319496 | tf_op jit(solution)/shard_map/ppermute | solution.py:491
  32.9 1.0 %shard_map.89.inner = f32[2048,128]{1,0:T(8,128)S(1)} custom-call(bf16[2112,128]{1,0:T(8,128)(2,1)S(1)} %get-tuple-element.113.p0, bf16[2112,128]{1,0:T(8,128)(2,1)S(1)} %get-tuple-element.114.p1, bf16[2112,128]{1,0:T(8,128)(2,1)S(1)} %get-tuple-element.115.p2, bf16[3,256,128]{2,1,0:T(8,128)(2,1)S(1)} %get-tuple-element.93.wb_ref), custom_call_target="tpu_custom_call" | custom-call | flops 402653184 | bytes 3145728 | tf_op jit(solution)/shard_map/pallas_call | solution.py:26
  33.9 2.1 %collective-permute-done.13.row_d.refs_3_ = bf16[416,128]{1,0:T(8,128)(2,1)S(1)} collective-permute-done((bf16[416,128]{1,0:T(8,128)(2,1)S(1)}, bf16[416,128]{1,0:T(8,128)(2,1)S(1)}, u32[]{:S(2)}, u32[]{:S(2)}) %collective-permute-start.13) | collective-permute-done | bytes 106528 | tf_op jit(solution)/shard_map/ppermute | solution.py:491
  36.0 1.4 %collective-permute-done.12.row_c.refs_2_ = bf16[416,128]{1,0:T(8,128)(2,1)S(1)} collective-permute-done((bf16[416,128]{1,0:T(8,128)(2,1)S(1)}, bf16[416,128]{1,0:T(8,128)(2,1)S(1)}, u32[]{:S(2)}, u32[]{:S(2)}) %collective-permute-start.12) | collective-permute-done | bytes 106528 | tf_op jit(solution)/shard_map/ppermute | solution.py:491
  37.7 1.2 %shard_map.90 = bf16[64,4096]{1,0:T(8,128)(2,1)} custom-call(bf16[416,128]{1,0:T(8,128)(2,1)S(1)} %shard_map.88.row_a.refs_0_, bf16[416,128]{1,0:T(8,128)(2,1)S(1)} %collective-permute-done.11.row_b.refs_1_, bf16[416,128]{1,0:T(8,128)(2,1)S(1)} %collective-permute-done.12.row_c.refs_2_, bf16[416,128]{1,0:T(8,128)(2,1)S(1)} %collective-permute-done.13.row_d.refs_3_, ...), custom_call_target="tpu_custom_call" | custom-call | bytes 2097152 | tf_op jit(solution)/shard_map/pallas_call | solution.py:26
  39.0 0.7 %shard_map.92 = (f32[64,576]{1,0:T(8,128)}, f32[1,64]{1,0:T(1,128)}) custom-call(f32[160,128]{1,0:T(8,128)S(1)} %shard_map.91.mine, f32[160,128]{1,0:T(8,128)S(1)} %collective-permute-done.14.other), custom_call_target="tpu_custom_call" | custom-call | tf_op jit(solution)/shard_map/pallas_call | solution.py:26
  (34 shorter events, 4.8 us)
Async XLA Ops:
  0.6 6.9 %copy-start.1 = (bf16[1,64,4096]{2,1,0:T(8,128)(2,1)S(1)}, bf16[1,64,4096]{2,1,0:T(8,128)(2,1)}, u32[]{:S(2)}) copy-start(bf16[1,64,4096]{2,1,0:T(8,128)(2,1)} %param.5) | copy-start | bytes 1572868
  1.7 5.7 %copy-start.3 = (bf16[576,64]{0,1:T(8,128)(2,1)S(1)}, bf16[576,64]{0,1:T(8,128)(2,1)}, u32[]{:S(2)}) copy-start(bf16[576,64]{0,1:T(8,128)(2,1)} %param.6) | copy-start | bytes 221188
  1.7 7.7 %collective-permute-start.2 = (bf16[64,128]{1,0:T(8,128)(2,1)S(1)}, bf16[64,128]{1,0:T(8,128)(2,1)S(1)}, u32[]{:S(2)}, u32[]{:S(2)}) collective-permute-start(bf16[64,128]{1,0:T(8,128)(2,1)S(1)} %shard_map.76.refs_0_), channel_id=1, source_target_pairs={{0,8},{1,9},{2,10},{3,11},{4,12},{5,13},{6,14},{7,15},{8,0},{9,1},... | collective-permute-start | bytes 49160 | tf_op jit(solution)/shard_map/ppermute | solution.py:491
  5.8 5.5 %collective-permute-start.1 = (bf16[64,128]{1,0:T(8,128)(2,1)S(1)}, bf16[64,128]{1,0:T(8,128)(2,1)S(1)}, u32[]{:S(2)}, u32[]{:S(2)}) collective-permute-start(bf16[64,128]{1,0:T(8,128)(2,1)S(1)} %shard_map.76.refs_0_), channel_id=1, source_target_pairs={{0,12},{1,13},{2,14},{3,15},{4,8},{5,9},{6,10},{7,11},{8,4},{9,5},... | collective-permute-start | bytes 49160 | tf_op jit(solution)/shard_map/ppermute | solution.py:491
  7.2 4.2 %collective-permute-start = (bf16[64,128]{1,0:T(8,128)(2,1)S(1)}, bf16[64,128]{1,0:T(8,128)(2,1)S(1)}, u32[]{:S(2)}, u32[]{:S(2)}) collective-permute-start(bf16[64,128]{1,0:T(8,128)(2,1)S(1)} %shard_map.76.refs_0_), channel_id=1, source_target_pairs={{0,4},{1,5},{2,6},{3,7},{4,0},{5,1},{6,2},{7,3},{8,12},{9,13},{10,... | collective-permute-start | bytes 49160 | tf_op jit(solution)/shard_map/ppermute | solution.py:491
  8.4 6.5 %copy-start = (bf16[1,64,4096]{2,1,0:T(8,128)(2,1)S(1)}, bf16[1,64,4096]{2,1,0:T(8,128)(2,1)}, u32[]{:S(2)}) copy-start(bf16[1,64,4096]{2,1,0:T(8,128)(2,1)} %param.8) | copy-start | bytes 1572868
  11.4 6.2 %collective-permute-start.5 = (bf16[256,128]{1,0:T(8,128)(2,1)S(1)}, bf16[256,128]{1,0:T(8,128)(2,1)S(1)}, u32[]{:S(2)}, u32[]{:S(2)}) collective-permute-start(bf16[256,128]{1,0:T(8,128)(2,1)S(1)} %shard_map.80.rows_a), channel_id=1, source_target_pairs={{0,3},{1,2},{2,1},{3,0},{4,7},{5,6},{6,5},{7,4},{8,11},{9,10},{10,... | collective-permute-start | bytes 196616 | tf_op jit(solution)/shard_map/ppermute | solution.py:491
  13.9 4.3 %collective-permute-start.4 = (bf16[256,128]{1,0:T(8,128)(2,1)S(1)}, bf16[256,128]{1,0:T(8,128)(2,1)S(1)}, u32[]{:S(2)}, u32[]{:S(2)}) collective-permute-start(bf16[256,128]{1,0:T(8,128)(2,1)S(1)} %shard_map.80.rows_a), channel_id=1, source_target_pairs={{0,2},{1,3},{2,0},{3,1},{4,6},{5,7},{6,4},{7,5},{8,10},{9,11},{10,... | collective-permute-start | bytes 196616 | tf_op jit(solution)/shard_map/ppermute | solution.py:491
  14.4 4.3 %collective-permute-start.3 = (bf16[256,128]{1,0:T(8,128)(2,1)S(1)}, bf16[256,128]{1,0:T(8,128)(2,1)S(1)}, u32[]{:S(2)}, u32[]{:S(2)}) collective-permute-start(bf16[256,128]{1,0:T(8,128)(2,1)S(1)} %shard_map.80.rows_a), channel_id=1, source_target_pairs={{0,1},{1,0},{2,3},{3,2},{4,5},{5,4},{6,7},{7,6},{8,9},{9,8},{10,11... | collective-permute-start | bytes 196616 | tf_op jit(solution)/shard_map/ppermute | solution.py:491
  14.9 0.7 %copy-start.4 = (f32[64]{0:T(128)S(1)}, f32[64]{0:T(128)}, u32[]{:S(2)}) copy-start(f32[64]{0:T(128)} %param.7) | copy-start | bytes 772
  14.9 3.7 %collective-permute-start.6 = (bf16[64,128]{1,0:T(8,128)(2,1)S(1)}, bf16[64,128]{1,0:T(8,128)(2,1)S(1)}, u32[]{:S(2)}, u32[]{:S(2)}) collective-permute-start(bf16[64,128]{1,0:T(8,128)(2,1)S(1)} %get-tuple-element.86), channel_id=1, source_target_pairs={{0,16},{16,0},{1,17},{17,1},{2,18},{18,2},{3,19},{19,3},{4,20},{20... | collective-permute-start | bytes 49160 | tf_op jit(solution)/shard_map/ppermute | solution.py:491
  15.6 1.7 %copy-start.2 = (s32[16,260]{1,0:T(8,128)S(1)}, s32[16,260]{1,0:T(8,128)}, u32[]{:S(2)}) copy-start(s32[16,260]{1,0:T(8,128)} %index_ref.1) | copy-start | bytes 49924
  20.0 1.3 %collective-permute-start.7 = (bf16[224,128]{1,0:T(8,128)(2,1)S(1)}, bf16[224,128]{1,0:T(8,128)(2,1)S(1)}, u32[]{:S(2)}, u32[]{:S(2)}) collective-permute-start(bf16[224,128]{1,0:T(8,128)(2,1)S(1)} %get-tuple-element.91), channel_id=1, source_target_pairs={{0,16},{16,0},{1,17},{17,1},{2,18},{18,2},{3,19},{19,3},{4,20},{20... | collective-permute-start | bytes 172040 | tf_op jit(solution)/shard_map/ppermute | solution.py:491
  21.3 6.4 %collective-permute-start.10 = (bf16[224,128]{1,0:T(8,128)(2,1)S(1)}, bf16[224,128]{1,0:T(8,128)(2,1)S(1)}, u32[]{:S(2)}, u32[]{:S(2)}) collective-permute-start(bf16[224,128]{1,0:T(8,128)(2,1)S(1)} %shard_map.85.refs_0_), channel_id=1, source_target_pairs={{0,8},{1,9},{2,10},{3,11},{4,12},{5,13},{6,14},{7,15},{8,0},{9,1},... | collective-permute-start | bytes 172040 | tf_op jit(solution)/shard_map/ppermute | solution.py:491
  22.6 6.2 %collective-permute-start.9 = (bf16[224,128]{1,0:T(8,128)(2,1)S(1)}, bf16[224,128]{1,0:T(8,128)(2,1)S(1)}, u32[]{:S(2)}, u32[]{:S(2)}) collective-permute-start(bf16[224,128]{1,0:T(8,128)(2,1)S(1)} %shard_map.85.refs_0_), channel_id=1, source_target_pairs={{0,12},{1,13},{2,14},{3,15},{4,8},{5,9},{6,10},{7,11},{8,4},{9,5},... | collective-permute-start | bytes 172040 | tf_op jit(solution)/shard_map/ppermute | solution.py:491
  23.6 5.7 %collective-permute-start.8 = (bf16[224,128]{1,0:T(8,128)(2,1)S(1)}, bf16[224,128]{1,0:T(8,128)(2,1)S(1)}, u32[]{:S(2)}, u32[]{:S(2)}) collective-permute-start(bf16[224,128]{1,0:T(8,128)(2,1)S(1)} %shard_map.85.refs_0_), channel_id=1, source_target_pairs={{0,4},{1,5},{2,6},{3,7},{4,0},{5,1},{6,2},{7,3},{8,12},{9,13},{10,... | collective-permute-start | bytes 172040 | tf_op jit(solution)/shard_map/ppermute | solution.py:491
  29.4 6.7 %collective-permute-start.13 = (bf16[416,128]{1,0:T(8,128)(2,1)S(1)}, bf16[416,128]{1,0:T(8,128)(2,1)S(1)}, u32[]{:S(2)}, u32[]{:S(2)}) collective-permute-start(bf16[416,128]{1,0:T(8,128)(2,1)S(1)} %shard_map.88.row_a.refs_0_), channel_id=1, source_target_pairs={{0,3},{1,2},{2,1},{3,0},{4,7},{5,6},{6,5},{7,4},{8,11},{9,10},{10,... | collective-permute-start | bytes 319496 | tf_op jit(solution)/shard_map/ppermute | solution.py:491
  30.9 6.5 %collective-permute-start.12 = (bf16[416,128]{1,0:T(8,128)(2,1)S(1)}, bf16[416,128]{1,0:T(8,128)(2,1)S(1)}, u32[]{:S(2)}, u32[]{:S(2)}) collective-permute-start(bf16[416,128]{1,0:T(8,128)(2,1)S(1)} %shard_map.88.row_a.refs_0_), channel_id=1, source_target_pairs={{0,2},{1,3},{2,0},{3,1},{4,6},{5,7},{6,4},{7,5},{8,10},{9,11},{10,... | collective-permute-start | bytes 319496 | tf_op jit(solution)/shard_map/ppermute | solution.py:491
  31.5 6.1 %collective-permute-start.11 = (bf16[416,128]{1,0:T(8,128)(2,1)S(1)}, bf16[416,128]{1,0:T(8,128)(2,1)S(1)}, u32[]{:S(2)}, u32[]{:S(2)}) collective-permute-start(bf16[416,128]{1,0:T(8,128)(2,1)S(1)} %shard_map.88.row_a.refs_0_), channel_id=1, source_target_pairs={{0,1},{1,0},{2,3},{3,2},{4,5},{5,4},{6,7},{7,6},{8,9},{9,8},{10,11... | collective-permute-start | bytes 319496 | tf_op jit(solution)/shard_map/ppermute | solution.py:491
  37.6 1.3 %collective-permute-start.14 = (f32[160,128]{1,0:T(8,128)S(1)}, f32[160,128]{1,0:T(8,128)S(1)}, u32[]{:S(2)}, u32[]{:S(2)}) collective-permute-start(f32[160,128]{1,0:T(8,128)S(1)} %shard_map.91.mine), channel_id=1, source_target_pairs={{0,16},{16,0},{1,17},{17,1},{2,18},{18,2},{3,19},{19,3},{4,20},{20... | collective-permute-start | bytes 245768 | tf_op jit(solution)/shard_map/ppermute | solution.py:491

commit v11 on v10

--- a/solution.py
+++ b/solution.py
@@ -81,7 +81,7 @@
         return now
 
     zero = jnp.zeros((SIDE, LANES), F32)
-    last = lax.fori_loop(0, PAIRS, step, zero, unroll=4)
+    last = lax.fori_loop(0, PAIRS, step, zero, unroll=8)
     put(PAIRS, last, zero)
 
 

time: 39.8 us -> 39.8 us (level)
  Pallas kernels: 9.65 us -> 9.04 us
  waiting for transfers between devices: 11 us -> 11.6 us
    ppermute x15, waiting for transfers between devices: 11 us -> 11.6 us  [swap(): return lax.ppermute(x, axis, [(i, i ^ k) for i in range(n)])]
    pallas_call x17, Pallas kernels: 9.65 us -> 9.04 us  [call(): pl.pallas_call(kernel, out_shape=shapes, in_specs=[whole] * len(args), ou...]
  transfers between devices with their start and end apart: 15 -> 15, of which waited for: 11 -> 11; matrix products, arithmetic and copies ran while one was open for 0% -> 0% of each run, Pallas kernels for 19% -> 17%
where the time goes in v11:
time: 39.8 us; the launch traced here: 39.7 us
  starting transfers between devices  16.5 us (41%)
  waiting for transfers between devices  11.6 us (29%)
  Pallas kernels  9.04 us (23%)
  local copies, waits for them, and re-layouts  1.71 us (4%)
  between operations  0.79 us (2%)
    ppermute x15, starting transfers between devices, swap(): return lax.ppermute(x, axis, [(i, i ^ k) for i in range(n)])  16.5 us
    ppermute x15, waiting for transfers between devices, swap(): return lax.ppermute(x, axis, [(i, i ^ k) for i in range(n)])  11.6 us
    pallas_call x17, Pallas kernels, call(): pl.pallas_call(kernel, out_shape=shapes, in_specs=[whole] * len(args), ou...  9.04 us
    slice x1, local copies, waits for them, and re-layouts, body(): x[SIDE - 16:]  1.04 us
  transfers between devices with their start and end apart: 15, of which 11 were waited for; matrix products, arithmetic and copies ran while one was open for 0% of the time, Pallas kernels for 17%

profile of v11, /device:TPU:0, one launch (start us, length us, event | category | flops | bytes accessed | tf_op | source)
XLA Modules:
  0.0 39.7 jit_solution(8389080905350560109)
XLA Ops:
  0.6 1.0 %slice_bitcast_fusion = (bf16[16,4096]{1,0:T(8,128)(2,1)S(1)}, bf16[16,4096]{1,0:T(8,128)(2,1)S(1)}) fusion(bf16[1,64,4096]{2,1,0:T(8,128)(2,1)} %param.5), kind=kLoop, calls=%fused_computation | loop fusion | bytes 524288 | tf_op jit(solution)/shard_map/slice | solution.py:542
  1.7 4.1 %collective-permute-start.2 = (bf16[64,128]{1,0:T(8,128)(2,1)S(1)}, bf16[64,128]{1,0:T(8,128)(2,1)S(1)}, u32[]{:S(2)}, u32[]{:S(2)}) collective-permute-start(bf16[64,128]{1,0:T(8,128)(2,1)S(1)} %shard_map.76.refs_0_), channel_id=1, source_target_pairs={{0,8},{1,9},{2,10},{3,11},{4,12},{5,13},{6,14},{7,15},{8,0},{9,1},... | collective-permute-start | bytes 49160 | tf_op jit(solution)/shard_map/ppermute | solution.py:491
  5.8 1.3 %collective-permute-start.1 = (bf16[64,128]{1,0:T(8,128)(2,1)S(1)}, bf16[64,128]{1,0:T(8,128)(2,1)S(1)}, u32[]{:S(2)}, u32[]{:S(2)}) collective-permute-start(bf16[64,128]{1,0:T(8,128)(2,1)S(1)} %shard_map.76.refs_0_), channel_id=1, source_target_pairs={{0,12},{1,13},{2,14},{3,15},{4,8},{5,9},{6,10},{7,11},{8,4},{9,5},... | collective-permute-start | bytes 49160 | tf_op jit(solution)/shard_map/ppermute | solution.py:491
  7.5 0.6 %shard_map.77 = (bf16[2112,128]{1,0:T(8,128)(2,1)S(1)}, bf16[2112,128]{1,0:T(8,128)(2,1)S(1)}, bf16[2112,128]{1,0:T(8,128)(2,1)S(1)}, f32[4,40,128]{2,1,0:T(8,128)S(1)}, bf16[64,128]{1,0:T(8,128)(2,1)S(1)}) custom-call(bf16[64,4096]{1,0:T(8,128)(2,1)S(1)} %bitcast.13), custom_call_target="tpu_custom_call" | custom-call | bytes 2097152 | tf_op jit(solution)/shard_map/pallas_call | solution.py:26
  8.1 1.0 %shard_map.79.s_ref = f32[2048,128]{1,0:T(8,128)S(1)} custom-call(bf16[2112,128]{1,0:T(8,128)(2,1)S(1)} %get-tuple-element.63.p0, bf16[2112,128]{1,0:T(8,128)(2,1)S(1)} %get-tuple-element.64.p1, bf16[2112,128]{1,0:T(8,128)(2,1)S(1)} %get-tuple-element.65.p2, bf16[3,128,256]{2,1,0:T(8,128)(2,1)S(1)} %get-tuple-element.66.w_ref), custom_call_target="tpu_custom_call" | custom-call | flops 402653184 | bytes 3145728 | tf_op jit(solution)/shard_map/pallas_call | solution.py:26
  9.1 2.2 %collective-permute-done.1.refs_2_ = bf16[64,128]{1,0:T(8,128)(2,1)S(1)} collective-permute-done((bf16[64,128]{1,0:T(8,128)(2,1)S(1)}, bf16[64,128]{1,0:T(8,128)(2,1)S(1)}, u32[]{:S(2)}, u32[]{:S(2)}) %collective-permute-start.1) | collective-permute-done | bytes 16416 | tf_op jit(solution)/shard_map/ppermute | solution.py:491
  11.4 2.5 %collective-permute-start.5 = (bf16[256,128]{1,0:T(8,128)(2,1)S(1)}, bf16[256,128]{1,0:T(8,128)(2,1)S(1)}, u32[]{:S(2)}, u32[]{:S(2)}) collective-permute-start(bf16[256,128]{1,0:T(8,128)(2,1)S(1)} %shard_map.80.rows_a), channel_id=1, source_target_pairs={{0,3},{1,2},{2,1},{3,0},{4,7},{5,6},{6,5},{7,4},{8,11},{9,10},{10,... | collective-permute-start | bytes 196616 | tf_op jit(solution)/shard_map/ppermute | solution.py:491
  14.9 0.6 %copy-done.4 = f32[64]{0:T(128)S(1)} copy-done((f32[64]{0:T(128)S(1)}, f32[64]{0:T(128)}, u32[]{:S(2)}) %copy-start.4) | copy-done | bytes 280
  15.6 1.7 %shard_map.82 = (bf16[2048,128]{1,0:T(8,128)(2,1)S(1)}, f32[3,128,256]{2,1,0:T(8,128)S(1)}, f32[8,128]{1,0:T(8,128)S(1)}, f32[64,128]{1,0:T(8,128)S(1)}) custom-call(f32[2048,128]{1,0:T(8,128)S(1)} %shard_map.79.s_ref, f32[1,64]{1,0:T(1,128)S(1)} %bitcast.15, bf16[64,4096]{1,0:T(8,128)(2,1)S(1)} %bitcast.11, bf16[2112,128]{1,0:T(8,128)(2,1)S(1)} %get-tuple-element.63.p0, ...), custom_call_target="tpu_custom_call" | custom-call | flops 402653184 | bytes 3145728 | tf_op jit(solution)/shard_map/pallas_call | solution.py:26
  18.7 1.3 %shard_map.83 = (f32[64,128]{1,0:T(8,128)S(1)}, bf16[128,128]{1,0:T(8,128)(2,1)S(1)}, bf16[160,128]{1,0:T(8,128)(2,1)S(1)}, bf16[224,128]{1,0:T(8,128)(2,1)S(1)}) custom-call(f32[2048,128]{1,0:T(8,128)S(1)} %shard_map.79.s_ref, f32[1,64]{1,0:T(1,128)S(1)} %bitcast.16, bf16[64,4096]{1,0:T(8,128)(2,1)S(1)} %bitcast.12, ...), custom_call_target="tpu_custom_call" | custom-call | bytes 1048576 | tf_op jit(solution)/shard_map/pallas_call | solution.py:26
  20.4 0.9 %collective-permute-done.7.other.rest_0_ = bf16[224,128]{1,0:T(8,128)(2,1)S(1)} collective-permute-done((bf16[224,128]{1,0:T(8,128)(2,1)S(1)}, bf16[224,128]{1,0:T(8,128)(2,1)S(1)}, u32[]{:S(2)}, u32[]{:S(2)}) %collective-permute-start.7) | collective-permute-done | bytes 57376 | tf_op jit(solution)/shard_map/ppermute | solution.py:491
  21.3 1.2 %collective-permute-start.10 = (bf16[224,128]{1,0:T(8,128)(2,1)S(1)}, bf16[224,128]{1,0:T(8,128)(2,1)S(1)}, u32[]{:S(2)}, u32[]{:S(2)}) collective-permute-start(bf16[224,128]{1,0:T(8,128)(2,1)S(1)} %shard_map.85.refs_0_), channel_id=1, source_target_pairs={{0,8},{1,9},{2,10},{3,11},{4,12},{5,13},{6,14},{7,15},{8,0},{9,1},... | collective-permute-start | bytes 172040 | tf_op jit(solution)/shard_map/ppermute | solution.py:491
  22.6 1.0 %collective-permute-start.9 = (bf16[224,128]{1,0:T(8,128)(2,1)S(1)}, bf16[224,128]{1,0:T(8,128)(2,1)S(1)}, u32[]{:S(2)}, u32[]{:S(2)}) collective-permute-start(bf16[224,128]{1,0:T(8,128)(2,1)S(1)} %shard_map.85.refs_0_), channel_id=1, source_target_pairs={{0,12},{1,13},{2,14},{3,15},{4,8},{5,9},{6,10},{7,11},{8,4},{9,5},... | collective-permute-start | bytes 172040 | tf_op jit(solution)/shard_map/ppermute | solution.py:491
  23.5 1.4 %collective-permute-start.8 = (bf16[224,128]{1,0:T(8,128)(2,1)S(1)}, bf16[224,128]{1,0:T(8,128)(2,1)S(1)}, u32[]{:S(2)}, u32[]{:S(2)}) collective-permute-start(bf16[224,128]{1,0:T(8,128)(2,1)S(1)} %shard_map.85.refs_0_), channel_id=1, source_target_pairs={{0,4},{1,5},{2,6},{3,7},{4,0},{5,1},{6,2},{7,3},{8,12},{9,13},{10,... | collective-permute-start | bytes 172040 | tf_op jit(solution)/shard_map/ppermute | solution.py:491
  25.7 2.0 %collective-permute-done.10.refs_3_ = bf16[224,128]{1,0:T(8,128)(2,1)S(1)} collective-permute-done((bf16[224,128]{1,0:T(8,128)(2,1)S(1)}, bf16[224,128]{1,0:T(8,128)(2,1)S(1)}, u32[]{:S(2)}, u32[]{:S(2)}) %collective-permute-start.10) | collective-permute-done | bytes 57376 | tf_op jit(solution)/shard_map/ppermute | solution.py:491
  27.7 1.0 %collective-permute-done.9.refs_2_ = bf16[224,128]{1,0:T(8,128)(2,1)S(1)} collective-permute-done((bf16[224,128]{1,0:T(8,128)(2,1)S(1)}, bf16[224,128]{1,0:T(8,128)(2,1)S(1)}, u32[]{:S(2)}, u32[]{:S(2)}) %collective-permute-start.9) | collective-permute-done | bytes 57376 | tf_op jit(solution)/shard_map/ppermute | solution.py:491
  28.7 0.6 %collective-permute-done.8.refs_1_ = bf16[224,128]{1,0:T(8,128)(2,1)S(1)} collective-permute-done((bf16[224,128]{1,0:T(8,128)(2,1)S(1)}, bf16[224,128]{1,0:T(8,128)(2,1)S(1)}, u32[]{:S(2)}, u32[]{:S(2)}) %collective-permute-start.8) | collective-permute-done | bytes 57376 | tf_op jit(solution)/shard_map/ppermute | solution.py:491
  29.4 1.6 %collective-permute-start.13 = (bf16[416,128]{1,0:T(8,128)(2,1)S(1)}, bf16[416,128]{1,0:T(8,128)(2,1)S(1)}, u32[]{:S(2)}, u32[]{:S(2)}) collective-permute-start(bf16[416,128]{1,0:T(8,128)(2,1)S(1)} %shard_map.88.row_a.refs_0_), channel_id=1, source_target_pairs={{0,3},{1,2},{2,1},{3,0},{4,7},{5,6},{6,5},{7,4},{8,11},{9,10},{10,... | collective-permute-start | bytes 319496 | tf_op jit(solution)/shard_map/ppermute | solution.py:491
  31.5 1.5 %collective-permute-start.11 = (bf16[416,128]{1,0:T(8,128)(2,1)S(1)}, bf16[416,128]{1,0:T(8,128)(2,1)S(1)}, u32[]{:S(2)}, u32[]{:S(2)}) collective-permute-start(bf16[416,128]{1,0:T(8,128)(2,1)S(1)} %shard_map.88.row_a.refs_0_), channel_id=1, source_target_pairs={{0,1},{1,0},{2,3},{3,2},{4,5},{5,4},{6,7},{7,6},{8,9},{9,8},{10,11... | collective-permute-start | bytes 319496 | tf_op jit(solution)/shard_map/ppermute | solution.py:491
  32.9 1.0 %shard_map.89.inner = f32[2048,128]{1,0:T(8,128)S(1)} custom-call(bf16[2112,128]{1,0:T(8,128)(2,1)S(1)} %get-tuple-element.113.p0, bf16[2112,128]{1,0:T(8,128)(2,1)S(1)} %get-tuple-element.114.p1, bf16[2112,128]{1,0:T(8,128)(2,1)S(1)} %get-tuple-element.115.p2, bf16[3,256,128]{2,1,0:T(8,128)(2,1)S(1)} %get-tuple-element.93.wb_ref), custom_call_target="tpu_custom_call" | custom-call | flops 402653184 | bytes 3145728 | tf_op jit(solution)/shard_map/pallas_call | solution.py:26
  33.9 2.1 %collective-permute-done.13.row_d.refs_3_ = bf16[416,128]{1,0:T(8,128)(2,1)S(1)} collective-permute-done((bf16[416,128]{1,0:T(8,128)(2,1)S(1)}, bf16[416,128]{1,0:T(8,128)(2,1)S(1)}, u32[]{:S(2)}, u32[]{:S(2)}) %collective-permute-start.13) | collective-permute-done | bytes 106528 | tf_op jit(solution)/shard_map/ppermute | solution.py:491
  36.1 1.4 %collective-permute-done.12.row_c.refs_2_ = bf16[416,128]{1,0:T(8,128)(2,1)S(1)} collective-permute-done((bf16[416,128]{1,0:T(8,128)(2,1)S(1)}, bf16[416,128]{1,0:T(8,128)(2,1)S(1)}, u32[]{:S(2)}, u32[]{:S(2)}) %collective-permute-start.12) | collective-permute-done | bytes 106528 | tf_op jit(solution)/shard_map/ppermute | solution.py:491
  37.7 1.2 %shard_map.90 = bf16[64,4096]{1,0:T(8,128)(2,1)} custom-call(bf16[416,128]{1,0:T(8,128)(2,1)S(1)} %shard_map.88.row_a.refs_0_, bf16[416,128]{1,0:T(8,128)(2,1)S(1)} %collective-permute-done.11.row_b.refs_1_, bf16[416,128]{1,0:T(8,128)(2,1)S(1)} %collective-permute-done.12.row_c.refs_2_, bf16[416,128]{1,0:T(8,128)(2,1)S(1)} %collective-permute-done.13.row_d.refs_3_, ...), custom_call_target="tpu_custom_call" | custom-call | bytes 2097152 | tf_op jit(solution)/shard_map/pallas_call | solution.py:26
  39.0 0.7 %shard_map.92 = (f32[64,576]{1,0:T(8,128)}, f32[1,64]{1,0:T(1,128)}) custom-call(f32[160,128]{1,0:T(8,128)S(1)} %shard_map.91.mine, f32[160,128]{1,0:T(8,128)S(1)} %collective-permute-done.14.other), custom_call_target="tpu_custom_call" | custom-call | tf_op jit(solution)/shard_map/pallas_call | solution.py:26
  (34 shorter events, 4.8 us)
Async XLA Ops:
  0.6 6.9 %copy-start.1 = (bf16[1,64,4096]{2,1,0:T(8,128)(2,1)S(1)}, bf16[1,64,4096]{2,1,0:T(8,128)(2,1)}, u32[]{:S(2)}) copy-start(bf16[1,64,4096]{2,1,0:T(8,128)(2,1)} %param.5) | copy-start | bytes 1572868
  1.7 5.7 %copy-start.3 = (bf16[576,64]{0,1:T(8,128)(2,1)S(1)}, bf16[576,64]{0,1:T(8,128)(2,1)}, u32[]{:S(2)}) copy-start(bf16[576,64]{0,1:T(8,128)(2,1)} %param.6) | copy-start | bytes 221188
  1.7 7.4 %collective-permute-start.2 = (bf16[64,128]{1,0:T(8,128)(2,1)S(1)}, bf16[64,128]{1,0:T(8,128)(2,1)S(1)}, u32[]{:S(2)}, u32[]{:S(2)}) collective-permute-start(bf16[64,128]{1,0:T(8,128)(2,1)S(1)} %shard_map.76.refs_0_), channel_id=1, source_target_pairs={{0,8},{1,9},{2,10},{3,11},{4,12},{5,13},{6,14},{7,15},{8,0},{9,1},... | collective-permute-start | bytes 49160 | tf_op jit(solution)/shard_map/ppermute | solution.py:491
  5.8 5.5 %collective-permute-start.1 = (bf16[64,128]{1,0:T(8,128)(2,1)S(1)}, bf16[64,128]{1,0:T(8,128)(2,1)S(1)}, u32[]{:S(2)}, u32[]{:S(2)}) collective-permute-start(bf16[64,128]{1,0:T(8,128)(2,1)S(1)} %shard_map.76.refs_0_), channel_id=1, source_target_pairs={{0,12},{1,13},{2,14},{3,15},{4,8},{5,9},{6,10},{7,11},{8,4},{9,5},... | collective-permute-start | bytes 49160 | tf_op jit(solution)/shard_map/ppermute | solution.py:491
  7.2 4.2 %collective-permute-start = (bf16[64,128]{1,0:T(8,128)(2,1)S(1)}, bf16[64,128]{1,0:T(8,128)(2,1)S(1)}, u32[]{:S(2)}, u32[]{:S(2)}) collective-permute-start(bf16[64,128]{1,0:T(8,128)(2,1)S(1)} %shard_map.76.refs_0_), channel_id=1, source_target_pairs={{0,4},{1,5},{2,6},{3,7},{4,0},{5,1},{6,2},{7,3},{8,12},{9,13},{10,... | collective-permute-start | bytes 49160 | tf_op jit(solution)/shard_map/ppermute | solution.py:491
  8.1 6.8 %copy-start = (bf16[1,64,4096]{2,1,0:T(8,128)(2,1)S(1)}, bf16[1,64,4096]{2,1,0:T(8,128)(2,1)}, u32[]{:S(2)}) copy-start(bf16[1,64,4096]{2,1,0:T(8,128)(2,1)} %param.8) | copy-start | bytes 1572868
  11.4 6.2 %collective-permute-start.5 = (bf16[256,128]{1,0:T(8,128)(2,1)S(1)}, bf16[256,128]{1,0:T(8,128)(2,1)S(1)}, u32[]{:S(2)}, u32[]{:S(2)}) collective-permute-start(bf16[256,128]{1,0:T(8,128)(2,1)S(1)} %shard_map.80.rows_a), channel_id=1, source_target_pairs={{0,3},{1,2},{2,1},{3,0},{4,7},{5,6},{6,5},{7,4},{8,11},{9,10},{10,... | collective-permute-start | bytes 196616 | tf_op jit(solution)/shard_map/ppermute | solution.py:491
  13.9 4.3 %collective-permute-start.4 = (bf16[256,128]{1,0:T(8,128)(2,1)S(1)}, bf16[256,128]{1,0:T(8,128)(2,1)S(1)}, u32[]{:S(2)}, u32[]{:S(2)}) collective-permute-start(bf16[256,128]{1,0:T(8,128)(2,1)S(1)} %shard_map.80.rows_a), channel_id=1, source_target_pairs={{0,2},{1,3},{2,0},{3,1},{4,6},{5,7},{6,4},{7,5},{8,10},{9,11},{10,... | collective-permute-start | bytes 196616 | tf_op jit(solution)/shard_map/ppermute | solution.py:491
  14.4 4.3 %collective-permute-start.3 = (bf16[256,128]{1,0:T(8,128)(2,1)S(1)}, bf16[256,128]{1,0:T(8,128)(2,1)S(1)}, u32[]{:S(2)}, u32[]{:S(2)}) collective-permute-start(bf16[256,128]{1,0:T(8,128)(2,1)S(1)} %shard_map.80.rows_a), channel_id=1, source_target_pairs={{0,1},{1,0},{2,3},{3,2},{4,5},{5,4},{6,7},{7,6},{8,9},{9,8},{10,11... | collective-permute-start | bytes 196616 | tf_op jit(solution)/shard_map/ppermute | solution.py:491
  14.9 0.7 %copy-start.4 = (f32[64]{0:T(128)S(1)}, f32[64]{0:T(128)}, u32[]{:S(2)}) copy-start(f32[64]{0:T(128)} %param.7) | copy-start | bytes 772
  14.9 3.7 %collective-permute-start.6 = (bf16[64,128]{1,0:T(8,128)(2,1)S(1)}, bf16[64,128]{1,0:T(8,128)(2,1)S(1)}, u32[]{:S(2)}, u32[]{:S(2)}) collective-permute-start(bf16[64,128]{1,0:T(8,128)(2,1)S(1)} %get-tuple-element.86), channel_id=1, source_target_pairs={{0,16},{16,0},{1,17},{17,1},{2,18},{18,2},{3,19},{19,3},{4,20},{20... | collective-permute-start | bytes 49160 | tf_op jit(solution)/shard_map/ppermute | solution.py:491
  15.6 1.7 %copy-start.2 = (s32[16,260]{1,0:T(8,128)S(1)}, s32[16,260]{1,0:T(8,128)}, u32[]{:S(2)}) copy-start(s32[16,260]{1,0:T(8,128)} %index_ref.1) | copy-start | bytes 49924
  20.0 1.3 %collective-permute-start.7 = (bf16[224,128]{1,0:T(8,128)(2,1)S(1)}, bf16[224,128]{1,0:T(8,128)(2,1)S(1)}, u32[]{:S(2)}, u32[]{:S(2)}) collective-permute-start(bf16[224,128]{1,0:T(8,128)(2,1)S(1)} %get-tuple-element.91), channel_id=1, source_target_pairs={{0,16},{16,0},{1,17},{17,1},{2,18},{18,2},{3,19},{19,3},{4,20},{20... | collective-permute-start | bytes 172040 | tf_op jit(solution)/shard_map/ppermute | solution.py:491
  21.3 6.4 %collective-permute-start.10 = (bf16[224,128]{1,0:T(8,128)(2,1)S(1)}, bf16[224,128]{1,0:T(8,128)(2,1)S(1)}, u32[]{:S(2)}, u32[]{:S(2)}) collective-permute-start(bf16[224,128]{1,0:T(8,128)(2,1)S(1)} %shard_map.85.refs_0_), channel_id=1, source_target_pairs={{0,8},{1,9},{2,10},{3,11},{4,12},{5,13},{6,14},{7,15},{8,0},{9,1},... | collective-permute-start | bytes 172040 | tf_op jit(solution)/shard_map/ppermute | solution.py:491
  22.6 6.2 %collective-permute-start.9 = (bf16[224,128]{1,0:T(8,128)(2,1)S(1)}, bf16[224,128]{1,0:T(8,128)(2,1)S(1)}, u32[]{:S(2)}, u32[]{:S(2)}) collective-permute-start(bf16[224,128]{1,0:T(8,128)(2,1)S(1)} %shard_map.85.refs_0_), channel_id=1, source_target_pairs={{0,12},{1,13},{2,14},{3,15},{4,8},{5,9},{6,10},{7,11},{8,4},{9,5},... | collective-permute-start | bytes 172040 | tf_op jit(solution)/shard_map/ppermute | solution.py:491
  23.5 5.8 %collective-permute-start.8 = (bf16[224,128]{1,0:T(8,128)(2,1)S(1)}, bf16[224,128]{1,0:T(8,128)(2,1)S(1)}, u32[]{:S(2)}, u32[]{:S(2)}) collective-permute-start(bf16[224,128]{1,0:T(8,128)(2,1)S(1)} %shard_map.85.refs_0_), channel_id=1, source_target_pairs={{0,4},{1,5},{2,6},{3,7},{4,0},{5,1},{6,2},{7,3},{8,12},{9,13},{10,... | collective-permute-start | bytes 172040 | tf_op jit(solution)/shard_map/ppermute | solution.py:491
  29.4 6.7 %collective-permute-start.13 = (bf16[416,128]{1,0:T(8,128)(2,1)S(1)}, bf16[416,128]{1,0:T(8,128)(2,1)S(1)}, u32[]{:S(2)}, u32[]{:S(2)}) collective-permute-start(bf16[416,128]{1,0:T(8,128)(2,1)S(1)} %shard_map.88.row_a.refs_0_), channel_id=1, source_target_pairs={{0,3},{1,2},{2,1},{3,0},{4,7},{5,6},{6,5},{7,4},{8,11},{9,10},{10,... | collective-permute-start | bytes 319496 | tf_op jit(solution)/shard_map/ppermute | solution.py:491
  30.9 6.5 %collective-permute-start.12 = (bf16[416,128]{1,0:T(8,128)(2,1)S(1)}, bf16[416,128]{1,0:T(8,128)(2,1)S(1)}, u32[]{:S(2)}, u32[]{:S(2)}) collective-permute-start(bf16[416,128]{1,0:T(8,128)(2,1)S(1)} %shard_map.88.row_a.refs_0_), channel_id=1, source_target_pairs={{0,2},{1,3},{2,0},{3,1},{4,6},{5,7},{6,4},{7,5},{8,10},{9,11},{10,... | collective-permute-start | bytes 319496 | tf_op jit(solution)/shard_map/ppermute | solution.py:491
  31.5 6.1 %collective-permute-start.11 = (bf16[416,128]{1,0:T(8,128)(2,1)S(1)}, bf16[416,128]{1,0:T(8,128)(2,1)S(1)}, u32[]{:S(2)}, u32[]{:S(2)}) collective-permute-start(bf16[416,128]{1,0:T(8,128)(2,1)S(1)} %shard_map.88.row_a.refs_0_), channel_id=1, source_target_pairs={{0,1},{1,0},{2,3},{3,2},{4,5},{5,4},{6,7},{7,6},{8,9},{9,8},{10,11... | collective-permute-start | bytes 319496 | tf_op jit(solution)/shard_map/ppermute | solution.py:491
  37.6 1.3 %collective-permute-start.14 = (f32[160,128]{1,0:T(8,128)S(1)}, f32[160,128]{1,0:T(8,128)S(1)}, u32[]{:S(2)}, u32[]{:S(2)}) collective-permute-start(f32[160,128]{1,0:T(8,128)S(1)} %shard_map.91.mine), channel_id=1, source_target_pairs={{0,16},{16,0},{1,17},{17,1},{2,18},{18,2},{3,19},{19,3},{4,20},{20... | collective-permute-start | bytes 245768 | tf_op jit(solution)/shard_map/ppermute | solution.py:491
